TPU v7x, 32 devices: a whole 2x2x4 slice. The times are simulated.
32 devices in a mesh: seq: 8 (over z, x), head: 4 (over y, core).
Axes of the slice: x: 2, y: 2, z: 4, core: 2. Of those that a mesh axis runs over, the one named last changes fastest.
Arguments:
- query: bfloat16 [4096, 16, 128], P('seq', 'head'), may hold values from -6 to 6
- key: bfloat16 [4096, 16, 128], P('seq', 'head'), may hold values from -6 to 6
- value: bfloat16 [4096, 16, 128], P('seq', 'head'), may hold values from -1.5 to 1.5
- beta: float32 [16, 4096], P('head', 'seq'), may hold values from 0.1 to 2
- log_decay: float32 [16, 4096], P('head', 'seq')
- out_weight: bfloat16 [2048, 2048], P('head'), may hold values from -0.125 to 0.125
Outputs:
- mixed: bfloat16 [4096, 2048], P(('seq', 'head'))
All inputs are finite; a program needn't handle non-finite values.
Results may differ from a plain program's by a relative error of at most 0.0075.
Values may be sent and summed in bfloat16 or wider, within the bound.
No kernel may reach another device: no remote copies, remote signals or barrier semaphores. Data moves between devices by JAX's collectives and lax.ppermute only.
A program may use at most 128 MiB of HBM per device.

v0:
```python
from functools import partial

import jax
import jax.numpy as jnp
from jax import lax
from jax.sharding import PartitionSpec as P

BLOCK = 128


EXACT = lax.Precision.HIGHEST


def prefix_2(value, axis, join, neutral):
    count, mine = (lax.axis_size(axis), lax.axis_index(axis))
    pieces = lax.all_gather(value, axis)
    total = jnp.full_like(value, 0) + jnp.asarray(neutral, value.dtype)

    def step(position, total):
        longer = join(total, pieces[position])
        return jnp.where(position < mine, longer, total)

    return lax.fori_loop(0, count - 1, step, total)


def unit_rows(tensor):
    widened = tensor.astype(jnp.float32)
    return widened * lax.rsqrt(jnp.sum(widened * widened, axis=-1, keepdims=True) + 1e-06)


def contract(pattern, left_side, right_side):
    return jnp.einsum(pattern, left_side, right_side, precision=EXACT)


def blocks_first(tensor, block_count):
    rows_here, head_count, feature_width = tensor.shape
    return tensor.reshape(
        block_count, rows_here // block_count, head_count, feature_width
    ).transpose(0, 2, 1, 3)


def prepare(query, key, value, beta, log_decay):
    rows_here, head_count, key_width = key.shape
    value_width = value.shape[-1]
    block_count = rows_here // BLOCK
    queries = blocks_first(unit_rows(query), block_count)
    keys_block = blocks_first(unit_rows(key), block_count)
    values_block = blocks_first(value.astype(jnp.float32), block_count)
    strengths = beta.reshape(head_count, block_count, BLOCK).transpose(1, 0, 2)
    log_sums = jnp.cumsum(
        log_decay.reshape(head_count, block_count, BLOCK).transpose(1, 0, 2), axis=-1
    )
    log_spans = log_sums[..., :, None] - log_sums[..., None, :]
    row_index = lax.broadcasted_iota(jnp.int32, (BLOCK, BLOCK), 0)
    col_index = lax.broadcasted_iota(jnp.int32, (BLOCK, BLOCK), 1)
    strict = row_index > col_index
    within = row_index >= col_index
    decay_in = jnp.where(within, jnp.exp(jnp.where(within, log_spans, 0.0)), 0.0)
    key_gram = contract("bhtk,bhsk->bhts", keys_block, keys_block)
    identity_block = jnp.eye(BLOCK, dtype=jnp.float32)
    unit_lower = identity_block + strengths[..., :, None] * key_gram * jnp.where(
        strict, decay_in, 0.0
    )
    growth = jnp.exp(log_sums)
    right_sides = jnp.concatenate(
        [strengths[..., None] * values_block, (strengths * growth)[..., None] * keys_block], axis=-1
    )
    solved = lax.linalg.triangular_solve(
        unit_lower, right_sides, left_side=True, lower=True, unit_diagonal=True
    )
    carried_values = solved[..., :value_width]
    key_factor = solved[..., value_width:]
    query_key = contract("bhtk,bhsk->bhts", queries, keys_block) * decay_in
    fading = keys_block * jnp.exp(log_sums[..., -1:] - log_sums)[..., None]
    end_decay = jnp.exp(log_sums[..., -1])
    return (queries, key_factor, carried_values, query_key, growth, fading, end_decay)


def advance(running_state, pieces, emitting):
    queries, key_factor, carried_values, query_key, growth, fading, end_decay = pieces
    fresh_terms = carried_values - contract("hck,hkw->hcw", key_factor, running_state)
    if emitting:
        result = growth[..., None] * contract("hck,hkw->hcw", queries, running_state) + contract(
            "hcs,hsw->hcw", query_key, fresh_terms
        )
    else:
        result = None
    running_state = end_decay[:, None, None] * running_state + contract(
        "hck,hcw->hkw", fading, fresh_terms
    )
    return (running_state, result)


def body(query, key, value, beta, log_decay, out_weight):
    rows_here, head_count, key_width = key.shape
    value_width = value.shape[-1]
    factors = prepare(query, key, value, beta, log_decay)
    queries, key_factor, carried_values, query_key, growth, fading, end_decay = factors
    block_count = queries.shape[0]
    identity_map = jnp.broadcast_to(
        jnp.eye(key_width, dtype=jnp.float32), (head_count, key_width, key_width)
    )
    identity_pair = jnp.concatenate(
        [identity_map, jnp.zeros((head_count, key_width, value_width), jnp.float32)], axis=-1
    )
    widened_values = jnp.concatenate(
        [jnp.zeros((block_count, head_count, BLOCK, key_width), jnp.float32), carried_values],
        axis=-1,
    )
    widened_pieces = (queries, key_factor, widened_values, query_key, growth, fading, end_decay)
    summary, local_rows = lax.scan(partial(advance, emitting=False), identity_pair, widened_pieces)

    def compose(earlier, later):
        applied = contract("hij,hjw->hiw", later[..., :key_width], earlier)
        return jnp.concatenate(
            [applied[..., :key_width], applied[..., key_width:] + later[..., key_width:]], axis=-1
        )

    prefix = prefix_2(summary, "seq", compose, identity_pair)
    entering = prefix[..., key_width:]
    final_state, outputs = lax.scan(partial(advance, emitting=True), entering, factors)
    attended = (
        outputs.transpose(0, 2, 1, 3)
        .reshape(rows_here, head_count * value_width)
        .astype(jnp.bfloat16)
    )
    mixed = lax.psum_scatter(
        jnp.dot(attended, out_weight, preferred_element_type=jnp.float32),
        "head",
        scatter_dimension=0,
        tiled=True,
    )
    return mixed.astype(jnp.bfloat16)


def solution(mesh):
    in_specs = (
        P("seq", "head", None),
        P("seq", "head", None),
        P("seq", "head", None),
        P("head", "seq"),
        P("head", "seq"),
        P("head", None),
    )
    out_specs = P(("seq", "head"), None)
    return jax.shard_map(body, mesh=mesh, in_specs=in_specs, out_specs=out_specs, check_vma=False)
```

profile of v0, /device:TPU:0, one launch (start us, length us, event | category | flops | bytes accessed | tf_op | source)
XLA Modules:
  0.0 370.7 jit_solution(18205353903779881452)
XLA Ops:
  6.6 2.4 reduce_window_sum.11
  12.9 3.4 fusion.33
  16.3 158.6 %custom-call.3 = f32[4,4,1,128,128]{3,4,2,1,0:T(8,128)} custom-call(f32[4,4,1,128,128]{4,3,2,1,0:T(8,128)} %fusion.33), custom_call_target="InvertDiagBlocksLowerTriangular" | custom-call | tf_op jit(solution)/shard_map/triangular_solve | solution.py:68
  178.0 2.0 fusion.25
  185.1 13.7 %while.38 = (s32[]{:T(128)}, f32[4,128,256]{2,1,0:T(8,128)S(1)}, f32[4,4]{1,0:T(4,128)S(1)}, f32[4,4,128,128]{2,3,1,0:T(8,128)}, f32[4,4,128,256]{3,2,1,0:T(8,128)}, /*index=5*/f32[4,4,128,128]{3,2,1,0:T(8,128)}) while((s32[]{:T(128)}, f32[4,128,256]{2,1,0:T(8,128)S(1)}, f32[4,4]{1,0:T(4,128)S(1)}, f32[4,4,128,128]{2,3,1,0:T(8,128)}, ...), condition=%wide.region_3.4_spmd.clone, body=%wide.region_2.0_spmd.sunk.clone | while | flops 403046400 | bytes 3671673 | solution.py:111
  185.2 1.7 convolution_subtract_fusion.6
  186.9 1.7 convolution_add_fusion.7
  188.6 1.7 convolution_subtract_fusion.6
  190.3 1.7 convolution_add_fusion.7
  192.0 1.7 convolution_subtract_fusion.6
  193.8 1.7 convolution_add_fusion.7
  195.4 1.7 convolution_subtract_fusion.6
  197.2 1.7 convolution_add_fusion.7
  203.9 3.4 convolution_multiply_fusion.1
  207.3 68.6 %all-gather.3.cloned.1.call-done = f32[32,128,256]{2,1,0:T(8,128)} async-done(((f32[4,128,256]{2,1,0:T(8,128)}), f32[32,128,256]{2,1,0:T(8,128)}) %all-gather.3.cloned.1.call-update) | async-done | bytes 4194320 | tf_op jit(solution)/shard_map/all_gather | solution.py:16
  275.9 13.2 %while.39 = (s32[]{:T(128)}, f32[4,128,256]{2,1,0:T(8,128)S(1)}, s32[]{:T(128)}, f32[8,4,128,256]{3,2,1,0:T(8,128)}) while((s32[]{:T(128)}, f32[4,128,256]{2,1,0:T(8,128)S(1)}, s32[]{:T(128)}, f32[8,4,128,256]{3,2,1,0:T(8,128)}) %tuple.95), condition=%wide.region_5.6_spmd.clone, body=%wide.region_4.5_spmd.sunk.clone | while | flops 201654272 | bytes 5242947 | solution.py:23
  289.2 24.9 %while.40 = (s32[]{:T(128)}, f32[4,128,128]{2,1,0:T(8,128)S(1)}, bf16[4,4,128,128]{3,2,1,0:T(8,128)(2,1)}, f32[4,4]{1,0:T(4,128)S(1)}, f32[4,4,128,128]{2,3,1,0:...) while((s32[]{:T(128)}, f32[4,128,128]{2,1,0:T(8,128)S(1)}, ...), condition=%wide.region_8.9_spmd.clone, body=%wide.region_7.8_spmd.sunk.clone | while | flops 402980864 | bytes 3941533 | solution.py:121
  292.0 2.0 fusion.119
  298.2 2.0 fusion.119
  304.4 2.0 fusion.119
  310.7 2.0 fusion.119
  315.6 3.2 fusion.41
  318.8 42.9 %reduce-scatter.2.cloned.1.call-done = f32[128,2048]{1,0:T(8,128)} async-done(((f32[512,2048]{1,0:T(8,128)}), f32[128,2048]{1,0:T(8,128)}) %reduce-scatter.2.cloned.1.call-update) | async-done | bytes 1048592 | tf_op jit(solution)/shard_map/reduce_scatter | solution.py:127
  361.7 2.1 convert_element_type.35
  (98 shorter events, 48.1 us)
Async XLA Ops:
  6.5 309.0 %copy-start = (bf16[512,2048]{1,0:T(8,128)(2,1)S(1)}, bf16[512,2048]{1,0:T(8,128)(2,1)}, u32[]{:S(2)}) copy-start(bf16[512,2048]{1,0:T(8,128)(2,1)} %param.17) | copy-start | bytes 6291460
  6.5 6.3 %copy-start.7 = (f32[4,512]{1,0:T(4,128)S(1)}, f32[4,512]{1,0:T(4,128)}, u32[]{:S(2)}) copy-start(f32[4,512]{1,0:T(4,128)} %param.15) | copy-start | bytes 24580
  6.5 269.4 %all-gather.3.cloned.1.call-start = ((), (), s32[]{:S(2)}) async-start(), calls=%async_computation.2 | async-start | bytes 4718592 | tf_op jit(solution)/shard_map/all_gather | solution.py:16
  12.7 163.6 %copy-start.3 = (f32[512,4,128]{2,0,1:T(8,128)}, f32[512,4,128]{2,0,1:T(8,128)S(1)}, u32[]{:S(2)}) copy-start(f32[512,4,128]{2,0,1:T(8,128)S(1)} %convert_multiply_fusion.2) | copy-start | bytes 3145732
  176.0 1.9 copy-start.6
  181.1 1.0 copy-start.2
  181.1 2.6 copy-start.5
  198.9 0.8 copy-start.1
  199.7 162.0 %reduce-scatter.2.cloned.1.call-start = ((), (), s32[]{:S(2)}) async-start(), calls=%async_computation.1 | async-start | bytes 5242880 | tf_op jit(solution)/shard_map/reduce_scatter | solution.py:127
  199.9 4.0 %copy-start.4 = (f32[512,4,128]{2,0,1:T(8,128)S(1)}, f32[512,4,128]{2,0,1:T(8,128)}, u32[]{:S(2)}) copy-start(f32[512,4,128]{2,0,1:T(8,128)} %copy-done.3) | copy-start | bytes 3145732
Sparse Core Ops, SparseCore 0:
  199.8 76.0 all-gather.2
  318.9 42.7 reduce-scatter.1
where the time goes:
time: 372 us; the launch traced here: 371 us
  other arithmetic  173 us (47%)
  waiting for transfers between devices  112 us (30%)
  matrix products  54.4 us (15%)
  local copies, waits for them, and re-layouts  17.4 us (5%)
  between operations  13.6 us (4%)
    another operation x4, other arithmetic, prepare(): lax.linalg.triangular_solve(unit_lower, right_sides, left_side=True, lowe...  159 us
    all_gather x1, waiting for transfers between devices, prefix_2(): pieces = lax.all_gather(value, axis)  68.6 us
    dot_general x33, matrix products, contract(): return jnp.einsum(pattern, left_side, right_side, precision=EXACT)  49.2 us
    reduce_scatter x1, waiting for transfers between devices, body(): lax.psum_scatter(jnp.dot(attended, out_weight, preferred_element_type=jnp...  42.9 us
    squeeze x7, local copies, waits for them, and re-layouts, step(): longer = join(total, pieces[position])  7.56 us
  transfers between devices with their start and end apart: 2, of which 2 were waited for; matrix products, arithmetic and copies ran while one was open for 2% of the time, Pallas kernels for 0%

commit v1 on v0

v1 whole, which is shorter than its diff:
```python
import functools

import jax
import jax.numpy as jnp
from jax import lax
from jax.experimental import pallas as pl
from jax.experimental.pallas import tpu as pltpu
from jax.sharding import PartitionSpec as P

C = 128
F32 = jnp.float32
BF16 = jnp.bfloat16
NN = (((1,), (0,)), ((), ()))
NT = (((1,), (1,)), ((), ()))
TN = (((0,), (0,)), ((), ()))
VMEM_LIMIT = 56 * 1024 * 1024


def dot(a, b, dims=NN):
    return lax.dot_general(a, b, dims, preferred_element_type=F32)


def split(x):
    high = x.astype(BF16)
    return high, (x - high.astype(F32)).astype(BF16)


def dot3(a, b, dims=NN):
    (ah, al), (bh, bl) = a, b
    return dot(ah, bh, dims) + (dot(al, bh, dims) + dot(ah, bl, dims))


def iotas():
    return (
        lax.broadcasted_iota(jnp.int32, (C, C), 0),
        lax.broadcasted_iota(jnp.int32, (C, C), 1),
    )


def to_column(row, eye):
    return jnp.sum(jnp.where(eye, row, 0.0), axis=1, keepdims=True)


def to_row(column, eye):
    return jnp.sum(jnp.where(eye, column, 0.0), axis=0, keepdims=True)


def head_row(ref, head, c):
    block = ref[:, c * C : (c + 1) * C]
    index = lax.broadcasted_iota(jnp.int32, block.shape, 0)
    return jnp.sum(jnp.where(index == head, block, 0.0), axis=0, keepdims=True)


def inverse_scale(rows):
    return lax.rsqrt(jnp.sum(rows * rows, axis=1, keepdims=True) + 1e-06)


def decay_parts(log_row, within, eye):
    column = jnp.sum(jnp.where(within, log_row, 0.0), axis=1, keepdims=True)
    row = to_row(column, eye)
    decay = jnp.where(within, jnp.exp(jnp.where(within, column - row, 0.0)), 0.0)
    return column, decay


def inverses(lowers, row, col):
    eye = jnp.where(row == col, 1.0, 0.0)
    found = [eye - jnp.where((row // 2) == (col // 2), a, 0.0) for a in lowers]
    parts = [split(a) for a in lowers]
    size = 2
    while size < C:
        mask = ((row // (2 * size)) == (col // (2 * size))) & ((row // size) != (col // size))
        zero = jnp.zeros((), BF16)
        blocks = [(jnp.where(mask, h, zero), jnp.where(mask, l, zero)) for h, l in parts]
        halves = [split(x) for x in found]
        middle = [split(dot3(a, x)) for a, x in zip(blocks, halves)]
        found = [x - dot3(h, y) for x, h, y in zip(found, halves, middle)]
        size *= 2
    return found


def local_kernel(heads, step_heads, k_ref, v_ref, beta_ref, log_ref, m_ref, ut_ref, wu_ref, n_ref, k32, v32):
    step = pl.program_id(0)
    chunks = beta_ref.shape[1] // C

    @pl.when(step == 0)
    def _():
        k32[...] = k_ref[...].astype(F32)
        v32[...] = v_ref[...].astype(F32)

    row, col = iotas()
    eye = row == col
    within = row >= col
    strict = row > col
    jobs = [(j, c) for j in range(step_heads) for c in range(chunks)]
    lowers, sides, fades, ends = [], [], [], []
    for j, c in jobs:
        head = step * step_heads + j
        rows = pl.ds(c * C * heads + head, C, stride=heads)
        raw = k32[rows, :]
        value = v32[rows, :]
        beta = to_column(head_row(beta_ref, head, c), eye)
        column, decay = decay_parts(head_row(log_ref, head, c), within, eye)
        scale = inverse_scale(raw)
        raw16 = raw.astype(BF16)
        gram = dot(raw16, raw16, NT)
        lowers.append(jnp.where(strict, gram * decay * (beta * scale) * to_row(scale, eye), 0.0))
        unit = raw * scale
        last = column[C - 1 : C, :]
        sides.append(jnp.concatenate([unit * (beta * jnp.exp(column)), value * beta], axis=1))
        fades.append(unit * jnp.exp(last - column))
        ends.append(jnp.exp(last))
    solved = [dot3(split(x), split(s)) for x, s in zip(inverses(lowers, row, col), sides)]
    maps = []
    for i, (j, c) in enumerate(jobs):
        wu_ref[j * chunks + c] = solved[i]
        both = dot3(split(fades[i]), split(solved[i]), TN)
        maps.append((jnp.where(eye, ends[i], 0.0) - both[:, :C], both[:, C:]))
    for j in range(step_heads):
        state = jnp.concatenate(maps[j * chunks], axis=1)
        for c in range(1, chunks):
            n_ref[j * chunks + c] = state
            moved, fresh = maps[j * chunks + c]
            state = dot3(split(moved), split(state))
            state = jnp.concatenate([state[:, :C], state[:, C:] + fresh], axis=1)
        m_ref[j] = state[:, :C].astype(m_ref.dtype)
        ut_ref[j] = state[:, C:].T.astype(ut_ref.dtype)


def local_maps(key, value, beta, log_decay, heads, step_heads):
    tokens = beta.shape[1]
    chunks = tokens // C
    whole = lambda shape: pl.BlockSpec(shape, lambda i: (0,) * len(shape))
    part = lambda shape: pl.BlockSpec(shape, lambda i: (i,) + (0,) * (len(shape) - 1))
    return pl.pallas_call(
        functools.partial(local_kernel, heads, step_heads),
        grid=(heads // step_heads,),
        in_specs=[
            whole((tokens * heads, C)),
            whole((tokens * heads, C)),
            whole((heads, tokens)),
            whole((heads, tokens)),
        ],
        out_specs=[
            part((step_heads, C, C)),
            part((step_heads, C, C)),
            part((step_heads * chunks, C, 2 * C)),
            part((step_heads * chunks, C, 2 * C)),
        ],
        out_shape=[
            jax.ShapeDtypeStruct((heads, C, C), BF16),
            jax.ShapeDtypeStruct((heads, C, C), BF16),
            jax.ShapeDtypeStruct((heads * chunks, C, 2 * C), F32),
            jax.ShapeDtypeStruct((heads * chunks, C, 2 * C), F32),
        ],
        scratch_shapes=[pltpu.VMEM((tokens * heads, C), F32), pltpu.VMEM((tokens * heads, C), F32)],
        compiler_params=pltpu.CompilerParams(vmem_limit_bytes=VMEM_LIMIT),
        name="local_maps",
    )(key, value, beta, log_decay)


def rows_kernel(heads, step_heads, q_ref, k_ref, log_ref, wu_ref, n_ref, out_ref, q32, k32):
    step = pl.program_id(0)
    chunks = log_ref.shape[1] // C

    @pl.when(step == 0)
    def _():
        q32[...] = q_ref[...].astype(F32)
        k32[...] = k_ref[...].astype(F32)

    row, col = iotas()
    eye = row == col
    within = row >= col
    for j in range(step_heads):
        head = step * step_heads + j
        for c in range(chunks):
            rows = pl.ds(c * C * heads + head, C, stride=heads)
            query, raw = q32[rows, :], k32[rows, :]
            column, decay = decay_parts(head_row(log_ref, head, c), within, eye)
            scale = inverse_scale(query)
            pairs = dot(query.astype(BF16), raw.astype(BF16), NT)
            pairs = pairs * decay * scale * to_row(inverse_scale(raw), eye)
            both = dot3(split(pairs), split(wu_ref[j * chunks + c]))
            reach = query * (scale * jnp.exp(column)) - both[:, :C]
            fresh = both[:, C:]
            if c > 0:
                earlier = dot3(split(reach), split(n_ref[j * chunks + c]))
                reach = earlier[:, :C]
                fresh = fresh + earlier[:, C:]
            out_ref[j, c * C : (c + 1) * C, :] = jnp.concatenate([reach, fresh], axis=1)


def row_maps(query, key, log_decay, wu, states, heads, step_heads):
    tokens = log_decay.shape[1]
    chunks = tokens // C
    whole = lambda shape: pl.BlockSpec(shape, lambda i: (0,) * len(shape))
    part = lambda shape: pl.BlockSpec(shape, lambda i: (i,) + (0,) * (len(shape) - 1))
    return pl.pallas_call(
        functools.partial(rows_kernel, heads, step_heads),
        grid=(heads // step_heads,),
        in_specs=[
            whole((tokens * heads, C)),
            whole((tokens * heads, C)),
            whole((heads, tokens)),
            part((step_heads * chunks, C, 2 * C)),
            part((step_heads * chunks, C, 2 * C)),
        ],
        out_specs=part((step_heads, tokens, 2 * C)),
        out_shape=jax.ShapeDtypeStruct((heads, tokens, 2 * C), F32),
        scratch_shapes=[pltpu.VMEM((tokens * heads, C), F32), pltpu.VMEM((tokens * heads, C), F32)],
        compiler_params=pltpu.CompilerParams(vmem_limit_bytes=VMEM_LIMIT),
        name="row_maps",
    )(query, key, log_decay, wu, states)


def chain_kernel(blocks, m_ref, ut_ref, out_ref):
    width = ut_ref.shape[1]
    state = jnp.zeros((width, C), F32)
    for d in range(blocks):
        out_ref[d] = state.astype(out_ref.dtype)
        if d + 1 < blocks:
            if d == 0:
                state = ut_ref[0].astype(F32)
            else:
                both = dot(jnp.concatenate(split(state), axis=0), m_ref[d], NT)
                state = both[:width] + both[width:] + ut_ref[d].astype(F32)


def chain(maps, adds):
    blocks, width = adds.shape[:2]
    return pl.pallas_call(
        functools.partial(chain_kernel, blocks),
        out_shape=jax.ShapeDtypeStruct((blocks, width, C), BF16),
        compiler_params=pltpu.CompilerParams(vmem_limit_bytes=VMEM_LIMIT),
        name="chain",
    )(maps, adds)


def apply_kernel(heads, rows_ref, st_ref, w_ref, out_ref):
    attended = []
    for h in range(heads):
        reach, fresh = rows_ref[h, :, :C], rows_ref[h, :, C:]
        high, low = split(reach)
        state = st_ref[h]
        attended.append((fresh + dot(high, state, NT) + dot(low, state, NT)).astype(BF16))
    out_ref[0] = dot(jnp.concatenate(attended, axis=1), w_ref[...]).astype(BF16)


def apply_and_project(rows, states_t, weight, groups):
    heads, tokens, _ = rows.shape
    block = tokens // groups
    depth, width = weight.shape
    return pl.pallas_call(
        functools.partial(apply_kernel, heads),
        grid=(groups,),
        in_specs=[
            pl.BlockSpec((heads, block, 2 * C), lambda i: (0, i, 0)),
            pl.BlockSpec((heads, C, C), lambda i: (0, 0, 0)),
            pl.BlockSpec((depth, width), lambda i: (0, 0)),
        ],
        out_specs=pl.BlockSpec((1, block, width), lambda i: (i, 0, 0)),
        out_shape=jax.ShapeDtypeStruct((groups, block, width), BF16),
        compiler_params=pltpu.CompilerParams(vmem_limit_bytes=VMEM_LIMIT),
        name="apply_and_project",
    )(rows, states_t, weight)


def body(query, key, value, beta, log_decay, out_weight):
    tokens, heads, _ = key.shape
    blocks = lax.axis_size("seq")
    groups = lax.axis_size("head")
    flat = lambda x: x.reshape(tokens * heads, C)
    q2, k2, v2 = flat(query), flat(key), flat(value)
    share = blocks // heads
    moved, added_t, wu, states = local_maps(k2, v2, beta, log_decay, heads, 1)
    send_m = jnp.broadcast_to(moved[:, None], (heads, share, C, C)).reshape(blocks, C, C)
    send_u = added_t.reshape(blocks, C // share, C)
    sent = lax.all_to_all(jnp.concatenate([send_m, send_u], axis=1), "seq", 0, 0, tiled=True)
    rows = row_maps(q2, k2, log_decay, wu, states, heads, 1)
    entering = chain(sent[:, :C], sent[:, C:])
    entering = lax.all_to_all(entering, "seq", 0, 0, tiled=True)
    parts = apply_and_project(rows, entering.reshape(heads, C, C), out_weight, groups)
    parts = lax.all_to_all(parts, "head", 0, 0, tiled=True)
    return jnp.sum(parts.astype(F32), axis=0).astype(BF16)


def solution(mesh):
    in_specs = (
        P("seq", "head", None),
        P("seq", "head", None),
        P("seq", "head", None),
        P("head", "seq"),
        P("head", "seq"),
        P("head", None),
    )
    out_specs = P(("seq", "head"), None)
    return jax.shard_map(body, mesh=mesh, in_specs=in_specs, out_specs=out_specs, check_vma=False)
```

time: 372 us -> 90.1 us (0.24)
  other arithmetic: 173 us -> 2.24 us
  waiting for transfers between devices: 112 us -> 0.08 us
  matrix products: 54.4 us -> 0 us
  blocking collectives: 0 us -> 48.4 us
  Pallas kernels: 0 us -> 32.4 us
  local copies, waits for them, and re-layouts: 17.4 us -> 2.96 us
  between operations: 13.6 us -> 0.02 us
    another operation x5 -> x0, other arithmetic: 161 us -> none  [the longest x4 159 us: prepare(): lax.linalg.triangular_solve(unit_lower, right_sides, left_side=True, lowe...]
    all_gather x1 -> x0, waiting for transfers between devices: 68.6 us -> none  [prefix_2(): pieces = lax.all_gather(value, axis)]
    dot_general x34 -> x0, matrix products: 52.4 us -> none  [the longest x33 49.2 us: contract(): return jnp.einsum(pattern, left_side, right_side, precision=EXACT)]
    all_to_all x0 -> x2, blocking collectives: none -> 48.4 us  [the longest x1 29.3 us: body(): parts = lax.all_to_all(parts, 'head', 0, 0, tiled=True)]
    reduce_scatter x1 -> x0, waiting for transfers between devices: 42.9 us -> none  [body(): lax.psum_scatter(jnp.dot(attended, out_weight, preferred_element_type=jnp...]
    pallas_call x0 -> x4, Pallas kernels: none -> 32.4 us  [the longest x1 16.9 us: local_maps(): pl.pallas_call(functools.partial(local_kernel, heads, step_heads), grid=(...]
    squeeze x7 -> x0, local copies, waits for them, and re-layouts: 7.56 us -> none  [step(): longer = join(total, pieces[position])]
    mul x4 -> x0, other arithmetic: 4.66 us -> none  [the longest x2 2.75 us: unit_rows(): widened * lax.rsqrt(jnp.sum(widened * widened, axis=-1, keepdims=True) +...]
  transfers between devices with their start and end apart: 2 -> 1, of which waited for: 2 -> 1; matrix products, arithmetic and copies ran while one was open for 2% -> 0% of each run, Pallas kernels for 0% -> 8%
where the time goes in v1:
time: 90.1 us; the launch traced here: 89.5 us
  blocking collectives  48.4 us (54%)
  Pallas kernels  32.4 us (36%)
  starting transfers between devices  3.37 us (4%)
  local copies, waits for them, and re-layouts  2.96 us (3%)
  other arithmetic  2.24 us (2%)
    all_to_all x1, blocking collectives, body(): parts = lax.all_to_all(parts, 'head', 0, 0, tiled=True)  29.3 us
    all_to_all x1, blocking collectives, body(): lax.all_to_all(jnp.concatenate([send_m, send_u], axis=1), 'seq', 0, 0, ti...  19.2 us
    pallas_call x1, Pallas kernels, local_maps(): pl.pallas_call(functools.partial(local_kernel, heads, step_heads), grid=(...  16.9 us
    pallas_call x1, Pallas kernels, row_maps(): pl.pallas_call(functools.partial(rows_kernel, heads, step_heads), grid=(h...  7.2 us
    pallas_call x1, Pallas kernels, apply_and_project(): pl.pallas_call(functools.partial(apply_kernel, heads), grid=(groups,), in...  5.91 us
    all_to_all x1, starting transfers between devices, body(): entering = lax.all_to_all(entering, 'seq', 0, 0, tiled=True)  3.37 us
    pallas_call x1, Pallas kernels, chain(): pl.pallas_call(functools.partial(chain_kernel, blocks), out_shape=jax.Sha...  2.44 us
  transfers between devices with their start and end apart: 1, of which 1 were waited for; matrix products, arithmetic and copies ran while one was open for 0% of the time, Pallas kernels for 8%

profile of v1, /device:TPU:0, one launch (start us, length us, event | category | flops | bytes accessed | tf_op | source)
XLA Modules:
  0.0 89.5 jit_solution(11891117630688793572)
XLA Ops:
  0.0 16.9 %local_maps.1 = (bf16[4,128,128]{2,1,0:T(8,128)(2,1)}, bf16[4,128,128]{2,1,0:T(8,128)(2,1)}, f32[16,128,256]{2,1,0:T(8,128)}, f32[16,128,256]{2,1,0:T(8,128)}) custom-call(bf16[2048,128]{1,0:T(8,128)(2,1)} %bitcast.6, bf16[2048,128]{1,0:T(8,128)(2,1)} %bitcast.11, f32[4,512]{1,0:T(4,128)} %beta_ref.1, f32[4,512]{1,0:T(4,128)} %log_ref.3), custom_call_target="tpu_custom_call" | custom-call | tf_op jit(solution)/shard_map/local_maps/pallas_call | solution.py:134
  16.9 0.9 %broadcast_in_dim.2 = bf16[4,2,128,128]{3,2,1,0:T(8,128)(2,1)S(1)} broadcast(bf16[4,128,128]{2,1,0:T(8,128)(2,1)} %get-tuple-element.11), dimensions={0,2,3} | broadcast | bytes 393216 | tf_op jit(solution)/shard_map/broadcast_in_dim | solution.py:275
  17.8 0.9 %pad_maximum_fusion = bf16[8,192,128]{2,1,0:T(8,128)(2,1)S(1)} fusion(bf16[8,64,128]{2,1,0:T(8,128)(2,1)} %bitcast.12, bf16[8,128,128]{2,1,0:T(8,128)(2,1)S(1)} %bitcast.8), kind=kLoop, calls=%fused_computation | loop fusion | flops 786432 | bytes 786432 | tf_op jit(solution)/shard_map/concatenate | solution.py:277
  18.7 19.2 %all_to_all.15 = bf16[8,192,128]{2,1,0:T(8,128)(2,1)S(1)} all-to-all(bf16[8,192,128]{2,1,0:T(8,128)(2,1)S(1)} %pad_maximum_fusion), channel_id=1, replica_groups=mesh['seq'=8,'head'=4] {'seq'}, dimensions={0} | all-to-all | bytes 786432 | tf_op jit(solution)/shard_map/all_to_all | solution.py:277
  37.9 0.7 slice.8.m_ref
  38.6 0.6 slice.9.ut_ref
  39.3 2.4 %chain.1 = bf16[8,64,128]{2,1,0:T(8,128)(2,1)} custom-call(bf16[8,128,128]{2,1,0:T(8,128)(2,1)} %slice.8.m_ref, bf16[8,64,128]{2,1,0:T(8,128)(2,1)} %slice.9.ut_ref), custom_call_target="tpu_custom_call" | custom-call | tf_op jit(solution)/shard_map/chain/pallas_call | solution.py:230
  41.7 3.4 %all-to-all-start.1 = ((bf16[8,64,128]{2,1,0:T(8,128)(2,1)}), bf16[8,64,128]{2,1,0:T(8,128)(2,1)S(1)}, u32[]{:S(2)}, u32[]{:S(2)}) async-start(bf16[8,64,128]{2,1,0:T(8,128)(2,1)} %chain.1), calls=%async_computation.1 | async-start | bytes 262144 | tf_op jit(solution)/shard_map/all_to_all | solution.py:280
  45.1 7.2 %row_maps.1.rows_ref = f32[4,512,256]{2,1,0:T(8,128)} custom-call(bf16[2048,128]{1,0:T(8,128)(2,1)} %bitcast.9, bf16[2048,128]{1,0:T(8,128)(2,1)} %bitcast.7, f32[4,512]{1,0:T(4,128)} %log_ref.3, f32[16,128,256]{2,1,0:T(8,128)} %get-tuple-element.9.wu_ref, f32[16,128,256]{2,1,0:T(8,128)} %get-tuple-element.10.n_ref), custom_call_target="tpu_custom_call" | custom-call | tf_op jit(solution)/shard_map/row_maps/pallas_call | solution.py:197
  52.3 0.1 all-to-all-done.1
  52.4 0.0 copy-start
  52.4 0.7 copy-done
  53.0 5.9 %apply_and_project.1 = bf16[4,128,2048]{2,1,0:T(8,128)(2,1)} custom-call(f32[4,512,256]{2,1,0:T(8,128)} %row_maps.1.rows_ref, bf16[4,128,128]{2,1,0:T(8,128)(2,1)} %bitcast.10, bf16[512,2048]{1,0:T(8,128)(2,1)} %w_ref.1), custom_call_target="tpu_custom_call" | custom-call | tf_op jit(solution)/shard_map/apply_and_project/pallas_call | solution.py:252
  58.9 29.3 %all_to_all.16 = bf16[4,128,2048]{2,1,0:T(8,128)(2,1)S(1)} all-to-all(bf16[4,128,2048]{2,1,0:T(8,128)(2,1)} %apply_and_project.1), channel_id=1, replica_groups=mesh['seq'=8,'head'=4] {'head'}, dimensions={0} | all-to-all | bytes 4194304 | tf_op jit(solution)/shard_map/all_to_all | solution.py:282
  88.2 1.3 %reduce_sum.12 = bf16[128,2048]{1,0:T(8,128)(2,1)} reduce(bf16[4,128,2048]{2,1,0:T(8,128)(2,1)S(1)} %all_to_all.16, bf16[]{:T(256)} %constant.2.clone.1), dimensions={0}, to_apply=%region_0.0 | reduce | flops 786432 | bytes 2621442 | tf_op jit(solution)/shard_map/reduce_sum | solution.py:283
Async XLA Ops:
  41.7 10.7 %all-to-all-start.1 = ((bf16[8,64,128]{2,1,0:T(8,128)(2,1)}), bf16[8,64,128]{2,1,0:T(8,128)(2,1)S(1)}, u32[]{:S(2)}, u32[]{:S(2)}) async-start(bf16[8,64,128]{2,1,0:T(8,128)(2,1)} %chain.1), calls=%async_computation.1 | async-start | bytes 262144 | tf_op jit(solution)/shard_map/all_to_all | solution.py:280
  52.4 0.7 copy-start

commit v2 on v1

--- a/solution.py
+++ b/solution.py
@@ -13,7 +13,7 @@
 NN = (((1,), (0,)), ((), ()))
 NT = (((1,), (1,)), ((), ()))
 TN = (((0,), (0,)), ((), ()))
-VMEM_LIMIT = 56 * 1024 * 1024
+MIB = 1024 * 1024
 
 
 def dot(a, b, dims=NN):
@@ -78,7 +78,8 @@
     return found
 
 
-def local_kernel(heads, step_heads, k_ref, v_ref, beta_ref, log_ref, m_ref, ut_ref, wu_ref, n_ref, k32, v32):
+def local_kernel(heads, step_heads, blocks, k_ref, v_ref, beta_ref, log_ref, wu_ref, n_ref, m_ref, ut_ref, *rest):
+    sends, (k32, v32) = rest[:blocks], rest[blocks:]
     step = pl.program_id(0)
     chunks = beta_ref.shape[1] // C
 
@@ -122,17 +123,31 @@
             moved, fresh = maps[j * chunks + c]
             state = dot3(split(moved), split(state))
             state = jnp.concatenate([state[:, :C], state[:, C:] + fresh], axis=1)
-        m_ref[j] = state[:, :C].astype(m_ref.dtype)
-        ut_ref[j] = state[:, C:].T.astype(ut_ref.dtype)
-
-
-def local_maps(key, value, beta, log_decay, heads, step_heads):
+        m_ref[step * step_heads + j] = state[:, :C].astype(BF16)
+        ut_ref[step * step_heads + j] = state[:, C:].T.astype(BF16)
+
+    if not blocks:
+        return
+
+    @pl.when(step == heads // step_heads - 1)
+    def _():
+        share = blocks // heads
+        width = C // share
+        for r in range(blocks):
+            target = lax.rem(lax.axis_index("seq") + blocks - r, blocks)
+            head, piece = target // share, lax.rem(target, share)
+            sends[r][:C, :] = m_ref[head]
+            sends[r][C:, :] = ut_ref[head, pl.ds(pl.multiple_of(piece * width, width), width), :]
+
+
+def local_maps(key, value, beta, log_decay, heads, step_heads, blocks):
     tokens = beta.shape[1]
+    tall = C + C * heads // blocks if blocks else 0
     chunks = tokens // C
     whole = lambda shape: pl.BlockSpec(shape, lambda i: (0,) * len(shape))
     part = lambda shape: pl.BlockSpec(shape, lambda i: (i,) + (0,) * (len(shape) - 1))
     return pl.pallas_call(
-        functools.partial(local_kernel, heads, step_heads),
+        functools.partial(local_kernel, heads, step_heads, blocks),
         grid=(heads // step_heads,),
         in_specs=[
             whole((tokens * heads, C)),
@@ -141,19 +156,24 @@
             whole((heads, tokens)),
         ],
         out_specs=[
-            part((step_heads, C, C)),
-            part((step_heads, C, C)),
             part((step_heads * chunks, C, 2 * C)),
             part((step_heads * chunks, C, 2 * C)),
-        ],
+            whole((heads, C, C)),
+            whole((heads, C, C)),
+        ]
+        + [whole((tall, C))] * blocks,
         out_shape=[
+            jax.ShapeDtypeStruct((heads * chunks, C, 2 * C), F32),
+            jax.ShapeDtypeStruct((heads * chunks, C, 2 * C), F32),
             jax.ShapeDtypeStruct((heads, C, C), BF16),
             jax.ShapeDtypeStruct((heads, C, C), BF16),
-            jax.ShapeDtypeStruct((heads * chunks, C, 2 * C), F32),
-            jax.ShapeDtypeStruct((heads * chunks, C, 2 * C), F32),
+        ]
+        + [jax.ShapeDtypeStruct((tall, C), BF16)] * blocks,
+        scratch_shapes=[
+            pltpu.VMEM((tokens * heads, C), F32),
+            pltpu.VMEM((tokens * heads, C), F32),
         ],
-        scratch_shapes=[pltpu.VMEM((tokens * heads, C), F32), pltpu.VMEM((tokens * heads, C), F32)],
-        compiler_params=pltpu.CompilerParams(vmem_limit_bytes=VMEM_LIMIT),
+        compiler_params=pltpu.CompilerParams(vmem_limit_bytes=24 * MIB),
         name="local_maps",
     )(key, value, beta, log_decay)
 
@@ -207,61 +227,141 @@
         out_specs=part((step_heads, tokens, 2 * C)),
         out_shape=jax.ShapeDtypeStruct((heads, tokens, 2 * C), F32),
         scratch_shapes=[pltpu.VMEM((tokens * heads, C), F32), pltpu.VMEM((tokens * heads, C), F32)],
-        compiler_params=pltpu.CompilerParams(vmem_limit_bytes=VMEM_LIMIT),
+        compiler_params=pltpu.CompilerParams(vmem_limit_bytes=24 * MIB),
+        cost_estimate=pl.CostEstimate(flops=4000000000, bytes_accessed=10000000, transcendentals=0),
         name="row_maps",
     )(query, key, log_decay, wu, states)
 
 
-def chain_kernel(blocks, m_ref, ut_ref, out_ref):
-    width = ut_ref.shape[1]
+def chain_kernel(blocks, *refs):
+    sends, outs, (held,) = refs[:blocks], refs[blocks : 2 * blocks], refs[2 * blocks :]
+    me = lax.axis_index("seq")
+    width = held.shape[1] - C
+    for r in range(blocks):
+        held[lax.rem(me + r, blocks)] = sends[r][...]
     state = jnp.zeros((width, C), F32)
+    states = []
     for d in range(blocks):
-        out_ref[d] = state.astype(out_ref.dtype)
+        states.append(state)
         if d + 1 < blocks:
+            added = held[d, C:, :].astype(F32)
             if d == 0:
-                state = ut_ref[0].astype(F32)
+                state = added
             else:
-                both = dot(jnp.concatenate(split(state), axis=0), m_ref[d], NT)
-                state = both[:width] + both[width:] + ut_ref[d].astype(F32)
-
-
-def chain(maps, adds):
-    blocks, width = adds.shape[:2]
+                both = dot(jnp.concatenate(split(state), axis=0), held[d, :C, :], NT)
+                state = both[:width] + both[width:] + added
+    for d in range(blocks):
+        held[d, :width, :] = states[d].astype(BF16)
+    for r in range(blocks):
+        outs[r][...] = held[lax.rem(me + r, blocks), :width, :]
+
+
+def chain(sent):
+    blocks = len(sent)
+    tall = sent[0].shape[0]
     return pl.pallas_call(
         functools.partial(chain_kernel, blocks),
-        out_shape=jax.ShapeDtypeStruct((blocks, width, C), BF16),
-        compiler_params=pltpu.CompilerParams(vmem_limit_bytes=VMEM_LIMIT),
+        out_shape=[jax.ShapeDtypeStruct((tall - C, C), BF16)] * blocks,
+        scratch_shapes=[pltpu.VMEM((blocks, tall, C), BF16)],
+        compiler_params=pltpu.CompilerParams(vmem_limit_bytes=4 * MIB),
         name="chain",
-    )(maps, adds)
-
-
-def apply_kernel(heads, rows_ref, st_ref, w_ref, out_ref):
+    )(*sent)
+
+
+def apply_kernel(heads, blocks, rows_ref, *refs):
+    entering, (keep_ref, send_ref, st_ref) = refs[:blocks], refs[blocks:]
+    step = pl.program_id(0)
+
+    @pl.when(step == 0)
+    def _():
+        if blocks == 1:
+            st_ref[...] = entering[0][...]
+            return
+        me = lax.axis_index("seq")
+        share = blocks // heads
+        width = C // share
+        for r in range(blocks):
+            source = lax.rem(me + blocks - r, blocks)
+            place = pl.multiple_of(lax.rem(source, share) * width, width)
+            st_ref[source // share, pl.ds(place, width), :] = entering[r][...]
+
     attended = []
     for h in range(heads):
         reach, fresh = rows_ref[h, :, :C], rows_ref[h, :, C:]
         high, low = split(reach)
         state = st_ref[h]
         attended.append((fresh + dot(high, state, NT) + dot(low, state, NT)).astype(BF16))
-    out_ref[0] = dot(jnp.concatenate(attended, axis=1), w_ref[...]).astype(BF16)
-
-
-def apply_and_project(rows, states_t, weight, groups):
+    attended = jnp.concatenate(attended, axis=1)
+    mine = lax.rem(step, 2) == lax.rem(lax.axis_index("head"), 2)
+
+    @pl.when(mine)
+    def _():
+        keep_ref[step // 2] = attended
+
+    @pl.when(jnp.logical_not(mine))
+    def _():
+        send_ref[step // 2] = attended
+
+
+def apply(rows, entering, groups):
     heads, tokens, _ = rows.shape
     block = tokens // groups
-    depth, width = weight.shape
+    blocks = len(entering)
+    out = jax.ShapeDtypeStruct((groups // 2, block, heads * C), BF16)
     return pl.pallas_call(
-        functools.partial(apply_kernel, heads),
+        functools.partial(apply_kernel, heads, blocks),
         grid=(groups,),
-        in_specs=[
-            pl.BlockSpec((heads, block, 2 * C), lambda i: (0, i, 0)),
-            pl.BlockSpec((heads, C, C), lambda i: (0, 0, 0)),
-            pl.BlockSpec((depth, width), lambda i: (0, 0)),
-        ],
-        out_specs=pl.BlockSpec((1, block, width), lambda i: (i, 0, 0)),
-        out_shape=jax.ShapeDtypeStruct((groups, block, width), BF16),
-        compiler_params=pltpu.CompilerParams(vmem_limit_bytes=VMEM_LIMIT),
-        name="apply_and_project",
-    )(rows, states_t, weight)
+        in_specs=[pl.BlockSpec((heads, block, 2 * C), lambda i: (0, i, 0))]
+        + [pl.BlockSpec(x.shape, lambda i, n=x.ndim: (0,) * n) for x in entering],
+        out_specs=[pl.BlockSpec(out.shape, lambda i: (0, 0, 0))] * 2,
+        out_shape=[out, out],
+        scratch_shapes=[pltpu.VMEM((heads, C, C), BF16)],
+        compiler_params=pltpu.CompilerParams(vmem_limit_bytes=14 * MIB),
+        name="apply",
+    )(rows, *entering)
+
+
+def project_kernel(other, keep_ref, got_ref, w_ref, w2_ref, out_ref):
+    pair = lax.axis_index("head") // 2
+    index = 1 - pair if other else pair
+    out_ref[...] = (dot(keep_ref[index], w_ref[...]) + dot(got_ref[index], w2_ref[...])).astype(out_ref.dtype)
+
+
+def project(other, keep, got, weight, weight2):
+    _, block, depth = keep.shape
+    width = weight.shape[1]
+    return pl.pallas_call(
+        functools.partial(project_kernel, other),
+        out_shape=jax.ShapeDtypeStruct((block, width), BF16 if other else F32),
+        compiler_params=pltpu.CompilerParams(vmem_limit_bytes=20 * MIB),
+        cost_estimate=pl.CostEstimate(
+            flops=4 * block * depth * width, bytes_accessed=4 * depth * width, transcendentals=0
+        ),
+        name="project",
+    )(keep, got, weight, weight2)
+
+
+def swap(x, axis, bit):
+    count = lax.axis_size(axis)
+    return lax.ppermute(x, axis, [(i, i ^ bit) for i in range(count)])
+
+
+def shift(x, axis, amount):
+    count = lax.axis_size(axis)
+    return lax.ppermute(x, axis, [(i, (i + amount) % count) for i in range(count)])
+
+
+def prefix(moved, added):
+    me = lax.axis_index("seq")
+    moved, added = lax.all_gather(moved, "seq"), lax.all_gather(added, "seq")
+
+    def step(d, state):
+        both = jnp.stack(split(state))
+        both = jnp.einsum("phwk,hik->phwi", both, moved[d], preferred_element_type=F32)
+        return jnp.where(d < me, both[0] + both[1] + added[d].astype(F32), state)
+
+    start = jnp.zeros(added.shape[1:], F32)
+    return lax.fori_loop(0, moved.shape[0] - 1, step, start).astype(BF16)
 
 
 def body(query, key, value, beta, log_decay, out_weight):
@@ -270,17 +370,22 @@
     groups = lax.axis_size("head")
     flat = lambda x: x.reshape(tokens * heads, C)
     q2, k2, v2 = flat(query), flat(key), flat(value)
-    share = blocks // heads
-    moved, added_t, wu, states = local_maps(k2, v2, beta, log_decay, heads, 1)
-    send_m = jnp.broadcast_to(moved[:, None], (heads, share, C, C)).reshape(blocks, C, C)
-    send_u = added_t.reshape(blocks, C // share, C)
-    sent = lax.all_to_all(jnp.concatenate([send_m, send_u], axis=1), "seq", 0, 0, tiled=True)
+    weight2 = swap(out_weight, "head", 1)
+    direct = blocks % heads == 0 and C * heads // blocks >= 64
+    wu, states, moved, added, *sends = local_maps(k2, v2, beta, log_decay, heads, 1, blocks if direct else 0)
     rows = row_maps(q2, k2, log_decay, wu, states, heads, 1)
-    entering = chain(sent[:, :C], sent[:, C:])
-    entering = lax.all_to_all(entering, "seq", 0, 0, tiled=True)
-    parts = apply_and_project(rows, entering.reshape(heads, C, C), out_weight, groups)
-    parts = lax.all_to_all(parts, "head", 0, 0, tiled=True)
-    return jnp.sum(parts.astype(F32), axis=0).astype(BF16)
+    if direct:
+        sent = [x if r == 0 else shift(x, "seq", -r) for r, x in enumerate(sends)]
+        sent, rows = lax.optimization_barrier((sent, rows))
+        entering = chain(sent)
+        entering = [x if r == 0 else shift(x, "seq", r) for r, x in enumerate(entering)]
+    else:
+        entering = [prefix(moved, added)]
+    keep, away = apply(rows, entering, groups)
+    got = swap(away, "head", 1)
+    theirs = swap(project(True, keep, got, out_weight, weight2), "head", 2)
+    mine = project(False, keep, got, out_weight, weight2)
+    return (mine + theirs.astype(F32)).astype(BF16)
 
 
 def solution(mesh):

time: 90.1 us -> 72.7 us (0.81)
  blocking collectives: 48.4 us -> 0 us
  starting transfers between devices: 3.37 us -> 25 us
  waiting for transfers between devices: 0.08 us -> 17.4 us
  Pallas kernels: 32.4 us -> 23.8 us
  local copies, waits for them, and re-layouts: 2.96 us -> 5.22 us
  other arithmetic: 2.24 us -> 0.9 us
    all_to_all x2 -> x0, blocking collectives: 48.4 us -> none  [the longest x1 29.3 us: body(): parts = lax.all_to_all(parts, 'head', 0, 0, tiled=True)]
    ppermute x0 -> x17, starting transfers between devices: none -> 25 us  [the longest x14 22.9 us: shift(): lax.ppermute(x, axis, [(i, (i + amount) % count) for i in range(count)])]
    ppermute x0 -> x17, waiting for transfers between devices: none -> 17.4 us  [the longest x3 13.2 us: swap(): return lax.ppermute(x, axis, [(i, i ^ bit) for i in range(count)])]
    pallas_call x3 -> x5, Pallas kernels: 25.2 us -> 19.3 us  [the longest x1 15.4 us: local_maps(): pl.pallas_call(functools.partial(local_kernel, heads, step_heads, blocks)...]
    unnamed x2 -> x14, local copies, waits for them, and re-layouts: 0.65 us -> 5.22 us
    all_to_all x1 -> x0, starting transfers between devices: 3.37 us -> none  [body(): entering = lax.all_to_all(entering, 'seq', 0, 0, tiled=True)]
    pallas_call x1, Pallas kernels: 7.2 us -> 4.45 us  [row_maps(): pl.pallas_call(functools.partial(rows_kernel, heads, step_heads), grid=(h...]
    slice x2 -> x0, local copies, waits for them, and re-layouts: 1.37 us -> none  [body(): entering = chain(sent[:, :C], sent[:, C:])]
  transfers between devices with their start and end apart: 1 -> 17, of which waited for: 1 -> 8; matrix products, arithmetic and copies ran while one was open for 0% -> 0% of each run, Pallas kernels for 8% -> 32%
where the time goes in v2:
time: 72.7 us; the launch traced here: 72.3 us
  starting transfers between devices  25 us (34%)
  Pallas kernels  23.8 us (33%)
  waiting for transfers between devices  17.4 us (24%)
  local copies, waits for them, and re-layouts  5.22 us (7%)
  other arithmetic  0.9 us (1%)
    ppermute x14, starting transfers between devices, shift(): lax.ppermute(x, axis, [(i, (i + amount) % count) for i in range(count)])  22.9 us
    pallas_call x1, Pallas kernels, local_maps(): pl.pallas_call(functools.partial(local_kernel, heads, step_heads, blocks)...  15.4 us
    ppermute x3, waiting for transfers between devices, swap(): return lax.ppermute(x, axis, [(i, i ^ bit) for i in range(count)])  13.2 us
    unnamed x14, local copies, waits for them, and re-layouts  5.22 us
    pallas_call x1, Pallas kernels, row_maps(): pl.pallas_call(functools.partial(rows_kernel, heads, step_heads), grid=(h...  4.45 us
    ppermute x14, waiting for transfers between devices, shift(): lax.ppermute(x, axis, [(i, (i + amount) % count) for i in range(count)])  4.13 us
    ppermute x3, starting transfers between devices, swap(): return lax.ppermute(x, axis, [(i, i ^ bit) for i in range(count)])  2.12 us
    pallas_call x1, Pallas kernels, apply(): pl.pallas_call(functools.partial(apply_kernel, heads, blocks), grid=(grou...  1.58 us
  transfers between devices with their start and end apart: 17, of which 8 were waited for; matrix products, arithmetic and copies ran while one was open for 0% of the time, Pallas kernels for 32%

profile of v2, /device:TPU:0, one launch (start us, length us, event | category | flops | bytes accessed | tf_op | source)
XLA Modules:
  0.0 72.3 jit_solution(16074422748539212039)
XLA Ops:
  0.5 1.0 %copy-done.1 = bf16[512,4,128]{2,1,0:T(4,128)(2,1)S(1)} copy-done((bf16[512,4,128]{2,1,0:T(4,128)(2,1)S(1)}, bf16[512,4,128]{2,1,0:T(4,128)(2,1)}, u32[]{:S(2)}) %copy-start.1) | copy-done | bytes 524312
  1.5 1.0 %copy-done.2 = bf16[512,4,128]{2,1,0:T(4,128)(2,1)S(1)} copy-done((bf16[512,4,128]{2,1,0:T(4,128)(2,1)S(1)}, bf16[512,4,128]{2,1,0:T(4,128)(2,1)}, u32[]{:S(2)}) %copy-start.2) | copy-done | bytes 524312
  3.9 15.4 %local_maps.1 = (f32[16,128,256]{2,1,0:T(8,128)S(1)}, f32[16,128,256]{2,1,0:T(8,128)S(1)}, bf16[4,128,128]{2,1,0:T(8,128)(2,1)}, bf16[4,128,128]{2,1,0:T(8,128)(...) custom-call(bf16[2048,128]{1,0:T(8,128)(2,1)S(1)} %bitcast.4, ...), custom_call_target="tpu_custom_call" | custom-call | tf_op jit(solution)/shard_map/local_maps/pallas_call | solution.py:149
  19.4 5.5 %collective-permute-start = (bf16[192,128]{1,0:T(8,128)(2,1)S(1)}, bf16[192,128]{1,0:T(8,128)(2,1)S(1)}, u32[]{:S(2)}, u32[]{:S(2)}) collective-permute-start(bf16[192,128]{1,0:T(8,128)(2,1)S(1)} %get-tuple-element.35), channel_id=1, source_target_pairs={{0,28},{4,0},{8,4},{12,8},{16,12},{20,16},{24,20},{28,24},{1,29},{... | collective-permute-start | bytes 147464 | tf_op jit(solution)/shard_map/ppermute | solution.py:351
  25.3 3.0 %collective-permute-start.3 = (bf16[192,128]{1,0:T(8,128)(2,1)S(1)}, bf16[192,128]{1,0:T(8,128)(2,1)S(1)}, u32[]{:S(2)}, u32[]{:S(2)}) collective-permute-start(bf16[192,128]{1,0:T(8,128)(2,1)S(1)} %get-tuple-element.38), channel_id=1, source_target_pairs={{0,16},{4,20},{8,24},{12,28},{16,0},{20,4},{24,8},{28,12},{1,17},{... | collective-permute-start | bytes 147464 | tf_op jit(solution)/shard_map/ppermute | solution.py:351
  29.0 1.2 %collective-permute-start.5 = (bf16[192,128]{1,0:T(8,128)(2,1)S(1)}, bf16[192,128]{1,0:T(8,128)(2,1)S(1)}, u32[]{:S(2)}, u32[]{:S(2)}) collective-permute-start(bf16[192,128]{1,0:T(8,128)(2,1)S(1)} %get-tuple-element.40), channel_id=1, source_target_pairs={{0,8},{4,12},{8,16},{12,20},{16,24},{20,28},{24,0},{28,4},{1,9},{5... | collective-permute-start | bytes 147464 | tf_op jit(solution)/shard_map/ppermute | solution.py:351
  30.3 3.0 %collective-permute-start.6 = (bf16[192,128]{1,0:T(8,128)(2,1)S(1)}, bf16[192,128]{1,0:T(8,128)(2,1)S(1)}, u32[]{:S(2)}, u32[]{:S(2)}) collective-permute-start(bf16[192,128]{1,0:T(8,128)(2,1)S(1)} %get-tuple-element.41), channel_id=1, source_target_pairs={{0,4},{4,8},{8,12},{12,16},{16,20},{20,24},{24,28},{28,0},{1,5},{5... | collective-permute-start | bytes 147464 | tf_op jit(solution)/shard_map/ppermute | solution.py:351
  34.1 1.0 %copy-done.6 = bf16[512,4,128]{2,1,0:T(4,128)(2,1)S(1)} copy-done((bf16[512,4,128]{2,1,0:T(4,128)(2,1)S(1)}, bf16[512,4,128]{2,1,0:T(4,128)(2,1)}, u32[]{:S(2)}) %copy-start.6) | copy-done | bytes 524312
  35.1 4.5 %row_maps.1.rows_ref = f32[4,512,256]{2,1,0:T(8,128)S(1)} custom-call(bf16[2048,128]{1,0:T(8,128)(2,1)S(1)} %bitcast.6, bf16[2048,128]{1,0:T(8,128)(2,1)S(1)} %bitcast.5, f32[4,512]{1,0:T(4,128)S(1)} %copy-done.5, f32[16,128,256]{2,1,0:T(8,128)S(1)} %get-tuple-element.42.wu_ref, f32[16,128,256]{2,1,0:T(8,128)S(1)} %get-tuple-element.43.n_ref), custom_call_target="tpu_custom_call" | custom-call | flops 4000000000 | bytes 10000000 | tf_op jit(solution)/shard_map/row_maps/pallas_call | solution.py:217
  39.6 0.9 %chain.1 = (bf16[64,128]{1,0:T(8,128)(2,1)S(1)}, bf16[64,128]{1,0:T(8,128)(2,1)S(1)}, bf16[64,128]{1,0:T(8,128)(2,1)S(1)}, bf16[64,128]{1,0:T(8,128)(2,1)S(1)}, ...) custom-call(bf16[192,128]{1,0:T(8,128)(2,1)S(1)} %get-tuple-element., ...), custom_call_target="tpu_custom_call" | custom-call | tf_op jit(solution)/shard_map/chain/pallas_call | solution.py:262
  40.5 1.5 %collective-permute-start.7 = (bf16[64,128]{1,0:T(8,128)(2,1)S(1)}, bf16[64,128]{1,0:T(8,128)(2,1)S(1)}, u32[]{:S(2)}, u32[]{:S(2)}) collective-permute-start(bf16[64,128]{1,0:T(8,128)(2,1)S(1)} %get-tuple-element.54), channel_id=1, source_target_pairs={{0,4},{4,8},{8,12},{12,16},{16,20},{20,24},{24,28},{28,0},{1,5},{5... | collective-permute-start | bytes 49160 | tf_op jit(solution)/shard_map/ppermute | solution.py:351
  42.0 0.9 %collective-permute-start.8 = (bf16[64,128]{1,0:T(8,128)(2,1)S(1)}, bf16[64,128]{1,0:T(8,128)(2,1)S(1)}, u32[]{:S(2)}, u32[]{:S(2)}) collective-permute-start(bf16[64,128]{1,0:T(8,128)(2,1)S(1)} %get-tuple-element.55), channel_id=1, source_target_pairs={{0,8},{4,12},{8,16},{12,20},{16,24},{20,28},{24,0},{28,4},{1,9},{5... | collective-permute-start | bytes 49160 | tf_op jit(solution)/shard_map/ppermute | solution.py:351
  42.9 3.0 %collective-permute-start.9 = (bf16[64,128]{1,0:T(8,128)(2,1)S(1)}, bf16[64,128]{1,0:T(8,128)(2,1)S(1)}, u32[]{:S(2)}, u32[]{:S(2)}) collective-permute-start(bf16[64,128]{1,0:T(8,128)(2,1)S(1)} %get-tuple-element.56), channel_id=1, source_target_pairs={{0,12},{4,16},{8,20},{12,24},{16,28},{20,0},{24,4},{28,8},{1,13},{... | collective-permute-start | bytes 49160 | tf_op jit(solution)/shard_map/ppermute | solution.py:351
  45.9 1.1 %collective-permute-done.7.refs_1_ = bf16[64,128]{1,0:T(8,128)(2,1)S(1)} collective-permute-done((bf16[64,128]{1,0:T(8,128)(2,1)S(1)}, bf16[64,128]{1,0:T(8,128)(2,1)S(1)}, u32[]{:S(2)}, u32[]{:S(2)}) %collective-permute-start.7) | collective-permute-done | bytes 16416 | tf_op jit(solution)/shard_map/ppermute | solution.py:351
  47.0 1.3 %collective-permute-start.11 = (bf16[64,128]{1,0:T(8,128)(2,1)S(1)}, bf16[64,128]{1,0:T(8,128)(2,1)S(1)}, u32[]{:S(2)}, u32[]{:S(2)}) collective-permute-start(bf16[64,128]{1,0:T(8,128)(2,1)S(1)} %get-tuple-element.58), channel_id=1, source_target_pairs={{0,20},{4,24},{8,28},{12,0},{16,4},{20,8},{24,12},{28,16},{1,21},{... | collective-permute-start | bytes 49160 | tf_op jit(solution)/shard_map/ppermute | solution.py:351
  48.3 1.3 %collective-permute-start.12 = (bf16[64,128]{1,0:T(8,128)(2,1)S(1)}, bf16[64,128]{1,0:T(8,128)(2,1)S(1)}, u32[]{:S(2)}, u32[]{:S(2)}) collective-permute-start(bf16[64,128]{1,0:T(8,128)(2,1)S(1)} %get-tuple-element.59), channel_id=1, source_target_pairs={{0,24},{4,28},{8,0},{12,4},{16,8},{20,12},{24,16},{28,20},{1,25},{... | collective-permute-start | bytes 49160 | tf_op jit(solution)/shard_map/ppermute | solution.py:351
  49.7 1.6 %collective-permute-start.13 = (bf16[64,128]{1,0:T(8,128)(2,1)S(1)}, bf16[64,128]{1,0:T(8,128)(2,1)S(1)}, u32[]{:S(2)}, u32[]{:S(2)}) collective-permute-start(bf16[64,128]{1,0:T(8,128)(2,1)S(1)} %get-tuple-element.60), channel_id=1, source_target_pairs={{0,28},{4,0},{8,4},{12,8},{16,12},{20,16},{24,20},{28,24},{1,29},{... | collective-permute-start | bytes 49160 | tf_op jit(solution)/shard_map/ppermute | solution.py:351
  52.1 1.4 %collective-permute-done.13.refs_7_ = bf16[64,128]{1,0:T(8,128)(2,1)S(1)} collective-permute-done((bf16[64,128]{1,0:T(8,128)(2,1)S(1)}, bf16[64,128]{1,0:T(8,128)(2,1)S(1)}, u32[]{:S(2)}, u32[]{:S(2)}) %collective-permute-start.13) | collective-permute-done | bytes 16416 | tf_op jit(solution)/shard_map/ppermute | solution.py:351
  53.5 1.6 %apply.1 = (bf16[2,128,512]{2,1,0:T(8,128)(2,1)S(1)}, bf16[2,128,512]{2,1,0:T(8,128)(2,1)S(1)}) custom-call(f32[4,512,256]{2,1,0:T(8,128)S(1)} %row_maps.1.rows_ref, bf16[64,128]{1,0:T(8,128)(2,1)S(1)} %get-tuple-element.53.refs_0_, bf16[64,128]{1,0:T(8,128)(2,1)S(1)} %collective-permute-done.7.refs_1_, bf16[64,128]{1,0:T(8,128)(2,1)S(1)} %collective-permute-done.8.refs_2_, ...), custom_call_target="tpu_custom_call" | custom-call | tf_op jit(solution)/shard_map/apply/pallas_call | solution.py:311
  55.1 1.5 %collective-permute-done.14.got_ref = bf16[2,128,512]{2,1,0:T(8,128)(2,1)S(1)} collective-permute-done((bf16[2,128,512]{2,1,0:T(8,128)(2,1)S(1)}, bf16[2,128,512]{2,1,0:T(8,128)(2,1)S(1)}, u32[]{:S(2)}, u32[]{:S(2)}) %collective-permute-start.14) | collective-permute-done | bytes 262176 | tf_op jit(solution)/shard_map/ppermute | solution.py:346
  56.7 0.7 project.3
  57.4 1.6 %collective-permute-start.16 = (bf16[128,2048]{1,0:T(8,128)(2,1)S(1)}, bf16[128,2048]{1,0:T(8,128)(2,1)S(1)}, u32[]{:S(2)}, u32[]{:S(2)}) collective-permute-start(bf16[128,2048]{1,0:T(8,128)(2,1)S(1)} %project.3), channel_id=1, source_target_pairs={{0,2},{1,3},{2,0},{3,1},{4,6},{5,7},{6,4},{7,5},{8,10},{9,11},{10,... | collective-permute-start | bytes 1572872 | tf_op jit(solution)/shard_map/ppermute | solution.py:346
  59.7 11.7 %collective-permute-done.16 = bf16[128,2048]{1,0:T(8,128)(2,1)S(1)} collective-permute-done((bf16[128,2048]{1,0:T(8,128)(2,1)S(1)}, bf16[128,2048]{1,0:T(8,128)(2,1)S(1)}, u32[]{:S(2)}, u32[]{:S(2)}) %collective-permute-start.16) | collective-permute-done | bytes 524320 | tf_op jit(solution)/shard_map/ppermute | solution.py:346
  71.4 0.9 %add_convert_fusion = bf16[128,2048]{1,0:T(8,128)(2,1)} fusion(f32[128,2048]{1,0:T(8,128)S(1)} %project.2, bf16[128,2048]{1,0:T(8,128)(2,1)S(1)} %collective-permute-done.16), kind=kLoop, calls=%fused_computation | loop fusion | flops 786432 | bytes 2097152 | tf_op jit(solution)/shard_map/convert_element_type | solution.py:388
  (31 shorter events, 5.4 us)
Async XLA Ops:
  0.0 56.7 %collective-permute-start.15 = (bf16[512,2048]{1,0:T(8,128)(2,1)}, bf16[512,2048]{1,0:T(8,128)(2,1)S(1)}, u32[]{:S(2)}, u32[]{:S(2)}) collective-permute-start(bf16[512,2048]{1,0:T(8,128)(2,1)} %w_ref.3), channel_id=1, source_target_pairs={{0,1},{1,0},{2,3},{3,2},{4,5},{5,4},{6,7},{7,6},{8,9},{9,8},{10,11... | collective-permute-start | bytes 6291464 | tf_op jit(solution)/shard_map/ppermute | solution.py:346
  0.5 1.0 %copy-start.1 = (bf16[512,4,128]{2,1,0:T(4,128)(2,1)S(1)}, bf16[512,4,128]{2,1,0:T(4,128)(2,1)}, u32[]{:S(2)}) copy-start(bf16[512,4,128]{2,1,0:T(4,128)(2,1)} %param.8) | copy-start | bytes 1572868
  1.5 1.0 %copy-start.2 = (bf16[512,4,128]{2,1,0:T(4,128)(2,1)S(1)}, bf16[512,4,128]{2,1,0:T(4,128)(2,1)}, u32[]{:S(2)}) copy-start(bf16[512,4,128]{2,1,0:T(4,128)(2,1)} %param.7) | copy-start | bytes 1572868
  2.5 0.7 copy-start.3
  3.2 0.7 copy-start.4
  19.4 9.0 %collective-permute-start = (bf16[192,128]{1,0:T(8,128)(2,1)S(1)}, bf16[192,128]{1,0:T(8,128)(2,1)S(1)}, u32[]{:S(2)}, u32[]{:S(2)}) collective-permute-start(bf16[192,128]{1,0:T(8,128)(2,1)S(1)} %get-tuple-element.35), channel_id=1, source_target_pairs={{0,28},{4,0},{8,4},{12,8},{16,12},{20,16},{24,20},{28,24},{1,29},{... | collective-permute-start | bytes 147464 | tf_op jit(solution)/shard_map/ppermute | solution.py:351
  24.9 4.1 %collective-permute-start.1 = (bf16[192,128]{1,0:T(8,128)(2,1)S(1)}, bf16[192,128]{1,0:T(8,128)(2,1)S(1)}, u32[]{:S(2)}, u32[]{:S(2)}) collective-permute-start(bf16[192,128]{1,0:T(8,128)(2,1)S(1)} %get-tuple-element.36), channel_id=1, source_target_pairs={{0,24},{4,28},{8,0},{12,4},{16,8},{20,12},{24,16},{28,20},{1,25},{... | collective-permute-start | bytes 147464 | tf_op jit(solution)/shard_map/ppermute | solution.py:351
  25.3 5.0 %collective-permute-start.2 = (bf16[192,128]{1,0:T(8,128)(2,1)S(1)}, bf16[192,128]{1,0:T(8,128)(2,1)S(1)}, u32[]{:S(2)}, u32[]{:S(2)}) collective-permute-start(bf16[192,128]{1,0:T(8,128)(2,1)S(1)} %get-tuple-element.37), channel_id=1, source_target_pairs={{0,20},{4,24},{8,28},{12,0},{16,4},{20,8},{24,12},{28,16},{1,21},{... | collective-permute-start | bytes 147464 | tf_op jit(solution)/shard_map/ppermute | solution.py:351
  25.3 14.2 %collective-permute-start.3 = (bf16[192,128]{1,0:T(8,128)(2,1)S(1)}, bf16[192,128]{1,0:T(8,128)(2,1)S(1)}, u32[]{:S(2)}, u32[]{:S(2)}) collective-permute-start(bf16[192,128]{1,0:T(8,128)(2,1)S(1)} %get-tuple-element.38), channel_id=1, source_target_pairs={{0,16},{4,20},{8,24},{12,28},{16,0},{20,4},{24,8},{28,12},{1,17},{... | collective-permute-start | bytes 147464 | tf_op jit(solution)/shard_map/ppermute | solution.py:351
  28.4 11.2 %collective-permute-start.4 = (bf16[192,128]{1,0:T(8,128)(2,1)S(1)}, bf16[192,128]{1,0:T(8,128)(2,1)S(1)}, u32[]{:S(2)}, u32[]{:S(2)}) collective-permute-start(bf16[192,128]{1,0:T(8,128)(2,1)S(1)} %get-tuple-element.39), channel_id=1, source_target_pairs={{0,12},{4,16},{8,20},{12,24},{16,28},{20,0},{24,4},{28,8},{1,13},{... | collective-permute-start | bytes 147464 | tf_op jit(solution)/shard_map/ppermute | solution.py:351
  29.0 10.6 %collective-permute-start.5 = (bf16[192,128]{1,0:T(8,128)(2,1)S(1)}, bf16[192,128]{1,0:T(8,128)(2,1)S(1)}, u32[]{:S(2)}, u32[]{:S(2)}) collective-permute-start(bf16[192,128]{1,0:T(8,128)(2,1)S(1)} %get-tuple-element.40), channel_id=1, source_target_pairs={{0,8},{4,12},{8,16},{12,20},{16,24},{20,28},{24,0},{28,4},{1,9},{5... | collective-permute-start | bytes 147464 | tf_op jit(solution)/shard_map/ppermute | solution.py:351
  30.3 9.3 %collective-permute-start.6 = (bf16[192,128]{1,0:T(8,128)(2,1)S(1)}, bf16[192,128]{1,0:T(8,128)(2,1)S(1)}, u32[]{:S(2)}, u32[]{:S(2)}) collective-permute-start(bf16[192,128]{1,0:T(8,128)(2,1)S(1)} %get-tuple-element.41), channel_id=1, source_target_pairs={{0,4},{4,8},{8,12},{12,16},{16,20},{20,24},{24,28},{28,0},{1,5},{5... | collective-permute-start | bytes 147464 | tf_op jit(solution)/shard_map/ppermute | solution.py:351
  33.4 0.7 copy-start.5
  34.1 1.0 %copy-start.6 = (bf16[512,4,128]{2,1,0:T(4,128)(2,1)S(1)}, bf16[512,4,128]{2,1,0:T(4,128)(2,1)}, u32[]{:S(2)}) copy-start(bf16[512,4,128]{2,1,0:T(4,128)(2,1)} %param.6) | copy-start | bytes 1572868
  39.6 17.1 %copy-start = (bf16[512,2048]{1,0:T(8,128)(2,1)S(1)}, bf16[512,2048]{1,0:T(8,128)(2,1)}, u32[]{:S(2)}) copy-start(bf16[512,2048]{1,0:T(8,128)(2,1)} %w_ref.3) | copy-start | bytes 6291460
  40.5 6.5 %collective-permute-start.7 = (bf16[64,128]{1,0:T(8,128)(2,1)S(1)}, bf16[64,128]{1,0:T(8,128)(2,1)S(1)}, u32[]{:S(2)}, u32[]{:S(2)}) collective-permute-start(bf16[64,128]{1,0:T(8,128)(2,1)S(1)} %get-tuple-element.54), channel_id=1, source_target_pairs={{0,4},{4,8},{8,12},{12,16},{16,20},{20,24},{24,28},{28,0},{1,5},{5... | collective-permute-start | bytes 49160 | tf_op jit(solution)/shard_map/ppermute | solution.py:351
  42.0 6.3 %collective-permute-start.8 = (bf16[64,128]{1,0:T(8,128)(2,1)S(1)}, bf16[64,128]{1,0:T(8,128)(2,1)S(1)}, u32[]{:S(2)}, u32[]{:S(2)}) collective-permute-start(bf16[64,128]{1,0:T(8,128)(2,1)S(1)} %get-tuple-element.55), channel_id=1, source_target_pairs={{0,8},{4,12},{8,16},{12,20},{16,24},{20,28},{24,0},{28,4},{1,9},{5... | collective-permute-start | bytes 49160 | tf_op jit(solution)/shard_map/ppermute | solution.py:351
  42.9 6.8 %collective-permute-start.9 = (bf16[64,128]{1,0:T(8,128)(2,1)S(1)}, bf16[64,128]{1,0:T(8,128)(2,1)S(1)}, u32[]{:S(2)}, u32[]{:S(2)}) collective-permute-start(bf16[64,128]{1,0:T(8,128)(2,1)S(1)} %get-tuple-element.56), channel_id=1, source_target_pairs={{0,12},{4,16},{8,20},{12,24},{16,28},{20,0},{24,4},{28,8},{1,13},{... | collective-permute-start | bytes 49160 | tf_op jit(solution)/shard_map/ppermute | solution.py:351
  45.9 5.4 %collective-permute-start.10 = (bf16[64,128]{1,0:T(8,128)(2,1)S(1)}, bf16[64,128]{1,0:T(8,128)(2,1)S(1)}, u32[]{:S(2)}, u32[]{:S(2)}) collective-permute-start(bf16[64,128]{1,0:T(8,128)(2,1)S(1)} %get-tuple-element.57), channel_id=1, source_target_pairs={{0,16},{4,20},{8,24},{12,28},{16,0},{20,4},{24,8},{28,12},{1,17},{... | collective-permute-start | bytes 49160 | tf_op jit(solution)/shard_map/ppermute | solution.py:351
  47.0 4.6 %collective-permute-start.11 = (bf16[64,128]{1,0:T(8,128)(2,1)S(1)}, bf16[64,128]{1,0:T(8,128)(2,1)S(1)}, u32[]{:S(2)}, u32[]{:S(2)}) collective-permute-start(bf16[64,128]{1,0:T(8,128)(2,1)S(1)} %get-tuple-element.58), channel_id=1, source_target_pairs={{0,20},{4,24},{8,28},{12,0},{16,4},{20,8},{24,12},{28,16},{1,21},{... | collective-permute-start | bytes 49160 | tf_op jit(solution)/shard_map/ppermute | solution.py:351
  48.3 3.7 %collective-permute-start.12 = (bf16[64,128]{1,0:T(8,128)(2,1)S(1)}, bf16[64,128]{1,0:T(8,128)(2,1)S(1)}, u32[]{:S(2)}, u32[]{:S(2)}) collective-permute-start(bf16[64,128]{1,0:T(8,128)(2,1)S(1)} %get-tuple-element.59), channel_id=1, source_target_pairs={{0,24},{4,28},{8,0},{12,4},{16,8},{20,12},{24,16},{28,20},{1,25},{... | collective-permute-start | bytes 49160 | tf_op jit(solution)/shard_map/ppermute | solution.py:351
  49.7 3.8 %collective-permute-start.13 = (bf16[64,128]{1,0:T(8,128)(2,1)S(1)}, bf16[64,128]{1,0:T(8,128)(2,1)S(1)}, u32[]{:S(2)}, u32[]{:S(2)}) collective-permute-start(bf16[64,128]{1,0:T(8,128)(2,1)S(1)} %get-tuple-element.60), channel_id=1, source_target_pairs={{0,28},{4,0},{8,4},{12,8},{16,12},{20,16},{24,20},{28,24},{1,29},{... | collective-permute-start | bytes 49160 | tf_op jit(solution)/shard_map/ppermute | solution.py:351
  55.0 1.6 %collective-permute-start.14 = (bf16[2,128,512]{2,1,0:T(8,128)(2,1)S(1)}, bf16[2,128,512]{2,1,0:T(8,128)(2,1)S(1)}, u32[]{:S(2)}, u32[]{:S(2)}) collective-permute-start(bf16[2,128,512]{2,1,0:T(8,128)(2,1)S(1)} %get-tuple-element.62), channel_id=1, source_target_pairs={{0,1},{1,0},{2,3},{3,2},{4,5},{5,4},{6,7},{7,6},{8,9},{9,8},{10,11... | collective-permute-start | bytes 786440 | tf_op jit(solution)/shard_map/ppermute | solution.py:346
  57.4 14.0 %collective-permute-start.16 = (bf16[128,2048]{1,0:T(8,128)(2,1)S(1)}, bf16[128,2048]{1,0:T(8,128)(2,1)S(1)}, u32[]{:S(2)}, u32[]{:S(2)}) collective-permute-start(bf16[128,2048]{1,0:T(8,128)(2,1)S(1)} %project.3), channel_id=1, source_target_pairs={{0,2},{1,3},{2,0},{3,1},{4,6},{5,7},{6,4},{7,5},{8,10},{9,11},{10,... | collective-permute-start | bytes 1572872 | tf_op jit(solution)/shard_map/ppermute | solution.py:346

commit v3 on v2

--- a/solution.py
+++ b/solution.py
@@ -8,6 +8,7 @@
 from jax.sharding import PartitionSpec as P
 
 C = 128
+B = 16
 F32 = jnp.float32
 BF16 = jnp.bfloat16
 NN = (((1,), (0,)), ((), ()))
@@ -25,9 +26,18 @@
     return high, (x - high.astype(F32)).astype(BF16)
 
 
-def dot3(a, b, dims=NN):
+def twice(x):
+    return jnp.concatenate([x, x], axis=0)
+
+
+def dot3(a, b):
     (ah, al), (bh, bl) = a, b
-    return dot(ah, bh, dims) + (dot(al, bh, dims) + dot(ah, bl, dims))
+    width = bh.shape[1]
+    left = jnp.concatenate([ah, al], axis=1)
+    if width > C:
+        return dot(left, twice(bh)) + dot(ah, bl)
+    both = dot(left, twice(jnp.concatenate([bh, bl], axis=1)))
+    return both[:, :width] + both[:, width:]
 
 
 def iotas():
@@ -62,106 +72,121 @@
     return column, decay
 
 
+def base_inverse(lower, row, col):
+    on_block = (row // B) == (col // B)
+    blocks = jnp.where(on_block, lower, 0.0)
+    packed = sum(blocks[i * B : (i + 1) * B] for i in range(1, C // B)) + blocks[:B]
+    r, c = row[:B], col[:B]
+    found = jnp.where(r == c % B, 1.0, 0.0)
+    first = (c // B) * B
+    for j in range(B - 1):
+        factor = jnp.take_along_axis(packed, first + j, axis=1)
+        found = found - factor * found[j : j + 1]
+    return jnp.where(on_block, jnp.concatenate([found] * (C // B), axis=0), 0.0)
+
+
+def odd_rows(x, size):
+    return jnp.concatenate([x[i : i + size] for i in range(size, C, 2 * size)], axis=0)
+
+
+def weave(even, odd, size):
+    parts = []
+    for i in range(0, C // 2, size):
+        parts += [even[i : i + size], odd[i : i + size]]
+    return jnp.concatenate(parts, axis=0)
+
+
+def even_rows(x, size):
+    return jnp.concatenate([x[i : i + size] for i in range(0, C, 2 * size)], axis=0)
+
+
 def inverses(lowers, row, col):
-    eye = jnp.where(row == col, 1.0, 0.0)
-    found = [eye - jnp.where((row // 2) == (col // 2), a, 0.0) for a in lowers]
+    found = [base_inverse(a, row, col) for a in lowers]
     parts = [split(a) for a in lowers]
-    size = 2
+    size = B
     while size < C:
-        mask = ((row // (2 * size)) == (col // (2 * size))) & ((row // size) != (col // size))
-        zero = jnp.zeros((), BF16)
-        blocks = [(jnp.where(mask, h, zero), jnp.where(mask, l, zero)) for h, l in parts]
+        r, c = odd_rows(row, size), odd_rows(col, size)
+        mask = ((r // (2 * size)) == (c // (2 * size))) & ((r // size) != (c // size))
+        nothing = jnp.zeros((C // 2, C), BF16)
+        joins = [tuple(jnp.where(mask, odd_rows(x, size), nothing) for x in part) for part in parts]
         halves = [split(x) for x in found]
-        middle = [split(dot3(a, x)) for a, x in zip(blocks, halves)]
-        found = [x - dot3(h, y) for x, h, y in zip(found, halves, middle)]
+        middle = [split(dot3(a, x)) for a, x in zip(joins, halves)]
+        middle = [tuple(weave(nothing, x, size) for x in part) for part in middle]
+        lows = [dot3(tuple(odd_rows(x, size) for x in h), y) for h, y in zip(halves, middle)]
+        found = [weave(even_rows(x, size), odd_rows(x, size) - y, size) for x, y in zip(found, lows)]
         size *= 2
     return found
 
 
-def local_kernel(heads, step_heads, blocks, k_ref, v_ref, beta_ref, log_ref, wu_ref, n_ref, m_ref, ut_ref, *rest):
-    sends, (k32, v32) = rest[:blocks], rest[blocks:]
-    step = pl.program_id(0)
+def local_kernel(heads, batch, blocks, k_hbm, v_hbm, beta_hbm, log_hbm, wu_ref, n_ref, m_ref, ut_ref, *rest):
+    sends, (k16, v16, beta_ref, log_ref, k32, v32, sems) = rest[:blocks], rest[blocks:]
+    pairs = ((k_hbm, k16), (log_hbm, log_ref), (beta_hbm, beta_ref), (v_hbm, v16))
+    copies = [pltpu.make_async_copy(x, y, sems.at[i]) for i, (x, y) in enumerate(pairs)]
+    for copy in copies:
+        copy.start()
+    for copy in copies:
+        copy.wait()
+    k32[...] = k16[...].astype(F32)
+    v32[...] = v16[...].astype(F32)
     chunks = beta_ref.shape[1] // C
-
-    @pl.when(step == 0)
-    def _():
-        k32[...] = k_ref[...].astype(F32)
-        v32[...] = v_ref[...].astype(F32)
-
     row, col = iotas()
     eye = row == col
     within = row >= col
     strict = row > col
-    jobs = [(j, c) for j in range(step_heads) for c in range(chunks)]
-    lowers, sides, fades, ends = [], [], [], []
-    for j, c in jobs:
-        head = step * step_heads + j
-        rows = pl.ds(c * C * heads + head, C, stride=heads)
-        raw = k32[rows, :]
-        value = v32[rows, :]
-        beta = to_column(head_row(beta_ref, head, c), eye)
-        column, decay = decay_parts(head_row(log_ref, head, c), within, eye)
-        scale = inverse_scale(raw)
-        raw16 = raw.astype(BF16)
-        gram = dot(raw16, raw16, NT)
-        lowers.append(jnp.where(strict, gram * decay * (beta * scale) * to_row(scale, eye), 0.0))
-        unit = raw * scale
-        last = column[C - 1 : C, :]
-        sides.append(jnp.concatenate([unit * (beta * jnp.exp(column)), value * beta], axis=1))
-        fades.append(unit * jnp.exp(last - column))
-        ends.append(jnp.exp(last))
-    solved = [dot3(split(x), split(s)) for x, s in zip(inverses(lowers, row, col), sides)]
-    maps = []
-    for i, (j, c) in enumerate(jobs):
-        wu_ref[j * chunks + c] = solved[i]
-        both = dot3(split(fades[i]), split(solved[i]), TN)
-        maps.append((jnp.where(eye, ends[i], 0.0) - both[:, :C], both[:, C:]))
-    for j in range(step_heads):
-        state = jnp.concatenate(maps[j * chunks], axis=1)
-        for c in range(1, chunks):
-            n_ref[j * chunks + c] = state
-            moved, fresh = maps[j * chunks + c]
-            state = dot3(split(moved), split(state))
-            state = jnp.concatenate([state[:, :C], state[:, C:] + fresh], axis=1)
-        m_ref[step * step_heads + j] = state[:, :C].astype(BF16)
-        ut_ref[step * step_heads + j] = state[:, C:].T.astype(BF16)
-
+    for start in range(0, heads, batch):
+        jobs = [(head, c) for head in range(start, start + batch) for c in range(chunks)]
+        lowers, sides, fades, ends = [], [], [], []
+        for head, c in jobs:
+            rows = pl.ds(c * C * heads + head, C, stride=heads)
+            raw = k32[rows, :]
+            value = v32[rows, :]
+            beta = to_column(beta_ref[head : head + 1, c * C : (c + 1) * C], eye)
+            column, decay = decay_parts(log_ref[head : head + 1, c * C : (c + 1) * C], within, eye)
+            scale = inverse_scale(raw)
+            raw16 = raw.astype(BF16)
+            gram = dot(raw16, raw16, NT)
+            lowers.append(jnp.where(strict, gram * decay * (beta * scale) * to_row(scale, eye), 0.0))
+            unit = raw * scale
+            last = column[C - 1 : C, :]
+            sides.append(jnp.concatenate([unit * (beta * jnp.exp(column)), value * beta], axis=1))
+            fades.append((unit * jnp.exp(last - column)).T)
+            ends.append(jnp.exp(last))
+        solved = [dot3(split(x), split(s)) for x, s in zip(inverses(lowers, row, col), sides)]
+        maps = []
+        for i, (head, c) in enumerate(jobs):
+            wu_ref[head * chunks + c] = solved[i]
+            both = dot3(split(fades[i]), split(solved[i]))
+            maps.append((jnp.where(eye, ends[i], 0.0) - both[:, :C], both[:, C:]))
+        for j in range(batch):
+            head = start + j
+            state = jnp.concatenate(maps[j * chunks], axis=1)
+            for c in range(1, chunks):
+                n_ref[head * chunks + c] = state
+                moved, fresh = maps[j * chunks + c]
+                state = dot3(split(moved), split(state))
+                state = jnp.concatenate([state[:, :C], state[:, C:] + fresh], axis=1)
+            m_ref[head] = state[:, :C].astype(BF16)
+            ut_ref[head] = state[:, C:].T.astype(BF16)
     if not blocks:
         return
-
-    @pl.when(step == heads // step_heads - 1)
-    def _():
-        share = blocks // heads
-        width = C // share
-        for r in range(blocks):
-            target = lax.rem(lax.axis_index("seq") + blocks - r, blocks)
-            head, piece = target // share, lax.rem(target, share)
-            sends[r][:C, :] = m_ref[head]
-            sends[r][C:, :] = ut_ref[head, pl.ds(pl.multiple_of(piece * width, width), width), :]
-
-
-def local_maps(key, value, beta, log_decay, heads, step_heads, blocks):
+    share = blocks // heads
+    width = C // share
+    for r in range(blocks):
+        target = lax.rem(lax.axis_index("seq") + blocks - r, blocks)
+        head, piece = target // share, lax.rem(target, share)
+        sends[r][:C, :] = m_ref[head]
+        sends[r][C:, :] = ut_ref[head, pl.ds(pl.multiple_of(piece * width, width), width), :]
+
+
+def local_maps(key, value, beta, log_decay, heads, batch, blocks):
     tokens = beta.shape[1]
     tall = C + C * heads // blocks if blocks else 0
     chunks = tokens // C
-    whole = lambda shape: pl.BlockSpec(shape, lambda i: (0,) * len(shape))
-    part = lambda shape: pl.BlockSpec(shape, lambda i: (i,) + (0,) * (len(shape) - 1))
+    here = pl.BlockSpec(memory_space=pltpu.VMEM)
     return pl.pallas_call(
-        functools.partial(local_kernel, heads, step_heads, blocks),
-        grid=(heads // step_heads,),
-        in_specs=[
-            whole((tokens * heads, C)),
-            whole((tokens * heads, C)),
-            whole((heads, tokens)),
-            whole((heads, tokens)),
-        ],
-        out_specs=[
-            part((step_heads * chunks, C, 2 * C)),
-            part((step_heads * chunks, C, 2 * C)),
-            whole((heads, C, C)),
-            whole((heads, C, C)),
-        ]
-        + [whole((tall, C))] * blocks,
+        functools.partial(local_kernel, heads, batch, blocks),
+        in_specs=[pl.BlockSpec(memory_space=pltpu.HBM)] * 4,
+        out_specs=[here] * (4 + blocks),
         out_shape=[
             jax.ShapeDtypeStruct((heads * chunks, C, 2 * C), F32),
             jax.ShapeDtypeStruct((heads * chunks, C, 2 * C), F32),
@@ -170,10 +195,15 @@
         ]
         + [jax.ShapeDtypeStruct((tall, C), BF16)] * blocks,
         scratch_shapes=[
+            pltpu.VMEM((tokens * heads, C), BF16),
+            pltpu.VMEM((tokens * heads, C), BF16),
+            pltpu.VMEM((heads, tokens), F32),
+            pltpu.VMEM((heads, tokens), F32),
             pltpu.VMEM((tokens * heads, C), F32),
             pltpu.VMEM((tokens * heads, C), F32),
+            pltpu.SemaphoreType.DMA((4,)),
         ],
-        compiler_params=pltpu.CompilerParams(vmem_limit_bytes=24 * MIB),
+        compiler_params=pltpu.CompilerParams(vmem_limit_bytes=32 * MIB),
         name="local_maps",
     )(key, value, beta, log_decay)
 
@@ -234,7 +264,7 @@
 
 
 def chain_kernel(blocks, *refs):
-    sends, outs, (held,) = refs[:blocks], refs[blocks : 2 * blocks], refs[2 * blocks :]
+    sends, (out_ref, held) = refs[:blocks], refs[blocks:]
     me = lax.axis_index("seq")
     width = held.shape[1] - C
     for r in range(blocks):
@@ -251,9 +281,7 @@
                 both = dot(jnp.concatenate(split(state), axis=0), held[d, :C, :], NT)
                 state = both[:width] + both[width:] + added
     for d in range(blocks):
-        held[d, :width, :] = states[d].astype(BF16)
-    for r in range(blocks):
-        outs[r][...] = held[lax.rem(me + r, blocks), :width, :]
+        out_ref[d] = states[d].astype(BF16)
 
 
 def chain(sent):
@@ -261,30 +289,15 @@
     tall = sent[0].shape[0]
     return pl.pallas_call(
         functools.partial(chain_kernel, blocks),
-        out_shape=[jax.ShapeDtypeStruct((tall - C, C), BF16)] * blocks,
+        out_shape=jax.ShapeDtypeStruct((blocks, tall - C, C), BF16),
         scratch_shapes=[pltpu.VMEM((blocks, tall, C), BF16)],
         compiler_params=pltpu.CompilerParams(vmem_limit_bytes=4 * MIB),
         name="chain",
     )(*sent)
 
 
-def apply_kernel(heads, blocks, rows_ref, *refs):
-    entering, (keep_ref, send_ref, st_ref) = refs[:blocks], refs[blocks:]
+def apply_kernel(heads, rows_ref, st_ref, keep_ref, send_ref):
     step = pl.program_id(0)
-
-    @pl.when(step == 0)
-    def _():
-        if blocks == 1:
-            st_ref[...] = entering[0][...]
-            return
-        me = lax.axis_index("seq")
-        share = blocks // heads
-        width = C // share
-        for r in range(blocks):
-            source = lax.rem(me + blocks - r, blocks)
-            place = pl.multiple_of(lax.rem(source, share) * width, width)
-            st_ref[source // share, pl.ds(place, width), :] = entering[r][...]
-
     attended = []
     for h in range(heads):
         reach, fresh = rows_ref[h, :, :C], rows_ref[h, :, C:]
@@ -303,22 +316,22 @@
         send_ref[step // 2] = attended
 
 
-def apply(rows, entering, groups):
+def apply(rows, states_t, groups):
     heads, tokens, _ = rows.shape
     block = tokens // groups
-    blocks = len(entering)
     out = jax.ShapeDtypeStruct((groups // 2, block, heads * C), BF16)
     return pl.pallas_call(
-        functools.partial(apply_kernel, heads, blocks),
+        functools.partial(apply_kernel, heads),
         grid=(groups,),
-        in_specs=[pl.BlockSpec((heads, block, 2 * C), lambda i: (0, i, 0))]
-        + [pl.BlockSpec(x.shape, lambda i, n=x.ndim: (0,) * n) for x in entering],
+        in_specs=[
+            pl.BlockSpec((heads, block, 2 * C), lambda i: (0, i, 0)),
+            pl.BlockSpec(states_t.shape, lambda i: (0, 0, 0)),
+        ],
         out_specs=[pl.BlockSpec(out.shape, lambda i: (0, 0, 0))] * 2,
         out_shape=[out, out],
-        scratch_shapes=[pltpu.VMEM((heads, C, C), BF16)],
         compiler_params=pltpu.CompilerParams(vmem_limit_bytes=14 * MIB),
         name="apply",
-    )(rows, *entering)
+    )(rows, states_t)
 
 
 def project_kernel(other, keep_ref, got_ref, w_ref, w2_ref, out_ref):
@@ -372,15 +385,14 @@
     q2, k2, v2 = flat(query), flat(key), flat(value)
     weight2 = swap(out_weight, "head", 1)
     direct = blocks % heads == 0 and C * heads // blocks >= 64
-    wu, states, moved, added, *sends = local_maps(k2, v2, beta, log_decay, heads, 1, blocks if direct else 0)
+    wu, states, moved, added, *sends = local_maps(k2, v2, beta, log_decay, heads, 2, blocks if direct else 0)
     rows = row_maps(q2, k2, log_decay, wu, states, heads, 1)
     if direct:
         sent = [x if r == 0 else shift(x, "seq", -r) for r, x in enumerate(sends)]
         sent, rows = lax.optimization_barrier((sent, rows))
-        entering = chain(sent)
-        entering = [x if r == 0 else shift(x, "seq", r) for r, x in enumerate(entering)]
+        entering = lax.all_to_all(chain(sent), "seq", 0, 0, tiled=True).reshape(heads, C, C)
     else:
-        entering = [prefix(moved, added)]
+        entering = prefix(moved, added)
     keep, away = apply(rows, entering, groups)
     got = swap(away, "head", 1)
     theirs = swap(project(True, keep, got, out_weight, weight2), "head", 2)

time: 72.7 us -> 63.2 us (0.87)
  blocking collectives: 0 us -> 11.7 us
  starting transfers between devices: 25 us -> 15.3 us
  Pallas kernels: 23.8 us -> 16.1 us
  waiting for transfers between devices: 17.4 us -> 14.1 us
    all_to_all x0 -> x1, blocking collectives: none -> 11.7 us  [body(): lax.all_to_all(chain(sent), 'seq', 0, 0, tiled=True).reshape(heads, C, C)]
    ppermute x14 -> x7, starting transfers between devices: 22.9 us -> 13.2 us  [shift(): lax.ppermute(x, axis, [(i, (i + amount) % count) for i in range(count)])]
    pallas_call x3, Pallas kernels: 17.9 us -> 10.5 us  [the longest x1 8.25 us: local_maps(): pl.pallas_call(functools.partial(local_kernel, heads, batch, blocks), in_...]
    ppermute x14 -> x7, waiting for transfers between devices: 4.13 us -> 0.82 us  [shift(): lax.ppermute(x, axis, [(i, (i + amount) % count) for i in range(count)])]
    unnamed x14 -> x12, local copies, waits for them, and re-layouts: 5.22 us -> 4.52 us
  transfers between devices with their start and end apart: 17 -> 10, of which waited for: 8 -> 4; matrix products, arithmetic and copies ran while one was open for 0% -> 0% of each run, Pallas kernels for 32% -> 25%
where the time goes in v3:
time: 63.2 us; the launch traced here: 62.8 us
  Pallas kernels  16.1 us (25%)
  starting transfers between devices  15.3 us (24%)
  waiting for transfers between devices  14.1 us (22%)
  blocking collectives  11.7 us (19%)
  local copies, waits for them, and re-layouts  4.52 us (7%)
  other arithmetic  0.9 us (1%)
    ppermute x3, waiting for transfers between devices, swap(): return lax.ppermute(x, axis, [(i, i ^ bit) for i in range(count)])  13.3 us
    ppermute x7, starting transfers between devices, shift(): lax.ppermute(x, axis, [(i, (i + amount) % count) for i in range(count)])  13.2 us
    all_to_all x1, blocking collectives, body(): lax.all_to_all(chain(sent), 'seq', 0, 0, tiled=True).reshape(heads, C, C)  11.7 us
    pallas_call x1, Pallas kernels, local_maps(): pl.pallas_call(functools.partial(local_kernel, heads, batch, blocks), in_...  8.25 us
    unnamed x12, local copies, waits for them, and re-layouts  4.52 us
    pallas_call x1, Pallas kernels, row_maps(): pl.pallas_call(functools.partial(rows_kernel, heads, step_heads), grid=(h...  4.16 us
    ppermute x3, starting transfers between devices, swap(): return lax.ppermute(x, axis, [(i, i ^ bit) for i in range(count)])  2.11 us
    pallas_call x1, Pallas kernels, apply(): pl.pallas_call(functools.partial(apply_kernel, heads), grid=(groups,), in...  1.44 us
  transfers between devices with their start and end apart: 10, of which 4 were waited for; matrix products, arithmetic and copies ran while one was open for 0% of the time, Pallas kernels for 25%

profile of v3, /device:TPU:0, one launch (start us, length us, event | category | flops | bytes accessed | tf_op | source)
XLA Modules:
  0.0 62.8 jit_solution(8242046312507388389)
XLA Ops:
  0.0 0.5 collective-permute-start.8
  0.5 1.0 %copy-done.1 = bf16[512,4,128]{2,1,0:T(4,128)(2,1)S(1)} copy-done((bf16[512,4,128]{2,1,0:T(4,128)(2,1)S(1)}, bf16[512,4,128]{2,1,0:T(4,128)(2,1)}, u32[]{:S(2)}) %copy-start.1) | copy-done | bytes 524312
  1.5 1.0 %copy-done.2 = bf16[512,4,128]{2,1,0:T(4,128)(2,1)S(1)} copy-done((bf16[512,4,128]{2,1,0:T(4,128)(2,1)S(1)}, bf16[512,4,128]{2,1,0:T(4,128)(2,1)}, u32[]{:S(2)}) %copy-start.2) | copy-done | bytes 524312
  2.5 0.7 %copy-done.3 = f32[4,512]{1,0:T(4,128)S(1)} copy-done((f32[4,512]{1,0:T(4,128)S(1)}, f32[4,512]{1,0:T(4,128)}, u32[]{:S(2)}) %copy-start.3) | copy-done | bytes 8216
  3.2 0.7 %copy-done.4 = f32[4,512]{1,0:T(4,128)S(1)} copy-done((f32[4,512]{1,0:T(4,128)S(1)}, f32[4,512]{1,0:T(4,128)}, u32[]{:S(2)}) %copy-start.4) | copy-done | bytes 8216
  3.9 8.2 %local_maps.1 = (f32[16,128,256]{2,1,0:T(8,128)S(1)}, f32[16,128,256]{2,1,0:T(8,128)S(1)}, bf16[4,128,128]{2,1,0:T(8,128)(2,1)}, bf16[4,128,128]{2,1,0:T(8,128)(...) custom-call(bf16[2048,128]{1,0:T(8,128)(2,1)S(1)} %bitcast.6, ...), custom_call_target="tpu_custom_call" | custom-call | tf_op jit(solution)/shard_map/local_maps/pallas_call | solution.py:186
  12.2 5.6 %collective-permute-start = (bf16[192,128]{1,0:T(8,128)(2,1)S(1)}, bf16[192,128]{1,0:T(8,128)(2,1)S(1)}, u32[]{:S(2)}, u32[]{:S(2)}) collective-permute-start(bf16[192,128]{1,0:T(8,128)(2,1)S(1)} %get-tuple-element.27), channel_id=1, source_target_pairs={{0,28},{4,0},{8,4},{12,8},{16,12},{20,16},{24,20},{28,24},{1,29},{... | collective-permute-start | bytes 147464 | tf_op jit(solution)/shard_map/ppermute | solution.py:364
  17.8 0.4 collective-permute-start.1
  18.2 3.0 %collective-permute-start.3 = (bf16[192,128]{1,0:T(8,128)(2,1)S(1)}, bf16[192,128]{1,0:T(8,128)(2,1)S(1)}, u32[]{:S(2)}, u32[]{:S(2)}) collective-permute-start(bf16[192,128]{1,0:T(8,128)(2,1)S(1)} %get-tuple-element.30), channel_id=1, source_target_pairs={{0,16},{4,20},{8,24},{12,28},{16,0},{20,4},{24,8},{28,12},{1,17},{... | collective-permute-start | bytes 147464 | tf_op jit(solution)/shard_map/ppermute | solution.py:364
  21.2 0.7 %collective-permute-done.1.refs_2_ = bf16[192,128]{1,0:T(8,128)(2,1)S(1)} collective-permute-done((bf16[192,128]{1,0:T(8,128)(2,1)S(1)}, bf16[192,128]{1,0:T(8,128)(2,1)S(1)}, u32[]{:S(2)}, u32[]{:S(2)}) %collective-permute-start.1) | collective-permute-done | bytes 49184 | tf_op jit(solution)/shard_map/ppermute | solution.py:364
  21.9 1.2 %collective-permute-start.5 = (bf16[192,128]{1,0:T(8,128)(2,1)S(1)}, bf16[192,128]{1,0:T(8,128)(2,1)S(1)}, u32[]{:S(2)}, u32[]{:S(2)}) collective-permute-start(bf16[192,128]{1,0:T(8,128)(2,1)S(1)} %get-tuple-element.32), channel_id=1, source_target_pairs={{0,8},{4,12},{8,16},{12,20},{16,24},{20,28},{24,0},{28,4},{1,9},{5... | collective-permute-start | bytes 147464 | tf_op jit(solution)/shard_map/ppermute | solution.py:364
  23.1 0.2 collective-permute-done.2.refs_3_
  23.2 3.0 %collective-permute-start.6 = (bf16[192,128]{1,0:T(8,128)(2,1)S(1)}, bf16[192,128]{1,0:T(8,128)(2,1)S(1)}, u32[]{:S(2)}, u32[]{:S(2)}) collective-permute-start(bf16[192,128]{1,0:T(8,128)(2,1)S(1)} %get-tuple-element.33), channel_id=1, source_target_pairs={{0,4},{4,8},{8,12},{12,16},{16,20},{20,24},{24,28},{28,0},{1,5},{5... | collective-permute-start | bytes 147464 | tf_op jit(solution)/shard_map/ppermute | solution.py:364
  26.2 1.0 %copy-done.5 = bf16[512,4,128]{2,1,0:T(4,128)(2,1)S(1)} copy-done((bf16[512,4,128]{2,1,0:T(4,128)(2,1)S(1)}, bf16[512,4,128]{2,1,0:T(4,128)(2,1)}, u32[]{:S(2)}) %copy-start.5) | copy-done | bytes 524312
  27.3 4.2 %row_maps.1.rows_ref = f32[4,512,256]{2,1,0:T(8,128)S(1)} custom-call(bf16[2048,128]{1,0:T(8,128)(2,1)S(1)} %bitcast.8, bf16[2048,128]{1,0:T(8,128)(2,1)S(1)} %bitcast.7, f32[4,512]{1,0:T(4,128)S(1)} %copy-done.4, f32[16,128,256]{2,1,0:T(8,128)S(1)} %get-tuple-element.34.wu_ref, f32[16,128,256]{2,1,0:T(8,128)S(1)} %get-tuple-element.35.n_ref), custom_call_target="tpu_custom_call" | custom-call | flops 4000000000 | bytes 10000000 | tf_op jit(solution)/shard_map/row_maps/pallas_call | solution.py:247
  31.5 0.8 %chain.1 = bf16[8,64,128]{2,1,0:T(8,128)(2,1)S(1)} custom-call(bf16[192,128]{1,0:T(8,128)(2,1)S(1)} %get-tuple-element.37.refs_0_, bf16[192,128]{1,0:T(8,128)(2,1)S(1)} %collective-permute-done.refs_1_, bf16[192,128]{1,0:T(8,128)(2,1)S(1)} %collective-permute-done.1.refs_2_, bf16[192,128]{1,0:T(8,128)(2,1)S(1)} %collective-permute-done.2.refs_3_, ...), custom_call_target="tpu_custom_call" | custom-call | tf_op jit(solution)/shard_map/chain/pallas_call | solution.py:290
  32.3 11.7 %all_to_all.5 = bf16[8,64,128]{2,1,0:T(8,128)(2,1)S(1)} all-to-all(bf16[8,64,128]{2,1,0:T(8,128)(2,1)S(1)} %chain.1), channel_id=1, replica_groups=mesh['seq'=8,'head'=4] {'seq'}, dimensions={0} | all-to-all | bytes 262144 | tf_op jit(solution)/shard_map/all_to_all | solution.py:393
  44.1 1.4 %apply.1 = (bf16[2,128,512]{2,1,0:T(8,128)(2,1)S(1)}, bf16[2,128,512]{2,1,0:T(8,128)(2,1)S(1)}) custom-call(f32[4,512,256]{2,1,0:T(8,128)S(1)} %row_maps.1.rows_ref, bf16[4,128,128]{2,1,0:T(8,128)(2,1)S(1)} %bitcast.4), custom_call_target="tpu_custom_call" | custom-call | tf_op jit(solution)/shard_map/apply/pallas_call | solution.py:323
  45.6 1.5 %collective-permute-done.7.got_ref = bf16[2,128,512]{2,1,0:T(8,128)(2,1)S(1)} collective-permute-done((bf16[2,128,512]{2,1,0:T(8,128)(2,1)S(1)}, bf16[2,128,512]{2,1,0:T(8,128)(2,1)S(1)}, u32[]{:S(2)}, u32[]{:S(2)}) %collective-permute-start.7) | collective-permute-done | bytes 262176 | tf_op jit(solution)/shard_map/ppermute | solution.py:359
  47.1 0.7 %project.3 = bf16[128,2048]{1,0:T(8,128)(2,1)S(1)} custom-call(bf16[2,128,512]{2,1,0:T(8,128)(2,1)S(1)} %get-tuple-element.45.keep_ref, bf16[2,128,512]{2,1,0:T(8,128)(2,1)S(1)} %collective-permute-done.7.got_ref, bf16[512,2048]{1,0:T(8,128)(2,1)S(1)} %copy-done, bf16[512,2048]{1,0:T(8,128)(2,1)S(1)} %collective-permute-done.8.w2_ref), custom_call_target="tpu_custom_call" | custom-call | flops 536870912 | bytes 4194304 | tf_op jit(solution)/shard_map/project/pallas_call | solution.py:346
  47.9 1.6 %collective-permute-start.9 = (bf16[128,2048]{1,0:T(8,128)(2,1)S(1)}, bf16[128,2048]{1,0:T(8,128)(2,1)S(1)}, u32[]{:S(2)}, u32[]{:S(2)}) collective-permute-start(bf16[128,2048]{1,0:T(8,128)(2,1)S(1)} %project.3), channel_id=1, source_target_pairs={{0,2},{1,3},{2,0},{3,1},{4,6},{5,7},{6,4},{7,5},{8,10},{9,11},{10,... | collective-permute-start | bytes 1572872 | tf_op jit(solution)/shard_map/ppermute | solution.py:359
  49.4 0.7 %project.2 = f32[128,2048]{1,0:T(8,128)S(1)} custom-call(bf16[2,128,512]{2,1,0:T(8,128)(2,1)S(1)} %get-tuple-element.45.keep_ref, bf16[2,128,512]{2,1,0:T(8,128)(2,1)S(1)} %collective-permute-done.7.got_ref, bf16[512,2048]{1,0:T(8,128)(2,1)S(1)} %copy-done, bf16[512,2048]{1,0:T(8,128)(2,1)S(1)} %collective-permute-done.8.w2_ref), custom_call_target="tpu_custom_call" | custom-call | flops 536870912 | bytes 4194304 | tf_op jit(solution)/shard_map/project/pallas_call | solution.py:346
  50.2 11.7 %collective-permute-done.9 = bf16[128,2048]{1,0:T(8,128)(2,1)S(1)} collective-permute-done((bf16[128,2048]{1,0:T(8,128)(2,1)S(1)}, bf16[128,2048]{1,0:T(8,128)(2,1)S(1)}, u32[]{:S(2)}, u32[]{:S(2)}) %collective-permute-start.9) | collective-permute-done | bytes 524320 | tf_op jit(solution)/shard_map/ppermute | solution.py:359
  61.9 0.9 %add_convert_fusion = bf16[128,2048]{1,0:T(8,128)(2,1)} fusion(f32[128,2048]{1,0:T(8,128)S(1)} %project.2, bf16[128,2048]{1,0:T(8,128)(2,1)S(1)} %collective-permute-done.9), kind=kLoop, calls=%fused_computation | loop fusion | flops 786432 | bytes 2097152 | tf_op jit(solution)/shard_map/convert_element_type | solution.py:400
  (16 shorter events, 0.1 us)
Async XLA Ops:
  0.0 47.1 %collective-permute-start.8 = (bf16[512,2048]{1,0:T(8,128)(2,1)}, bf16[512,2048]{1,0:T(8,128)(2,1)S(1)}, u32[]{:S(2)}, u32[]{:S(2)}) collective-permute-start(bf16[512,2048]{1,0:T(8,128)(2,1)} %w_ref.3), channel_id=1, source_target_pairs={{0,1},{1,0},{2,3},{3,2},{4,5},{5,4},{6,7},{7,6},{8,9},{9,8},{10,11... | collective-permute-start | bytes 6291464 | tf_op jit(solution)/shard_map/ppermute | solution.py:359
  0.5 1.0 %copy-start.1 = (bf16[512,4,128]{2,1,0:T(4,128)(2,1)S(1)}, bf16[512,4,128]{2,1,0:T(4,128)(2,1)}, u32[]{:S(2)}) copy-start(bf16[512,4,128]{2,1,0:T(4,128)(2,1)} %param.8) | copy-start | bytes 1572868
  1.5 1.0 %copy-start.2 = (bf16[512,4,128]{2,1,0:T(4,128)(2,1)S(1)}, bf16[512,4,128]{2,1,0:T(4,128)(2,1)}, u32[]{:S(2)}) copy-start(bf16[512,4,128]{2,1,0:T(4,128)(2,1)} %param.7) | copy-start | bytes 1572868
  2.5 0.7 %copy-start.3 = (f32[4,512]{1,0:T(4,128)S(1)}, f32[4,512]{1,0:T(4,128)}, u32[]{:S(2)}) copy-start(f32[4,512]{1,0:T(4,128)} %beta_hbm.1) | copy-start | bytes 24580
  3.2 0.7 %copy-start.4 = (f32[4,512]{1,0:T(4,128)S(1)}, f32[4,512]{1,0:T(4,128)}, u32[]{:S(2)}) copy-start(f32[4,512]{1,0:T(4,128)} %log_ref.1) | copy-start | bytes 24580
  12.2 9.0 %collective-permute-start = (bf16[192,128]{1,0:T(8,128)(2,1)S(1)}, bf16[192,128]{1,0:T(8,128)(2,1)S(1)}, u32[]{:S(2)}, u32[]{:S(2)}) collective-permute-start(bf16[192,128]{1,0:T(8,128)(2,1)S(1)} %get-tuple-element.27), channel_id=1, source_target_pairs={{0,28},{4,0},{8,4},{12,8},{16,12},{20,16},{24,20},{28,24},{1,29},{... | collective-permute-start | bytes 147464 | tf_op jit(solution)/shard_map/ppermute | solution.py:364
  17.8 4.1 %collective-permute-start.1 = (bf16[192,128]{1,0:T(8,128)(2,1)S(1)}, bf16[192,128]{1,0:T(8,128)(2,1)S(1)}, u32[]{:S(2)}, u32[]{:S(2)}) collective-permute-start(bf16[192,128]{1,0:T(8,128)(2,1)S(1)} %get-tuple-element.28), channel_id=1, source_target_pairs={{0,24},{4,28},{8,0},{12,4},{16,8},{20,12},{24,16},{28,20},{1,25},{... | collective-permute-start | bytes 147464 | tf_op jit(solution)/shard_map/ppermute | solution.py:364
  18.2 5.0 %collective-permute-start.2 = (bf16[192,128]{1,0:T(8,128)(2,1)S(1)}, bf16[192,128]{1,0:T(8,128)(2,1)S(1)}, u32[]{:S(2)}, u32[]{:S(2)}) collective-permute-start(bf16[192,128]{1,0:T(8,128)(2,1)S(1)} %get-tuple-element.29), channel_id=1, source_target_pairs={{0,20},{4,24},{8,28},{12,0},{16,4},{20,8},{24,12},{28,16},{1,21},{... | collective-permute-start | bytes 147464 | tf_op jit(solution)/shard_map/ppermute | solution.py:364
  18.2 13.2 %collective-permute-start.3 = (bf16[192,128]{1,0:T(8,128)(2,1)S(1)}, bf16[192,128]{1,0:T(8,128)(2,1)S(1)}, u32[]{:S(2)}, u32[]{:S(2)}) collective-permute-start(bf16[192,128]{1,0:T(8,128)(2,1)S(1)} %get-tuple-element.30), channel_id=1, source_target_pairs={{0,16},{4,20},{8,24},{12,28},{16,0},{20,4},{24,8},{28,12},{1,17},{... | collective-permute-start | bytes 147464 | tf_op jit(solution)/shard_map/ppermute | solution.py:364
  21.2 10.2 %collective-permute-start.4 = (bf16[192,128]{1,0:T(8,128)(2,1)S(1)}, bf16[192,128]{1,0:T(8,128)(2,1)S(1)}, u32[]{:S(2)}, u32[]{:S(2)}) collective-permute-start(bf16[192,128]{1,0:T(8,128)(2,1)S(1)} %get-tuple-element.31), channel_id=1, source_target_pairs={{0,12},{4,16},{8,20},{12,24},{16,28},{20,0},{24,4},{28,8},{1,13},{... | collective-permute-start | bytes 147464 | tf_op jit(solution)/shard_map/ppermute | solution.py:364
  21.9 9.6 %collective-permute-start.5 = (bf16[192,128]{1,0:T(8,128)(2,1)S(1)}, bf16[192,128]{1,0:T(8,128)(2,1)S(1)}, u32[]{:S(2)}, u32[]{:S(2)}) collective-permute-start(bf16[192,128]{1,0:T(8,128)(2,1)S(1)} %get-tuple-element.32), channel_id=1, source_target_pairs={{0,8},{4,12},{8,16},{12,20},{16,24},{20,28},{24,0},{28,4},{1,9},{5... | collective-permute-start | bytes 147464 | tf_op jit(solution)/shard_map/ppermute | solution.py:364
  23.2 8.3 %collective-permute-start.6 = (bf16[192,128]{1,0:T(8,128)(2,1)S(1)}, bf16[192,128]{1,0:T(8,128)(2,1)S(1)}, u32[]{:S(2)}, u32[]{:S(2)}) collective-permute-start(bf16[192,128]{1,0:T(8,128)(2,1)S(1)} %get-tuple-element.33), channel_id=1, source_target_pairs={{0,4},{4,8},{8,12},{12,16},{16,20},{20,24},{24,28},{28,0},{1,5},{5... | collective-permute-start | bytes 147464 | tf_op jit(solution)/shard_map/ppermute | solution.py:364
  26.2 1.0 %copy-start.5 = (bf16[512,4,128]{2,1,0:T(4,128)(2,1)S(1)}, bf16[512,4,128]{2,1,0:T(4,128)(2,1)}, u32[]{:S(2)}) copy-start(bf16[512,4,128]{2,1,0:T(4,128)(2,1)} %param.6) | copy-start | bytes 1572868
  31.5 15.7 %copy-start = (bf16[512,2048]{1,0:T(8,128)(2,1)S(1)}, bf16[512,2048]{1,0:T(8,128)(2,1)}, u32[]{:S(2)}) copy-start(bf16[512,2048]{1,0:T(8,128)(2,1)} %w_ref.3) | copy-start | bytes 6291460
  45.5 1.6 %collective-permute-start.7 = (bf16[2,128,512]{2,1,0:T(8,128)(2,1)S(1)}, bf16[2,128,512]{2,1,0:T(8,128)(2,1)S(1)}, u32[]{:S(2)}, u32[]{:S(2)}) collective-permute-start(bf16[2,128,512]{2,1,0:T(8,128)(2,1)S(1)} %get-tuple-element.46), channel_id=1, source_target_pairs={{0,1},{1,0},{2,3},{3,2},{4,5},{5,4},{6,7},{7,6},{8,9},{9,8},{10,11... | collective-permute-start | bytes 786440 | tf_op jit(solution)/shard_map/ppermute | solution.py:359
  47.9 14.0 %collective-permute-start.9 = (bf16[128,2048]{1,0:T(8,128)(2,1)S(1)}, bf16[128,2048]{1,0:T(8,128)(2,1)S(1)}, u32[]{:S(2)}, u32[]{:S(2)}) collective-permute-start(bf16[128,2048]{1,0:T(8,128)(2,1)S(1)} %project.3), channel_id=1, source_target_pairs={{0,2},{1,3},{2,0},{3,1},{4,6},{5,7},{6,4},{7,5},{8,10},{9,11},{10,... | collective-permute-start | bytes 1572872 | tf_op jit(solution)/shard_map/ppermute | solution.py:359

commit v4 on v3

v4 whole, which is shorter than its diff:
```python
import functools

import jax
import jax.numpy as jnp
from jax import lax
from jax.experimental import pallas as pl
from jax.experimental.pallas import tpu as pltpu
from jax.sharding import PartitionSpec as P

C = 128
B = 16
F32 = jnp.float32
BF16 = jnp.bfloat16
NN = (((1,), (0,)), ((), ()))
NT = (((1,), (1,)), ((), ()))
TN = (((0,), (0,)), ((), ()))
MIB = 1024 * 1024


def dot(a, b, dims=NN):
    return lax.dot_general(a, b, dims, preferred_element_type=F32)


def split(x):
    high = x.astype(BF16)
    return high, (x - high.astype(F32)).astype(BF16)


def twice(x):
    return jnp.concatenate([x, x], axis=0)


def dot3(a, b):
    (ah, al), (bh, bl) = a, b
    width = bh.shape[1]
    left = jnp.concatenate([ah, al], axis=1)
    if width > C:
        return dot(left, twice(bh)) + dot(ah, bl)
    both = dot(left, twice(jnp.concatenate([bh, bl], axis=1)))
    return both[:, :width] + both[:, width:]


def iotas():
    return (
        lax.broadcasted_iota(jnp.int32, (C, C), 0),
        lax.broadcasted_iota(jnp.int32, (C, C), 1),
    )


def to_column(row, eye):
    return jnp.sum(jnp.where(eye, row, 0.0), axis=1, keepdims=True)


def to_row(column, eye):
    return jnp.sum(jnp.where(eye, column, 0.0), axis=0, keepdims=True)


def inverse_scale(rows):
    return lax.rsqrt(jnp.sum(rows * rows, axis=1, keepdims=True) + 1e-06)


def decay_parts(log_row, within, eye):
    column = jnp.sum(jnp.where(within, log_row, 0.0), axis=1, keepdims=True)
    row = to_row(column, eye)
    decay = jnp.where(within, jnp.exp(jnp.where(within, column - row, 0.0)), 0.0)
    return column, decay


def base_inverse(lower, row, col):
    on_block = (row // B) == (col // B)
    blocks = jnp.where(on_block, lower, 0.0)
    packed = sum(blocks[i * B : (i + 1) * B] for i in range(1, C // B)) + blocks[:B]
    r, c = row[:B], col[:B]
    found = jnp.where(r == c % B, 1.0, 0.0)
    first = (c // B) * B
    for j in range(B - 1):
        factor = jnp.take_along_axis(packed, first + j, axis=1)
        found = found - factor * found[j : j + 1]
    return jnp.where(on_block, jnp.concatenate([found] * (C // B), axis=0), 0.0)


def odd_rows(x, size):
    return jnp.concatenate([x[i : i + size] for i in range(size, C, 2 * size)], axis=0)


def weave(even, odd, size):
    parts = []
    for i in range(0, C // 2, size):
        parts += [even[i : i + size], odd[i : i + size]]
    return jnp.concatenate(parts, axis=0)


def even_rows(x, size):
    return jnp.concatenate([x[i : i + size] for i in range(0, C, 2 * size)], axis=0)


def inverses(lowers, row, col):
    found = [base_inverse(a, row, col) for a in lowers]
    parts = [split(a) for a in lowers]
    size = B
    while size < C:
        r, c = odd_rows(row, size), odd_rows(col, size)
        mask = ((r // (2 * size)) == (c // (2 * size))) & ((r // size) != (c // size))
        nothing = jnp.zeros((C // 2, C), BF16)
        joins = [tuple(jnp.where(mask, odd_rows(x, size), nothing) for x in part) for part in parts]
        halves = [split(x) for x in found]
        middle = [split(dot3(a, x)) for a, x in zip(joins, halves)]
        middle = [tuple(weave(nothing, x, size) for x in part) for part in middle]
        lows = [dot3(tuple(odd_rows(x, size) for x in h), y) for h, y in zip(halves, middle)]
        found = [weave(even_rows(x, size), odd_rows(x, size) - y, size) for x, y in zip(found, lows)]
        size *= 2
    return found


def first_heads(heads, phase):
    return (phase, phase + heads // 2)


def fetch(pairs, sems):
    copies = [pltpu.make_async_copy(x, y, sems.at[i]) for i, (x, y) in enumerate(pairs)]
    for copy in copies:
        copy.start()
    for copy in copies:
        copy.wait()


def in_hbm(*arrays):
    return [pltpu.with_memory_space_constraint(x, pltpu.HBM) for x in arrays]


def chunk_rows(heads, head, c):
    return pl.ds(c * C * heads + head, C, stride=heads)


def tokens_of(ref, head, c):
    return ref[head : head + 1, c * C : (c + 1) * C]


def local_body(heads, phase, k32, v32, beta_ref, log_ref, wu_ref, n_ref, own_ref, send_ref):
    chunks = beta_ref.shape[1] // C
    row, col = iotas()
    eye = row == col
    within = row >= col
    strict = row > col
    pair = first_heads(heads, phase)
    jobs = [(head, c) for head in pair for c in range(chunks)]
    lowers, sides, fades, ends = [], [], [], []
    for head, c in jobs:
        raw = k32[chunk_rows(heads, head, c), :]
        value = v32[chunk_rows(heads, head, c), :]
        beta = to_column(tokens_of(beta_ref, head, c), eye)
        column, decay = decay_parts(tokens_of(log_ref, head, c), within, eye)
        scale = inverse_scale(raw)
        raw16 = raw.astype(BF16)
        gram = dot(raw16, raw16, NT)
        lowers.append(jnp.where(strict, gram * decay * (beta * scale) * to_row(scale, eye), 0.0))
        unit = raw * scale
        last = column[C - 1 : C, :]
        sides.append(jnp.concatenate([unit * (beta * jnp.exp(column)), value * beta], axis=1))
        fades.append((unit * jnp.exp(last - column)).T)
        ends.append(jnp.exp(last))
    solved = [dot3(split(x), split(s)) for x, s in zip(inverses(lowers, row, col), sides)]
    maps = []
    for i in range(len(jobs)):
        wu_ref[i] = solved[i]
        both = dot3(split(fades[i]), split(solved[i]))
        maps.append((jnp.where(eye, ends[i], 0.0) - both[:, :C], both[:, C:]))
    totals = []
    for j in range(2):
        state = jnp.concatenate(maps[j * chunks], axis=1)
        for c in range(1, chunks):
            n_ref[j * chunks + c] = state
            moved, fresh = maps[j * chunks + c]
            state = dot3(split(moved), split(state))
            state = jnp.concatenate([state[:, :C], state[:, C:] + fresh], axis=1)
        totals.append(state)
    even = lax.rem(lax.axis_index("seq"), 2) == 0
    own_ref[...] = jnp.where(even, totals[0], totals[1])
    send_ref[...] = jnp.where(even, totals[1], totals[0]).astype(BF16)


def first_kernel(heads, k_hbm, v_hbm, beta_hbm, log_hbm, k32, v32, beta_ref, log_ref, wu, n, own, send, k16, v16, sems):
    fetch(((k_hbm, k16), (log_hbm, log_ref), (beta_hbm, beta_ref), (v_hbm, v16)), sems)
    k32[...] = k16[...].astype(F32)
    v32[...] = v16[...].astype(F32)
    local_body(heads, 0, k32, v32, beta_ref, log_ref, wu, n, own, send)


def local_shapes(tokens):
    chunks = tokens // C
    return [
        jax.ShapeDtypeStruct((2 * chunks, C, 2 * C), F32),
        jax.ShapeDtypeStruct((2 * chunks, C, 2 * C), F32),
        jax.ShapeDtypeStruct((C, 2 * C), F32),
        jax.ShapeDtypeStruct((C, 2 * C), BF16),
    ]


def first_maps(key, value, beta, log_decay):
    heads, tokens = beta.shape
    here = pl.BlockSpec(memory_space=pltpu.VMEM)
    wide = jax.ShapeDtypeStruct(key.shape, F32)
    small = jax.ShapeDtypeStruct(beta.shape, F32)
    return pl.pallas_call(
        functools.partial(first_kernel, heads),
        in_specs=[pl.BlockSpec(memory_space=pltpu.HBM)] * 4,
        out_specs=[here] * 8,
        out_shape=[wide, wide, small, small] + local_shapes(tokens),
        scratch_shapes=[
            pltpu.VMEM(key.shape, BF16),
            pltpu.VMEM(key.shape, BF16),
            pltpu.SemaphoreType.DMA((4,)),
        ],
        compiler_params=pltpu.CompilerParams(vmem_limit_bytes=24 * MIB),
        name="first_maps",
    )(*in_hbm(key, value, beta, log_decay))


def more_maps(phase, key, value, beta, log_decay):
    heads, tokens = beta.shape
    here = pl.BlockSpec(memory_space=pltpu.VMEM)
    return pl.pallas_call(
        functools.partial(local_body, heads, phase),
        in_specs=[here] * 4,
        out_specs=[here] * 4,
        out_shape=local_shapes(tokens),
        compiler_params=pltpu.CompilerParams(vmem_limit_bytes=24 * MIB),
        cost_estimate=pl.CostEstimate(flops=4000000000, bytes_accessed=10000000, transcendentals=0),
        name="more_maps",
    )(key, value, beta, log_decay)


def rows_kernel(heads, phase, q_hbm, k32, log_ref, wu_ref, n_ref, out_ref, q16, q32, sems):
    fetch(((q_hbm, q16),), sems)
    q32[...] = q16[...].astype(F32)
    chunks = log_ref.shape[1] // C
    row, col = iotas()
    eye = row == col
    within = row >= col
    for j, head in enumerate(first_heads(heads, phase)):
        for c in range(chunks):
            query, raw = q32[chunk_rows(heads, head, c), :], k32[chunk_rows(heads, head, c), :]
            column, decay = decay_parts(tokens_of(log_ref, head, c), within, eye)
            scale = inverse_scale(query)
            pairs = dot(query.astype(BF16), raw.astype(BF16), NT)
            pairs = pairs * decay * scale * to_row(inverse_scale(raw), eye)
            both = dot3(split(pairs), split(wu_ref[j * chunks + c]))
            reach = query * (scale * jnp.exp(column)) - both[:, :C]
            fresh = both[:, C:]
            if c > 0:
                earlier = dot3(split(reach), split(n_ref[j * chunks + c]))
                reach = earlier[:, :C]
                fresh = fresh + earlier[:, C:]
            out_ref[j, c * C : (c + 1) * C, :] = jnp.concatenate([reach, fresh], axis=1)


def row_maps(phase, query, k32, log_decay, wu, states):
    heads, tokens = log_decay.shape
    here = pl.BlockSpec(memory_space=pltpu.VMEM)
    return pl.pallas_call(
        functools.partial(rows_kernel, heads, phase),
        in_specs=[pl.BlockSpec(memory_space=pltpu.HBM)] + [here] * 4,
        out_specs=here,
        out_shape=jax.ShapeDtypeStruct((2, tokens, 2 * C), F32),
        scratch_shapes=[
            pltpu.VMEM(query.shape, BF16),
            pltpu.VMEM(query.shape, F32),
            pltpu.SemaphoreType.DMA((1,)),
        ],
        compiler_params=pltpu.CompilerParams(vmem_limit_bytes=16 * MIB),
        cost_estimate=pl.CostEstimate(flops=2000000000, bytes_accessed=8000000, transcendentals=0),
        name="row_maps",
    )(*in_hbm(query), k32, log_decay, wu, states)


def on_pairs(kernel, out_shape, *args):
    here = pl.BlockSpec(memory_space=pltpu.VMEM)
    return pl.pallas_call(
        kernel,
        in_specs=[here] * len(args),
        out_specs=[here] * len(out_shape),
        out_shape=out_shape,
        compiler_params=pltpu.CompilerParams(vmem_limit_bytes=8 * MIB),
        name=kernel.__name__,
    )(*args)


def pair_total(own0, own1, got0, got1, first_ref, total_ref, m_ref, u_ref):
    even = lax.rem(lax.axis_index("seq"), 2) == 0
    for i, (own_ref, got_ref) in enumerate(((own0, got0), (own1, got1))):
        own, got = own_ref[...], got_ref[...].astype(F32)
        first = jnp.where(even, own, got)
        second = jnp.where(even, got, own)
        first_ref[i] = first
        total = dot3(split(second[:, :C]), split(first))
        total = jnp.concatenate([total[:, :C], total[:, C:] + second[:, C:]], axis=1)
        total_ref[i] = total
        m_ref[i] = total[:, :C].astype(BF16)
        u_ref[i] = total[:, C:].astype(BF16)


def moved_on(maps, state16, added):
    high, low = split(maps)
    return dot(jnp.concatenate([high, low], axis=1), twice(state16)) + added


def next_state(total_ref, u_ref, out_ref):
    for i in range(total_ref.shape[0]):
        out_ref[i] = moved_on(total_ref[i, :, :C], u_ref[i], total_ref[i, :, C:]).astype(BF16)


def both_states(entering, first, i, keep_ref, send_ref):
    middle = moved_on(first[:, :C], entering, first[:, C:]).astype(BF16)
    even = lax.rem(lax.axis_index("seq"), 2) == 0
    keep_ref[i] = jnp.where(even, entering, middle)
    send_ref[i] = jnp.where(even, middle, entering)


def entering_of_four(first_ref, u_ref, m_ref, near_ref, far_ref, keep_ref, send_ref):
    place = lax.axis_index("seq") // 2
    for i in range(first_ref.shape[0]):
        last = (dot(m_ref[i], far_ref[i]) + u_ref[i].astype(F32)).astype(BF16)
        entering = jnp.where(place == 1, u_ref[i], jnp.where(place == 2, near_ref[i], last))
        entering = jnp.where(place == 0, jnp.zeros_like(entering), entering)
        both_states(entering, first_ref[i], i, keep_ref, send_ref)


def entering_given(first_ref, entering_ref, keep_ref, send_ref):
    for i in range(first_ref.shape[0]):
        both_states(entering_ref[i], first_ref[i], i, keep_ref, send_ref)


def prefix(maps, added):
    count = lax.axis_size("seq")
    groups = [list(range(i, count, 2)) for i in range(2)]
    me = lax.axis_index("seq") // 2
    maps, added = (lax.all_gather(x, "seq", axis_index_groups=groups) for x in (maps, added))

    def step(d, state):
        longer = jnp.einsum("hik,phkw->hiw", maps[d], jnp.stack(split(state)), preferred_element_type=F32)
        return jnp.where(d < me, longer + added[d].astype(F32), state)

    start = jnp.zeros(added.shape[1:], F32)
    return lax.fori_loop(0, count // 2 - 1, step, start).astype(BF16)


def apply_kernel(heads, rows0_ref, rows1_ref, keep_st, got_st, keep_ref, send_ref):
    step = pl.program_id(0)
    even = lax.rem(lax.axis_index("seq"), 2) == 0
    attended = []
    for h in range(heads):
        phase, side = h % 2, h // 2
        rows_ref = (rows0_ref, rows1_ref)[phase]
        reach, fresh = rows_ref[side, :, :C], rows_ref[side, :, C:]
        mine = even if side == 0 else jnp.logical_not(even)
        state = jnp.where(mine, keep_st[phase], got_st[phase])
        attended.append(moved_on(reach, state, fresh).astype(BF16))
    attended = jnp.concatenate(attended, axis=1)
    mine = lax.rem(step, 2) == lax.rem(lax.axis_index("head"), 2)

    @pl.when(mine)
    def _():
        keep_ref[step // 2] = attended

    @pl.when(jnp.logical_not(mine))
    def _():
        send_ref[step // 2] = attended


def apply(rows, keep_st, got_st, groups):
    _, tokens, _ = rows[0].shape
    heads = 2 * len(rows)
    block = tokens // groups
    out = jax.ShapeDtypeStruct((groups // 2, block, heads * C), BF16)
    states = pl.BlockSpec(keep_st.shape, lambda i: (0, 0, 0))
    return pl.pallas_call(
        functools.partial(apply_kernel, heads),
        grid=(groups,),
        in_specs=[pl.BlockSpec((2, block, 2 * C), lambda i: (0, i, 0))] * 2 + [states] * 2,
        out_specs=[pl.BlockSpec(out.shape, lambda i: (0, 0, 0))] * 2,
        out_shape=[out, out],
        compiler_params=pltpu.CompilerParams(vmem_limit_bytes=14 * MIB),
        name="apply",
    )(*rows, keep_st, got_st)


def project_kernel(other, keep_ref, got_ref, w_ref, w2_ref, out_ref):
    pair = lax.axis_index("head") // 2
    index = 1 - pair if other else pair
    out_ref[...] = (dot(keep_ref[index], w_ref[...]) + dot(got_ref[index], w2_ref[...])).astype(out_ref.dtype)


def project(other, keep, got, weight, weight2):
    _, block, depth = keep.shape
    width = weight.shape[1]
    return pl.pallas_call(
        functools.partial(project_kernel, other),
        out_shape=jax.ShapeDtypeStruct((block, width), BF16 if other else F32),
        compiler_params=pltpu.CompilerParams(vmem_limit_bytes=20 * MIB),
        cost_estimate=pl.CostEstimate(
            flops=4 * block * depth * width, bytes_accessed=4 * depth * width, transcendentals=0
        ),
        name="project",
    )(keep, got, weight, weight2)


def swap(x, axis, bit):
    count = lax.axis_size(axis)
    return lax.ppermute(x, axis, [(i, i ^ bit) for i in range(count)])


def body(query, key, value, beta, log_decay, out_weight):
    tokens, heads, _ = key.shape
    count = lax.axis_size("seq")
    flat = lambda x: x.reshape(tokens * heads, C)
    weight2 = swap(out_weight, "head", 1)
    k32, v32, beta, log_decay, wu0, n0, own0, send0 = first_maps(flat(key), flat(value), beta, log_decay)
    got0 = swap(send0, "seq", 1)
    wu1, n1, own1, send1 = more_maps(1, k32, v32, beta, log_decay)
    got1 = swap(send1, "seq", 1)
    rows = [row_maps(p, flat(query), k32, log_decay, *x) for p, x in enumerate(((wu0, n0), (wu1, n1)))]
    wide = jax.ShapeDtypeStruct((2, C, 2 * C), F32)
    square = jax.ShapeDtypeStruct((2, C, C), BF16)
    first, total, maps, added = on_pairs(pair_total, [wide, wide, square, square], own0, own1, got0, got1)
    if count == 8:
        added = swap(added, "seq", 2)
        maps = swap(maps, "seq", 2)
        (state,) = on_pairs(next_state, [square], total, added)
        near = lax.ppermute(state, "seq", [(2, 4), (3, 5)])
        far = lax.ppermute(state, "seq", [(2, 6), (3, 7)])
        keep, send = on_pairs(entering_of_four, [square, square], first, added, maps, near, far)
    else:
        keep, send = on_pairs(entering_given, [square, square], first, prefix(maps, added))
    got = swap(send, "seq", 1)
    keep, away = apply(rows, keep, got, lax.axis_size("head"))
    got = swap(away, "head", 1)
    theirs = swap(project(True, keep, got, out_weight, weight2), "head", 2)
    mine = project(False, keep, got, out_weight, weight2)
    return (mine + theirs.astype(F32)).astype(BF16)


def solution(mesh):
    in_specs = (
        P("seq", "head", None),
        P("seq", "head", None),
        P("seq", "head", None),
        P("head", "seq"),
        P("head", "seq"),
        P("head", None),
    )
    out_specs = P(("seq", "head"), None)
    return jax.shard_map(body, mesh=mesh, in_specs=in_specs, out_specs=out_specs, check_vma=False)
```

time: 63.2 us -> 51.3 us (0.81)
  the two profiles are of different devices: /device:TPU:0 before, /device:TPU:12 now
where the time goes in v4:
time: 51.3 us; the launch traced here: 51.1 us
  waiting for transfers between devices  21.2 us (41%)
  Pallas kernels  18 us (35%)
  starting transfers between devices  10.8 us (21%)
  other arithmetic  0.9 us (2%)
    ppermute x8, waiting for transfers between devices, swap(): return lax.ppermute(x, axis, [(i, i ^ bit) for i in range(count)])  21.2 us
    ppermute x8, starting transfers between devices, swap(): return lax.ppermute(x, axis, [(i, i ^ bit) for i in range(count)])  5.48 us
    pallas_call x2, Pallas kernels, row_maps(): pl.pallas_call(functools.partial(rows_kernel, heads, phase), in_specs=[pl...  5.45 us
    pallas_call x1, Pallas kernels, first_maps(): pl.pallas_call(functools.partial(first_kernel, heads), in_specs=[pl.Block...  5.23 us
    pallas_call x1, Pallas kernels, more_maps(): pl.pallas_call(functools.partial(local_body, heads, phase), in_specs=[her...  3.9 us
    ppermute x1, starting transfers between devices, body(): near = lax.ppermute(state, 'seq', [(2, 4), (3, 5)])  3.58 us
    ppermute x1, starting transfers between devices, body(): far = lax.ppermute(state, 'seq', [(2, 6), (3, 7)])  1.76 us
    pallas_call x2, Pallas kernels, project(): pl.pallas_call(functools.partial(project_kernel, other), out_shape=jax.Sh...  1.43 us
  transfers between devices with their start and end apart: 10, of which 5 were waited for; matrix products, arithmetic and copies ran while one was open for 0% of the time, Pallas kernels for 34%

profile of v4, /device:TPU:12, one launch (start us, length us, event | category | flops | bytes accessed | tf_op | source)
XLA Modules:
  0.0 51.1 jit_solution(1034290591780559562)
XLA Ops:
  0.0 5.2 %first_maps.1 = (f32[2048,128]{1,0:T(8,128)S(1)}, f32[2048,128]{1,0:T(8,128)S(1)}, f32[4,512]{1,0:T(4,128)S(1)}, f32[4,512]{1,0:T(4,128)S(1)}, f32[8,128,256]{2,...) custom-call(bf16[2048,128]{1,0:T(8,128)(2,1)} %bitcast.3, ...), custom_call_target="tpu_custom_call" | custom-call | tf_op jit(solution)/shard_map/first_maps/pallas_call | solution.py:204
  5.2 1.6 %collective-permute-start = (bf16[128,256]{1,0:T(8,128)(2,1)S(1)}, bf16[128,256]{1,0:T(8,128)(2,1)S(1)}, u32[]{:S(2)}, u32[]{:S(2)}) collective-permute-start(bf16[128,256]{1,0:T(8,128)(2,1)S(1)} %get-tuple-element.35), channel_id=1, source_target_pairs={{0,4},{4,0},{8,12},{12,8},{16,20},{20,16},{24,28},{28,24},{1,5},{5... | collective-permute-start | bytes 196616 | tf_op jit(solution)/shard_map/ppermute | solution.py:409
  6.8 3.9 %more_maps.1 = (f32[8,128,256]{2,1,0:T(8,128)S(1)}, f32[8,128,256]{2,1,0:T(8,128)S(1)}, f32[128,256]{1,0:T(8,128)S(1)}, bf16[128,256]{1,0:T(8,128)(2,1)S(1)}) custom-call(f32[2048,128]{1,0:T(8,128)S(1)} %get-tuple-element.25.k32, f32[2048,128]{1,0:T(8,128)S(1)} %get-tuple-element.29.v32, f32[4,512]{1,0:T(4,128)S(1)} %get-tuple-element.30.beta_ref, ...), custom_call_target="tpu_custom_call" | custom-call | flops 4000000000 | bytes 10000000 | tf_op jit(solution)/shard_map/more_maps/pallas_call | solution.py:222
  10.7 0.6 %collective-permute-start.1 = (bf16[128,256]{1,0:T(8,128)(2,1)S(1)}, bf16[128,256]{1,0:T(8,128)(2,1)S(1)}, u32[]{:S(2)}, u32[]{:S(2)}) collective-permute-start(bf16[128,256]{1,0:T(8,128)(2,1)S(1)} %get-tuple-element.36), channel_id=1, source_target_pairs={{0,4},{4,0},{8,12},{12,8},{16,20},{20,16},{24,28},{28,24},{1,5},{5... | collective-permute-start | bytes 196616 | tf_op jit(solution)/shard_map/ppermute | solution.py:409
  11.3 3.7 %collective-permute-done.1.got1 = bf16[128,256]{1,0:T(8,128)(2,1)S(1)} collective-permute-done((bf16[128,256]{1,0:T(8,128)(2,1)S(1)}, bf16[128,256]{1,0:T(8,128)(2,1)S(1)}, u32[]{:S(2)}, u32[]{:S(2)}) %collective-permute-start.1) | collective-permute-done | bytes 65568 | tf_op jit(solution)/shard_map/ppermute | solution.py:409
  15.0 0.3 pair_total.1
  15.3 0.5 %collective-permute-start.2 = (bf16[2,128,128]{2,1,0:T(8,128)(2,1)S(1)}, bf16[2,128,128]{2,1,0:T(8,128)(2,1)S(1)}, u32[]{:S(2)}, u32[]{:S(2)}) collective-permute-start(bf16[2,128,128]{2,1,0:T(8,128)(2,1)S(1)} %get-tuple-element.38), channel_id=1, source_target_pairs={{0,8},{4,12},{8,0},{12,4},{16,24},{20,28},{24,16},{28,20},{1,9},{5... | collective-permute-start | bytes 196616 | tf_op jit(solution)/shard_map/ppermute | solution.py:409
  15.8 1.6 %collective-permute-start.3 = (bf16[2,128,128]{2,1,0:T(8,128)(2,1)S(1)}, bf16[2,128,128]{2,1,0:T(8,128)(2,1)S(1)}, u32[]{:S(2)}, u32[]{:S(2)}) collective-permute-start(bf16[2,128,128]{2,1,0:T(8,128)(2,1)S(1)} %get-tuple-element.39), channel_id=1, source_target_pairs={{0,8},{4,12},{8,0},{12,4},{16,24},{20,28},{24,16},{28,20},{1,9},{5... | collective-permute-start | bytes 196616 | tf_op jit(solution)/shard_map/ppermute | solution.py:409
  17.4 2.2 %collective-permute-done.2.u_ref = bf16[2,128,128]{2,1,0:T(8,128)(2,1)S(1)} collective-permute-done((bf16[2,128,128]{2,1,0:T(8,128)(2,1)S(1)}, bf16[2,128,128]{2,1,0:T(8,128)(2,1)S(1)}, u32[]{:S(2)}, u32[]{:S(2)}) %collective-permute-start.2) | collective-permute-done | bytes 65568 | tf_op jit(solution)/shard_map/ppermute | solution.py:409
  19.6 0.2 next_state.1
  19.8 3.6 %collective-permute-start.4 = (bf16[2,128,128]{2,1,0:T(8,128)(2,1)S(1)}, bf16[2,128,128]{2,1,0:T(8,128)(2,1)S(1)}, u32[]{:S(2)}, u32[]{:S(2)}) collective-permute-start(bf16[2,128,128]{2,1,0:T(8,128)(2,1)S(1)} %next_state.1), channel_id=1, source_target_pairs={{8,16},{12,20},{9,17},{13,21},{10,18},{14,22},{11,19},{15,23}} | collective-permute-start | bytes 196616 | tf_op jit(solution)/shard_map/ppermute | solution.py:429
  23.4 1.8 %collective-permute-start.5 = (bf16[2,128,128]{2,1,0:T(8,128)(2,1)S(1)}, bf16[2,128,128]{2,1,0:T(8,128)(2,1)S(1)}, u32[]{:S(2)}, u32[]{:S(2)}) collective-permute-start(bf16[2,128,128]{2,1,0:T(8,128)(2,1)S(1)} %next_state.1), channel_id=1, source_target_pairs={{8,24},{12,28},{9,25},{13,29},{10,26},{14,30},{11,27},{15,31}} | collective-permute-start | bytes 196616 | tf_op jit(solution)/shard_map/ppermute | solution.py:430
  25.2 2.7 %row_maps.2.rows0_ref = f32[2,512,256]{2,1,0:T(8,128)S(1)} custom-call(bf16[2048,128]{1,0:T(8,128)(2,1)} %bitcast.5, f32[2048,128]{1,0:T(8,128)S(1)} %get-tuple-element.25.k32, f32[4,512]{1,0:T(4,128)S(1)} %get-tuple-element.26.log_ref, f32[8,128,256]{2,1,0:T(8,128)S(1)} %get-tuple-element.27.wu_ref, f32[8,128,256]{2,1,0:T(8,128)S(1)} %get-tuple-element.28.n_ref), custom_call_target="tpu_custom_call" | custom-call | flops 2000000000 | bytes 8000000 | tf_op jit(solution)/shard_map/row_maps/pallas_call | solution.py:260
  28.0 0.3 entering_of_four.1
  28.3 0.6 %collective-permute-start.6 = (bf16[2,128,128]{2,1,0:T(8,128)(2,1)S(1)}, bf16[2,128,128]{2,1,0:T(8,128)(2,1)S(1)}, u32[]{:S(2)}, u32[]{:S(2)}) collective-permute-start(bf16[2,128,128]{2,1,0:T(8,128)(2,1)S(1)} %get-tuple-element.42), channel_id=1, source_target_pairs={{0,4},{4,0},{8,12},{12,8},{16,20},{20,16},{24,28},{28,24},{1,5},{5... | collective-permute-start | bytes 196616 | tf_op jit(solution)/shard_map/ppermute | solution.py:409
  28.9 2.7 %row_maps.3.rows1_ref = f32[2,512,256]{2,1,0:T(8,128)S(1)} custom-call(bf16[2048,128]{1,0:T(8,128)(2,1)} %bitcast.6, f32[2048,128]{1,0:T(8,128)S(1)} %get-tuple-element.25.k32, f32[4,512]{1,0:T(4,128)S(1)} %get-tuple-element.26.log_ref, f32[8,128,256]{2,1,0:T(8,128)S(1)} %get-tuple-element.31.wu_ref, f32[8,128,256]{2,1,0:T(8,128)S(1)} %get-tuple-element.32.n_ref), custom_call_target="tpu_custom_call" | custom-call | flops 2000000000 | bytes 8000000 | tf_op jit(solution)/shard_map/row_maps/pallas_call | solution.py:260
  31.6 1.0 %collective-permute-done.6.got_st = bf16[2,128,128]{2,1,0:T(8,128)(2,1)S(1)} collective-permute-done((bf16[2,128,128]{2,1,0:T(8,128)(2,1)S(1)}, bf16[2,128,128]{2,1,0:T(8,128)(2,1)S(1)}, u32[]{:S(2)}, u32[]{:S(2)}) %collective-permute-start.6) | collective-permute-done | bytes 65568 | tf_op jit(solution)/shard_map/ppermute | solution.py:409
  32.6 1.2 %apply.1 = (bf16[2,128,512]{2,1,0:T(8,128)(2,1)S(1)}, bf16[2,128,512]{2,1,0:T(8,128)(2,1)S(1)}) custom-call(f32[2,512,256]{2,1,0:T(8,128)S(1)} %row_maps.2.rows0_ref, f32[2,512,256]{2,1,0:T(8,128)S(1)} %row_maps.3.rows1_ref, bf16[2,128,128]{2,1,0:T(8,128)(2,1)S(1)} %get-tuple-element.41.keep_st, bf16[2,128,128]{2,1,0:T(8,128)(2,1)S(1)} %collective-permute-done.6.got_st), custom_call_target="tpu_custom_call" | custom-call | tf_op jit(solution)/shard_map/apply/pallas_call | solution.py:376
  33.9 1.5 %collective-permute-done.7.got_ref = bf16[2,128,512]{2,1,0:T(8,128)(2,1)S(1)} collective-permute-done((bf16[2,128,512]{2,1,0:T(8,128)(2,1)S(1)}, bf16[2,128,512]{2,1,0:T(8,128)(2,1)S(1)}, u32[]{:S(2)}, u32[]{:S(2)}) %collective-permute-start.7) | collective-permute-done | bytes 262176 | tf_op jit(solution)/shard_map/ppermute | solution.py:409
  35.4 0.7 %project.3 = bf16[128,2048]{1,0:T(8,128)(2,1)S(1)} custom-call(bf16[2,128,512]{2,1,0:T(8,128)(2,1)S(1)} %get-tuple-element.43.keep_ref, bf16[2,128,512]{2,1,0:T(8,128)(2,1)S(1)} %collective-permute-done.7.got_ref, bf16[512,2048]{1,0:T(8,128)(2,1)S(1)} %copy-done, bf16[512,2048]{1,0:T(8,128)(2,1)S(1)} %collective-permute-done.8.w2_ref), custom_call_target="tpu_custom_call" | custom-call | flops 536870912 | bytes 4194304 | tf_op jit(solution)/shard_map/project/pallas_call | solution.py:396
  36.2 0.6 %collective-permute-start.9 = (bf16[128,2048]{1,0:T(8,128)(2,1)S(1)}, bf16[128,2048]{1,0:T(8,128)(2,1)S(1)}, u32[]{:S(2)}, u32[]{:S(2)}) collective-permute-start(bf16[128,2048]{1,0:T(8,128)(2,1)S(1)} %project.3), channel_id=1, source_target_pairs={{0,2},{1,3},{2,0},{3,1},{4,6},{5,7},{6,4},{7,5},{8,10},{9,11},{10,... | collective-permute-start | bytes 1572872 | tf_op jit(solution)/shard_map/ppermute | solution.py:409
  36.7 0.7 %project.2 = f32[128,2048]{1,0:T(8,128)S(1)} custom-call(bf16[2,128,512]{2,1,0:T(8,128)(2,1)S(1)} %get-tuple-element.43.keep_ref, bf16[2,128,512]{2,1,0:T(8,128)(2,1)S(1)} %collective-permute-done.7.got_ref, bf16[512,2048]{1,0:T(8,128)(2,1)S(1)} %copy-done, bf16[512,2048]{1,0:T(8,128)(2,1)S(1)} %collective-permute-done.8.w2_ref), custom_call_target="tpu_custom_call" | custom-call | flops 536870912 | bytes 4194304 | tf_op jit(solution)/shard_map/project/pallas_call | solution.py:396
  37.5 12.7 %collective-permute-done.9 = bf16[128,2048]{1,0:T(8,128)(2,1)S(1)} collective-permute-done((bf16[128,2048]{1,0:T(8,128)(2,1)S(1)}, bf16[128,2048]{1,0:T(8,128)(2,1)S(1)}, u32[]{:S(2)}, u32[]{:S(2)}) %collective-permute-start.9) | collective-permute-done | bytes 524320 | tf_op jit(solution)/shard_map/ppermute | solution.py:409
  50.2 0.9 %add_convert_fusion = bf16[128,2048]{1,0:T(8,128)(2,1)} fusion(f32[128,2048]{1,0:T(8,128)S(1)} %project.2, bf16[128,2048]{1,0:T(8,128)(2,1)S(1)} %collective-permute-done.9), kind=kLoop, calls=%fused_computation | loop fusion | flops 786432 | bytes 2097152 | tf_op jit(solution)/shard_map/convert_element_type | solution.py:439
  (9 shorter events, 0.1 us)
Async XLA Ops:
  0.0 35.4 %collective-permute-start.8 = (bf16[512,2048]{1,0:T(8,128)(2,1)}, bf16[512,2048]{1,0:T(8,128)(2,1)S(1)}, u32[]{:S(2)}, u32[]{:S(2)}) collective-permute-start(bf16[512,2048]{1,0:T(8,128)(2,1)} %w_ref.3), channel_id=1, source_target_pairs={{0,1},{1,0},{2,3},{3,2},{4,5},{5,4},{6,7},{7,6},{8,9},{9,8},{10,11... | collective-permute-start | bytes 6291464 | tf_op jit(solution)/shard_map/ppermute | solution.py:409
  5.2 6.1 %collective-permute-start = (bf16[128,256]{1,0:T(8,128)(2,1)S(1)}, bf16[128,256]{1,0:T(8,128)(2,1)S(1)}, u32[]{:S(2)}, u32[]{:S(2)}) collective-permute-start(bf16[128,256]{1,0:T(8,128)(2,1)S(1)} %get-tuple-element.35), channel_id=1, source_target_pairs={{0,4},{4,0},{8,12},{12,8},{16,20},{20,16},{24,28},{28,24},{1,5},{5... | collective-permute-start | bytes 196616 | tf_op jit(solution)/shard_map/ppermute | solution.py:409
  10.7 4.3 %collective-permute-start.1 = (bf16[128,256]{1,0:T(8,128)(2,1)S(1)}, bf16[128,256]{1,0:T(8,128)(2,1)S(1)}, u32[]{:S(2)}, u32[]{:S(2)}) collective-permute-start(bf16[128,256]{1,0:T(8,128)(2,1)S(1)} %get-tuple-element.36), channel_id=1, source_target_pairs={{0,4},{4,0},{8,12},{12,8},{16,20},{20,16},{24,28},{28,24},{1,5},{5... | collective-permute-start | bytes 196616 | tf_op jit(solution)/shard_map/ppermute | solution.py:409
  15.3 4.3 %collective-permute-start.2 = (bf16[2,128,128]{2,1,0:T(8,128)(2,1)S(1)}, bf16[2,128,128]{2,1,0:T(8,128)(2,1)S(1)}, u32[]{:S(2)}, u32[]{:S(2)}) collective-permute-start(bf16[2,128,128]{2,1,0:T(8,128)(2,1)S(1)} %get-tuple-element.38), channel_id=1, source_target_pairs={{0,8},{4,12},{8,0},{12,4},{16,24},{20,28},{24,16},{28,20},{1,9},{5... | collective-permute-start | bytes 196616 | tf_op jit(solution)/shard_map/ppermute | solution.py:409
  15.8 12.1 %collective-permute-start.3 = (bf16[2,128,128]{2,1,0:T(8,128)(2,1)S(1)}, bf16[2,128,128]{2,1,0:T(8,128)(2,1)S(1)}, u32[]{:S(2)}, u32[]{:S(2)}) collective-permute-start(bf16[2,128,128]{2,1,0:T(8,128)(2,1)S(1)} %get-tuple-element.39), channel_id=1, source_target_pairs={{0,8},{4,12},{8,0},{12,4},{16,24},{20,28},{24,16},{28,20},{1,9},{5... | collective-permute-start | bytes 196616 | tf_op jit(solution)/shard_map/ppermute | solution.py:409
  19.8 8.1 %collective-permute-start.4 = (bf16[2,128,128]{2,1,0:T(8,128)(2,1)S(1)}, bf16[2,128,128]{2,1,0:T(8,128)(2,1)S(1)}, u32[]{:S(2)}, u32[]{:S(2)}) collective-permute-start(bf16[2,128,128]{2,1,0:T(8,128)(2,1)S(1)} %next_state.1), channel_id=1, source_target_pairs={{8,16},{12,20},{9,17},{13,21},{10,18},{14,22},{11,19},{15,23}} | collective-permute-start | bytes 196616 | tf_op jit(solution)/shard_map/ppermute | solution.py:429
  23.4 4.5 %collective-permute-start.5 = (bf16[2,128,128]{2,1,0:T(8,128)(2,1)S(1)}, bf16[2,128,128]{2,1,0:T(8,128)(2,1)S(1)}, u32[]{:S(2)}, u32[]{:S(2)}) collective-permute-start(bf16[2,128,128]{2,1,0:T(8,128)(2,1)S(1)} %next_state.1), channel_id=1, source_target_pairs={{8,24},{12,28},{9,25},{13,29},{10,26},{14,30},{11,27},{15,31}} | collective-permute-start | bytes 196616 | tf_op jit(solution)/shard_map/ppermute | solution.py:430
  28.3 4.3 %collective-permute-start.6 = (bf16[2,128,128]{2,1,0:T(8,128)(2,1)S(1)}, bf16[2,128,128]{2,1,0:T(8,128)(2,1)S(1)}, u32[]{:S(2)}, u32[]{:S(2)}) collective-permute-start(bf16[2,128,128]{2,1,0:T(8,128)(2,1)S(1)} %get-tuple-element.42), channel_id=1, source_target_pairs={{0,4},{4,0},{8,12},{12,8},{16,20},{20,16},{24,28},{28,24},{1,5},{5... | collective-permute-start | bytes 196616 | tf_op jit(solution)/shard_map/ppermute | solution.py:409
  31.6 3.8 %copy-start = (bf16[512,2048]{1,0:T(8,128)(2,1)S(1)}, bf16[512,2048]{1,0:T(8,128)(2,1)}, u32[]{:S(2)}) copy-start(bf16[512,2048]{1,0:T(8,128)(2,1)} %w_ref.3) | copy-start | bytes 6291460
  33.8 1.6 %collective-permute-start.7 = (bf16[2,128,512]{2,1,0:T(8,128)(2,1)S(1)}, bf16[2,128,512]{2,1,0:T(8,128)(2,1)S(1)}, u32[]{:S(2)}, u32[]{:S(2)}) collective-permute-start(bf16[2,128,512]{2,1,0:T(8,128)(2,1)S(1)} %get-tuple-element.44), channel_id=1, source_target_pairs={{0,1},{1,0},{2,3},{3,2},{4,5},{5,4},{6,7},{7,6},{8,9},{9,8},{10,11... | collective-permute-start | bytes 786440 | tf_op jit(solution)/shard_map/ppermute | solution.py:409
  36.2 14.0 %collective-permute-start.9 = (bf16[128,2048]{1,0:T(8,128)(2,1)S(1)}, bf16[128,2048]{1,0:T(8,128)(2,1)S(1)}, u32[]{:S(2)}, u32[]{:S(2)}) collective-permute-start(bf16[128,2048]{1,0:T(8,128)(2,1)S(1)} %project.3), channel_id=1, source_target_pairs={{0,2},{1,3},{2,0},{3,1},{4,6},{5,7},{6,4},{7,5},{8,10},{9,11},{10,... | collective-permute-start | bytes 1572872 | tf_op jit(solution)/shard_map/ppermute | solution.py:409

commit v5 on v4

--- a/solution.py
+++ b/solution.py
@@ -285,7 +285,7 @@
     )(*args)
 
 
-def pair_total(own0, own1, got0, got1, first_ref, total_ref, m_ref, u_ref):
+def pair_total(own0, own1, got0, got1, first_ref, total_ref, send_ref):
     even = lax.rem(lax.axis_index("seq"), 2) == 0
     for i, (own_ref, got_ref) in enumerate(((own0, got0), (own1, got1))):
         own, got = own_ref[...], got_ref[...].astype(F32)
@@ -295,8 +295,7 @@
         total = dot3(split(second[:, :C]), split(first))
         total = jnp.concatenate([total[:, :C], total[:, C:] + second[:, C:]], axis=1)
         total_ref[i] = total
-        m_ref[i] = total[:, :C].astype(BF16)
-        u_ref[i] = total[:, C:].astype(BF16)
+        send_ref[i] = total.astype(BF16)
 
 
 def moved_on(maps, state16, added):
@@ -304,9 +303,13 @@
     return dot(jnp.concatenate([high, low], axis=1), twice(state16)) + added
 
 
-def next_state(total_ref, u_ref, out_ref):
+def next_state(total_ref, got_ref, out_ref):
+    even = lax.rem(lax.axis_index("seq") // 2, 2) == 0
     for i in range(total_ref.shape[0]):
-        out_ref[i] = moved_on(total_ref[i, :, :C], u_ref[i], total_ref[i, :, C:]).astype(BF16)
+        own, got = total_ref[i], got_ref[i]
+        later = jnp.where(even, got.astype(F32), own)
+        state = jnp.where(even, own[:, C:].astype(BF16), got[:, C:])
+        out_ref[i] = moved_on(later[:, :C], state, later[:, C:]).astype(BF16)
 
 
 def both_states(entering, first, i, keep_ref, send_ref):
@@ -316,11 +319,12 @@
     send_ref[i] = jnp.where(even, middle, entering)
 
 
-def entering_of_four(first_ref, u_ref, m_ref, near_ref, far_ref, keep_ref, send_ref):
+def entering_of_four(first_ref, got_ref, lower_ref, keep_ref, send_ref):
     place = lax.axis_index("seq") // 2
     for i in range(first_ref.shape[0]):
-        last = (dot(m_ref[i], far_ref[i]) + u_ref[i].astype(F32)).astype(BF16)
-        entering = jnp.where(place == 1, u_ref[i], jnp.where(place == 2, near_ref[i], last))
+        got, lower = got_ref[i], lower_ref[i]
+        last = (dot(got[:, :C], lower) + got[:, C:].astype(F32)).astype(BF16)
+        entering = jnp.where(place == 1, got[:, C:], jnp.where(place == 2, lower, last))
         entering = jnp.where(place == 0, jnp.zeros_like(entering), entering)
         both_states(entering, first_ref[i], i, keep_ref, send_ref)
 
@@ -330,11 +334,12 @@
         both_states(entering_ref[i], first_ref[i], i, keep_ref, send_ref)
 
 
-def prefix(maps, added):
+def prefix(totals):
     count = lax.axis_size("seq")
     groups = [list(range(i, count, 2)) for i in range(2)]
     me = lax.axis_index("seq") // 2
-    maps, added = (lax.all_gather(x, "seq", axis_index_groups=groups) for x in (maps, added))
+    totals = lax.all_gather(totals, "seq", axis_index_groups=groups)
+    maps, added = totals[..., :C], totals[..., C:]
 
     def step(d, state):
         longer = jnp.einsum("hik,phkw->hiw", maps[d], jnp.stack(split(state)), preferred_element_type=F32)
@@ -418,21 +423,24 @@
     got0 = swap(send0, "seq", 1)
     wu1, n1, own1, send1 = more_maps(1, k32, v32, beta, log_decay)
     got1 = swap(send1, "seq", 1)
-    rows = [row_maps(p, flat(query), k32, log_decay, *x) for p, x in enumerate(((wu0, n0), (wu1, n1)))]
+    wu0, got0 = lax.optimization_barrier((wu0, got0))
+    rows0 = row_maps(0, flat(query), k32, log_decay, wu0, n0)
+    rows1 = row_maps(1, flat(query), k32, log_decay, wu1, n1)
+    rows0, got1 = lax.optimization_barrier((rows0, got1))
     wide = jax.ShapeDtypeStruct((2, C, 2 * C), F32)
+    narrow = jax.ShapeDtypeStruct((2, C, 2 * C), BF16)
     square = jax.ShapeDtypeStruct((2, C, C), BF16)
-    first, total, maps, added = on_pairs(pair_total, [wide, wide, square, square], own0, own1, got0, got1)
+    first, total, total16 = on_pairs(pair_total, [wide, wide, narrow], own0, own1, got0, got1)
     if count == 8:
-        added = swap(added, "seq", 2)
-        maps = swap(maps, "seq", 2)
-        (state,) = on_pairs(next_state, [square], total, added)
-        near = lax.ppermute(state, "seq", [(2, 4), (3, 5)])
-        far = lax.ppermute(state, "seq", [(2, 6), (3, 7)])
-        keep, send = on_pairs(entering_of_four, [square, square], first, added, maps, near, far)
+        other = swap(total16, "seq", 2)
+        (state,) = on_pairs(next_state, [square], total, other)
+        lower = swap(state, "seq", 4)
+        rows1, lower = lax.optimization_barrier((rows1, lower))
+        keep, send = on_pairs(entering_of_four, [square, square], first, other, lower)
     else:
-        keep, send = on_pairs(entering_given, [square, square], first, prefix(maps, added))
+        keep, send = on_pairs(entering_given, [square, square], first, prefix(total16))
     got = swap(send, "seq", 1)
-    keep, away = apply(rows, keep, got, lax.axis_size("head"))
+    keep, away = apply((rows0, rows1), keep, got, lax.axis_size("head"))
     got = swap(away, "head", 1)
     theirs = swap(project(True, keep, got, out_weight, weight2), "head", 2)
     mine = project(False, keep, got, out_weight, weight2)

time: 51.3 us -> 50.8 us (level)
  the two profiles are of different devices: /device:TPU:12 before, /device:TPU:0 now
where the time goes in v5:
time: 50.8 us; the launch traced here: 50.5 us
  waiting for transfers between devices  21.5 us (42%)
  Pallas kernels  18 us (35%)
  starting transfers between devices  10 us (20%)
  other arithmetic  0.9 us (2%)
    ppermute x8, waiting for transfers between devices, swap(): return lax.ppermute(x, axis, [(i, i ^ bit) for i in range(count)])  21.5 us
    ppermute x8, starting transfers between devices, swap(): return lax.ppermute(x, axis, [(i, i ^ bit) for i in range(count)])  10 us
    pallas_call x2, Pallas kernels, row_maps(): pl.pallas_call(functools.partial(rows_kernel, heads, phase), in_specs=[pl...  5.45 us
    pallas_call x1, Pallas kernels, first_maps(): pl.pallas_call(functools.partial(first_kernel, heads), in_specs=[pl.Block...  5.23 us
    pallas_call x1, Pallas kernels, more_maps(): pl.pallas_call(functools.partial(local_body, heads, phase), in_specs=[her...  3.9 us
    pallas_call x2, Pallas kernels, project(): pl.pallas_call(functools.partial(project_kernel, other), out_shape=jax.Sh...  1.43 us
    pallas_call x1, Pallas kernels, apply(): pl.pallas_call(functools.partial(apply_kernel, heads), grid=(groups,), in...  1.2 us
  transfers between devices with their start and end apart: 8, of which 5 were waited for; matrix products, arithmetic and copies ran while one was open for 0% of the time, Pallas kernels for 34%

profile of v5, /device:TPU:0, one launch (start us, length us, event | category | flops | bytes accessed | tf_op | source)
XLA Modules:
  0.0 50.5 jit_solution(15291907225874612645)
XLA Ops:
  0.0 0.5 collective-permute-start.6
  0.5 5.2 %first_maps.1 = (f32[2048,128]{1,0:T(8,128)S(1)}, f32[2048,128]{1,0:T(8,128)S(1)}, f32[4,512]{1,0:T(4,128)S(1)}, f32[4,512]{1,0:T(4,128)S(1)}, f32[8,128,256]{2,...) custom-call(bf16[2048,128]{1,0:T(8,128)(2,1)} %bitcast.3, ...), custom_call_target="tpu_custom_call" | custom-call | tf_op jit(solution)/shard_map/first_maps/pallas_call | solution.py:204
  5.7 2.6 %collective-permute-start = (bf16[128,256]{1,0:T(8,128)(2,1)S(1)}, bf16[128,256]{1,0:T(8,128)(2,1)S(1)}, u32[]{:S(2)}, u32[]{:S(2)}) collective-permute-start(bf16[128,256]{1,0:T(8,128)(2,1)S(1)} %get-tuple-element.33), channel_id=1, source_target_pairs={{0,4},{4,0},{8,12},{12,8},{16,20},{20,16},{24,28},{28,24},{1,5},{5... | collective-permute-start | bytes 196616 | tf_op jit(solution)/shard_map/ppermute | solution.py:414
  8.2 3.9 %more_maps.1 = (f32[8,128,256]{2,1,0:T(8,128)S(1)}, f32[8,128,256]{2,1,0:T(8,128)S(1)}, f32[128,256]{1,0:T(8,128)S(1)}, bf16[128,256]{1,0:T(8,128)(2,1)S(1)}) custom-call(f32[2048,128]{1,0:T(8,128)S(1)} %get-tuple-element.30.k32, f32[2048,128]{1,0:T(8,128)S(1)} %get-tuple-element.36.v32, f32[4,512]{1,0:T(4,128)S(1)} %get-tuple-element.37.beta_ref, ...), custom_call_target="tpu_custom_call" | custom-call | flops 4000000000 | bytes 10000000 | tf_op jit(solution)/shard_map/more_maps/pallas_call | solution.py:222
  12.2 0.1 collective-permute-start.1
  12.2 2.7 %row_maps.2.rows0_ref = f32[2,512,256]{2,1,0:T(8,128)S(1)} custom-call(bf16[2048,128]{1,0:T(8,128)(2,1)} %bitcast.5, f32[2048,128]{1,0:T(8,128)S(1)} %get-tuple-element.30.k32, f32[4,512]{1,0:T(4,128)S(1)} %get-tuple-element.31.log_ref, f32[8,128,256]{2,1,0:T(8,128)S(1)} %get-tuple-element.34.wu_ref, f32[8,128,256]{2,1,0:T(8,128)S(1)} %get-tuple-element.35.n_ref), custom_call_target="tpu_custom_call" | custom-call | flops 2000000000 | bytes 8000000 | tf_op jit(solution)/shard_map/row_maps/pallas_call | solution.py:260
  15.0 1.5 %collective-permute-done.1.got1 = bf16[128,256]{1,0:T(8,128)(2,1)S(1)} collective-permute-done((bf16[128,256]{1,0:T(8,128)(2,1)S(1)}, bf16[128,256]{1,0:T(8,128)(2,1)S(1)}, u32[]{:S(2)}, u32[]{:S(2)}) %collective-permute-start.1) | collective-permute-done | bytes 65568 | tf_op jit(solution)/shard_map/ppermute | solution.py:414
  16.5 0.3 pair_total.1
  16.8 1.6 %collective-permute-start.2 = (bf16[2,128,256]{2,1,0:T(8,128)(2,1)S(1)}, bf16[2,128,256]{2,1,0:T(8,128)(2,1)S(1)}, u32[]{:S(2)}, u32[]{:S(2)}) collective-permute-start(bf16[2,128,256]{2,1,0:T(8,128)(2,1)S(1)} %get-tuple-element.47), channel_id=1, source_target_pairs={{0,8},{4,12},{8,0},{12,4},{16,24},{20,28},{24,16},{28,20},{1,9},{5... | collective-permute-start | bytes 393224 | tf_op jit(solution)/shard_map/ppermute | solution.py:414
  18.4 3.4 %collective-permute-done.2.got_ref = bf16[2,128,256]{2,1,0:T(8,128)(2,1)S(1)} collective-permute-done((bf16[2,128,256]{2,1,0:T(8,128)(2,1)S(1)}, bf16[2,128,256]{2,1,0:T(8,128)(2,1)S(1)}, u32[]{:S(2)}, u32[]{:S(2)}) %collective-permute-start.2) | collective-permute-done | bytes 131104 | tf_op jit(solution)/shard_map/ppermute | solution.py:414
  21.8 0.2 next_state.1
  22.0 2.7 %collective-permute-start.3 = (bf16[2,128,128]{2,1,0:T(8,128)(2,1)S(1)}, bf16[2,128,128]{2,1,0:T(8,128)(2,1)S(1)}, u32[]{:S(2)}, u32[]{:S(2)}) collective-permute-start(bf16[2,128,128]{2,1,0:T(8,128)(2,1)S(1)} %next_state.1), channel_id=1, source_target_pairs={{0,16},{4,20},{8,24},{12,28},{16,0},{20,4},{24,8},{28,12},{1,17},{... | collective-permute-start | bytes 196616 | tf_op jit(solution)/shard_map/ppermute | solution.py:414
  24.6 2.7 %row_maps.3.rows1_ref = f32[2,512,256]{2,1,0:T(8,128)S(1)} custom-call(bf16[2048,128]{1,0:T(8,128)(2,1)} %bitcast.6, f32[2048,128]{1,0:T(8,128)S(1)} %get-tuple-element.30.k32, f32[4,512]{1,0:T(4,128)S(1)} %get-tuple-element.31.log_ref, f32[8,128,256]{2,1,0:T(8,128)S(1)} %get-tuple-element.40.wu_ref, f32[8,128,256]{2,1,0:T(8,128)S(1)} %get-tuple-element.41.n_ref), custom_call_target="tpu_custom_call" | custom-call | flops 2000000000 | bytes 8000000 | tf_op jit(solution)/shard_map/row_maps/pallas_call | solution.py:260
  27.4 0.3 entering_of_four.1
  27.7 1.0 %collective-permute-start.4 = (bf16[2,128,128]{2,1,0:T(8,128)(2,1)S(1)}, bf16[2,128,128]{2,1,0:T(8,128)(2,1)S(1)}, u32[]{:S(2)}, u32[]{:S(2)}) collective-permute-start(bf16[2,128,128]{2,1,0:T(8,128)(2,1)S(1)} %get-tuple-element.52), channel_id=1, source_target_pairs={{0,4},{4,0},{8,12},{12,8},{16,20},{20,16},{24,28},{28,24},{1,5},{5... | collective-permute-start | bytes 196616 | tf_op jit(solution)/shard_map/ppermute | solution.py:414
  28.7 3.4 %collective-permute-done.4.got_st = bf16[2,128,128]{2,1,0:T(8,128)(2,1)S(1)} collective-permute-done((bf16[2,128,128]{2,1,0:T(8,128)(2,1)S(1)}, bf16[2,128,128]{2,1,0:T(8,128)(2,1)S(1)}, u32[]{:S(2)}, u32[]{:S(2)}) %collective-permute-start.4) | collective-permute-done | bytes 65568 | tf_op jit(solution)/shard_map/ppermute | solution.py:414
  32.1 1.2 %apply.1 = (bf16[2,128,512]{2,1,0:T(8,128)(2,1)S(1)}, bf16[2,128,512]{2,1,0:T(8,128)(2,1)S(1)}) custom-call(f32[2,512,256]{2,1,0:T(8,128)S(1)} %row_maps.2.rows0_ref, f32[2,512,256]{2,1,0:T(8,128)S(1)} %row_maps.3.rows1_ref, bf16[2,128,128]{2,1,0:T(8,128)(2,1)S(1)} %get-tuple-element.51.keep_st, bf16[2,128,128]{2,1,0:T(8,128)(2,1)S(1)} %collective-permute-done.4.got_st), custom_call_target="tpu_custom_call" | custom-call | tf_op jit(solution)/shard_map/apply/pallas_call | solution.py:381
  33.3 0.1 collective-permute-start.5
  33.4 1.5 %collective-permute-done.5.got_ref = bf16[2,128,512]{2,1,0:T(8,128)(2,1)S(1)} collective-permute-done((bf16[2,128,512]{2,1,0:T(8,128)(2,1)S(1)}, bf16[2,128,512]{2,1,0:T(8,128)(2,1)S(1)}, u32[]{:S(2)}, u32[]{:S(2)}) %collective-permute-start.5) | collective-permute-done | bytes 262176 | tf_op jit(solution)/shard_map/ppermute | solution.py:414
  34.9 0.7 %project.3 = bf16[128,2048]{1,0:T(8,128)(2,1)S(1)} custom-call(bf16[2,128,512]{2,1,0:T(8,128)(2,1)S(1)} %get-tuple-element.53.keep_ref, bf16[2,128,512]{2,1,0:T(8,128)(2,1)S(1)} %collective-permute-done.5.got_ref, bf16[512,2048]{1,0:T(8,128)(2,1)S(1)} %copy-done, bf16[512,2048]{1,0:T(8,128)(2,1)S(1)} %collective-permute-done.6.w2_ref), custom_call_target="tpu_custom_call" | custom-call | flops 536870912 | bytes 4194304 | tf_op jit(solution)/shard_map/project/pallas_call | solution.py:401
  35.6 1.6 %collective-permute-start.7 = (bf16[128,2048]{1,0:T(8,128)(2,1)S(1)}, bf16[128,2048]{1,0:T(8,128)(2,1)S(1)}, u32[]{:S(2)}, u32[]{:S(2)}) collective-permute-start(bf16[128,2048]{1,0:T(8,128)(2,1)S(1)} %project.3), channel_id=1, source_target_pairs={{0,2},{1,3},{2,0},{3,1},{4,6},{5,7},{6,4},{7,5},{8,10},{9,11},{10,... | collective-permute-start | bytes 1572872 | tf_op jit(solution)/shard_map/ppermute | solution.py:414
  37.2 0.7 %project.2 = f32[128,2048]{1,0:T(8,128)S(1)} custom-call(bf16[2,128,512]{2,1,0:T(8,128)(2,1)S(1)} %get-tuple-element.53.keep_ref, bf16[2,128,512]{2,1,0:T(8,128)(2,1)S(1)} %collective-permute-done.5.got_ref, bf16[512,2048]{1,0:T(8,128)(2,1)S(1)} %copy-done, bf16[512,2048]{1,0:T(8,128)(2,1)S(1)} %collective-permute-done.6.w2_ref), custom_call_target="tpu_custom_call" | custom-call | flops 536870912 | bytes 4194304 | tf_op jit(solution)/shard_map/project/pallas_call | solution.py:401
  37.9 11.7 %collective-permute-done.7 = bf16[128,2048]{1,0:T(8,128)(2,1)S(1)} collective-permute-done((bf16[128,2048]{1,0:T(8,128)(2,1)S(1)}, bf16[128,2048]{1,0:T(8,128)(2,1)S(1)}, u32[]{:S(2)}, u32[]{:S(2)}) %collective-permute-start.7) | collective-permute-done | bytes 524320 | tf_op jit(solution)/shard_map/ppermute | solution.py:414
  49.6 0.9 %add_convert_fusion = bf16[128,2048]{1,0:T(8,128)(2,1)} fusion(f32[128,2048]{1,0:T(8,128)S(1)} %project.2, bf16[128,2048]{1,0:T(8,128)(2,1)S(1)} %collective-permute-done.7), kind=kLoop, calls=%fused_computation | loop fusion | flops 786432 | bytes 2097152 | tf_op jit(solution)/shard_map/convert_element_type | solution.py:447
  (5 shorter events, 0.0 us)
Async XLA Ops:
  0.0 34.9 %collective-permute-start.6 = (bf16[512,2048]{1,0:T(8,128)(2,1)}, bf16[512,2048]{1,0:T(8,128)(2,1)S(1)}, u32[]{:S(2)}, u32[]{:S(2)}) collective-permute-start(bf16[512,2048]{1,0:T(8,128)(2,1)} %w_ref.3), channel_id=1, source_target_pairs={{0,1},{1,0},{2,3},{3,2},{4,5},{5,4},{6,7},{7,6},{8,9},{9,8},{10,11... | collective-permute-start | bytes 6291464 | tf_op jit(solution)/shard_map/ppermute | solution.py:414
  5.7 6.5 %collective-permute-start = (bf16[128,256]{1,0:T(8,128)(2,1)S(1)}, bf16[128,256]{1,0:T(8,128)(2,1)S(1)}, u32[]{:S(2)}, u32[]{:S(2)}) collective-permute-start(bf16[128,256]{1,0:T(8,128)(2,1)S(1)} %get-tuple-element.33), channel_id=1, source_target_pairs={{0,4},{4,0},{8,12},{12,8},{16,20},{20,16},{24,28},{28,24},{1,5},{5... | collective-permute-start | bytes 196616 | tf_op jit(solution)/shard_map/ppermute | solution.py:414
  12.2 4.3 %collective-permute-start.1 = (bf16[128,256]{1,0:T(8,128)(2,1)S(1)}, bf16[128,256]{1,0:T(8,128)(2,1)S(1)}, u32[]{:S(2)}, u32[]{:S(2)}) collective-permute-start(bf16[128,256]{1,0:T(8,128)(2,1)S(1)} %get-tuple-element.38), channel_id=1, source_target_pairs={{0,4},{4,0},{8,12},{12,8},{16,20},{20,16},{24,28},{28,24},{1,5},{5... | collective-permute-start | bytes 196616 | tf_op jit(solution)/shard_map/ppermute | solution.py:414
  16.8 5.0 %collective-permute-start.2 = (bf16[2,128,256]{2,1,0:T(8,128)(2,1)S(1)}, bf16[2,128,256]{2,1,0:T(8,128)(2,1)S(1)}, u32[]{:S(2)}, u32[]{:S(2)}) collective-permute-start(bf16[2,128,256]{2,1,0:T(8,128)(2,1)S(1)} %get-tuple-element.47), channel_id=1, source_target_pairs={{0,8},{4,12},{8,0},{12,4},{16,24},{20,28},{24,16},{28,20},{1,9},{5... | collective-permute-start | bytes 393224 | tf_op jit(solution)/shard_map/ppermute | solution.py:414
  22.0 5.4 %collective-permute-start.3 = (bf16[2,128,128]{2,1,0:T(8,128)(2,1)S(1)}, bf16[2,128,128]{2,1,0:T(8,128)(2,1)S(1)}, u32[]{:S(2)}, u32[]{:S(2)}) collective-permute-start(bf16[2,128,128]{2,1,0:T(8,128)(2,1)S(1)} %next_state.1), channel_id=1, source_target_pairs={{0,16},{4,20},{8,24},{12,28},{16,0},{20,4},{24,8},{28,12},{1,17},{... | collective-permute-start | bytes 196616 | tf_op jit(solution)/shard_map/ppermute | solution.py:414
  27.4 7.5 %copy-start = (bf16[512,2048]{1,0:T(8,128)(2,1)S(1)}, bf16[512,2048]{1,0:T(8,128)(2,1)}, u32[]{:S(2)}) copy-start(bf16[512,2048]{1,0:T(8,128)(2,1)} %w_ref.3) | copy-start | bytes 6291460
  27.7 4.3 %collective-permute-start.4 = (bf16[2,128,128]{2,1,0:T(8,128)(2,1)S(1)}, bf16[2,128,128]{2,1,0:T(8,128)(2,1)S(1)}, u32[]{:S(2)}, u32[]{:S(2)}) collective-permute-start(bf16[2,128,128]{2,1,0:T(8,128)(2,1)S(1)} %get-tuple-element.52), channel_id=1, source_target_pairs={{0,4},{4,0},{8,12},{12,8},{16,20},{20,16},{24,28},{28,24},{1,5},{5... | collective-permute-start | bytes 196616 | tf_op jit(solution)/shard_map/ppermute | solution.py:414
  33.3 1.6 %collective-permute-start.5 = (bf16[2,128,512]{2,1,0:T(8,128)(2,1)S(1)}, bf16[2,128,512]{2,1,0:T(8,128)(2,1)S(1)}, u32[]{:S(2)}, u32[]{:S(2)}) collective-permute-start(bf16[2,128,512]{2,1,0:T(8,128)(2,1)S(1)} %get-tuple-element.54), channel_id=1, source_target_pairs={{0,1},{1,0},{2,3},{3,2},{4,5},{5,4},{6,7},{7,6},{8,9},{9,8},{10,11... | collective-permute-start | bytes 786440 | tf_op jit(solution)/shard_map/ppermute | solution.py:414
  35.6 14.0 %collective-permute-start.7 = (bf16[128,2048]{1,0:T(8,128)(2,1)S(1)}, bf16[128,2048]{1,0:T(8,128)(2,1)S(1)}, u32[]{:S(2)}, u32[]{:S(2)}) collective-permute-start(bf16[128,2048]{1,0:T(8,128)(2,1)S(1)} %project.3), channel_id=1, source_target_pairs={{0,2},{1,3},{2,0},{3,1},{4,6},{5,7},{6,4},{7,5},{8,10},{9,11},{10,... | collective-permute-start | bytes 1572872 | tf_op jit(solution)/shard_map/ppermute | solution.py:414

commit v6 on v3

v6 whole, which is shorter than its diff:
```python
import functools

import jax
import jax.numpy as jnp
from jax import lax
from jax.experimental import pallas as pl
from jax.experimental.pallas import tpu as pltpu
from jax.sharding import PartitionSpec as P

C = 128
B = 16
F32 = jnp.float32
BF16 = jnp.bfloat16
NN = (((1,), (0,)), ((), ()))
NT = (((1,), (1,)), ((), ()))
TN = (((0,), (0,)), ((), ()))
MIB = 1024 * 1024


def dot(a, b, dims=NN):
    return lax.dot_general(a, b, dims, preferred_element_type=F32)


def split(x):
    high = x.astype(BF16)
    return high, (x - high.astype(F32)).astype(BF16)


def twice(x):
    return jnp.concatenate([x, x], axis=0)


def dot3(a, b):
    (ah, al), (bh, bl) = a, b
    width = bh.shape[1]
    left = jnp.concatenate([ah, al], axis=1)
    if width > C:
        return dot(left, twice(bh)) + dot(ah, bl)
    both = dot(left, twice(jnp.concatenate([bh, bl], axis=1)))
    return both[:, :width] + both[:, width:]


def iotas():
    return (
        lax.broadcasted_iota(jnp.int32, (C, C), 0),
        lax.broadcasted_iota(jnp.int32, (C, C), 1),
    )


def to_column(row, eye):
    return jnp.sum(jnp.where(eye, row, 0.0), axis=1, keepdims=True)


def to_row(column, eye):
    return jnp.sum(jnp.where(eye, column, 0.0), axis=0, keepdims=True)


def inverse_scale(rows):
    return lax.rsqrt(jnp.sum(rows * rows, axis=1, keepdims=True) + 1e-06)


def decay_parts(log_row, within, eye):
    column = jnp.sum(jnp.where(within, log_row, 0.0), axis=1, keepdims=True)
    row = to_row(column, eye)
    decay = jnp.where(within, jnp.exp(jnp.where(within, column - row, 0.0)), 0.0)
    return column, decay


def base_inverse(lower, row, col):
    on_block = (row // B) == (col // B)
    blocks = jnp.where(on_block, lower, 0.0)
    packed = sum(blocks[i * B : (i + 1) * B] for i in range(1, C // B)) + blocks[:B]
    r, c = row[:B], col[:B]
    found = jnp.where(r == c % B, 1.0, 0.0)
    first = (c // B) * B
    for j in range(B - 1):
        factor = jnp.take_along_axis(packed, first + j, axis=1)
        found = found - factor * found[j : j + 1]
    return jnp.where(on_block, jnp.concatenate([found] * (C // B), axis=0), 0.0)


def odd_rows(x, size):
    return jnp.concatenate([x[i : i + size] for i in range(size, C, 2 * size)], axis=0)


def weave(even, odd, size):
    parts = []
    for i in range(0, C // 2, size):
        parts += [even[i : i + size], odd[i : i + size]]
    return jnp.concatenate(parts, axis=0)


def even_rows(x, size):
    return jnp.concatenate([x[i : i + size] for i in range(0, C, 2 * size)], axis=0)


def inverses(lowers, row, col):
    found = [base_inverse(a, row, col) for a in lowers]
    parts = [split(a) for a in lowers]
    size = B
    while size < C:
        r, c = odd_rows(row, size), odd_rows(col, size)
        mask = ((r // (2 * size)) == (c // (2 * size))) & ((r // size) != (c // size))
        nothing = jnp.zeros((C // 2, C), BF16)
        joins = [tuple(jnp.where(mask, odd_rows(x, size), nothing) for x in part) for part in parts]
        halves = [split(x) for x in found]
        middle = [split(dot3(a, x)) for a, x in zip(joins, halves)]
        middle = [tuple(weave(nothing, x, size) for x in part) for part in middle]
        lows = [dot3(tuple(odd_rows(x, size) for x in h), y) for h, y in zip(halves, middle)]
        found = [weave(even_rows(x, size), odd_rows(x, size) - y, size) for x, y in zip(found, lows)]
        size *= 2
    return found


def fetch(pairs, sems):
    copies = [pltpu.make_async_copy(x, y, sems.at[i]) for i, (x, y) in enumerate(pairs)]
    for copy in copies:
        copy.start()
    for copy in copies:
        copy.wait()


def in_hbm(*arrays):
    return [pltpu.with_memory_space_constraint(x, pltpu.HBM) for x in arrays]


def chunk_rows(heads, head, c):
    return pl.ds(c * C * heads + head, C, stride=heads)


def tokens_of(ref, head, c):
    return ref[head : head + 1, c * C : (c + 1) * C]


def local_maps_kernel(heads, batch, k_hbm, v_hbm, beta_hbm, log_hbm, k32, log_ref, wu_ref, n_ref, own_ref, *rest):
    sends, (k16, v16, v32, beta_ref, all_ref, sems) = rest[: heads - 1], rest[heads - 1 :]
    fetch(((k_hbm, k16), (log_hbm, log_ref), (beta_hbm, beta_ref), (v_hbm, v16)), sems)
    k32[...] = k16[...].astype(F32)
    v32[...] = v16[...].astype(F32)
    chunks = beta_ref.shape[1] // C
    row, col = iotas()
    eye = row == col
    within = row >= col
    strict = row > col
    for start in range(0, heads, batch):
        jobs = [(head, c) for head in range(start, start + batch) for c in range(chunks)]
        lowers, sides, fades, ends = [], [], [], []
        for head, c in jobs:
            raw = k32[chunk_rows(heads, head, c), :]
            value = v32[chunk_rows(heads, head, c), :]
            beta = to_column(tokens_of(beta_ref, head, c), eye)
            column, decay = decay_parts(tokens_of(log_ref, head, c), within, eye)
            scale = inverse_scale(raw)
            raw16 = raw.astype(BF16)
            gram = dot(raw16, raw16, NT)
            lowers.append(jnp.where(strict, gram * decay * (beta * scale) * to_row(scale, eye), 0.0))
            unit = raw * scale
            last = column[C - 1 : C, :]
            sides.append(jnp.concatenate([unit * (beta * jnp.exp(column)), value * beta], axis=1))
            fades.append((unit * jnp.exp(last - column)).T)
            ends.append(jnp.exp(last))
        solved = [dot3(split(x), split(s)) for x, s in zip(inverses(lowers, row, col), sides)]
        maps = []
        for i, (head, c) in enumerate(jobs):
            wu_ref[head * chunks + c] = solved[i]
            both = dot3(split(fades[i]), split(solved[i]))
            maps.append((jnp.where(eye, ends[i], 0.0) - both[:, :C], both[:, C:]))
        for j in range(batch):
            state = jnp.concatenate(maps[j * chunks], axis=1)
            for c in range(1, chunks):
                n_ref[(start + j) * chunks + c] = state
                moved, fresh = maps[j * chunks + c]
                state = dot3(split(moved), split(state))
                state = jnp.concatenate([state[:, :C], state[:, C:] + fresh], axis=1)
            all_ref[start + j] = state
    place = lax.rem(lax.axis_index("seq"), heads)
    own_ref[...] = all_ref[place]
    for r in range(1, heads):
        sends[r - 1][...] = all_ref[other_place(place, r, heads)].astype(BF16)


def other_place(place, r, heads):
    result = place
    for i in range(heads):
        result = jnp.where(place == i, i ^ r, result)
    return result


def local_maps(key, value, beta, log_decay, batch):
    heads, tokens = beta.shape
    chunks = tokens // C
    here = pl.BlockSpec(memory_space=pltpu.VMEM)
    return pl.pallas_call(
        functools.partial(local_maps_kernel, heads, batch),
        in_specs=[pl.BlockSpec(memory_space=pltpu.HBM)] * 4,
        out_specs=[here] * (4 + heads),
        out_shape=[
            jax.ShapeDtypeStruct(key.shape, F32),
            jax.ShapeDtypeStruct(beta.shape, F32),
            jax.ShapeDtypeStruct((heads * chunks, C, 2 * C), F32),
            jax.ShapeDtypeStruct((heads * chunks, C, 2 * C), F32),
            jax.ShapeDtypeStruct((C, 2 * C), F32),
        ]
        + [jax.ShapeDtypeStruct((C, 2 * C), BF16)] * (heads - 1),
        scratch_shapes=[
            pltpu.VMEM(key.shape, BF16),
            pltpu.VMEM(key.shape, BF16),
            pltpu.VMEM(key.shape, F32),
            pltpu.VMEM(beta.shape, F32),
            pltpu.VMEM((heads, C, 2 * C), F32),
            pltpu.SemaphoreType.DMA((4,)),
        ],
        compiler_params=pltpu.CompilerParams(vmem_limit_bytes=32 * MIB),
        name="local_maps",
    )(*in_hbm(key, value, beta, log_decay))


def rows_kernel(heads, mine, q_hbm, k32, log_ref, wu_ref, n_ref, out_ref, q16, q32, sems):
    fetch(((q_hbm, q16),), sems)
    q32[...] = q16[...].astype(F32)
    chunks = log_ref.shape[1] // C
    row, col = iotas()
    eye = row == col
    within = row >= col
    for j, head in enumerate(mine):
        for c in range(chunks):
            query, raw = q32[chunk_rows(heads, head, c), :], k32[chunk_rows(heads, head, c), :]
            column, decay = decay_parts(tokens_of(log_ref, head, c), within, eye)
            scale = inverse_scale(query)
            pairs = dot(query.astype(BF16), raw.astype(BF16), NT)
            pairs = pairs * decay * scale * to_row(inverse_scale(raw), eye)
            both = dot3(split(pairs), split(wu_ref[head * chunks + c]))
            reach = query * (scale * jnp.exp(column)) - both[:, :C]
            fresh = both[:, C:]
            if c > 0:
                earlier = dot3(split(reach), split(n_ref[head * chunks + c]))
                reach = earlier[:, :C]
                fresh = fresh + earlier[:, C:]
            out_ref[j, c * C : (c + 1) * C, :] = jnp.concatenate([reach, fresh], axis=1)


def row_maps(mine, query, k32, log_decay, wu, states):
    heads, tokens = log_decay.shape
    here = pl.BlockSpec(memory_space=pltpu.VMEM)
    return pl.pallas_call(
        functools.partial(rows_kernel, heads, mine),
        in_specs=[pl.BlockSpec(memory_space=pltpu.HBM)] + [here] * 4,
        out_specs=here,
        out_shape=jax.ShapeDtypeStruct((len(mine), tokens, 2 * C), F32),
        scratch_shapes=[
            pltpu.VMEM(query.shape, BF16),
            pltpu.VMEM(query.shape, F32),
            pltpu.SemaphoreType.DMA((1,)),
        ],
        compiler_params=pltpu.CompilerParams(vmem_limit_bytes=16 * MIB),
        cost_estimate=pl.CostEstimate(flops=2000000000, bytes_accessed=8000000, transcendentals=0),
        name="row_maps",
    )(*in_hbm(query), k32, log_decay, wu, states)


def small_call(kernel, out_shape, *args):
    here = pl.BlockSpec(memory_space=pltpu.VMEM)
    return pl.pallas_call(
        kernel,
        in_specs=[here] * len(args),
        out_specs=[here] * len(out_shape),
        out_shape=out_shape,
        compiler_params=pltpu.CompilerParams(vmem_limit_bytes=8 * MIB),
        name=kernel.__name__,
    )(*args)


def moved_on(maps, state16, added):
    high, low = split(maps)
    return dot(jnp.concatenate([high, low], axis=1), twice(state16)) + added


def in_order(own_ref, got_refs, held):
    heads = held.shape[0]
    place = lax.rem(lax.axis_index("seq"), heads)
    held[place] = own_ref[...]
    for r, got in enumerate(got_refs, 1):
        held[other_place(place, r, heads)] = got[...].astype(F32)
    return place


def group_state(own_ref, *refs):
    got_refs, (held, out_ref) = refs[:-2], refs[-2:]
    in_order(own_ref, got_refs, held)
    state = held[0, :, C:].astype(BF16)
    for i in range(1, held.shape[0]):
        state = moved_on(held[i, :, :C], state, held[i, :, C:]).astype(BF16)
    out_ref[...] = state


def group_total(own_ref, *refs):
    got_refs, (held, out_ref) = refs[:-2], refs[-2:]
    in_order(own_ref, got_refs, held)
    total = held[0]
    for i in range(1, held.shape[0]):
        later = held[i]
        total = dot3(split(later[:, :C]), split(total))
        total = jnp.concatenate([total[:, :C], total[:, C:] + later[:, C:]], axis=1)
    out_ref[...] = total.astype(BF16)


def group_states(held, state, keep_ref, send_refs, states):
    heads = held.shape[0]
    for i in range(heads):
        states[i] = state
        if i + 1 < heads:
            state = moved_on(held[i, :, :C], state, held[i, :, C:]).astype(BF16)
    place = lax.rem(lax.axis_index("seq"), heads)
    keep_ref[...] = states[place]
    for r, send in enumerate(send_refs, 1):
        send[...] = states[other_place(place, r, heads)]


def states_of_upper(held, lower_ref, keep_ref, *refs):
    lower = lower_ref[...]
    state = jnp.where(lax.axis_index("seq") < held.shape[0], jnp.zeros_like(lower), lower)
    group_states(held, state, keep_ref, refs[:-1], refs[-1])


def states_given(held, state_ref, keep_ref, *refs):
    group_states(held, state_ref[...], keep_ref, refs[:-1], refs[-1])


def prefix(total, heads):
    count = lax.axis_size("seq")
    groups = [list(range(i, count, heads)) for i in range(heads)]
    me = lax.axis_index("seq") // heads
    totals = lax.all_gather(total, "seq", axis_index_groups=groups)

    def step(d, state):
        longer = jnp.einsum("ik,pkw->iw", totals[d, :, :C], jnp.stack(split(state)), preferred_element_type=F32)
        return jnp.where(d < me, longer + totals[d, :, C:].astype(F32), state)

    start = jnp.zeros((C, C), F32)
    return lax.fori_loop(0, count // heads - 1, step, start).astype(BF16)


def apply_kernel(heads, rows0_ref, rows1_ref, *refs):
    states, (keep_ref, send_ref, held) = refs[:heads], refs[heads:]
    step = pl.program_id(0)

    @pl.when(step == 0)
    def _():
        place = lax.rem(lax.axis_index("seq"), heads)
        for r in range(heads):
            held[other_place(place, r, heads)] = states[r][...]

    attended = []
    for h in range(heads):
        rows_ref = (rows0_ref, rows1_ref)[h // (heads // 2)]
        reach, fresh = rows_ref[h % (heads // 2), :, :C], rows_ref[h % (heads // 2), :, C:]
        attended.append(moved_on(reach, held[h], fresh).astype(BF16))
    attended = jnp.concatenate(attended, axis=1)
    mine = lax.rem(step, 2) == lax.rem(lax.axis_index("head"), 2)

    @pl.when(mine)
    def _():
        keep_ref[step // 2] = attended

    @pl.when(jnp.logical_not(mine))
    def _():
        send_ref[step // 2] = attended


def apply(rows, states, groups):
    _, tokens, _ = rows[0].shape
    heads = len(states)
    block = tokens // groups
    out = jax.ShapeDtypeStruct((groups // 2, block, heads * C), BF16)
    return pl.pallas_call(
        functools.partial(apply_kernel, heads),
        grid=(groups,),
        in_specs=[pl.BlockSpec((heads // 2, block, 2 * C), lambda i: (0, i, 0))] * 2
        + [pl.BlockSpec((C, C), lambda i: (0, 0))] * heads,
        out_specs=[pl.BlockSpec(out.shape, lambda i: (0, 0, 0))] * 2,
        out_shape=[out, out],
        scratch_shapes=[pltpu.VMEM((heads, C, C), BF16)],
        compiler_params=pltpu.CompilerParams(vmem_limit_bytes=14 * MIB),
        name="apply",
    )(*rows, *states)


def project_kernel(other, keep_ref, got_ref, w_ref, w2_ref, out_ref):
    pair = lax.axis_index("head") // 2
    index = 1 - pair if other else pair
    out_ref[...] = (dot(keep_ref[index], w_ref[...]) + dot(got_ref[index], w2_ref[...])).astype(out_ref.dtype)


def project(other, keep, got, weight, weight2):
    _, block, depth = keep.shape
    width = weight.shape[1]
    return pl.pallas_call(
        functools.partial(project_kernel, other),
        out_shape=jax.ShapeDtypeStruct((block, width), BF16 if other else F32),
        compiler_params=pltpu.CompilerParams(vmem_limit_bytes=20 * MIB),
        cost_estimate=pl.CostEstimate(
            flops=4 * block * depth * width, bytes_accessed=4 * depth * width, transcendentals=0
        ),
        name="project",
    )(keep, got, weight, weight2)


def swap(x, axis, bit):
    count = lax.axis_size(axis)
    return lax.ppermute(x, axis, [(i, i ^ bit) for i in range(count)])


def body(query, key, value, beta, log_decay, out_weight):
    tokens, heads, _ = key.shape
    count = lax.axis_size("seq")
    flat = lambda x: x.reshape(tokens * heads, C)
    weight2 = swap(out_weight, "head", 1)
    k32, logs, wu, states, own, *sends = local_maps(flat(key), flat(value), beta, log_decay, 2)
    got = [swap(x, "seq", r) for r, x in enumerate(sends, 1)]
    half = heads // 2
    rows0 = row_maps(range(half), flat(query), k32, logs, wu, states)
    rows1 = row_maps(range(half, heads), flat(query), k32, logs, wu, states)
    rows0, got = lax.optimization_barrier((rows0, got))
    wide = jax.ShapeDtypeStruct((heads, C, 2 * C), F32)
    square = jax.ShapeDtypeStruct((C, C), BF16)
    outs = [square] * heads + [jax.ShapeDtypeStruct((heads, C, C), BF16)]
    if count == 2 * heads:
        held, state = small_call(group_state, [wide, square], own, *got)
        lower = swap(state, "seq", heads)
        rows1, lower = lax.optimization_barrier((rows1, lower))
        keep, *sends = small_call(states_of_upper, outs, held, lower)
    else:
        total16 = jax.ShapeDtypeStruct((C, 2 * C), BF16)
        held, total = small_call(group_total, [wide, total16], own, *got)
        keep, *sends = small_call(states_given, outs, held, prefix(total, heads))
    entering = [keep] + [swap(x, "seq", r) for r, x in enumerate(sends[: heads - 1], 1)]
    keep, away = apply((rows0, rows1), entering, lax.axis_size("head"))
    got = swap(away, "head", 1)
    theirs = swap(project(True, keep, got, out_weight, weight2), "head", 2)
    mine = project(False, keep, got, out_weight, weight2)
    return (mine + theirs.astype(F32)).astype(BF16)


def solution(mesh):
    in_specs = (
        P("seq", "head", None),
        P("seq", "head", None),
        P("seq", "head", None),
        P("head", "seq"),
        P("head", "seq"),
        P("head", None),
    )
    out_specs = P(("seq", "head"), None)
    return jax.shard_map(body, mesh=mesh, in_specs=in_specs, out_specs=out_specs, check_vma=False)
```

time: 63.2 us -> 51 us (0.81)
  blocking collectives: 11.7 us -> 0 us
  waiting for transfers between devices: 14.1 us -> 18.9 us
  local copies, waits for them, and re-layouts: 4.52 us -> 0.01 us
  starting transfers between devices: 15.3 us -> 12.4 us
  Pallas kernels: 16.1 us -> 18.5 us
    ppermute x7 -> x0, starting transfers between devices: 13.2 us -> none  [shift(): lax.ppermute(x, axis, [(i, (i + amount) % count) for i in range(count)])]
    all_to_all x1 -> x0, blocking collectives: 11.7 us -> none  [body(): lax.all_to_all(chain(sent), 'seq', 0, 0, tiled=True).reshape(heads, C, C)]
    ppermute x3 -> x10, starting transfers between devices: 2.11 us -> 12.4 us  [swap(): return lax.ppermute(x, axis, [(i, i ^ bit) for i in range(count)])]
    ppermute x3 -> x10, waiting for transfers between devices: 13.3 us -> 18.9 us  [swap(): return lax.ppermute(x, axis, [(i, i ^ bit) for i in range(count)])]
    unnamed x12 -> x2, local copies, waits for them, and re-layouts: 4.52 us -> 0.01 us
    pallas_call x3 -> x5, Pallas kernels: 13.2 us -> 15.8 us  [the longest x1 8.73 us: local_maps(): pl.pallas_call(functools.partial(local_maps_kernel, heads, batch), in_spe...]
    ppermute x7 -> x0, waiting for transfers between devices: 0.82 us -> none  [shift(): lax.ppermute(x, axis, [(i, (i + amount) % count) for i in range(count)])]
  transfers between devices with their start and end apart: 10 -> 10, of which waited for: 4 -> 7; matrix products, arithmetic and copies ran while one was open for 0% -> 0% of each run, Pallas kernels for 25% -> 35%
where the time goes in v6:
time: 51 us; the launch traced here: 50.8 us
  waiting for transfers between devices  18.9 us (37%)
  Pallas kernels  18.5 us (36%)
  starting transfers between devices  12.4 us (24%)
  other arithmetic  0.9 us (2%)
    ppermute x10, waiting for transfers between devices, swap(): return lax.ppermute(x, axis, [(i, i ^ bit) for i in range(count)])  18.9 us
    ppermute x10, starting transfers between devices, swap(): return lax.ppermute(x, axis, [(i, i ^ bit) for i in range(count)])  12.4 us
    pallas_call x1, Pallas kernels, local_maps(): pl.pallas_call(functools.partial(local_maps_kernel, heads, batch), in_spe...  8.73 us
    pallas_call x2, Pallas kernels, row_maps(): pl.pallas_call(functools.partial(rows_kernel, heads, mine), in_specs=[pl....  5.46 us
    pallas_call x2, Pallas kernels, small_call(): pl.pallas_call(kernel, in_specs=[here] * len(args), out_specs=[here] * le...  1.65 us
    pallas_call x2, Pallas kernels, project(): pl.pallas_call(functools.partial(project_kernel, other), out_shape=jax.Sh...  1.44 us
    pallas_call x1, Pallas kernels, apply(): pl.pallas_call(functools.partial(apply_kernel, heads), grid=(groups,), in...  1.21 us
  transfers between devices with their start and end apart: 10, of which 7 were waited for; matrix products, arithmetic and copies ran while one was open for 0% of the time, Pallas kernels for 35%

profile of v6, /device:TPU:0, one launch (start us, length us, event | category | flops | bytes accessed | tf_op | source)
XLA Modules:
  0.0 50.8 jit_solution(7708885219791596500)
XLA Ops:
  0.0 0.5 collective-permute-start.8
  0.5 8.7 %local_maps.1 = (f32[2048,128]{1,0:T(8,128)S(1)}, f32[4,512]{1,0:T(4,128)S(1)}, f32[16,128,256]{2,1,0:T(8,128)S(1)}, f32[16,128,256]{2,1,0:T(8,128)S(1)}, f32[12...) custom-call(bf16[2048,128]{1,0:T(8,128)(2,1)} %bitcast.3, ...), custom_call_target="tpu_custom_call" | custom-call | tf_op jit(solution)/shard_map/local_maps/pallas_call | solution.py:193
  9.2 2.6 %collective-permute-start = (bf16[128,256]{1,0:T(8,128)(2,1)S(1)}, bf16[128,256]{1,0:T(8,128)(2,1)S(1)}, u32[]{:S(2)}, u32[]{:S(2)}) collective-permute-start(bf16[128,256]{1,0:T(8,128)(2,1)S(1)} %get-tuple-element.31), channel_id=1, source_target_pairs={{0,4},{4,0},{8,12},{12,8},{16,20},{20,16},{24,28},{28,24},{1,5},{5... | collective-permute-start | bytes 196616 | tf_op jit(solution)/shard_map/ppermute | solution.py:410
  11.7 1.6 %collective-permute-start.1 = (bf16[128,256]{1,0:T(8,128)(2,1)S(1)}, bf16[128,256]{1,0:T(8,128)(2,1)S(1)}, u32[]{:S(2)}, u32[]{:S(2)}) collective-permute-start(bf16[128,256]{1,0:T(8,128)(2,1)S(1)} %get-tuple-element.32), channel_id=1, source_target_pairs={{0,8},{4,12},{8,0},{12,4},{16,24},{20,28},{24,16},{28,20},{1,9},{5... | collective-permute-start | bytes 196616 | tf_op jit(solution)/shard_map/ppermute | solution.py:410
  13.3 2.7 %row_maps.2.rows0_ref = f32[2,512,256]{2,1,0:T(8,128)S(1)} custom-call(bf16[2048,128]{1,0:T(8,128)(2,1)} %bitcast.5, f32[2048,128]{1,0:T(8,128)S(1)} %get-tuple-element.27.k32, f32[4,512]{1,0:T(4,128)S(1)} %get-tuple-element.28.log_ref, f32[16,128,256]{2,1,0:T(8,128)S(1)} %get-tuple-element.29.wu_ref, f32[16,128,256]{2,1,0:T(8,128)S(1)} %get-tuple-element.30.n_ref), custom_call_target="tpu_custom_call" | custom-call | flops 2000000000 | bytes 8000000 | tf_op jit(solution)/shard_map/row_maps/pallas_call | solution.py:245
  16.1 0.2 collective-permute-done.1.refs_1_
  16.3 2.2 %collective-permute-done.2.refs_2_ = bf16[128,256]{1,0:T(8,128)(2,1)S(1)} collective-permute-done((bf16[128,256]{1,0:T(8,128)(2,1)S(1)}, bf16[128,256]{1,0:T(8,128)(2,1)S(1)}, u32[]{:S(2)}, u32[]{:S(2)}) %collective-permute-start.2) | collective-permute-done | bytes 65568 | tf_op jit(solution)/shard_map/ppermute | solution.py:410
  18.5 0.5 group_state.1
  19.0 2.7 %collective-permute-start.3 = (bf16[128,128]{1,0:T(8,128)(2,1)S(1)}, bf16[128,128]{1,0:T(8,128)(2,1)S(1)}, u32[]{:S(2)}, u32[]{:S(2)}) collective-permute-start(bf16[128,128]{1,0:T(8,128)(2,1)S(1)} %get-tuple-element.39), channel_id=1, source_target_pairs={{0,16},{4,20},{8,24},{12,28},{16,0},{20,4},{24,8},{28,12},{1,17},{... | collective-permute-start | bytes 98312 | tf_op jit(solution)/shard_map/ppermute | solution.py:410
  21.6 2.7 %row_maps.3.rows1_ref = f32[2,512,256]{2,1,0:T(8,128)S(1)} custom-call(bf16[2048,128]{1,0:T(8,128)(2,1)} %bitcast.6, f32[2048,128]{1,0:T(8,128)S(1)} %get-tuple-element.27.k32, f32[4,512]{1,0:T(4,128)S(1)} %get-tuple-element.28.log_ref, f32[16,128,256]{2,1,0:T(8,128)S(1)} %get-tuple-element.29.wu_ref, f32[16,128,256]{2,1,0:T(8,128)S(1)} %get-tuple-element.30.n_ref), custom_call_target="tpu_custom_call" | custom-call | flops 2000000000 | bytes 8000000 | tf_op jit(solution)/shard_map/row_maps/pallas_call | solution.py:245
  24.4 1.2 %states_of_upper.1 = (bf16[128,128]{1,0:T(8,128)(2,1)S(1)}, bf16[128,128]{1,0:T(8,128)(2,1)S(1)}, bf16[128,128]{1,0:T(8,128)(2,1)S(1)}, bf16[128,128]{1,0:T(8,128)(2,1)S(1)}, bf16[4,128,128]{2,1,0:T(8,128)(2,1)}) custom-call(f32[4,128,256]{2,1,0:T(8,128)S(1)} %get-tuple-element.41.held, bf16[128,128]{1,0:T(8,128)(2,1)S(1)} %collective-permute-done.3.lower_ref), custom_call_target="tpu_custom_call" | custom-call | tf_op jit(solution)/shard_map/states_of_upper/pallas_call | solution.py:263
  25.6 0.5 %collective-permute-start.4 = (bf16[128,128]{1,0:T(8,128)(2,1)S(1)}, bf16[128,128]{1,0:T(8,128)(2,1)S(1)}, u32[]{:S(2)}, u32[]{:S(2)}) collective-permute-start(bf16[128,128]{1,0:T(8,128)(2,1)S(1)} %get-tuple-element.44), channel_id=1, source_target_pairs={{0,4},{4,0},{8,12},{12,8},{16,20},{20,16},{24,28},{28,24},{1,5},{5... | collective-permute-start | bytes 98312 | tf_op jit(solution)/shard_map/ppermute | solution.py:410
  26.1 1.4 %collective-permute-start.5 = (bf16[128,128]{1,0:T(8,128)(2,1)S(1)}, bf16[128,128]{1,0:T(8,128)(2,1)S(1)}, u32[]{:S(2)}, u32[]{:S(2)}) collective-permute-start(bf16[128,128]{1,0:T(8,128)(2,1)S(1)} %get-tuple-element.45), channel_id=1, source_target_pairs={{0,8},{4,12},{8,0},{12,4},{16,24},{20,28},{24,16},{28,20},{1,9},{5... | collective-permute-start | bytes 98312 | tf_op jit(solution)/shard_map/ppermute | solution.py:410
  27.5 1.6 %collective-permute-start.6 = (bf16[128,128]{1,0:T(8,128)(2,1)S(1)}, bf16[128,128]{1,0:T(8,128)(2,1)S(1)}, u32[]{:S(2)}, u32[]{:S(2)}) collective-permute-start(bf16[128,128]{1,0:T(8,128)(2,1)S(1)} %get-tuple-element.46), channel_id=1, source_target_pairs={{0,12},{4,8},{8,4},{12,0},{16,28},{20,24},{24,20},{28,16},{1,13},{... | collective-permute-start | bytes 98312 | tf_op jit(solution)/shard_map/ppermute | solution.py:410
  29.0 0.8 %collective-permute-done.4.refs_1_ = bf16[128,128]{1,0:T(8,128)(2,1)S(1)} collective-permute-done((bf16[128,128]{1,0:T(8,128)(2,1)S(1)}, bf16[128,128]{1,0:T(8,128)(2,1)S(1)}, u32[]{:S(2)}, u32[]{:S(2)}) %collective-permute-start.4) | collective-permute-done | bytes 32800 | tf_op jit(solution)/shard_map/ppermute | solution.py:410
  29.8 0.2 collective-permute-done.5.refs_2_
  30.0 2.3 %collective-permute-done.6.refs_3_ = bf16[128,128]{1,0:T(8,128)(2,1)S(1)} collective-permute-done((bf16[128,128]{1,0:T(8,128)(2,1)S(1)}, bf16[128,128]{1,0:T(8,128)(2,1)S(1)}, u32[]{:S(2)}, u32[]{:S(2)}) %collective-permute-start.6) | collective-permute-done | bytes 32800 | tf_op jit(solution)/shard_map/ppermute | solution.py:410
  32.3 1.2 %apply.1 = (bf16[2,128,512]{2,1,0:T(8,128)(2,1)S(1)}, bf16[2,128,512]{2,1,0:T(8,128)(2,1)S(1)}) custom-call(f32[2,512,256]{2,1,0:T(8,128)S(1)} %row_maps.2.rows0_ref, f32[2,512,256]{2,1,0:T(8,128)S(1)} %row_maps.3.rows1_ref, bf16[128,128]{1,0:T(8,128)(2,1)S(1)} %get-tuple-element.43.refs_0_, bf16[128,128]{1,0:T(8,128)(2,1)S(1)} %collective-permute-done.4.refs_1_, ...), custom_call_target="tpu_custom_call" | custom-call | tf_op jit(solution)/shard_map/apply/pallas_call | solution.py:375
  33.6 1.5 %collective-permute-done.7.got_ref = bf16[2,128,512]{2,1,0:T(8,128)(2,1)S(1)} collective-permute-done((bf16[2,128,512]{2,1,0:T(8,128)(2,1)S(1)}, bf16[2,128,512]{2,1,0:T(8,128)(2,1)S(1)}, u32[]{:S(2)}, u32[]{:S(2)}) %collective-permute-start.7) | collective-permute-done | bytes 262176 | tf_op jit(solution)/shard_map/ppermute | solution.py:410
  35.1 0.7 %project.3 = bf16[128,2048]{1,0:T(8,128)(2,1)S(1)} custom-call(bf16[2,128,512]{2,1,0:T(8,128)(2,1)S(1)} %get-tuple-element.47.keep_ref, bf16[2,128,512]{2,1,0:T(8,128)(2,1)S(1)} %collective-permute-done.7.got_ref, bf16[512,2048]{1,0:T(8,128)(2,1)S(1)} %copy-done, bf16[512,2048]{1,0:T(8,128)(2,1)S(1)} %collective-permute-done.8.w2_ref), custom_call_target="tpu_custom_call" | custom-call | flops 536870912 | bytes 4194304 | tf_op jit(solution)/shard_map/project/pallas_call | solution.py:397
  35.9 1.6 %collective-permute-start.9 = (bf16[128,2048]{1,0:T(8,128)(2,1)S(1)}, bf16[128,2048]{1,0:T(8,128)(2,1)S(1)}, u32[]{:S(2)}, u32[]{:S(2)}) collective-permute-start(bf16[128,2048]{1,0:T(8,128)(2,1)S(1)} %project.3), channel_id=1, source_target_pairs={{0,2},{1,3},{2,0},{3,1},{4,6},{5,7},{6,4},{7,5},{8,10},{9,11},{10,... | collective-permute-start | bytes 1572872 | tf_op jit(solution)/shard_map/ppermute | solution.py:410
  37.4 0.7 %project.2 = f32[128,2048]{1,0:T(8,128)S(1)} custom-call(bf16[2,128,512]{2,1,0:T(8,128)(2,1)S(1)} %get-tuple-element.47.keep_ref, bf16[2,128,512]{2,1,0:T(8,128)(2,1)S(1)} %collective-permute-done.7.got_ref, bf16[512,2048]{1,0:T(8,128)(2,1)S(1)} %copy-done, bf16[512,2048]{1,0:T(8,128)(2,1)S(1)} %collective-permute-done.8.w2_ref), custom_call_target="tpu_custom_call" | custom-call | flops 536870912 | bytes 4194304 | tf_op jit(solution)/shard_map/project/pallas_call | solution.py:397
  38.2 11.7 %collective-permute-done.9 = bf16[128,2048]{1,0:T(8,128)(2,1)S(1)} collective-permute-done((bf16[128,2048]{1,0:T(8,128)(2,1)S(1)}, bf16[128,2048]{1,0:T(8,128)(2,1)S(1)}, u32[]{:S(2)}, u32[]{:S(2)}) %collective-permute-start.9) | collective-permute-done | bytes 524320 | tf_op jit(solution)/shard_map/ppermute | solution.py:410
  49.9 0.9 %add_convert_fusion = bf16[128,2048]{1,0:T(8,128)(2,1)} fusion(f32[128,2048]{1,0:T(8,128)S(1)} %project.2, bf16[128,2048]{1,0:T(8,128)(2,1)S(1)} %collective-permute-done.9), kind=kLoop, calls=%fused_computation | loop fusion | flops 786432 | bytes 2097152 | tf_op jit(solution)/shard_map/convert_element_type | solution.py:441
  (7 shorter events, 0.1 us)
Async XLA Ops:
  0.0 35.1 %collective-permute-start.8 = (bf16[512,2048]{1,0:T(8,128)(2,1)}, bf16[512,2048]{1,0:T(8,128)(2,1)S(1)}, u32[]{:S(2)}, u32[]{:S(2)}) collective-permute-start(bf16[512,2048]{1,0:T(8,128)(2,1)} %w_ref.3), channel_id=1, source_target_pairs={{0,1},{1,0},{2,3},{3,2},{4,5},{5,4},{6,7},{7,6},{8,9},{9,8},{10,11... | collective-permute-start | bytes 6291464 | tf_op jit(solution)/shard_map/ppermute | solution.py:410
  9.2 6.9 %collective-permute-start = (bf16[128,256]{1,0:T(8,128)(2,1)S(1)}, bf16[128,256]{1,0:T(8,128)(2,1)S(1)}, u32[]{:S(2)}, u32[]{:S(2)}) collective-permute-start(bf16[128,256]{1,0:T(8,128)(2,1)S(1)} %get-tuple-element.31), channel_id=1, source_target_pairs={{0,4},{4,0},{8,12},{12,8},{16,20},{20,16},{24,28},{28,24},{1,5},{5... | collective-permute-start | bytes 196616 | tf_op jit(solution)/shard_map/ppermute | solution.py:410
  11.7 4.5 %collective-permute-start.1 = (bf16[128,256]{1,0:T(8,128)(2,1)S(1)}, bf16[128,256]{1,0:T(8,128)(2,1)S(1)}, u32[]{:S(2)}, u32[]{:S(2)}) collective-permute-start(bf16[128,256]{1,0:T(8,128)(2,1)S(1)} %get-tuple-element.32), channel_id=1, source_target_pairs={{0,8},{4,12},{8,0},{12,4},{16,24},{20,28},{24,16},{28,20},{1,9},{5... | collective-permute-start | bytes 196616 | tf_op jit(solution)/shard_map/ppermute | solution.py:410
  13.3 5.2 %collective-permute-start.2 = (bf16[128,256]{1,0:T(8,128)(2,1)S(1)}, bf16[128,256]{1,0:T(8,128)(2,1)S(1)}, u32[]{:S(2)}, u32[]{:S(2)}) collective-permute-start(bf16[128,256]{1,0:T(8,128)(2,1)S(1)} %get-tuple-element.33), channel_id=1, source_target_pairs={{0,12},{4,8},{8,4},{12,0},{16,28},{20,24},{24,20},{28,16},{1,13},{... | collective-permute-start | bytes 196616 | tf_op jit(solution)/shard_map/ppermute | solution.py:410
  19.0 5.4 %collective-permute-start.3 = (bf16[128,128]{1,0:T(8,128)(2,1)S(1)}, bf16[128,128]{1,0:T(8,128)(2,1)S(1)}, u32[]{:S(2)}, u32[]{:S(2)}) collective-permute-start(bf16[128,128]{1,0:T(8,128)(2,1)S(1)} %get-tuple-element.39), channel_id=1, source_target_pairs={{0,16},{4,20},{8,24},{12,28},{16,0},{20,4},{24,8},{28,12},{1,17},{... | collective-permute-start | bytes 98312 | tf_op jit(solution)/shard_map/ppermute | solution.py:410
  24.4 10.7 %copy-start = (bf16[512,2048]{1,0:T(8,128)(2,1)S(1)}, bf16[512,2048]{1,0:T(8,128)(2,1)}, u32[]{:S(2)}) copy-start(bf16[512,2048]{1,0:T(8,128)(2,1)} %w_ref.3) | copy-start | bytes 6291460
  25.6 4.3 %collective-permute-start.4 = (bf16[128,128]{1,0:T(8,128)(2,1)S(1)}, bf16[128,128]{1,0:T(8,128)(2,1)S(1)}, u32[]{:S(2)}, u32[]{:S(2)}) collective-permute-start(bf16[128,128]{1,0:T(8,128)(2,1)S(1)} %get-tuple-element.44), channel_id=1, source_target_pairs={{0,4},{4,0},{8,12},{12,8},{16,20},{20,16},{24,28},{28,24},{1,5},{5... | collective-permute-start | bytes 98312 | tf_op jit(solution)/shard_map/ppermute | solution.py:410
  26.1 3.9 %collective-permute-start.5 = (bf16[128,128]{1,0:T(8,128)(2,1)S(1)}, bf16[128,128]{1,0:T(8,128)(2,1)S(1)}, u32[]{:S(2)}, u32[]{:S(2)}) collective-permute-start(bf16[128,128]{1,0:T(8,128)(2,1)S(1)} %get-tuple-element.45), channel_id=1, source_target_pairs={{0,8},{4,12},{8,0},{12,4},{16,24},{20,28},{24,16},{28,20},{1,9},{5... | collective-permute-start | bytes 98312 | tf_op jit(solution)/shard_map/ppermute | solution.py:410
  27.5 4.8 %collective-permute-start.6 = (bf16[128,128]{1,0:T(8,128)(2,1)S(1)}, bf16[128,128]{1,0:T(8,128)(2,1)S(1)}, u32[]{:S(2)}, u32[]{:S(2)}) collective-permute-start(bf16[128,128]{1,0:T(8,128)(2,1)S(1)} %get-tuple-element.46), channel_id=1, source_target_pairs={{0,12},{4,8},{8,4},{12,0},{16,28},{20,24},{24,20},{28,16},{1,13},{... | collective-permute-start | bytes 98312 | tf_op jit(solution)/shard_map/ppermute | solution.py:410
  33.5 1.6 %collective-permute-start.7 = (bf16[2,128,512]{2,1,0:T(8,128)(2,1)S(1)}, bf16[2,128,512]{2,1,0:T(8,128)(2,1)S(1)}, u32[]{:S(2)}, u32[]{:S(2)}) collective-permute-start(bf16[2,128,512]{2,1,0:T(8,128)(2,1)S(1)} %get-tuple-element.48), channel_id=1, source_target_pairs={{0,1},{1,0},{2,3},{3,2},{4,5},{5,4},{6,7},{7,6},{8,9},{9,8},{10,11... | collective-permute-start | bytes 786440 | tf_op jit(solution)/shard_map/ppermute | solution.py:410
  35.9 14.0 %collective-permute-start.9 = (bf16[128,2048]{1,0:T(8,128)(2,1)S(1)}, bf16[128,2048]{1,0:T(8,128)(2,1)S(1)}, u32[]{:S(2)}, u32[]{:S(2)}) collective-permute-start(bf16[128,2048]{1,0:T(8,128)(2,1)S(1)} %project.3), channel_id=1, source_target_pairs={{0,2},{1,3},{2,0},{3,1},{4,6},{5,7},{6,4},{7,5},{8,10},{9,11},{10,... | collective-permute-start | bytes 1572872 | tf_op jit(solution)/shard_map/ppermute | solution.py:410

commit v7 on v6

--- a/solution.py
+++ b/solution.py
@@ -59,11 +59,22 @@
     return lax.rsqrt(jnp.sum(rows * rows, axis=1, keepdims=True) + 1e-06)
 
 
-def decay_parts(log_row, within, eye):
-    column = jnp.sum(jnp.where(within, log_row, 0.0), axis=1, keepdims=True)
-    row = to_row(column, eye)
-    decay = jnp.where(within, jnp.exp(jnp.where(within, column - row, 0.0)), 0.0)
-    return column, decay
+def three(x):
+    high, rest = x.astype(BF16), x
+    rest = rest - high.astype(F32)
+    return (high,) + split(rest)
+
+
+def running_sums(rows, upper):
+    return sum(dot(x, upper) for x in reversed(three(rows)))
+
+
+def spread_columns(row, eye, ones):
+    parts = three(jnp.broadcast_to(row, (16, C)))
+    high, middle, low = (
+        jnp.where(eye, jnp.concatenate([x] * (C // 16), axis=0), jnp.zeros((), BF16)) for x in parts
+    )
+    return dot(jnp.concatenate([high, middle], axis=1), twice(ones)) + dot(low, ones)
 
 
 def base_inverse(lower, row, col):
@@ -132,8 +143,12 @@
     return ref[head : head + 1, c * C : (c + 1) * C]
 
 
-def local_maps_kernel(heads, batch, k_hbm, v_hbm, beta_hbm, log_hbm, k32, log_ref, wu_ref, n_ref, own_ref, *rest):
-    sends, (k16, v16, v32, beta_ref, all_ref, sems) = rest[: heads - 1], rest[heads - 1 :]
+def per_chunk(ref):
+    return jnp.concatenate([ref[:, i : i + C] for i in range(0, ref.shape[1], C)], axis=0)
+
+
+def local_maps_kernel(heads, batch, k_hbm, v_hbm, beta_hbm, log_hbm, k32, sums_ref, mix_ref, wu_ref, n_ref, own_ref, *rest):
+    sends, (k16, v16, v32, beta_ref, log_ref, all_ref, sems) = rest[: heads - 1], rest[heads - 1 :]
     fetch(((k_hbm, k16), (log_hbm, log_ref), (beta_hbm, beta_ref), (v_hbm, v16)), sems)
     k32[...] = k16[...].astype(F32)
     v32[...] = v16[...].astype(F32)
@@ -142,29 +157,44 @@
     eye = row == col
     within = row >= col
     strict = row > col
+    one = jnp.ones((C, C), BF16)
+    eye16 = jnp.where(eye, one, jnp.zeros((), BF16))
+    sums = running_sums(per_chunk(log_ref), jnp.where(row <= col, one, jnp.zeros((), BF16)))
+    sums_ref[...] = sums
+    grown = jnp.exp(sums)
+    faded = jnp.exp(sums[:, C - 1 :] - sums)
+    betas = per_chunk(beta_ref)
     for start in range(0, heads, batch):
         jobs = [(head, c) for head in range(start, start + batch) for c in range(chunks)]
-        lowers, sides, fades, ends = [], [], [], []
+        lowers, raws, values, fades, lengths = [], [], [], [], []
         for head, c in jobs:
-            raw = k32[chunk_rows(heads, head, c), :]
-            value = v32[chunk_rows(heads, head, c), :]
-            beta = to_column(tokens_of(beta_ref, head, c), eye)
-            column, decay = decay_parts(tokens_of(log_ref, head, c), within, eye)
-            scale = inverse_scale(raw)
-            raw16 = raw.astype(BF16)
-            gram = dot(raw16, raw16, NT)
-            lowers.append(jnp.where(strict, gram * decay * (beta * scale) * to_row(scale, eye), 0.0))
-            unit = raw * scale
-            last = column[C - 1 : C, :]
-            sides.append(jnp.concatenate([unit * (beta * jnp.exp(column)), value * beta], axis=1))
-            fades.append((unit * jnp.exp(last - column)).T)
-            ends.append(jnp.exp(last))
-        solved = [dot3(split(x), split(s)) for x, s in zip(inverses(lowers, row, col), sides)]
+            at = slice(c * heads + head, c * heads + head + 1)
+            raw = k32[chunk_rows(heads, head, c), :].astype(BF16)
+            raws.append(raw)
+            values.append(v32[chunk_rows(heads, head, c), :].astype(BF16))
+            both = dot(jnp.concatenate([raw, eye16], axis=0), raw, NT)
+            gram, turned = both[:C], both[C:]
+            square = to_row(gram, eye) + 1e-06
+            scale = lax.rsqrt(square)
+            lengths.append(square * scale)
+            strength = betas[at] * (scale * scale)
+            span = spread_columns(sums[at], eye, one) - sums[at]
+            mix = jnp.where(within, jnp.exp(span), 0.0) * strength
+            mix_ref[head * chunks + c] = mix
+            lowers.append(jnp.where(strict, gram * mix, 0.0))
+            fades.append(turned * (strength * faded[at]))
+        solved = []
+        for i, found in enumerate(inverses(lowers, row, col)):
+            at = slice(jobs[i][1] * heads + jobs[i][0], jobs[i][1] * heads + jobs[i][0] + 1)
+            kept = dot(jnp.concatenate(split(found * grown[at]), axis=1), twice(raws[i]))
+            fresh = dot(jnp.concatenate(split(found * lengths[i]), axis=1), twice(values[i]))
+            solved.append(jnp.concatenate([kept, fresh], axis=1))
         maps = []
         for i, (head, c) in enumerate(jobs):
             wu_ref[head * chunks + c] = solved[i]
             both = dot3(split(fades[i]), split(solved[i]))
-            maps.append((jnp.where(eye, ends[i], 0.0) - both[:, :C], both[:, C:]))
+            end = grown[c * heads + head : c * heads + head + 1, C - 1 :]
+            maps.append((jnp.where(eye, end, 0.0) - both[:, :C], both[:, C:]))
         for j in range(batch):
             state = jnp.concatenate(maps[j * chunks], axis=1)
             for c in range(1, chunks):
@@ -188,17 +218,18 @@
 
 def local_maps(key, value, beta, log_decay, batch):
     heads, tokens = beta.shape
-    chunks = tokens // C
+    count = heads * (tokens // C)
     here = pl.BlockSpec(memory_space=pltpu.VMEM)
     return pl.pallas_call(
         functools.partial(local_maps_kernel, heads, batch),
         in_specs=[pl.BlockSpec(memory_space=pltpu.HBM)] * 4,
-        out_specs=[here] * (4 + heads),
+        out_specs=[here] * (5 + heads),
         out_shape=[
             jax.ShapeDtypeStruct(key.shape, F32),
-            jax.ShapeDtypeStruct(beta.shape, F32),
-            jax.ShapeDtypeStruct((heads * chunks, C, 2 * C), F32),
-            jax.ShapeDtypeStruct((heads * chunks, C, 2 * C), F32),
+            jax.ShapeDtypeStruct((count, C), F32),
+            jax.ShapeDtypeStruct((count, C, C), F32),
+            jax.ShapeDtypeStruct((count, C, 2 * C), F32),
+            jax.ShapeDtypeStruct((count, C, 2 * C), F32),
             jax.ShapeDtypeStruct((C, 2 * C), F32),
         ]
         + [jax.ShapeDtypeStruct((C, 2 * C), BF16)] * (heads - 1),
@@ -207,6 +238,7 @@
             pltpu.VMEM(key.shape, BF16),
             pltpu.VMEM(key.shape, F32),
             pltpu.VMEM(beta.shape, F32),
+            pltpu.VMEM(beta.shape, F32),
             pltpu.VMEM((heads, C, 2 * C), F32),
             pltpu.SemaphoreType.DMA((4,)),
         ],
@@ -215,36 +247,35 @@
     )(*in_hbm(key, value, beta, log_decay))
 
 
-def rows_kernel(heads, mine, q_hbm, k32, log_ref, wu_ref, n_ref, out_ref, q16, q32, sems):
+def rows_kernel(heads, mine, q_hbm, k32, sums_ref, mix_ref, wu_ref, n_ref, out_ref, q16, q32, sems):
     fetch(((q_hbm, q16),), sems)
     q32[...] = q16[...].astype(F32)
-    chunks = log_ref.shape[1] // C
+    chunks = q16.shape[0] // (heads * C)
     row, col = iotas()
     eye = row == col
-    within = row >= col
     for j, head in enumerate(mine):
         for c in range(chunks):
+            i = head * chunks + c
             query, raw = q32[chunk_rows(heads, head, c), :], k32[chunk_rows(heads, head, c), :]
-            column, decay = decay_parts(tokens_of(log_ref, head, c), within, eye)
+            grown = to_column(jnp.exp(sums_ref[c * heads + head : c * heads + head + 1, :]), eye)
+            pairs = dot(query.astype(BF16), raw.astype(BF16), NT) * mix_ref[i]
+            both = dot3(split(pairs), split(wu_ref[i]))
             scale = inverse_scale(query)
-            pairs = dot(query.astype(BF16), raw.astype(BF16), NT)
-            pairs = pairs * decay * scale * to_row(inverse_scale(raw), eye)
-            both = dot3(split(pairs), split(wu_ref[head * chunks + c]))
-            reach = query * (scale * jnp.exp(column)) - both[:, :C]
-            fresh = both[:, C:]
+            reach = (query * grown - both[:, :C]) * scale
+            fresh = both[:, C:] * scale
             if c > 0:
-                earlier = dot3(split(reach), split(n_ref[head * chunks + c]))
+                earlier = dot3(split(reach), split(n_ref[i]))
                 reach = earlier[:, :C]
                 fresh = fresh + earlier[:, C:]
             out_ref[j, c * C : (c + 1) * C, :] = jnp.concatenate([reach, fresh], axis=1)
 
 
-def row_maps(mine, query, k32, log_decay, wu, states):
-    heads, tokens = log_decay.shape
+def row_maps(heads, mine, query, k32, sums, mix, wu, states):
+    tokens = query.shape[0] // heads
     here = pl.BlockSpec(memory_space=pltpu.VMEM)
     return pl.pallas_call(
         functools.partial(rows_kernel, heads, mine),
-        in_specs=[pl.BlockSpec(memory_space=pltpu.HBM)] + [here] * 4,
+        in_specs=[pl.BlockSpec(memory_space=pltpu.HBM)] + [here] * 5,
         out_specs=here,
         out_shape=jax.ShapeDtypeStruct((len(mine), tokens, 2 * C), F32),
         scratch_shapes=[
@@ -255,7 +286,7 @@
         compiler_params=pltpu.CompilerParams(vmem_limit_bytes=16 * MIB),
         cost_estimate=pl.CostEstimate(flops=2000000000, bytes_accessed=8000000, transcendentals=0),
         name="row_maps",
-    )(*in_hbm(query), k32, log_decay, wu, states)
+    )(*in_hbm(query), k32, sums, mix, wu, states)
 
 
 def small_call(kernel, out_shape, *args):
@@ -415,11 +446,11 @@
     count = lax.axis_size("seq")
     flat = lambda x: x.reshape(tokens * heads, C)
     weight2 = swap(out_weight, "head", 1)
-    k32, logs, wu, states, own, *sends = local_maps(flat(key), flat(value), beta, log_decay, 2)
-    got = [swap(x, "seq", r) for r, x in enumerate(sends, 1)]
+    k32, *chunk_maps, own, send1, send2, send3 = local_maps(flat(key), flat(value), beta, log_decay, 2)
+    got = [swap(x, "seq", r) for r, x in enumerate((send1, send2, send3), 1)]
     half = heads // 2
-    rows0 = row_maps(range(half), flat(query), k32, logs, wu, states)
-    rows1 = row_maps(range(half, heads), flat(query), k32, logs, wu, states)
+    rows0 = row_maps(heads, range(half), flat(query), k32, *chunk_maps)
+    rows1 = row_maps(heads, range(half, heads), flat(query), k32, *chunk_maps)
     rows0, got = lax.optimization_barrier((rows0, got))
     wide = jax.ShapeDtypeStruct((heads, C, 2 * C), F32)
     square = jax.ShapeDtypeStruct((C, C), BF16)
@@ -427,7 +458,6 @@
     if count == 2 * heads:
         held, state = small_call(group_state, [wide, square], own, *got)
         lower = swap(state, "seq", heads)
-        rows1, lower = lax.optimization_barrier((rows1, lower))
         keep, *sends = small_call(states_of_upper, outs, held, lower)
     else:
         total16 = jax.ShapeDtypeStruct((C, 2 * C), BF16)

time: 51 us -> 49.8 us (0.976)
  Pallas kernels: 18.5 us -> 17.7 us
    pallas_call x1, Pallas kernels: 8.73 us -> 8.02 us  [local_maps(): pl.pallas_call(functools.partial(local_maps_kernel, heads, batch), in_spe...]
  transfers between devices with their start and end apart: 10 -> 10, of which waited for: 7 -> 6; matrix products, arithmetic and copies ran while one was open for 0% -> 0% of each run, Pallas kernels for 35% -> 34%
where the time goes in v7:
time: 49.8 us; the launch traced here: 49.5 us
  waiting for transfers between devices  18.5 us (37%)
  Pallas kernels  17.7 us (36%)
  starting transfers between devices  12.4 us (25%)
  other arithmetic  0.9 us (2%)
    ppermute x10, waiting for transfers between devices, swap(): return lax.ppermute(x, axis, [(i, i ^ bit) for i in range(count)])  18.5 us
    ppermute x10, starting transfers between devices, swap(): return lax.ppermute(x, axis, [(i, i ^ bit) for i in range(count)])  12.4 us
    pallas_call x1, Pallas kernels, local_maps(): pl.pallas_call(functools.partial(local_maps_kernel, heads, batch), in_spe...  8.02 us
    pallas_call x2, Pallas kernels, row_maps(): pl.pallas_call(functools.partial(rows_kernel, heads, mine), in_specs=[pl....  5.38 us
    pallas_call x2, Pallas kernels, small_call(): pl.pallas_call(kernel, in_specs=[here] * len(args), out_specs=[here] * le...  1.65 us
    pallas_call x2, Pallas kernels, project(): pl.pallas_call(functools.partial(project_kernel, other), out_shape=jax.Sh...  1.44 us
    pallas_call x1, Pallas kernels, apply(): pl.pallas_call(functools.partial(apply_kernel, heads), grid=(groups,), in...  1.21 us
  transfers between devices with their start and end apart: 10, of which 6 were waited for; matrix products, arithmetic and copies ran while one was open for 0% of the time, Pallas kernels for 34%

profile of v7, /device:TPU:0, one launch (start us, length us, event | category | flops | bytes accessed | tf_op | source)
XLA Modules:
  0.0 49.5 jit_solution(1543413553231601792)
XLA Ops:
  0.0 0.5 collective-permute-start.8
  0.5 8.0 %local_maps.1 = (f32[2048,128]{1,0:T(8,128)S(1)}, f32[16,128]{1,0:T(8,128)S(1)}, f32[16,128,128]{2,1,0:T(8,128)S(1)}, f32[16,128,256]{2,1,0:T(8,128)S(1)}, f32[1...) custom-call(bf16[2048,128]{1,0:T(8,128)(2,1)} %bitcast.5, ...), custom_call_target="tpu_custom_call" | custom-call | tf_op jit(solution)/shard_map/local_maps/pallas_call | solution.py:223
  8.5 2.6 %collective-permute-start = (bf16[128,256]{1,0:T(8,128)(2,1)S(1)}, bf16[128,256]{1,0:T(8,128)(2,1)S(1)}, u32[]{:S(2)}, u32[]{:S(2)}) collective-permute-start(bf16[128,256]{1,0:T(8,128)(2,1)S(1)} %get-tuple-element.31), channel_id=1, source_target_pairs={{0,4},{4,0},{8,12},{12,8},{16,20},{20,16},{24,28},{28,24},{1,5},{5... | collective-permute-start | bytes 196616 | tf_op jit(solution)/shard_map/ppermute | solution.py:441
  11.0 1.6 %collective-permute-start.1 = (bf16[128,256]{1,0:T(8,128)(2,1)S(1)}, bf16[128,256]{1,0:T(8,128)(2,1)S(1)}, u32[]{:S(2)}, u32[]{:S(2)}) collective-permute-start(bf16[128,256]{1,0:T(8,128)(2,1)S(1)} %get-tuple-element.32), channel_id=1, source_target_pairs={{0,8},{4,12},{8,0},{12,4},{16,24},{20,28},{24,16},{28,20},{1,9},{5... | collective-permute-start | bytes 196616 | tf_op jit(solution)/shard_map/ppermute | solution.py:441
  12.6 2.7 %row_maps.2.rows0_ref = f32[2,512,256]{2,1,0:T(8,128)S(1)} custom-call(bf16[2048,128]{1,0:T(8,128)(2,1)} %bitcast.3, f32[2048,128]{1,0:T(8,128)S(1)} %get-tuple-element.26.k32, f32[16,128]{1,0:T(8,128)S(1)} %get-tuple-element.27.sums_ref, f32[16,128,128]{2,1,0:T(8,128)S(1)} %get-tuple-element.28.mix_ref, f32[16,128,256]{2,1,0:T(8,128)S(1)} %get-tuple-element.29.wu_ref, ...), custom_call_target="tpu_custom_call" | custom-call | flops 2000000000 | bytes 8000000 | tf_op jit(solution)/shard_map/row_maps/pallas_call | solution.py:276
  15.3 0.2 collective-permute-done.1.refs_1_
  15.5 2.2 %collective-permute-done.2.refs_2_ = bf16[128,256]{1,0:T(8,128)(2,1)S(1)} collective-permute-done((bf16[128,256]{1,0:T(8,128)(2,1)S(1)}, bf16[128,256]{1,0:T(8,128)(2,1)S(1)}, u32[]{:S(2)}, u32[]{:S(2)}) %collective-permute-start.2) | collective-permute-done | bytes 65568 | tf_op jit(solution)/shard_map/ppermute | solution.py:441
  17.8 0.5 %group_state.1 = (f32[4,128,256]{2,1,0:T(8,128)S(1)}, bf16[128,128]{1,0:T(8,128)(2,1)S(1)}) custom-call(f32[128,256]{1,0:T(8,128)S(1)} %get-tuple-element.35.own_ref, bf16[128,256]{1,0:T(8,128)(2,1)S(1)} %collective-permute-done.refs_0_, bf16[128,256]{1,0:T(8,128)(2,1)S(1)} %collective-permute-done.1.refs_1_, bf16[128,256]{1,0:T(8,128)(2,1)S(1)} %collective-permute-done.2.refs_2_), custom_call_target="tpu_custom_call" | custom-call | tf_op jit(solution)/shard_map/group_state/pallas_call | solution.py:294
  18.3 2.6 %collective-permute-start.3 = (bf16[128,128]{1,0:T(8,128)(2,1)S(1)}, bf16[128,128]{1,0:T(8,128)(2,1)S(1)}, u32[]{:S(2)}, u32[]{:S(2)}) collective-permute-start(bf16[128,128]{1,0:T(8,128)(2,1)S(1)} %get-tuple-element.40), channel_id=1, source_target_pairs={{0,16},{4,20},{8,24},{12,28},{16,0},{20,4},{24,8},{28,12},{1,17},{... | collective-permute-start | bytes 98312 | tf_op jit(solution)/shard_map/ppermute | solution.py:441
  20.9 2.5 %collective-permute-done.3.lower_ref = bf16[128,128]{1,0:T(8,128)(2,1)S(1)} collective-permute-done((bf16[128,128]{1,0:T(8,128)(2,1)S(1)}, bf16[128,128]{1,0:T(8,128)(2,1)S(1)}, u32[]{:S(2)}, u32[]{:S(2)}) %collective-permute-start.3) | collective-permute-done | bytes 32800 | tf_op jit(solution)/shard_map/ppermute | solution.py:441
  23.4 1.1 %states_of_upper.1 = (bf16[128,128]{1,0:T(8,128)(2,1)S(1)}, bf16[128,128]{1,0:T(8,128)(2,1)S(1)}, bf16[128,128]{1,0:T(8,128)(2,1)S(1)}, bf16[128,128]{1,0:T(8,128)(2,1)S(1)}, bf16[4,128,128]{2,1,0:T(8,128)(2,1)}) custom-call(f32[4,128,256]{2,1,0:T(8,128)S(1)} %get-tuple-element.39.held, bf16[128,128]{1,0:T(8,128)(2,1)S(1)} %collective-permute-done.3.lower_ref), custom_call_target="tpu_custom_call" | custom-call | tf_op jit(solution)/shard_map/states_of_upper/pallas_call | solution.py:294
  24.6 0.3 collective-permute-start.4
  24.8 1.4 %collective-permute-start.5 = (bf16[128,128]{1,0:T(8,128)(2,1)S(1)}, bf16[128,128]{1,0:T(8,128)(2,1)S(1)}, u32[]{:S(2)}, u32[]{:S(2)}) collective-permute-start(bf16[128,128]{1,0:T(8,128)(2,1)S(1)} %get-tuple-element.43), channel_id=1, source_target_pairs={{0,8},{4,12},{8,0},{12,4},{16,24},{20,28},{24,16},{28,20},{1,9},{5... | collective-permute-start | bytes 98312 | tf_op jit(solution)/shard_map/ppermute | solution.py:441
  26.2 1.8 %collective-permute-start.6 = (bf16[128,128]{1,0:T(8,128)(2,1)S(1)}, bf16[128,128]{1,0:T(8,128)(2,1)S(1)}, u32[]{:S(2)}, u32[]{:S(2)}) collective-permute-start(bf16[128,128]{1,0:T(8,128)(2,1)S(1)} %get-tuple-element.44), channel_id=1, source_target_pairs={{0,12},{4,8},{8,4},{12,0},{16,28},{20,24},{24,20},{28,16},{1,13},{... | collective-permute-start | bytes 98312 | tf_op jit(solution)/shard_map/ppermute | solution.py:441
  28.1 2.7 %row_maps.3.rows1_ref = f32[2,512,256]{2,1,0:T(8,128)S(1)} custom-call(bf16[2048,128]{1,0:T(8,128)(2,1)} %bitcast.4, f32[2048,128]{1,0:T(8,128)S(1)} %get-tuple-element.26.k32, f32[16,128]{1,0:T(8,128)S(1)} %get-tuple-element.27.sums_ref, f32[16,128,128]{2,1,0:T(8,128)S(1)} %get-tuple-element.28.mix_ref, f32[16,128,256]{2,1,0:T(8,128)S(1)} %get-tuple-element.29.wu_ref, ...), custom_call_target="tpu_custom_call" | custom-call | flops 2000000000 | bytes 8000000 | tf_op jit(solution)/shard_map/row_maps/pallas_call | solution.py:276
  30.8 0.3 collective-permute-done.6.refs_3_
  31.1 1.2 %apply.1 = (bf16[2,128,512]{2,1,0:T(8,128)(2,1)S(1)}, bf16[2,128,512]{2,1,0:T(8,128)(2,1)S(1)}) custom-call(f32[2,512,256]{2,1,0:T(8,128)S(1)} %row_maps.2.rows0_ref, f32[2,512,256]{2,1,0:T(8,128)S(1)} %row_maps.3.rows1_ref, bf16[128,128]{1,0:T(8,128)(2,1)S(1)} %get-tuple-element.41.refs_0_, bf16[128,128]{1,0:T(8,128)(2,1)S(1)} %collective-permute-done.4.refs_1_, ...), custom_call_target="tpu_custom_call" | custom-call | tf_op jit(solution)/shard_map/apply/pallas_call | solution.py:406
  32.3 0.1 collective-permute-start.7
  32.3 1.5 %collective-permute-done.7.got_ref = bf16[2,128,512]{2,1,0:T(8,128)(2,1)S(1)} collective-permute-done((bf16[2,128,512]{2,1,0:T(8,128)(2,1)S(1)}, bf16[2,128,512]{2,1,0:T(8,128)(2,1)S(1)}, u32[]{:S(2)}, u32[]{:S(2)}) %collective-permute-start.7) | collective-permute-done | bytes 262176 | tf_op jit(solution)/shard_map/ppermute | solution.py:441
  33.9 0.7 %project.3 = bf16[128,2048]{1,0:T(8,128)(2,1)S(1)} custom-call(bf16[2,128,512]{2,1,0:T(8,128)(2,1)S(1)} %get-tuple-element.45.keep_ref, bf16[2,128,512]{2,1,0:T(8,128)(2,1)S(1)} %collective-permute-done.7.got_ref, bf16[512,2048]{1,0:T(8,128)(2,1)S(1)} %copy-done, bf16[512,2048]{1,0:T(8,128)(2,1)S(1)} %collective-permute-done.8.w2_ref), custom_call_target="tpu_custom_call" | custom-call | flops 536870912 | bytes 4194304 | tf_op jit(solution)/shard_map/project/pallas_call | solution.py:428
  34.6 1.6 %collective-permute-start.9 = (bf16[128,2048]{1,0:T(8,128)(2,1)S(1)}, bf16[128,2048]{1,0:T(8,128)(2,1)S(1)}, u32[]{:S(2)}, u32[]{:S(2)}) collective-permute-start(bf16[128,2048]{1,0:T(8,128)(2,1)S(1)} %project.3), channel_id=1, source_target_pairs={{0,2},{1,3},{2,0},{3,1},{4,6},{5,7},{6,4},{7,5},{8,10},{9,11},{10,... | collective-permute-start | bytes 1572872 | tf_op jit(solution)/shard_map/ppermute | solution.py:441
  36.2 0.7 %project.2 = f32[128,2048]{1,0:T(8,128)S(1)} custom-call(bf16[2,128,512]{2,1,0:T(8,128)(2,1)S(1)} %get-tuple-element.45.keep_ref, bf16[2,128,512]{2,1,0:T(8,128)(2,1)S(1)} %collective-permute-done.7.got_ref, bf16[512,2048]{1,0:T(8,128)(2,1)S(1)} %copy-done, bf16[512,2048]{1,0:T(8,128)(2,1)S(1)} %collective-permute-done.8.w2_ref), custom_call_target="tpu_custom_call" | custom-call | flops 536870912 | bytes 4194304 | tf_op jit(solution)/shard_map/project/pallas_call | solution.py:428
  36.9 11.7 %collective-permute-done.9 = bf16[128,2048]{1,0:T(8,128)(2,1)S(1)} collective-permute-done((bf16[128,2048]{1,0:T(8,128)(2,1)S(1)}, bf16[128,2048]{1,0:T(8,128)(2,1)S(1)}, u32[]{:S(2)}, u32[]{:S(2)}) %collective-permute-start.9) | collective-permute-done | bytes 524320 | tf_op jit(solution)/shard_map/ppermute | solution.py:441
  48.6 0.9 %add_convert_fusion = bf16[128,2048]{1,0:T(8,128)(2,1)} fusion(f32[128,2048]{1,0:T(8,128)S(1)} %project.2, bf16[128,2048]{1,0:T(8,128)(2,1)S(1)} %collective-permute-done.9), kind=kLoop, calls=%fused_computation | loop fusion | flops 786432 | bytes 2097152 | tf_op jit(solution)/shard_map/convert_element_type | solution.py:471
  (7 shorter events, 0.0 us)
Async XLA Ops:
  0.0 33.9 %collective-permute-start.8 = (bf16[512,2048]{1,0:T(8,128)(2,1)}, bf16[512,2048]{1,0:T(8,128)(2,1)S(1)}, u32[]{:S(2)}, u32[]{:S(2)}) collective-permute-start(bf16[512,2048]{1,0:T(8,128)(2,1)} %w_ref.3), channel_id=1, source_target_pairs={{0,1},{1,0},{2,3},{3,2},{4,5},{5,4},{6,7},{7,6},{8,9},{9,8},{10,11... | collective-permute-start | bytes 6291464 | tf_op jit(solution)/shard_map/ppermute | solution.py:441
  8.5 6.8 %collective-permute-start = (bf16[128,256]{1,0:T(8,128)(2,1)S(1)}, bf16[128,256]{1,0:T(8,128)(2,1)S(1)}, u32[]{:S(2)}, u32[]{:S(2)}) collective-permute-start(bf16[128,256]{1,0:T(8,128)(2,1)S(1)} %get-tuple-element.31), channel_id=1, source_target_pairs={{0,4},{4,0},{8,12},{12,8},{16,20},{20,16},{24,28},{28,24},{1,5},{5... | collective-permute-start | bytes 196616 | tf_op jit(solution)/shard_map/ppermute | solution.py:441
  11.0 4.5 %collective-permute-start.1 = (bf16[128,256]{1,0:T(8,128)(2,1)S(1)}, bf16[128,256]{1,0:T(8,128)(2,1)S(1)}, u32[]{:S(2)}, u32[]{:S(2)}) collective-permute-start(bf16[128,256]{1,0:T(8,128)(2,1)S(1)} %get-tuple-element.32), channel_id=1, source_target_pairs={{0,8},{4,12},{8,0},{12,4},{16,24},{20,28},{24,16},{28,20},{1,9},{5... | collective-permute-start | bytes 196616 | tf_op jit(solution)/shard_map/ppermute | solution.py:441
  12.6 5.2 %collective-permute-start.2 = (bf16[128,256]{1,0:T(8,128)(2,1)S(1)}, bf16[128,256]{1,0:T(8,128)(2,1)S(1)}, u32[]{:S(2)}, u32[]{:S(2)}) collective-permute-start(bf16[128,256]{1,0:T(8,128)(2,1)S(1)} %get-tuple-element.33), channel_id=1, source_target_pairs={{0,12},{4,8},{8,4},{12,0},{16,28},{20,24},{24,20},{28,16},{1,13},{... | collective-permute-start | bytes 196616 | tf_op jit(solution)/shard_map/ppermute | solution.py:441
  18.3 5.1 %collective-permute-start.3 = (bf16[128,128]{1,0:T(8,128)(2,1)S(1)}, bf16[128,128]{1,0:T(8,128)(2,1)S(1)}, u32[]{:S(2)}, u32[]{:S(2)}) collective-permute-start(bf16[128,128]{1,0:T(8,128)(2,1)S(1)} %get-tuple-element.40), channel_id=1, source_target_pairs={{0,16},{4,20},{8,24},{12,28},{16,0},{20,4},{24,8},{28,12},{1,17},{... | collective-permute-start | bytes 98312 | tf_op jit(solution)/shard_map/ppermute | solution.py:441
  24.6 6.2 %collective-permute-start.4 = (bf16[128,128]{1,0:T(8,128)(2,1)S(1)}, bf16[128,128]{1,0:T(8,128)(2,1)S(1)}, u32[]{:S(2)}, u32[]{:S(2)}) collective-permute-start(bf16[128,128]{1,0:T(8,128)(2,1)S(1)} %get-tuple-element.42), channel_id=1, source_target_pairs={{0,4},{4,0},{8,12},{12,8},{16,20},{20,16},{24,28},{28,24},{1,5},{5... | collective-permute-start | bytes 98312 | tf_op jit(solution)/shard_map/ppermute | solution.py:441
  24.8 5.9 %collective-permute-start.5 = (bf16[128,128]{1,0:T(8,128)(2,1)S(1)}, bf16[128,128]{1,0:T(8,128)(2,1)S(1)}, u32[]{:S(2)}, u32[]{:S(2)}) collective-permute-start(bf16[128,128]{1,0:T(8,128)(2,1)S(1)} %get-tuple-element.43), channel_id=1, source_target_pairs={{0,8},{4,12},{8,0},{12,4},{16,24},{20,28},{24,16},{28,20},{1,9},{5... | collective-permute-start | bytes 98312 | tf_op jit(solution)/shard_map/ppermute | solution.py:441
  26.2 4.8 %collective-permute-start.6 = (bf16[128,128]{1,0:T(8,128)(2,1)S(1)}, bf16[128,128]{1,0:T(8,128)(2,1)S(1)}, u32[]{:S(2)}, u32[]{:S(2)}) collective-permute-start(bf16[128,128]{1,0:T(8,128)(2,1)S(1)} %get-tuple-element.44), channel_id=1, source_target_pairs={{0,12},{4,8},{8,4},{12,0},{16,28},{20,24},{24,20},{28,16},{1,13},{... | collective-permute-start | bytes 98312 | tf_op jit(solution)/shard_map/ppermute | solution.py:441
  30.8 3.1 %copy-start = (bf16[512,2048]{1,0:T(8,128)(2,1)S(1)}, bf16[512,2048]{1,0:T(8,128)(2,1)}, u32[]{:S(2)}) copy-start(bf16[512,2048]{1,0:T(8,128)(2,1)} %w_ref.3) | copy-start | bytes 6291460
  32.3 1.6 %collective-permute-start.7 = (bf16[2,128,512]{2,1,0:T(8,128)(2,1)S(1)}, bf16[2,128,512]{2,1,0:T(8,128)(2,1)S(1)}, u32[]{:S(2)}, u32[]{:S(2)}) collective-permute-start(bf16[2,128,512]{2,1,0:T(8,128)(2,1)S(1)} %get-tuple-element.46), channel_id=1, source_target_pairs={{0,1},{1,0},{2,3},{3,2},{4,5},{5,4},{6,7},{7,6},{8,9},{9,8},{10,11... | collective-permute-start | bytes 786440 | tf_op jit(solution)/shard_map/ppermute | solution.py:441
  34.6 14.0 %collective-permute-start.9 = (bf16[128,2048]{1,0:T(8,128)(2,1)S(1)}, bf16[128,2048]{1,0:T(8,128)(2,1)S(1)}, u32[]{:S(2)}, u32[]{:S(2)}) collective-permute-start(bf16[128,2048]{1,0:T(8,128)(2,1)S(1)} %project.3), channel_id=1, source_target_pairs={{0,2},{1,3},{2,0},{3,1},{4,6},{5,7},{6,4},{7,5},{8,10},{9,11},{10,... | collective-permute-start | bytes 1572872 | tf_op jit(solution)/shard_map/ppermute | solution.py:441

commit v8 on v7

--- a/solution.py
+++ b/solution.py
@@ -123,10 +123,11 @@
     return found
 
 
-def fetch(pairs, sems):
+def fetch(pairs, sems, late):
     copies = [pltpu.make_async_copy(x, y, sems.at[i]) for i, (x, y) in enumerate(pairs)]
     for copy in copies:
         copy.start()
+    late.start()
     for copy in copies:
         copy.wait()
 
@@ -147,9 +148,10 @@
     return jnp.concatenate([ref[:, i : i + C] for i in range(0, ref.shape[1], C)], axis=0)
 
 
-def local_maps_kernel(heads, batch, k_hbm, v_hbm, beta_hbm, log_hbm, k32, sums_ref, mix_ref, wu_ref, n_ref, own_ref, *rest):
+def local_maps_kernel(heads, batch, k_hbm, v_hbm, beta_hbm, log_hbm, q_hbm, q16, k32, sums_ref, mix_ref, wu_ref, n_ref, own_ref, *rest):
     sends, (k16, v16, v32, beta_ref, log_ref, all_ref, sems) = rest[: heads - 1], rest[heads - 1 :]
-    fetch(((k_hbm, k16), (log_hbm, log_ref), (beta_hbm, beta_ref), (v_hbm, v16)), sems)
+    late = pltpu.make_async_copy(q_hbm, q16, sems.at[4])
+    fetch(((k_hbm, k16), (log_hbm, log_ref), (beta_hbm, beta_ref), (v_hbm, v16)), sems, late)
     k32[...] = k16[...].astype(F32)
     v32[...] = v16[...].astype(F32)
     chunks = beta_ref.shape[1] // C
@@ -207,6 +209,7 @@
     own_ref[...] = all_ref[place]
     for r in range(1, heads):
         sends[r - 1][...] = all_ref[other_place(place, r, heads)].astype(BF16)
+    late.wait()
 
 
 def other_place(place, r, heads):
@@ -216,15 +219,16 @@
     return result
 
 
-def local_maps(key, value, beta, log_decay, batch):
+def local_maps(key, value, beta, log_decay, query, batch):
     heads, tokens = beta.shape
     count = heads * (tokens // C)
     here = pl.BlockSpec(memory_space=pltpu.VMEM)
     return pl.pallas_call(
         functools.partial(local_maps_kernel, heads, batch),
-        in_specs=[pl.BlockSpec(memory_space=pltpu.HBM)] * 4,
-        out_specs=[here] * (5 + heads),
+        in_specs=[pl.BlockSpec(memory_space=pltpu.HBM)] * 5,
+        out_specs=[here] * (6 + heads),
         out_shape=[
+            jax.ShapeDtypeStruct(query.shape, BF16),
             jax.ShapeDtypeStruct(key.shape, F32),
             jax.ShapeDtypeStruct((count, C), F32),
             jax.ShapeDtypeStruct((count, C, C), F32),
@@ -240,15 +244,14 @@
             pltpu.VMEM(beta.shape, F32),
             pltpu.VMEM(beta.shape, F32),
             pltpu.VMEM((heads, C, 2 * C), F32),
-            pltpu.SemaphoreType.DMA((4,)),
+            pltpu.SemaphoreType.DMA((5,)),
         ],
         compiler_params=pltpu.CompilerParams(vmem_limit_bytes=32 * MIB),
         name="local_maps",
-    )(*in_hbm(key, value, beta, log_decay))
-
-
-def rows_kernel(heads, mine, q_hbm, k32, sums_ref, mix_ref, wu_ref, n_ref, out_ref, q16, q32, sems):
-    fetch(((q_hbm, q16),), sems)
+    )(*in_hbm(key, value, beta, log_decay, query))
+
+
+def rows_kernel(heads, mine, q16, k32, sums_ref, mix_ref, wu_ref, n_ref, out_ref, q32):
     q32[...] = q16[...].astype(F32)
     chunks = q16.shape[0] // (heads * C)
     row, col = iotas()
@@ -275,18 +278,14 @@
     here = pl.BlockSpec(memory_space=pltpu.VMEM)
     return pl.pallas_call(
         functools.partial(rows_kernel, heads, mine),
-        in_specs=[pl.BlockSpec(memory_space=pltpu.HBM)] + [here] * 5,
+        in_specs=[here] * 6,
         out_specs=here,
         out_shape=jax.ShapeDtypeStruct((len(mine), tokens, 2 * C), F32),
-        scratch_shapes=[
-            pltpu.VMEM(query.shape, BF16),
-            pltpu.VMEM(query.shape, F32),
-            pltpu.SemaphoreType.DMA((1,)),
-        ],
+        scratch_shapes=[pltpu.VMEM(query.shape, F32)],
         compiler_params=pltpu.CompilerParams(vmem_limit_bytes=16 * MIB),
         cost_estimate=pl.CostEstimate(flops=2000000000, bytes_accessed=8000000, transcendentals=0),
         name="row_maps",
-    )(*in_hbm(query), k32, sums, mix, wu, states)
+    )(query, k32, sums, mix, wu, states)
 
 
 def small_call(kernel, out_shape, *args):
@@ -324,37 +323,44 @@
     out_ref[...] = state
 
 
-def group_total(own_ref, *refs):
-    got_refs, (held, out_ref) = refs[:-2], refs[-2:]
-    in_order(own_ref, got_refs, held)
-    total = held[0]
-    for i in range(1, held.shape[0]):
+def group_prefix(held, high_ref, low_ref, added_ref, total_ref):
+    row, col = iotas()
+    eye = jnp.where(row == col, 1.0, 0.0)
+    total = jnp.concatenate([eye, jnp.zeros((C, C), F32)], axis=1)
+    for i in range(held.shape[0]):
+        high_ref[i], low_ref[i] = split(total[:, :C])
+        added_ref[i] = total[:, C:]
         later = held[i]
-        total = dot3(split(later[:, :C]), split(total))
-        total = jnp.concatenate([total[:, :C], total[:, C:] + later[:, C:]], axis=1)
-    out_ref[...] = total.astype(BF16)
-
-
-def group_states(held, state, keep_ref, send_refs, states):
-    heads = held.shape[0]
+        if i == 0:
+            total = later
+        else:
+            total = dot3(split(later[:, :C]), split(total))
+            total = jnp.concatenate([total[:, :C], total[:, C:] + later[:, C:]], axis=1)
+    total_ref[...] = total.astype(BF16)
+
+
+def group_states(upper_only, high_ref, low_ref, added_ref, state_ref, keep_ref, *refs):
+    sends, states = refs[:-1], refs[-1]
+    heads = added_ref.shape[0]
+    state = state_ref[...]
+    if upper_only:
+        state = jnp.where(lax.axis_index("seq") < heads, jnp.zeros_like(state), state)
+    both = twice(state)
     for i in range(heads):
-        states[i] = state
-        if i + 1 < heads:
-            state = moved_on(held[i, :, :C], state, held[i, :, C:]).astype(BF16)
+        maps = jnp.concatenate([high_ref[i], low_ref[i]], axis=1)
+        states[i] = (dot(maps, both) + added_ref[i]).astype(BF16)
     place = lax.rem(lax.axis_index("seq"), heads)
     keep_ref[...] = states[place]
-    for r, send in enumerate(send_refs, 1):
+    for r, send in enumerate(sends, 1):
         send[...] = states[other_place(place, r, heads)]
 
 
-def states_of_upper(held, lower_ref, keep_ref, *refs):
-    lower = lower_ref[...]
-    state = jnp.where(lax.axis_index("seq") < held.shape[0], jnp.zeros_like(lower), lower)
-    group_states(held, state, keep_ref, refs[:-1], refs[-1])
-
-
-def states_given(held, state_ref, keep_ref, *refs):
-    group_states(held, state_ref[...], keep_ref, refs[:-1], refs[-1])
+def states_of_upper(*refs):
+    group_states(True, *refs)
+
+
+def states_given(*refs):
+    group_states(False, *refs)
 
 
 def prefix(total, heads):
@@ -371,47 +377,36 @@
     return lax.fori_loop(0, count // heads - 1, step, start).astype(BF16)
 
 
-def apply_kernel(heads, rows0_ref, rows1_ref, *refs):
-    states, (keep_ref, send_ref, held) = refs[:heads], refs[heads:]
-    step = pl.program_id(0)
-
-    @pl.when(step == 0)
-    def _():
-        place = lax.rem(lax.axis_index("seq"), heads)
-        for r in range(heads):
-            held[other_place(place, r, heads)] = states[r][...]
-
-    attended = []
-    for h in range(heads):
-        rows_ref = (rows0_ref, rows1_ref)[h // (heads // 2)]
-        reach, fresh = rows_ref[h % (heads // 2), :, :C], rows_ref[h % (heads // 2), :, C:]
-        attended.append(moved_on(reach, held[h], fresh).astype(BF16))
-    attended = jnp.concatenate(attended, axis=1)
-    mine = lax.rem(step, 2) == lax.rem(lax.axis_index("head"), 2)
-
-    @pl.when(mine)
-    def _():
-        keep_ref[step // 2] = attended
-
-    @pl.when(jnp.logical_not(mine))
-    def _():
-        send_ref[step // 2] = attended
+def apply_kernel(groups, rows0_ref, rows1_ref, *refs):
+    states, (keep_ref, send_ref, held) = refs[:-3], refs[-3:]
+    heads = len(states)
+    half, tokens, _ = rows0_ref.shape
+    block = tokens // groups
+    place = lax.rem(lax.axis_index("seq"), heads)
+    for r in range(heads):
+        held[other_place(place, r, heads)] = states[r][...]
+    core = lax.rem(lax.axis_index("head"), 2)
+    for out_ref, parity in ((send_ref, 1 - core), (keep_ref, core)):
+        for i in range(groups // 2):
+            rows = pl.ds(pl.multiple_of((2 * i + parity) * block, block), block)
+            for h in range(heads):
+                ref = (rows0_ref, rows1_ref)[h // half]
+                attended = moved_on(ref[h % half, rows, :C], held[h], ref[h % half, rows, C:])
+                out_ref[i, :, h * C : (h + 1) * C] = attended.astype(BF16)
 
 
 def apply(rows, states, groups):
     _, tokens, _ = rows[0].shape
     heads = len(states)
-    block = tokens // groups
-    out = jax.ShapeDtypeStruct((groups // 2, block, heads * C), BF16)
+    here = pl.BlockSpec(memory_space=pltpu.VMEM)
+    out = jax.ShapeDtypeStruct((groups // 2, tokens // groups, heads * C), BF16)
     return pl.pallas_call(
-        functools.partial(apply_kernel, heads),
-        grid=(groups,),
-        in_specs=[pl.BlockSpec((heads // 2, block, 2 * C), lambda i: (0, i, 0))] * 2
-        + [pl.BlockSpec((C, C), lambda i: (0, 0))] * heads,
-        out_specs=[pl.BlockSpec(out.shape, lambda i: (0, 0, 0))] * 2,
+        functools.partial(apply_kernel, groups),
+        in_specs=[here] * (2 + heads),
+        out_specs=[here] * 2,
         out_shape=[out, out],
         scratch_shapes=[pltpu.VMEM((heads, C, C), BF16)],
-        compiler_params=pltpu.CompilerParams(vmem_limit_bytes=14 * MIB),
+        compiler_params=pltpu.CompilerParams(vmem_limit_bytes=8 * MIB),
         name="apply",
     )(*rows, *states)
 
@@ -446,23 +441,29 @@
     count = lax.axis_size("seq")
     flat = lambda x: x.reshape(tokens * heads, C)
     weight2 = swap(out_weight, "head", 1)
-    k32, *chunk_maps, own, send1, send2, send3 = local_maps(flat(key), flat(value), beta, log_decay, 2)
+    q16, k32, *chunk_maps, own, send1, send2, send3 = local_maps(
+        flat(key), flat(value), beta, log_decay, flat(query), heads
+    )
     got = [swap(x, "seq", r) for r, x in enumerate((send1, send2, send3), 1)]
     half = heads // 2
-    rows0 = row_maps(heads, range(half), flat(query), k32, *chunk_maps)
-    rows1 = row_maps(heads, range(half, heads), flat(query), k32, *chunk_maps)
+    rows0 = row_maps(heads, range(half), q16, k32, *chunk_maps)
+    rows1 = row_maps(heads, range(half, heads), q16, k32, *chunk_maps)
     rows0, got = lax.optimization_barrier((rows0, got))
     wide = jax.ShapeDtypeStruct((heads, C, 2 * C), F32)
     square = jax.ShapeDtypeStruct((C, C), BF16)
-    outs = [square] * heads + [jax.ShapeDtypeStruct((heads, C, C), BF16)]
+    squares = jax.ShapeDtypeStruct((heads, C, C), BF16)
+    added = jax.ShapeDtypeStruct((heads, C, C), F32)
+    held, state = small_call(group_state, [wide, square], own, *got)
+    *maps, total = small_call(
+        group_prefix, [squares, squares, added, jax.ShapeDtypeStruct((C, 2 * C), BF16)], held
+    )
+    outs = [square] * heads + [squares]
     if count == 2 * heads:
-        held, state = small_call(group_state, [wide, square], own, *got)
         lower = swap(state, "seq", heads)
-        keep, *sends = small_call(states_of_upper, outs, held, lower)
+        maps, lower = lax.optimization_barrier((maps, lower))
+        keep, *sends = small_call(states_of_upper, outs, *maps, lower)
     else:
-        total16 = jax.ShapeDtypeStruct((C, 2 * C), BF16)
-        held, total = small_call(group_total, [wide, total16], own, *got)
-        keep, *sends = small_call(states_given, outs, held, prefix(total, heads))
+        keep, *sends = small_call(states_given, outs, *maps, prefix(total, heads))
     entering = [keep] + [swap(x, "seq", r) for r, x in enumerate(sends[: heads - 1], 1)]
     keep, away = apply((rows0, rows1), entering, lax.axis_size("head"))
     got = swap(away, "head", 1)

time: 49.8 us -> 47.8 us (0.960)
  Pallas kernels: 17.7 us -> 14.9 us
  waiting for transfers between devices: 18.5 us -> 19.4 us
    pallas_call x3, Pallas kernels: 6.58 us -> 3.71 us  [the longest x2 3.26 us: row_maps(): pl.pallas_call(functools.partial(rows_kernel, heads, mine), in_specs=[her...]
    pallas_call x2 -> x3, Pallas kernels: 1.65 us -> 2.6 us  [small_call(): pl.pallas_call(kernel, in_specs=[here] * len(args), out_specs=[here] * le...]
    ppermute x10, waiting for transfers between devices: 18.5 us -> 19.4 us  [swap(): return lax.ppermute(x, axis, [(i, i ^ bit) for i in range(count)])]
    pallas_call x1, Pallas kernels: 8.02 us -> 7.12 us  [local_maps(): pl.pallas_call(functools.partial(local_maps_kernel, heads, batch), in_spe...]
  transfers between devices with their start and end apart: 10 -> 10, of which waited for: 6 -> 6; matrix products, arithmetic and copies ran while one was open for 0% -> 0% of each run, Pallas kernels for 34% -> 30%
where the time goes in v8:
time: 47.8 us; the launch traced here: 47.6 us
  waiting for transfers between devices  19.4 us (41%)
  Pallas kernels  14.9 us (31%)
  starting transfers between devices  12.4 us (26%)
  other arithmetic  0.9 us (2%)
    ppermute x10, waiting for transfers between devices, swap(): return lax.ppermute(x, axis, [(i, i ^ bit) for i in range(count)])  19.4 us
    ppermute x10, starting transfers between devices, swap(): return lax.ppermute(x, axis, [(i, i ^ bit) for i in range(count)])  12.4 us
    pallas_call x1, Pallas kernels, local_maps(): pl.pallas_call(functools.partial(local_maps_kernel, heads, batch), in_spe...  7.12 us
    pallas_call x2, Pallas kernels, row_maps(): pl.pallas_call(functools.partial(rows_kernel, heads, mine), in_specs=[her...  3.26 us
    pallas_call x3, Pallas kernels, small_call(): pl.pallas_call(kernel, in_specs=[here] * len(args), out_specs=[here] * le...  2.6 us
    pallas_call x2, Pallas kernels, project(): pl.pallas_call(functools.partial(project_kernel, other), out_shape=jax.Sh...  1.43 us
  transfers between devices with their start and end apart: 10, of which 6 were waited for; matrix products, arithmetic and copies ran while one was open for 0% of the time, Pallas kernels for 30%

profile of v8, /device:TPU:0, one launch (start us, length us, event | category | flops | bytes accessed | tf_op | source)
XLA Modules:
  0.0 47.6 jit_solution(8663986610162280575)
XLA Ops:
  0.0 0.5 collective-permute-start.8
  0.5 7.1 %local_maps.1 = (bf16[2048,128]{1,0:T(8,128)(2,1)S(1)}, f32[2048,128]{1,0:T(8,128)S(1)}, f32[16,128]{1,0:T(8,128)S(1)}, f32[16,128,128]{2,1,0:T(8,128)S(1)}, f32...) custom-call(bf16[2048,128]{1,0:T(8,128)(2,1)} %bitcast.3, ...), custom_call_target="tpu_custom_call" | custom-call | tf_op jit(solution)/shard_map/local_maps/pallas_call | solution.py:226
  7.6 2.6 %collective-permute-start = (bf16[128,256]{1,0:T(8,128)(2,1)S(1)}, bf16[128,256]{1,0:T(8,128)(2,1)S(1)}, u32[]{:S(2)}, u32[]{:S(2)}) collective-permute-start(bf16[128,256]{1,0:T(8,128)(2,1)S(1)} %get-tuple-element.40), channel_id=1, source_target_pairs={{0,4},{4,0},{8,12},{12,8},{16,20},{20,16},{24,28},{28,24},{1,5},{5... | collective-permute-start | bytes 196616 | tf_op jit(solution)/shard_map/ppermute | solution.py:436
  10.1 1.6 %collective-permute-start.1 = (bf16[128,256]{1,0:T(8,128)(2,1)S(1)}, bf16[128,256]{1,0:T(8,128)(2,1)S(1)}, u32[]{:S(2)}, u32[]{:S(2)}) collective-permute-start(bf16[128,256]{1,0:T(8,128)(2,1)S(1)} %get-tuple-element.41), channel_id=1, source_target_pairs={{0,8},{4,12},{8,0},{12,4},{16,24},{20,28},{24,16},{28,20},{1,9},{5... | collective-permute-start | bytes 196616 | tf_op jit(solution)/shard_map/ppermute | solution.py:436
  11.7 1.6 %row_maps.2.rows0_ref = f32[2,512,256]{2,1,0:T(8,128)S(1)} custom-call(bf16[2048,128]{1,0:T(8,128)(2,1)S(1)} %get-tuple-element.34.q16, f32[2048,128]{1,0:T(8,128)S(1)} %get-tuple-element.35.k32, f32[16,128]{1,0:T(8,128)S(1)} %get-tuple-element.36.sums_ref, f32[16,128,128]{2,1,0:T(8,128)S(1)} %get-tuple-element.37.mix_ref, ...), custom_call_target="tpu_custom_call" | custom-call | flops 2000000000 | bytes 8000000 | tf_op jit(solution)/shard_map/row_maps/pallas_call | solution.py:279
  13.4 1.3 %collective-permute-done.1.refs_1_ = bf16[128,256]{1,0:T(8,128)(2,1)S(1)} collective-permute-done((bf16[128,256]{1,0:T(8,128)(2,1)S(1)}, bf16[128,256]{1,0:T(8,128)(2,1)S(1)}, u32[]{:S(2)}, u32[]{:S(2)}) %collective-permute-start.1) | collective-permute-done | bytes 65568 | tf_op jit(solution)/shard_map/ppermute | solution.py:436
  14.6 2.2 %collective-permute-done.2.refs_2_ = bf16[128,256]{1,0:T(8,128)(2,1)S(1)} collective-permute-done((bf16[128,256]{1,0:T(8,128)(2,1)S(1)}, bf16[128,256]{1,0:T(8,128)(2,1)S(1)}, u32[]{:S(2)}, u32[]{:S(2)}) %collective-permute-start.2) | collective-permute-done | bytes 65568 | tf_op jit(solution)/shard_map/ppermute | solution.py:436
  16.9 0.5 %group_state.1 = (f32[4,128,256]{2,1,0:T(8,128)S(1)}, bf16[128,128]{1,0:T(8,128)(2,1)S(1)}) custom-call(f32[128,256]{1,0:T(8,128)S(1)} %get-tuple-element.44.own_ref, bf16[128,256]{1,0:T(8,128)(2,1)S(1)} %collective-permute-done.refs_0_, bf16[128,256]{1,0:T(8,128)(2,1)S(1)} %collective-permute-done.1.refs_1_, bf16[128,256]{1,0:T(8,128)(2,1)S(1)} %collective-permute-done.2.refs_2_), custom_call_target="tpu_custom_call" | custom-call | tf_op jit(solution)/shard_map/group_state/pallas_call | solution.py:293
  17.4 2.7 %collective-permute-start.3 = (bf16[128,128]{1,0:T(8,128)(2,1)S(1)}, bf16[128,128]{1,0:T(8,128)(2,1)S(1)}, u32[]{:S(2)}, u32[]{:S(2)}) collective-permute-start(bf16[128,128]{1,0:T(8,128)(2,1)S(1)} %get-tuple-element.52), channel_id=1, source_target_pairs={{0,16},{4,20},{8,24},{12,28},{16,0},{20,4},{24,8},{28,12},{1,17},{... | collective-permute-start | bytes 98312 | tf_op jit(solution)/shard_map/ppermute | solution.py:436
  20.0 1.2 %group_prefix.1 = (bf16[4,128,128]{2,1,0:T(8,128)(2,1)S(1)}, bf16[4,128,128]{2,1,0:T(8,128)(2,1)S(1)}, f32[4,128,128]{2,1,0:T(8,128)S(1)}, bf16[128,256]{1,0:T(8,128)(2,1)}) custom-call(f32[4,128,256]{2,1,0:T(8,128)S(1)} %get-tuple-element.48.held), custom_call_target="tpu_custom_call" | custom-call | tf_op jit(solution)/shard_map/group_prefix/pallas_call | solution.py:293
  21.3 1.3 %collective-permute-done.3.refs_3_ = bf16[128,128]{1,0:T(8,128)(2,1)S(1)} collective-permute-done((bf16[128,128]{1,0:T(8,128)(2,1)S(1)}, bf16[128,128]{1,0:T(8,128)(2,1)S(1)}, u32[]{:S(2)}, u32[]{:S(2)}) %collective-permute-start.3) | collective-permute-done | bytes 32800 | tf_op jit(solution)/shard_map/ppermute | solution.py:436
  22.5 0.9 %states_of_upper.1 = (bf16[128,128]{1,0:T(8,128)(2,1)S(1)}, bf16[128,128]{1,0:T(8,128)(2,1)S(1)}, bf16[128,128]{1,0:T(8,128)(2,1)S(1)}, bf16[128,128]{1,0:T(8,128)(2,1)S(1)}, bf16[4,128,128]{2,1,0:T(8,128)(2,1)}) custom-call(bf16[4,128,128]{2,1,0:T(8,128)(2,1)S(1)} %get-tuple-element.53.refs_0_, bf16[4,128,128]{2,1,0:T(8,128)(2,1)S(1)} %get-tuple-element.54.refs_1_, ...), custom_call_target="tpu_custom_call" | custom-call | tf_op jit(solution)/shard_map/states_of_upper/pallas_call | solution.py:293
  23.4 0.3 collective-permute-start.4
  23.7 1.4 %collective-permute-start.5 = (bf16[128,128]{1,0:T(8,128)(2,1)S(1)}, bf16[128,128]{1,0:T(8,128)(2,1)S(1)}, u32[]{:S(2)}, u32[]{:S(2)}) collective-permute-start(bf16[128,128]{1,0:T(8,128)(2,1)S(1)} %get-tuple-element.59), channel_id=1, source_target_pairs={{0,8},{4,12},{8,0},{12,4},{16,24},{20,28},{24,16},{28,20},{1,9},{5... | collective-permute-start | bytes 98312 | tf_op jit(solution)/shard_map/ppermute | solution.py:436
  25.1 1.8 %collective-permute-start.6 = (bf16[128,128]{1,0:T(8,128)(2,1)S(1)}, bf16[128,128]{1,0:T(8,128)(2,1)S(1)}, u32[]{:S(2)}, u32[]{:S(2)}) collective-permute-start(bf16[128,128]{1,0:T(8,128)(2,1)S(1)} %get-tuple-element.60), channel_id=1, source_target_pairs={{0,12},{4,8},{8,4},{12,0},{16,28},{20,24},{24,20},{28,16},{1,13},{... | collective-permute-start | bytes 98312 | tf_op jit(solution)/shard_map/ppermute | solution.py:436
  26.9 1.6 %row_maps.3.rows1_ref = f32[2,512,256]{2,1,0:T(8,128)S(1)} custom-call(bf16[2048,128]{1,0:T(8,128)(2,1)S(1)} %get-tuple-element.34.q16, f32[2048,128]{1,0:T(8,128)S(1)} %get-tuple-element.35.k32, f32[16,128]{1,0:T(8,128)S(1)} %get-tuple-element.36.sums_ref, f32[16,128,128]{2,1,0:T(8,128)S(1)} %get-tuple-element.37.mix_ref, ...), custom_call_target="tpu_custom_call" | custom-call | flops 2000000000 | bytes 8000000 | tf_op jit(solution)/shard_map/row_maps/pallas_call | solution.py:279
  28.6 1.3 %collective-permute-done.6.refs_3_ = bf16[128,128]{1,0:T(8,128)(2,1)S(1)} collective-permute-done((bf16[128,128]{1,0:T(8,128)(2,1)S(1)}, bf16[128,128]{1,0:T(8,128)(2,1)S(1)}, u32[]{:S(2)}, u32[]{:S(2)}) %collective-permute-start.6) | collective-permute-done | bytes 32800 | tf_op jit(solution)/shard_map/ppermute | solution.py:436
  29.9 0.4 apply.1
  30.4 1.5 %collective-permute-done.7.got_ref = bf16[2,128,512]{2,1,0:T(8,128)(2,1)S(1)} collective-permute-done((bf16[2,128,512]{2,1,0:T(8,128)(2,1)S(1)}, bf16[2,128,512]{2,1,0:T(8,128)(2,1)S(1)}, u32[]{:S(2)}, u32[]{:S(2)}) %collective-permute-start.7) | collective-permute-done | bytes 262176 | tf_op jit(solution)/shard_map/ppermute | solution.py:436
  32.0 0.7 %project.3 = bf16[128,2048]{1,0:T(8,128)(2,1)S(1)} custom-call(bf16[2,128,512]{2,1,0:T(8,128)(2,1)S(1)} %get-tuple-element.61.keep_ref, bf16[2,128,512]{2,1,0:T(8,128)(2,1)S(1)} %collective-permute-done.7.got_ref, bf16[512,2048]{1,0:T(8,128)(2,1)S(1)} %copy-done, bf16[512,2048]{1,0:T(8,128)(2,1)S(1)} %collective-permute-done.8.w2_ref), custom_call_target="tpu_custom_call" | custom-call | flops 536870912 | bytes 4194304 | tf_op jit(solution)/shard_map/project/pallas_call | solution.py:423
  32.7 1.6 %collective-permute-start.9 = (bf16[128,2048]{1,0:T(8,128)(2,1)S(1)}, bf16[128,2048]{1,0:T(8,128)(2,1)S(1)}, u32[]{:S(2)}, u32[]{:S(2)}) collective-permute-start(bf16[128,2048]{1,0:T(8,128)(2,1)S(1)} %project.3), channel_id=1, source_target_pairs={{0,2},{1,3},{2,0},{3,1},{4,6},{5,7},{6,4},{7,5},{8,10},{9,11},{10,... | collective-permute-start | bytes 1572872 | tf_op jit(solution)/shard_map/ppermute | solution.py:436
  34.3 0.7 %project.2 = f32[128,2048]{1,0:T(8,128)S(1)} custom-call(bf16[2,128,512]{2,1,0:T(8,128)(2,1)S(1)} %get-tuple-element.61.keep_ref, bf16[2,128,512]{2,1,0:T(8,128)(2,1)S(1)} %collective-permute-done.7.got_ref, bf16[512,2048]{1,0:T(8,128)(2,1)S(1)} %copy-done, bf16[512,2048]{1,0:T(8,128)(2,1)S(1)} %collective-permute-done.8.w2_ref), custom_call_target="tpu_custom_call" | custom-call | flops 536870912 | bytes 4194304 | tf_op jit(solution)/shard_map/project/pallas_call | solution.py:423
  35.0 11.7 %collective-permute-done.9 = bf16[128,2048]{1,0:T(8,128)(2,1)S(1)} collective-permute-done((bf16[128,2048]{1,0:T(8,128)(2,1)S(1)}, bf16[128,2048]{1,0:T(8,128)(2,1)S(1)}, u32[]{:S(2)}, u32[]{:S(2)}) %collective-permute-start.9) | collective-permute-done | bytes 524320 | tf_op jit(solution)/shard_map/ppermute | solution.py:436
  46.7 0.9 %add_convert_fusion = bf16[128,2048]{1,0:T(8,128)(2,1)} fusion(f32[128,2048]{1,0:T(8,128)S(1)} %project.2, bf16[128,2048]{1,0:T(8,128)(2,1)S(1)} %collective-permute-done.9), kind=kLoop, calls=%fused_computation | loop fusion | flops 786432 | bytes 2097152 | tf_op jit(solution)/shard_map/convert_element_type | solution.py:472
  (8 shorter events, 0.1 us)
Async XLA Ops:
  0.0 32.0 %collective-permute-start.8 = (bf16[512,2048]{1,0:T(8,128)(2,1)}, bf16[512,2048]{1,0:T(8,128)(2,1)S(1)}, u32[]{:S(2)}, u32[]{:S(2)}) collective-permute-start(bf16[512,2048]{1,0:T(8,128)(2,1)} %w_ref.3), channel_id=1, source_target_pairs={{0,1},{1,0},{2,3},{3,2},{4,5},{5,4},{6,7},{7,6},{8,9},{9,8},{10,11... | collective-permute-start | bytes 6291464 | tf_op jit(solution)/shard_map/ppermute | solution.py:436
  7.6 5.8 %collective-permute-start = (bf16[128,256]{1,0:T(8,128)(2,1)S(1)}, bf16[128,256]{1,0:T(8,128)(2,1)S(1)}, u32[]{:S(2)}, u32[]{:S(2)}) collective-permute-start(bf16[128,256]{1,0:T(8,128)(2,1)S(1)} %get-tuple-element.40), channel_id=1, source_target_pairs={{0,4},{4,0},{8,12},{12,8},{16,20},{20,16},{24,28},{28,24},{1,5},{5... | collective-permute-start | bytes 196616 | tf_op jit(solution)/shard_map/ppermute | solution.py:436
  10.1 4.5 %collective-permute-start.1 = (bf16[128,256]{1,0:T(8,128)(2,1)S(1)}, bf16[128,256]{1,0:T(8,128)(2,1)S(1)}, u32[]{:S(2)}, u32[]{:S(2)}) collective-permute-start(bf16[128,256]{1,0:T(8,128)(2,1)S(1)} %get-tuple-element.41), channel_id=1, source_target_pairs={{0,8},{4,12},{8,0},{12,4},{16,24},{20,28},{24,16},{28,20},{1,9},{5... | collective-permute-start | bytes 196616 | tf_op jit(solution)/shard_map/ppermute | solution.py:436
  11.7 5.2 %collective-permute-start.2 = (bf16[128,256]{1,0:T(8,128)(2,1)S(1)}, bf16[128,256]{1,0:T(8,128)(2,1)S(1)}, u32[]{:S(2)}, u32[]{:S(2)}) collective-permute-start(bf16[128,256]{1,0:T(8,128)(2,1)S(1)} %get-tuple-element.42), channel_id=1, source_target_pairs={{0,12},{4,8},{8,4},{12,0},{16,28},{20,24},{24,20},{28,16},{1,13},{... | collective-permute-start | bytes 196616 | tf_op jit(solution)/shard_map/ppermute | solution.py:436
  17.4 5.1 %collective-permute-start.3 = (bf16[128,128]{1,0:T(8,128)(2,1)S(1)}, bf16[128,128]{1,0:T(8,128)(2,1)S(1)}, u32[]{:S(2)}, u32[]{:S(2)}) collective-permute-start(bf16[128,128]{1,0:T(8,128)(2,1)S(1)} %get-tuple-element.52), channel_id=1, source_target_pairs={{0,16},{4,20},{8,24},{12,28},{16,0},{20,4},{24,8},{28,12},{1,17},{... | collective-permute-start | bytes 98312 | tf_op jit(solution)/shard_map/ppermute | solution.py:436
  23.4 5.1 %collective-permute-start.4 = (bf16[128,128]{1,0:T(8,128)(2,1)S(1)}, bf16[128,128]{1,0:T(8,128)(2,1)S(1)}, u32[]{:S(2)}, u32[]{:S(2)}) collective-permute-start(bf16[128,128]{1,0:T(8,128)(2,1)S(1)} %get-tuple-element.58), channel_id=1, source_target_pairs={{0,4},{4,0},{8,12},{12,8},{16,20},{20,16},{24,28},{28,24},{1,5},{5... | collective-permute-start | bytes 98312 | tf_op jit(solution)/shard_map/ppermute | solution.py:436
  23.7 4.9 %collective-permute-start.5 = (bf16[128,128]{1,0:T(8,128)(2,1)S(1)}, bf16[128,128]{1,0:T(8,128)(2,1)S(1)}, u32[]{:S(2)}, u32[]{:S(2)}) collective-permute-start(bf16[128,128]{1,0:T(8,128)(2,1)S(1)} %get-tuple-element.59), channel_id=1, source_target_pairs={{0,8},{4,12},{8,0},{12,4},{16,24},{20,28},{24,16},{28,20},{1,9},{5... | collective-permute-start | bytes 98312 | tf_op jit(solution)/shard_map/ppermute | solution.py:436
  25.1 4.8 %collective-permute-start.6 = (bf16[128,128]{1,0:T(8,128)(2,1)S(1)}, bf16[128,128]{1,0:T(8,128)(2,1)S(1)}, u32[]{:S(2)}, u32[]{:S(2)}) collective-permute-start(bf16[128,128]{1,0:T(8,128)(2,1)S(1)} %get-tuple-element.60), channel_id=1, source_target_pairs={{0,12},{4,8},{8,4},{12,0},{16,28},{20,24},{24,20},{28,16},{1,13},{... | collective-permute-start | bytes 98312 | tf_op jit(solution)/shard_map/ppermute | solution.py:436
  28.6 3.4 %copy-start = (bf16[512,2048]{1,0:T(8,128)(2,1)S(1)}, bf16[512,2048]{1,0:T(8,128)(2,1)}, u32[]{:S(2)}) copy-start(bf16[512,2048]{1,0:T(8,128)(2,1)} %w_ref.3) | copy-start | bytes 6291460
  30.4 1.6 %collective-permute-start.7 = (bf16[2,128,512]{2,1,0:T(8,128)(2,1)S(1)}, bf16[2,128,512]{2,1,0:T(8,128)(2,1)S(1)}, u32[]{:S(2)}, u32[]{:S(2)}) collective-permute-start(bf16[2,128,512]{2,1,0:T(8,128)(2,1)S(1)} %get-tuple-element.62), channel_id=1, source_target_pairs={{0,1},{1,0},{2,3},{3,2},{4,5},{5,4},{6,7},{7,6},{8,9},{9,8},{10,11... | collective-permute-start | bytes 786440 | tf_op jit(solution)/shard_map/ppermute | solution.py:436
  32.7 14.0 %collective-permute-start.9 = (bf16[128,2048]{1,0:T(8,128)(2,1)S(1)}, bf16[128,2048]{1,0:T(8,128)(2,1)S(1)}, u32[]{:S(2)}, u32[]{:S(2)}) collective-permute-start(bf16[128,2048]{1,0:T(8,128)(2,1)S(1)} %project.3), channel_id=1, source_target_pairs={{0,2},{1,3},{2,0},{3,1},{4,6},{5,7},{6,4},{7,5},{8,10},{9,11},{10,... | collective-permute-start | bytes 1572872 | tf_op jit(solution)/shard_map/ppermute | solution.py:436

commit v9 on v8

--- a/solution.py
+++ b/solution.py
@@ -148,8 +148,7 @@
     return jnp.concatenate([ref[:, i : i + C] for i in range(0, ref.shape[1], C)], axis=0)
 
 
-def local_maps_kernel(heads, batch, k_hbm, v_hbm, beta_hbm, log_hbm, q_hbm, q16, k32, sums_ref, mix_ref, wu_ref, n_ref, own_ref, *rest):
-    sends, (k16, v16, v32, beta_ref, log_ref, all_ref, sems) = rest[: heads - 1], rest[heads - 1 :]
+def local_maps_kernel(heads, batch, k_hbm, v_hbm, beta_hbm, log_hbm, q_hbm, q16, k32, sums_ref, mix_ref, wu_ref, n_ref, own_ref, send_ref, k16, v16, v32, beta_ref, log_ref, all_ref, sems):
     late = pltpu.make_async_copy(q_hbm, q16, sems.at[4])
     fetch(((k_hbm, k16), (log_hbm, log_ref), (beta_hbm, beta_ref), (v_hbm, v16)), sems, late)
     k32[...] = k16[...].astype(F32)
@@ -205,18 +204,10 @@
                 state = dot3(split(moved), split(state))
                 state = jnp.concatenate([state[:, :C], state[:, C:] + fresh], axis=1)
             all_ref[start + j] = state
+            send_ref[start + j] = state.astype(BF16)
     place = lax.rem(lax.axis_index("seq"), heads)
     own_ref[...] = all_ref[place]
-    for r in range(1, heads):
-        sends[r - 1][...] = all_ref[other_place(place, r, heads)].astype(BF16)
     late.wait()
-
-
-def other_place(place, r, heads):
-    result = place
-    for i in range(heads):
-        result = jnp.where(place == i, i ^ r, result)
-    return result
 
 
 def local_maps(key, value, beta, log_decay, query, batch):
@@ -226,7 +217,7 @@
     return pl.pallas_call(
         functools.partial(local_maps_kernel, heads, batch),
         in_specs=[pl.BlockSpec(memory_space=pltpu.HBM)] * 5,
-        out_specs=[here] * (6 + heads),
+        out_specs=[here] * 8,
         out_shape=[
             jax.ShapeDtypeStruct(query.shape, BF16),
             jax.ShapeDtypeStruct(key.shape, F32),
@@ -235,8 +226,8 @@
             jax.ShapeDtypeStruct((count, C, 2 * C), F32),
             jax.ShapeDtypeStruct((count, C, 2 * C), F32),
             jax.ShapeDtypeStruct((C, 2 * C), F32),
-        ]
-        + [jax.ShapeDtypeStruct((C, 2 * C), BF16)] * (heads - 1),
+            jax.ShapeDtypeStruct((heads, C, 2 * C), BF16),
+        ],
         scratch_shapes=[
             pltpu.VMEM(key.shape, BF16),
             pltpu.VMEM(key.shape, BF16),
@@ -305,20 +296,12 @@
     return dot(jnp.concatenate([high, low], axis=1), twice(state16)) + added
 
 
-def in_order(own_ref, got_refs, held):
+def group_state(own_ref, got_ref, held, out_ref):
     heads = held.shape[0]
-    place = lax.rem(lax.axis_index("seq"), heads)
-    held[place] = own_ref[...]
-    for r, got in enumerate(got_refs, 1):
-        held[other_place(place, r, heads)] = got[...].astype(F32)
-    return place
-
-
-def group_state(own_ref, *refs):
-    got_refs, (held, out_ref) = refs[:-2], refs[-2:]
-    in_order(own_ref, got_refs, held)
+    held[...] = got_ref[...].astype(F32)
+    held[lax.rem(lax.axis_index("seq"), heads)] = own_ref[...]
     state = held[0, :, C:].astype(BF16)
-    for i in range(1, held.shape[0]):
+    for i in range(1, heads):
         state = moved_on(held[i, :, :C], state, held[i, :, C:]).astype(BF16)
     out_ref[...] = state
 
@@ -339,8 +322,7 @@
     total_ref[...] = total.astype(BF16)
 
 
-def group_states(upper_only, high_ref, low_ref, added_ref, state_ref, keep_ref, *refs):
-    sends, states = refs[:-1], refs[-1]
+def group_states(upper_only, high_ref, low_ref, added_ref, state_ref, out_ref):
     heads = added_ref.shape[0]
     state = state_ref[...]
     if upper_only:
@@ -348,11 +330,7 @@
     both = twice(state)
     for i in range(heads):
         maps = jnp.concatenate([high_ref[i], low_ref[i]], axis=1)
-        states[i] = (dot(maps, both) + added_ref[i]).astype(BF16)
-    place = lax.rem(lax.axis_index("seq"), heads)
-    keep_ref[...] = states[place]
-    for r, send in enumerate(sends, 1):
-        send[...] = states[other_place(place, r, heads)]
+        out_ref[i] = (dot(maps, both) + added_ref[i]).astype(BF16)
 
 
 def states_of_upper(*refs):
@@ -377,14 +355,10 @@
     return lax.fori_loop(0, count // heads - 1, step, start).astype(BF16)
 
 
-def apply_kernel(groups, rows0_ref, rows1_ref, *refs):
-    states, (keep_ref, send_ref, held) = refs[:-3], refs[-3:]
-    heads = len(states)
+def apply_kernel(groups, rows0_ref, rows1_ref, held, keep_ref, send_ref):
+    heads = held.shape[0]
     half, tokens, _ = rows0_ref.shape
     block = tokens // groups
-    place = lax.rem(lax.axis_index("seq"), heads)
-    for r in range(heads):
-        held[other_place(place, r, heads)] = states[r][...]
     core = lax.rem(lax.axis_index("head"), 2)
     for out_ref, parity in ((send_ref, 1 - core), (keep_ref, core)):
         for i in range(groups // 2):
@@ -397,18 +371,17 @@
 
 def apply(rows, states, groups):
     _, tokens, _ = rows[0].shape
-    heads = len(states)
+    heads = states.shape[0]
     here = pl.BlockSpec(memory_space=pltpu.VMEM)
     out = jax.ShapeDtypeStruct((groups // 2, tokens // groups, heads * C), BF16)
     return pl.pallas_call(
         functools.partial(apply_kernel, groups),
-        in_specs=[here] * (2 + heads),
+        in_specs=[here] * 3,
         out_specs=[here] * 2,
         out_shape=[out, out],
-        scratch_shapes=[pltpu.VMEM((heads, C, C), BF16)],
         compiler_params=pltpu.CompilerParams(vmem_limit_bytes=8 * MIB),
         name="apply",
-    )(*rows, *states)
+    )(*rows, states)
 
 
 def project_kernel(other, keep_ref, got_ref, w_ref, w2_ref, out_ref):
@@ -436,36 +409,39 @@
     return lax.ppermute(x, axis, [(i, i ^ bit) for i in range(count)])
 
 
+def share_out(parts):
+    size, count = parts.shape[0], lax.axis_size("seq")
+    groups = [list(range(i, i + size)) for i in range(0, count, size)]
+    return lax.all_to_all(parts, "seq", 0, 0, axis_index_groups=groups, tiled=True)
+
+
 def body(query, key, value, beta, log_decay, out_weight):
     tokens, heads, _ = key.shape
     count = lax.axis_size("seq")
     flat = lambda x: x.reshape(tokens * heads, C)
     weight2 = swap(out_weight, "head", 1)
-    q16, k32, *chunk_maps, own, send1, send2, send3 = local_maps(
+    q16, k32, *chunk_maps, own, send = local_maps(
         flat(key), flat(value), beta, log_decay, flat(query), heads
     )
-    got = [swap(x, "seq", r) for r, x in enumerate((send1, send2, send3), 1)]
+    got = share_out(send)
     half = heads // 2
     rows0 = row_maps(heads, range(half), q16, k32, *chunk_maps)
     rows1 = row_maps(heads, range(half, heads), q16, k32, *chunk_maps)
-    rows0, got = lax.optimization_barrier((rows0, got))
     wide = jax.ShapeDtypeStruct((heads, C, 2 * C), F32)
     square = jax.ShapeDtypeStruct((C, C), BF16)
     squares = jax.ShapeDtypeStruct((heads, C, C), BF16)
     added = jax.ShapeDtypeStruct((heads, C, C), F32)
-    held, state = small_call(group_state, [wide, square], own, *got)
+    held, state = small_call(group_state, [wide, square], own, got)
     *maps, total = small_call(
         group_prefix, [squares, squares, added, jax.ShapeDtypeStruct((C, 2 * C), BF16)], held
     )
-    outs = [square] * heads + [squares]
     if count == 2 * heads:
         lower = swap(state, "seq", heads)
         maps, lower = lax.optimization_barrier((maps, lower))
-        keep, *sends = small_call(states_of_upper, outs, *maps, lower)
+        (states,) = small_call(states_of_upper, [squares], *maps, lower)
     else:
-        keep, *sends = small_call(states_given, outs, *maps, prefix(total, heads))
-    entering = [keep] + [swap(x, "seq", r) for r, x in enumerate(sends[: heads - 1], 1)]
-    keep, away = apply((rows0, rows1), entering, lax.axis_size("head"))
+        (states,) = small_call(states_given, [squares], *maps, prefix(total, heads))
+    keep, away = apply((rows0, rows1), share_out(states), lax.axis_size("head"))
     got = swap(away, "head", 1)
     theirs = swap(project(True, keep, got, out_weight, weight2), "head", 2)
     mine = project(False, keep, got, out_weight, weight2)

time: 47.8 us -> 62.6 us (1.31)
  local copies, waits for them, and re-layouts: 0.01 us -> 11.5 us
  blocking collectives: 0 us -> 11 us
  waiting for transfers between devices: 19.4 us -> 12.7 us
  starting transfers between devices: 12.4 us -> 8.09 us
  Pallas kernels: 14.9 us -> 18 us
    unnamed x2 -> x22, local copies, waits for them, and re-layouts: 0.01 us -> 11.5 us
    all_to_all x0 -> x1, blocking collectives: none -> 11 us  [share_out(): lax.all_to_all(parts, 'seq', 0, 0, axis_index_groups=groups, tiled=True)]
    ppermute x10 -> x4, starting transfers between devices: 12.4 us -> 4.76 us  [swap(): return lax.ppermute(x, axis, [(i, i ^ bit) for i in range(count)])]
    ppermute x10 -> x4, waiting for transfers between devices: 19.4 us -> 12.6 us  [swap(): return lax.ppermute(x, axis, [(i, i ^ bit) for i in range(count)])]
    all_to_all x0 -> x1, starting transfers between devices: none -> 3.32 us  [share_out(): lax.all_to_all(parts, 'seq', 0, 0, axis_index_groups=groups, tiled=True)]
    pallas_call x2, Pallas kernels: 1.43 us -> 4.62 us  [project(): pl.pallas_call(functools.partial(project_kernel, other), out_shape=jax.Sh...]
  transfers between devices with their start and end apart: 10 -> 5, of which waited for: 6 -> 3; matrix products, arithmetic and copies ran while one was open for 0% -> 0% of each run, Pallas kernels for 30% -> 25%
where the time goes in v9:
time: 62.6 us; the launch traced here: 62.2 us
  Pallas kernels  18 us (29%)
  waiting for transfers between devices  12.7 us (20%)
  local copies, waits for them, and re-layouts  11.5 us (18%)
  blocking collectives  11 us (18%)
  starting transfers between devices  8.09 us (13%)
  other arithmetic  0.9 us (1%)
    ppermute x4, waiting for transfers between devices, swap(): return lax.ppermute(x, axis, [(i, i ^ bit) for i in range(count)])  12.6 us
    unnamed x22, local copies, waits for them, and re-layouts  11.5 us
    all_to_all x1, blocking collectives, share_out(): lax.all_to_all(parts, 'seq', 0, 0, axis_index_groups=groups, tiled=True)  11 us
    pallas_call x1, Pallas kernels, local_maps(): pl.pallas_call(functools.partial(local_maps_kernel, heads, batch), in_spe...  7.07 us
    ppermute x4, starting transfers between devices, swap(): return lax.ppermute(x, axis, [(i, i ^ bit) for i in range(count)])  4.76 us
    pallas_call x2, Pallas kernels, project(): pl.pallas_call(functools.partial(project_kernel, other), out_shape=jax.Sh...  4.62 us
    all_to_all x1, starting transfers between devices, share_out(): lax.all_to_all(parts, 'seq', 0, 0, axis_index_groups=groups, tiled=True)  3.32 us
    pallas_call x2, Pallas kernels, row_maps(): pl.pallas_call(functools.partial(rows_kernel, heads, mine), in_specs=[her...  3.26 us
  transfers between devices with their start and end apart: 5, of which 3 were waited for; matrix products, arithmetic and copies ran while one was open for 0% of the time, Pallas kernels for 25%

profile of v9, /device:TPU:0, one launch (start us, length us, event | category | flops | bytes accessed | tf_op | source)
XLA Modules:
  0.0 62.2 jit_solution(8585697542613849274)
XLA Ops:
  0.5 7.1 %local_maps.1 = (bf16[2048,128]{1,0:T(8,128)(2,1)S(1)}, f32[2048,128]{1,0:T(8,128)S(1)}, f32[16,128]{1,0:T(8,128)S(1)}, f32[16,128,128]{2,1,0:T(8,128)S(1)}, f32...) custom-call(bf16[2048,128]{1,0:T(8,128)(2,1)} %bitcast.3, ...), custom_call_target="tpu_custom_call" | custom-call | tf_op jit(solution)/shard_map/local_maps/pallas_call | solution.py:217
  7.5 1.3 %copy-done = f32[16,128,256]{2,1,0:T(8,128)} copy-done((f32[16,128,256]{2,1,0:T(8,128)}, f32[16,128,256]{2,1,0:T(8,128)S(1)}, u32[]{:S(2)}) %copy-start) | copy-done | bytes 2097176
  8.8 1.0 %copy-done.3 = f32[16,128,128]{2,1,0:T(8,128)} copy-done((f32[16,128,128]{2,1,0:T(8,128)}, f32[16,128,128]{2,1,0:T(8,128)S(1)}, u32[]{:S(2)}) %copy-start.3) | copy-done | bytes 1048600
  10.6 11.0 %all_to_all.10.got_ref = bf16[4,128,256]{2,1,0:T(8,128)(2,1)S(1)} all-to-all(bf16[4,128,256]{2,1,0:T(8,128)(2,1)S(1)} %get-tuple-element.31), channel_id=1, replica_groups={{0,4,8,12},{16,20,24,28},{1,5,9,13},{17,21,25,29},{2,6,10,14},{18,22,26..., dimensions={0} | all-to-all | bytes 524288 | tf_op jit(solution)/shard_map/all_to_all | solution.py:415
  22.1 2.7 %collective-permute-start = (bf16[128,128]{1,0:T(8,128)(2,1)S(1)}, bf16[128,128]{1,0:T(8,128)(2,1)S(1)}, u32[]{:S(2)}, u32[]{:S(2)}) collective-permute-start(bf16[128,128]{1,0:T(8,128)(2,1)S(1)} %get-tuple-element.36), channel_id=1, source_target_pairs={{0,16},{4,20},{8,24},{12,28},{16,0},{20,4},{24,8},{28,12},{1,17},{... | collective-permute-start | bytes 98312 | tf_op jit(solution)/shard_map/ppermute | solution.py:409
  24.7 1.2 %group_prefix.1 = (bf16[4,128,128]{2,1,0:T(8,128)(2,1)S(1)}, bf16[4,128,128]{2,1,0:T(8,128)(2,1)S(1)}, f32[4,128,128]{2,1,0:T(8,128)S(1)}, bf16[128,256]{1,0:T(8,128)(2,1)}) custom-call(f32[4,128,256]{2,1,0:T(8,128)S(1)} %get-tuple-element.32.held), custom_call_target="tpu_custom_call" | custom-call | tf_op jit(solution)/shard_map/group_prefix/pallas_call | solution.py:284
  26.0 1.0 %collective-permute-done.refs_3_ = bf16[128,128]{1,0:T(8,128)(2,1)S(1)} collective-permute-done((bf16[128,128]{1,0:T(8,128)(2,1)S(1)}, bf16[128,128]{1,0:T(8,128)(2,1)S(1)}, u32[]{:S(2)}, u32[]{:S(2)}) %collective-permute-start) | collective-permute-done | bytes 32800 | tf_op jit(solution)/shard_map/ppermute | solution.py:409
  27.0 0.9 %states_of_upper.1 = bf16[4,128,128]{2,1,0:T(8,128)(2,1)} custom-call(bf16[4,128,128]{2,1,0:T(8,128)(2,1)S(1)} %get-tuple-element.37.refs_0_, bf16[4,128,128]{2,1,0:T(8,128)(2,1)S(1)} %get-tuple-element.38.refs_1_, f32[4,128,128]{2,1,0:T(8,128)S(1)} %get-tuple-element.39.refs_2_, bf16[128,128]{1,0:T(8,128)(2,1)S(1)} %collective-permute-done.refs_3_), custom_call_target="tpu_custom_call" | custom-call | tf_op jit(solution)/shard_map/states_of_upper/pallas_call | solution.py:284
  27.8 3.3 %all-to-all-start.1 = ((bf16[4,128,128]{2,1,0:T(8,128)(2,1)}), bf16[4,128,128]{2,1,0:T(8,128)(2,1)S(1)}, u32[]{:S(2)}, u32[]{:S(2)}) async-start(bf16[4,128,128]{2,1,0:T(8,128)(2,1)} %states_of_upper.1), calls=%async_computation.1 | async-start | bytes 262144 | tf_op jit(solution)/shard_map/all_to_all | solution.py:415
  31.2 1.6 %copy-done.1 = f32[16,128,256]{2,1,0:T(8,128)S(1)} copy-done((f32[16,128,256]{2,1,0:T(8,128)S(1)}, f32[16,128,256]{2,1,0:T(8,128)}, u32[]{:S(2)}) %copy-start.1) | copy-done | bytes 2097176
  32.8 1.2 %copy-done.4 = f32[16,128,128]{2,1,0:T(8,128)S(1)} copy-done((f32[16,128,128]{2,1,0:T(8,128)S(1)}, f32[16,128,128]{2,1,0:T(8,128)}, u32[]{:S(2)}) %copy-start.4) | copy-done | bytes 1048600
  34.0 1.0 %copy-done.10 = bf16[2048,128]{1,0:T(8,128)(2,1)S(1)} copy-done((bf16[2048,128]{1,0:T(8,128)(2,1)S(1)}, bf16[2048,128]{1,0:T(8,128)(2,1)}, u32[]{:S(2)}) %copy-start.10) | copy-done | bytes 524312
  35.0 1.6 %row_maps.3.rows1_ref = f32[2,512,256]{2,1,0:T(8,128)S(1)} custom-call(bf16[2048,128]{1,0:T(8,128)(2,1)S(1)} %copy-done.10, f32[2048,128]{1,0:T(8,128)S(1)} %get-tuple-element.25.k32, f32[16,128]{1,0:T(8,128)S(1)} %get-tuple-element.26.sums_ref, f32[16,128,128]{2,1,0:T(8,128)S(1)} %copy-done.4, f32[16,128,256]{2,1,0:T(8,128)S(1)} %get-tuple-element.28.wu_ref, ...), custom_call_target="tpu_custom_call" | custom-call | flops 2000000000 | bytes 8000000 | tf_op jit(solution)/shard_map/row_maps/pallas_call | solution.py:270
  36.7 1.0 %copy-done.5 = f32[2,512,256]{2,1,0:T(8,128)} copy-done((f32[2,512,256]{2,1,0:T(8,128)}, f32[2,512,256]{2,1,0:T(8,128)S(1)}, u32[]{:S(2)}) %copy-start.5) | copy-done | bytes 1048600
  37.7 1.6 %row_maps.2.rows0_ref = f32[2,512,256]{2,1,0:T(8,128)S(1)} custom-call(bf16[2048,128]{1,0:T(8,128)(2,1)S(1)} %copy-done.10, f32[2048,128]{1,0:T(8,128)S(1)} %get-tuple-element.25.k32, f32[16,128]{1,0:T(8,128)S(1)} %get-tuple-element.26.sums_ref, f32[16,128,128]{2,1,0:T(8,128)S(1)} %copy-done.4, f32[16,128,256]{2,1,0:T(8,128)S(1)} %get-tuple-element.28.wu_ref, ...), custom_call_target="tpu_custom_call" | custom-call | flops 2000000000 | bytes 8000000 | tf_op jit(solution)/shard_map/row_maps/pallas_call | solution.py:270
  39.3 1.0 %copy-done.7 = f32[2,512,256]{2,1,0:T(8,128)} copy-done((f32[2,512,256]{2,1,0:T(8,128)}, f32[2,512,256]{2,1,0:T(8,128)S(1)}, u32[]{:S(2)}) %copy-start.7) | copy-done | bytes 1048600
  40.3 1.4 %copy-done.6 = f32[2,512,256]{2,1,0:T(8,128)S(1)} copy-done((f32[2,512,256]{2,1,0:T(8,128)S(1)}, f32[2,512,256]{2,1,0:T(8,128)}, u32[]{:S(2)}) %copy-start.6) | copy-done | bytes 1048600
  41.7 1.2 %copy-done.8 = f32[2,512,256]{2,1,0:T(8,128)S(1)} copy-done((f32[2,512,256]{2,1,0:T(8,128)S(1)}, f32[2,512,256]{2,1,0:T(8,128)}, u32[]{:S(2)}) %copy-start.8) | copy-done | bytes 1048600
  43.4 1.5 %collective-permute-done.1.got_ref = bf16[2,128,512]{2,1,0:T(8,128)(2,1)S(1)} collective-permute-done((bf16[2,128,512]{2,1,0:T(8,128)(2,1)S(1)}, bf16[2,128,512]{2,1,0:T(8,128)(2,1)S(1)}, u32[]{:S(2)}, u32[]{:S(2)}) %collective-permute-start.1) | collective-permute-done | bytes 262176 | tf_op jit(solution)/shard_map/ppermute | solution.py:409
  44.9 2.3 %project.3 = bf16[128,2048]{1,0:T(8,128)(2,1)S(1)} custom-call(bf16[2,128,512]{2,1,0:T(8,128)(2,1)S(1)} %get-tuple-element.41.keep_ref, bf16[2,128,512]{2,1,0:T(8,128)(2,1)S(1)} %collective-permute-done.1.got_ref, bf16[512,2048]{1,0:T(8,128)(2,1)S(1)} %copy-done.2, bf16[512,2048]{1,0:T(8,128)(2,1)} %collective-permute-done.2.w2_ref), custom_call_target="tpu_custom_call" | custom-call | flops 536870912 | bytes 4194304 | tf_op jit(solution)/shard_map/project/pallas_call | solution.py:396
  47.2 1.6 %collective-permute-start.3 = (bf16[128,2048]{1,0:T(8,128)(2,1)S(1)}, bf16[128,2048]{1,0:T(8,128)(2,1)S(1)}, u32[]{:S(2)}, u32[]{:S(2)}) collective-permute-start(bf16[128,2048]{1,0:T(8,128)(2,1)S(1)} %project.3), channel_id=1, source_target_pairs={{0,2},{1,3},{2,0},{3,1},{4,6},{5,7},{6,4},{7,5},{8,10},{9,11},{10,... | collective-permute-start | bytes 1572872 | tf_op jit(solution)/shard_map/ppermute | solution.py:409
  48.8 2.3 %project.2 = f32[128,2048]{1,0:T(8,128)S(1)} custom-call(bf16[2,128,512]{2,1,0:T(8,128)(2,1)S(1)} %get-tuple-element.41.keep_ref, bf16[2,128,512]{2,1,0:T(8,128)(2,1)S(1)} %collective-permute-done.1.got_ref, bf16[512,2048]{1,0:T(8,128)(2,1)S(1)} %copy-done.2, bf16[512,2048]{1,0:T(8,128)(2,1)} %collective-permute-done.2.w2_ref), custom_call_target="tpu_custom_call" | custom-call | flops 536870912 | bytes 4194304 | tf_op jit(solution)/shard_map/project/pallas_call | solution.py:396
  51.1 10.1 %collective-permute-done.3 = bf16[128,2048]{1,0:T(8,128)(2,1)S(1)} collective-permute-done((bf16[128,2048]{1,0:T(8,128)(2,1)S(1)}, bf16[128,2048]{1,0:T(8,128)(2,1)S(1)}, u32[]{:S(2)}, u32[]{:S(2)}) %collective-permute-start.3) | collective-permute-done | bytes 524320 | tf_op jit(solution)/shard_map/ppermute | solution.py:409
  61.3 0.9 %add_convert_fusion = bf16[128,2048]{1,0:T(8,128)(2,1)} fusion(f32[128,2048]{1,0:T(8,128)S(1)} %project.2, bf16[128,2048]{1,0:T(8,128)(2,1)S(1)} %collective-permute-done.3), kind=kLoop, calls=%fused_computation | loop fusion | flops 786432 | bytes 2097152 | tf_op jit(solution)/shard_map/convert_element_type | solution.py:448
  (19 shorter events, 2.3 us)
Async XLA Ops:
  0.0 44.9 %collective-permute-start.2 = (bf16[512,2048]{1,0:T(8,128)(2,1)}, bf16[512,2048]{1,0:T(8,128)(2,1)}, u32[]{:S(2)}, u32[]{:S(2)}) collective-permute-start(bf16[512,2048]{1,0:T(8,128)(2,1)} %w_ref.3), channel_id=1, source_target_pairs={{0,1},{1,0},{2,3},{3,2},{4,5},{5,4},{6,7},{7,6},{8,9},{9,8},{10,11... | collective-permute-start | bytes 6291464 | tf_op jit(solution)/shard_map/ppermute | solution.py:409
  7.5 1.3 %copy-start = (f32[16,128,256]{2,1,0:T(8,128)}, f32[16,128,256]{2,1,0:T(8,128)S(1)}, u32[]{:S(2)}) copy-start(f32[16,128,256]{2,1,0:T(8,128)S(1)} %get-tuple-element.29.n_ref) | copy-start | bytes 6291460
  8.8 1.0 %copy-start.3 = (f32[16,128,128]{2,1,0:T(8,128)}, f32[16,128,128]{2,1,0:T(8,128)S(1)}, u32[]{:S(2)}) copy-start(f32[16,128,128]{2,1,0:T(8,128)S(1)} %get-tuple-element.27.mix_ref) | copy-start | bytes 3145732
  9.8 0.8 %copy-start.9 = (bf16[2048,128]{1,0:T(8,128)(2,1)}, bf16[2048,128]{1,0:T(8,128)(2,1)S(1)}, u32[]{:S(2)}) copy-start(bf16[2048,128]{1,0:T(8,128)(2,1)S(1)} %get-tuple-element.24.q16) | copy-start | bytes 1572868
  22.1 4.9 %collective-permute-start = (bf16[128,128]{1,0:T(8,128)(2,1)S(1)}, bf16[128,128]{1,0:T(8,128)(2,1)S(1)}, u32[]{:S(2)}, u32[]{:S(2)}) collective-permute-start(bf16[128,128]{1,0:T(8,128)(2,1)S(1)} %get-tuple-element.36), channel_id=1, source_target_pairs={{0,16},{4,20},{8,24},{12,28},{16,0},{20,4},{24,8},{28,12},{1,17},{... | collective-permute-start | bytes 98312 | tf_op jit(solution)/shard_map/ppermute | solution.py:409
  27.8 12.4 %all-to-all-start.1 = ((bf16[4,128,128]{2,1,0:T(8,128)(2,1)}), bf16[4,128,128]{2,1,0:T(8,128)(2,1)S(1)}, u32[]{:S(2)}, u32[]{:S(2)}) async-start(bf16[4,128,128]{2,1,0:T(8,128)(2,1)} %states_of_upper.1), calls=%async_computation.1 | async-start | bytes 262144 | tf_op jit(solution)/shard_map/all_to_all | solution.py:415
  31.2 1.6 %copy-start.1 = (f32[16,128,256]{2,1,0:T(8,128)S(1)}, f32[16,128,256]{2,1,0:T(8,128)}, u32[]{:S(2)}) copy-start(f32[16,128,256]{2,1,0:T(8,128)} %copy-done) | copy-start | bytes 6291460
  32.8 1.2 %copy-start.4 = (f32[16,128,128]{2,1,0:T(8,128)S(1)}, f32[16,128,128]{2,1,0:T(8,128)}, u32[]{:S(2)}) copy-start(f32[16,128,128]{2,1,0:T(8,128)} %copy-done.3) | copy-start | bytes 3145732
  34.0 1.0 %copy-start.10 = (bf16[2048,128]{1,0:T(8,128)(2,1)S(1)}, bf16[2048,128]{1,0:T(8,128)(2,1)}, u32[]{:S(2)}) copy-start(bf16[2048,128]{1,0:T(8,128)(2,1)} %copy-done.9) | copy-start | bytes 1572868
  36.7 1.0 %copy-start.5 = (f32[2,512,256]{2,1,0:T(8,128)}, f32[2,512,256]{2,1,0:T(8,128)S(1)}, u32[]{:S(2)}) copy-start(f32[2,512,256]{2,1,0:T(8,128)S(1)} %row_maps.3.rows1_ref) | copy-start | bytes 3145732
  39.3 1.0 %copy-start.7 = (f32[2,512,256]{2,1,0:T(8,128)}, f32[2,512,256]{2,1,0:T(8,128)S(1)}, u32[]{:S(2)}) copy-start(f32[2,512,256]{2,1,0:T(8,128)S(1)} %row_maps.2.rows0_ref) | copy-start | bytes 3145732
  40.3 4.6 %copy-start.2 = (bf16[512,2048]{1,0:T(8,128)(2,1)S(1)}, bf16[512,2048]{1,0:T(8,128)(2,1)}, u32[]{:S(2)}) copy-start(bf16[512,2048]{1,0:T(8,128)(2,1)} %w_ref.3) | copy-start | bytes 6291460
  40.3 1.4 %copy-start.6 = (f32[2,512,256]{2,1,0:T(8,128)S(1)}, f32[2,512,256]{2,1,0:T(8,128)}, u32[]{:S(2)}) copy-start(f32[2,512,256]{2,1,0:T(8,128)} %copy-done.5) | copy-start | bytes 3145732
  41.7 1.2 %copy-start.8 = (f32[2,512,256]{2,1,0:T(8,128)S(1)}, f32[2,512,256]{2,1,0:T(8,128)}, u32[]{:S(2)}) copy-start(f32[2,512,256]{2,1,0:T(8,128)} %copy-done.7) | copy-start | bytes 3145732
  43.3 1.6 %collective-permute-start.1 = (bf16[2,128,512]{2,1,0:T(8,128)(2,1)S(1)}, bf16[2,128,512]{2,1,0:T(8,128)(2,1)S(1)}, u32[]{:S(2)}, u32[]{:S(2)}) collective-permute-start(bf16[2,128,512]{2,1,0:T(8,128)(2,1)S(1)} %get-tuple-element.42), channel_id=1, source_target_pairs={{0,1},{1,0},{2,3},{3,2},{4,5},{5,4},{6,7},{7,6},{8,9},{9,8},{10,11... | collective-permute-start | bytes 786440 | tf_op jit(solution)/shard_map/ppermute | solution.py:409
  47.2 14.0 %collective-permute-start.3 = (bf16[128,2048]{1,0:T(8,128)(2,1)S(1)}, bf16[128,2048]{1,0:T(8,128)(2,1)S(1)}, u32[]{:S(2)}, u32[]{:S(2)}) collective-permute-start(bf16[128,2048]{1,0:T(8,128)(2,1)S(1)} %project.3), channel_id=1, source_target_pairs={{0,2},{1,3},{2,0},{3,1},{4,6},{5,7},{6,4},{7,5},{8,10},{9,11},{10,... | collective-permute-start | bytes 1572872 | tf_op jit(solution)/shard_map/ppermute | solution.py:409

commit v10 on v8

--- a/solution.py
+++ b/solution.py
@@ -32,12 +32,7 @@
 
 def dot3(a, b):
     (ah, al), (bh, bl) = a, b
-    width = bh.shape[1]
-    left = jnp.concatenate([ah, al], axis=1)
-    if width > C:
-        return dot(left, twice(bh)) + dot(ah, bl)
-    both = dot(left, twice(jnp.concatenate([bh, bl], axis=1)))
-    return both[:, :width] + both[:, width:]
+    return dot(jnp.concatenate([ah, al, ah], axis=1), jnp.concatenate([bh, bh, bl], axis=0))
 
 
 def iotas():
@@ -74,7 +69,7 @@
     high, middle, low = (
         jnp.where(eye, jnp.concatenate([x] * (C // 16), axis=0), jnp.zeros((), BF16)) for x in parts
     )
-    return dot(jnp.concatenate([high, middle], axis=1), twice(ones)) + dot(low, ones)
+    return dot(jnp.concatenate([high, middle, low], axis=1), jnp.concatenate([ones] * 3, axis=0))
 
 
 def base_inverse(lower, row, col):
@@ -108,17 +103,23 @@
 def inverses(lowers, row, col):
     found = [base_inverse(a, row, col) for a in lowers]
     parts = [split(a) for a in lowers]
+    halves = [split(x) for x in found]
     size = B
     while size < C:
         r, c = odd_rows(row, size), odd_rows(col, size)
         mask = ((r // (2 * size)) == (c // (2 * size))) & ((r // size) != (c // size))
         nothing = jnp.zeros((C // 2, C), BF16)
         joins = [tuple(jnp.where(mask, odd_rows(x, size), nothing) for x in part) for part in parts]
-        halves = [split(x) for x in found]
         middle = [split(dot3(a, x)) for a, x in zip(joins, halves)]
         middle = [tuple(weave(nothing, x, size) for x in part) for part in middle]
         lows = [dot3(tuple(odd_rows(x, size) for x in h), y) for h, y in zip(halves, middle)]
-        found = [weave(even_rows(x, size), odd_rows(x, size) - y, size) for x, y in zip(found, lows)]
+        lows = [odd_rows(x, size) - y for x, y in zip(found, lows)]
+        found = [weave(even_rows(x, size), y, size) for x, y in zip(found, lows)]
+        if 2 * size < C:
+            halves = [
+                tuple(weave(even_rows(x, size), y, size) for x, y in zip(h, split(low)))
+                for h, low in zip(halves, lows)
+            ]
         size *= 2
     return found
 
@@ -411,17 +412,18 @@
     )(*rows, *states)
 
 
-def project_kernel(other, keep_ref, got_ref, w_ref, w2_ref, out_ref):
+def project_kernel(other, start, keep_ref, got_ref, w_ref, w2_ref, out_ref):
     pair = lax.axis_index("head") // 2
     index = 1 - pair if other else pair
-    out_ref[...] = (dot(keep_ref[index], w_ref[...]) + dot(got_ref[index], w2_ref[...])).astype(out_ref.dtype)
-
-
-def project(other, keep, got, weight, weight2):
+    columns = slice(start, start + out_ref.shape[1])
+    shares = dot(keep_ref[index], w_ref[:, columns]) + dot(got_ref[index], w2_ref[:, columns])
+    out_ref[...] = shares.astype(out_ref.dtype)
+
+
+def project(other, start, width, keep, got, weight, weight2):
     _, block, depth = keep.shape
-    width = weight.shape[1]
     return pl.pallas_call(
-        functools.partial(project_kernel, other),
+        functools.partial(project_kernel, other, start),
         out_shape=jax.ShapeDtypeStruct((block, width), BF16 if other else F32),
         compiler_params=pltpu.CompilerParams(vmem_limit_bytes=20 * MIB),
         cost_estimate=pl.CostEstimate(
@@ -429,6 +431,25 @@
         ),
         name="project",
     )(keep, got, weight, weight2)
+
+
+def add_kernel(mine_ref, theirs_ref, *refs):
+    refs[-1][...] = (mine_ref[...] + theirs_ref[...].astype(F32)).astype(BF16)
+
+
+def add_part(index, parts, mine, theirs, earlier):
+    block, width = mine.shape
+    here = pl.BlockSpec(memory_space=pltpu.VMEM)
+    return pl.pallas_call(
+        add_kernel,
+        grid=(1,),
+        in_specs=[here, here] + [pl.BlockSpec(memory_space=pl.ANY)] * len(earlier),
+        out_specs=pl.BlockSpec((block, width), lambda i: (0, index)),
+        out_shape=jax.ShapeDtypeStruct((block, width * parts), BF16),
+        input_output_aliases={2: 0} if earlier else {},
+        compiler_params=pltpu.CompilerParams(vmem_limit_bytes=8 * MIB),
+        name="add_part",
+    )(mine, theirs, *earlier)
 
 
 def swap(x, axis, bit):
@@ -467,9 +488,16 @@
     entering = [keep] + [swap(x, "seq", r) for r, x in enumerate(sends[: heads - 1], 1)]
     keep, away = apply((rows0, rows1), entering, lax.axis_size("head"))
     got = swap(away, "head", 1)
-    theirs = swap(project(True, keep, got, out_weight, weight2), "head", 2)
-    mine = project(False, keep, got, out_weight, weight2)
-    return (mine + theirs.astype(F32)).astype(BF16)
+    parts = 2
+    width = out_weight.shape[1] // parts
+    ranges = [(i * width, width) for i in range(parts)]
+    args = (keep, got, out_weight, weight2)
+    theirs = [swap(project(True, *x, *args), "head", 2) for x in ranges]
+    mine = [project(False, *x, *args) for x in ranges]
+    mixed = []
+    for i in range(parts):
+        mixed = [add_part(i, parts, mine[i], theirs[i], mixed)]
+    return mixed[0]
 
 
 def solution(mesh):

time: 47.8 us -> 47.7 us (level)
  Pallas kernels: 14.9 us -> 17.2 us
  waiting for transfers between devices: 19.4 us -> 17.2 us
  other arithmetic: 0.9 us -> 0 us
  starting transfers between devices: 12.4 us -> 13 us
    ppermute x10 -> x11, waiting for transfers between devices: 19.4 us -> 17.2 us  [swap(): return lax.ppermute(x, axis, [(i, i ^ bit) for i in range(count)])]
    pallas_call x2 -> x6, Pallas kernels: 1.43 us -> 3.27 us  [the longest x4 1.78 us: project(): pl.pallas_call(functools.partial(project_kernel, other, start), out_shape...]
    convert_element_type x1 -> x0, other arithmetic: 0.9 us -> none  [body(): return (mine + theirs.astype(F32)).astype(BF16)]
    ppermute x10 -> x11, starting transfers between devices: 12.4 us -> 13 us  [swap(): return lax.ppermute(x, axis, [(i, i ^ bit) for i in range(count)])]
  transfers between devices with their start and end apart: 10 -> 11, of which waited for: 6 -> 7; matrix products, arithmetic and copies ran while one was open for 0% -> 0% of each run, Pallas kernels for 30% -> 34%
where the time goes in v10:
time: 47.7 us; the launch traced here: 47.5 us
  Pallas kernels  17.2 us (36%)
  waiting for transfers between devices  17.2 us (36%)
  starting transfers between devices  13 us (27%)
    ppermute x11, waiting for transfers between devices, swap(): return lax.ppermute(x, axis, [(i, i ^ bit) for i in range(count)])  17.2 us
    ppermute x11, starting transfers between devices, swap(): return lax.ppermute(x, axis, [(i, i ^ bit) for i in range(count)])  13 us
    pallas_call x1, Pallas kernels, local_maps(): pl.pallas_call(functools.partial(local_maps_kernel, heads, batch), in_spe...  7.42 us
    pallas_call x2, Pallas kernels, row_maps(): pl.pallas_call(functools.partial(rows_kernel, heads, mine), in_specs=[her...  3.4 us
    pallas_call x3, Pallas kernels, small_call(): pl.pallas_call(kernel, in_specs=[here] * len(args), out_specs=[here] * le...  2.63 us
    pallas_call x4, Pallas kernels, project(): pl.pallas_call(functools.partial(project_kernel, other, start), out_shape...  1.78 us
    pallas_call x2, Pallas kernels, add_part(): pl.pallas_call(add_kernel, grid=(1,), in_specs=[here, here] + [pl.BlockSp...  1.5 us
  transfers between devices with their start and end apart: 11, of which 7 were waited for; matrix products, arithmetic and copies ran while one was open for 0% of the time, Pallas kernels for 34%

profile of v10, /device:TPU:0, one launch (start us, length us, event | category | flops | bytes accessed | tf_op | source)
XLA Modules:
  0.0 47.5 jit_solution(1960979514550558811)
XLA Ops:
  0.0 0.5 collective-permute-start.8
  0.5 7.4 %local_maps.1 = (bf16[2048,128]{1,0:T(8,128)(2,1)S(1)}, f32[2048,128]{1,0:T(8,128)S(1)}, f32[16,128]{1,0:T(8,128)S(1)}, f32[16,128,128]{2,1,0:T(8,128)S(1)}, f32...) custom-call(bf16[2048,128]{1,0:T(8,128)(2,1)} %bitcast.3, ...), custom_call_target="tpu_custom_call" | custom-call | tf_op jit(solution)/shard_map/local_maps/pallas_call | solution.py:227
  7.9 2.6 %collective-permute-start = (bf16[128,256]{1,0:T(8,128)(2,1)S(1)}, bf16[128,256]{1,0:T(8,128)(2,1)S(1)}, u32[]{:S(2)}, u32[]{:S(2)}) collective-permute-start(bf16[128,256]{1,0:T(8,128)(2,1)S(1)} %get-tuple-element.40), channel_id=1, source_target_pairs={{0,4},{4,0},{8,12},{12,8},{16,20},{20,16},{24,28},{28,24},{1,5},{5... | collective-permute-start | bytes 196616 | tf_op jit(solution)/shard_map/ppermute | solution.py:457
  10.4 1.6 %collective-permute-start.1 = (bf16[128,256]{1,0:T(8,128)(2,1)S(1)}, bf16[128,256]{1,0:T(8,128)(2,1)S(1)}, u32[]{:S(2)}, u32[]{:S(2)}) collective-permute-start(bf16[128,256]{1,0:T(8,128)(2,1)S(1)} %get-tuple-element.41), channel_id=1, source_target_pairs={{0,8},{4,12},{8,0},{12,4},{16,24},{20,28},{24,16},{28,20},{1,9},{5... | collective-permute-start | bytes 196616 | tf_op jit(solution)/shard_map/ppermute | solution.py:457
  12.0 1.7 %row_maps.2.rows0_ref = f32[2,512,256]{2,1,0:T(8,128)S(1)} custom-call(bf16[2048,128]{1,0:T(8,128)(2,1)S(1)} %get-tuple-element.34.q16, f32[2048,128]{1,0:T(8,128)S(1)} %get-tuple-element.35.k32, f32[16,128]{1,0:T(8,128)S(1)} %get-tuple-element.36.sums_ref, f32[16,128,128]{2,1,0:T(8,128)S(1)} %get-tuple-element.37.mix_ref, ...), custom_call_target="tpu_custom_call" | custom-call | flops 2000000000 | bytes 8000000 | tf_op jit(solution)/shard_map/row_maps/pallas_call | solution.py:280
  13.7 1.2 %collective-permute-done.1.refs_1_ = bf16[128,256]{1,0:T(8,128)(2,1)S(1)} collective-permute-done((bf16[128,256]{1,0:T(8,128)(2,1)S(1)}, bf16[128,256]{1,0:T(8,128)(2,1)S(1)}, u32[]{:S(2)}, u32[]{:S(2)}) %collective-permute-start.1) | collective-permute-done | bytes 65568 | tf_op jit(solution)/shard_map/ppermute | solution.py:457
  15.0 2.2 %collective-permute-done.2.refs_2_ = bf16[128,256]{1,0:T(8,128)(2,1)S(1)} collective-permute-done((bf16[128,256]{1,0:T(8,128)(2,1)S(1)}, bf16[128,256]{1,0:T(8,128)(2,1)S(1)}, u32[]{:S(2)}, u32[]{:S(2)}) %collective-permute-start.2) | collective-permute-done | bytes 65568 | tf_op jit(solution)/shard_map/ppermute | solution.py:457
  17.2 0.5 %group_state.1 = (f32[4,128,256]{2,1,0:T(8,128)S(1)}, bf16[128,128]{1,0:T(8,128)(2,1)S(1)}) custom-call(f32[128,256]{1,0:T(8,128)S(1)} %get-tuple-element.44.own_ref, bf16[128,256]{1,0:T(8,128)(2,1)S(1)} %collective-permute-done.refs_0_, bf16[128,256]{1,0:T(8,128)(2,1)S(1)} %collective-permute-done.1.refs_1_, bf16[128,256]{1,0:T(8,128)(2,1)S(1)} %collective-permute-done.2.refs_2_), custom_call_target="tpu_custom_call" | custom-call | tf_op jit(solution)/shard_map/group_state/pallas_call | solution.py:294
  17.7 2.7 %collective-permute-start.3 = (bf16[128,128]{1,0:T(8,128)(2,1)S(1)}, bf16[128,128]{1,0:T(8,128)(2,1)S(1)}, u32[]{:S(2)}, u32[]{:S(2)}) collective-permute-start(bf16[128,128]{1,0:T(8,128)(2,1)S(1)} %get-tuple-element.52), channel_id=1, source_target_pairs={{0,16},{4,20},{8,24},{12,28},{16,0},{20,4},{24,8},{28,12},{1,17},{... | collective-permute-start | bytes 98312 | tf_op jit(solution)/shard_map/ppermute | solution.py:457
  20.3 1.2 %group_prefix.1 = (bf16[4,128,128]{2,1,0:T(8,128)(2,1)S(1)}, bf16[4,128,128]{2,1,0:T(8,128)(2,1)S(1)}, f32[4,128,128]{2,1,0:T(8,128)S(1)}, bf16[128,256]{1,0:T(8,128)(2,1)}) custom-call(f32[4,128,256]{2,1,0:T(8,128)S(1)} %get-tuple-element.48.held), custom_call_target="tpu_custom_call" | custom-call | tf_op jit(solution)/shard_map/group_prefix/pallas_call | solution.py:294
  21.6 1.3 %collective-permute-done.3.refs_3_ = bf16[128,128]{1,0:T(8,128)(2,1)S(1)} collective-permute-done((bf16[128,128]{1,0:T(8,128)(2,1)S(1)}, bf16[128,128]{1,0:T(8,128)(2,1)S(1)}, u32[]{:S(2)}, u32[]{:S(2)}) %collective-permute-start.3) | collective-permute-done | bytes 32800 | tf_op jit(solution)/shard_map/ppermute | solution.py:457
  22.8 0.9 %states_of_upper.1 = (bf16[128,128]{1,0:T(8,128)(2,1)S(1)}, bf16[128,128]{1,0:T(8,128)(2,1)S(1)}, bf16[128,128]{1,0:T(8,128)(2,1)S(1)}, bf16[128,128]{1,0:T(8,128)(2,1)S(1)}, bf16[4,128,128]{2,1,0:T(8,128)(2,1)}) custom-call(bf16[4,128,128]{2,1,0:T(8,128)(2,1)S(1)} %get-tuple-element.53.refs_0_, bf16[4,128,128]{2,1,0:T(8,128)(2,1)S(1)} %get-tuple-element.54.refs_1_, ...), custom_call_target="tpu_custom_call" | custom-call | tf_op jit(solution)/shard_map/states_of_upper/pallas_call | solution.py:294
  24.0 1.4 %collective-permute-start.5 = (bf16[128,128]{1,0:T(8,128)(2,1)S(1)}, bf16[128,128]{1,0:T(8,128)(2,1)S(1)}, u32[]{:S(2)}, u32[]{:S(2)}) collective-permute-start(bf16[128,128]{1,0:T(8,128)(2,1)S(1)} %get-tuple-element.59), channel_id=1, source_target_pairs={{0,8},{4,12},{8,0},{12,4},{16,24},{20,28},{24,16},{28,20},{1,9},{5... | collective-permute-start | bytes 98312 | tf_op jit(solution)/shard_map/ppermute | solution.py:457
  25.4 1.8 %collective-permute-start.6 = (bf16[128,128]{1,0:T(8,128)(2,1)S(1)}, bf16[128,128]{1,0:T(8,128)(2,1)S(1)}, u32[]{:S(2)}, u32[]{:S(2)}) collective-permute-start(bf16[128,128]{1,0:T(8,128)(2,1)S(1)} %get-tuple-element.60), channel_id=1, source_target_pairs={{0,12},{4,8},{8,4},{12,0},{16,28},{20,24},{24,20},{28,16},{1,13},{... | collective-permute-start | bytes 98312 | tf_op jit(solution)/shard_map/ppermute | solution.py:457
  27.2 1.7 %row_maps.3.rows1_ref = f32[2,512,256]{2,1,0:T(8,128)S(1)} custom-call(bf16[2048,128]{1,0:T(8,128)(2,1)S(1)} %get-tuple-element.34.q16, f32[2048,128]{1,0:T(8,128)S(1)} %get-tuple-element.35.k32, f32[16,128]{1,0:T(8,128)S(1)} %get-tuple-element.36.sums_ref, f32[16,128,128]{2,1,0:T(8,128)S(1)} %get-tuple-element.37.mix_ref, ...), custom_call_target="tpu_custom_call" | custom-call | flops 2000000000 | bytes 8000000 | tf_op jit(solution)/shard_map/row_maps/pallas_call | solution.py:280
  29.0 1.2 %collective-permute-done.6.refs_3_ = bf16[128,128]{1,0:T(8,128)(2,1)S(1)} collective-permute-done((bf16[128,128]{1,0:T(8,128)(2,1)S(1)}, bf16[128,128]{1,0:T(8,128)(2,1)S(1)}, u32[]{:S(2)}, u32[]{:S(2)}) %collective-permute-start.6) | collective-permute-done | bytes 32800 | tf_op jit(solution)/shard_map/ppermute | solution.py:457
  30.7 1.5 %collective-permute-done.7.got_ref = bf16[2,128,512]{2,1,0:T(8,128)(2,1)S(1)} collective-permute-done((bf16[2,128,512]{2,1,0:T(8,128)(2,1)S(1)}, bf16[2,128,512]{2,1,0:T(8,128)(2,1)S(1)}, u32[]{:S(2)}, u32[]{:S(2)}) %collective-permute-start.7) | collective-permute-done | bytes 262176 | tf_op jit(solution)/shard_map/ppermute | solution.py:457
  32.3 0.4 project.7
  32.7 1.6 %collective-permute-start.10 = (bf16[128,1024]{1,0:T(8,128)(2,1)S(1)}, bf16[128,1024]{1,0:T(8,128)(2,1)S(1)}, u32[]{:S(2)}, u32[]{:S(2)}) collective-permute-start(bf16[128,1024]{1,0:T(8,128)(2,1)S(1)} %project.7), channel_id=1, source_target_pairs={{0,2},{1,3},{2,0},{3,1},{4,6},{5,7},{6,4},{7,5},{8,10},{9,11},{10,... | collective-permute-start | bytes 786440 | tf_op jit(solution)/shard_map/ppermute | solution.py:457
  34.8 0.6 %collective-permute-start.9 = (bf16[128,1024]{1,0:T(8,128)(2,1)S(1)}, bf16[128,1024]{1,0:T(8,128)(2,1)S(1)}, u32[]{:S(2)}, u32[]{:S(2)}) collective-permute-start(bf16[128,1024]{1,0:T(8,128)(2,1)S(1)} %project.5), channel_id=1, source_target_pairs={{0,2},{1,3},{2,0},{3,1},{4,6},{5,7},{6,4},{7,5},{8,10},{9,11},{10,... | collective-permute-start | bytes 786440 | tf_op jit(solution)/shard_map/ppermute | solution.py:457
  36.2 5.7 %collective-permute-done.10.theirs_ref = bf16[128,1024]{1,0:T(8,128)(2,1)S(1)} collective-permute-done((bf16[128,1024]{1,0:T(8,128)(2,1)S(1)}, bf16[128,1024]{1,0:T(8,128)(2,1)S(1)}, u32[]{:S(2)}, u32[]{:S(2)}) %collective-permute-start.10) | collective-permute-done | bytes 262176 | tf_op jit(solution)/shard_map/ppermute | solution.py:457
  41.9 0.7 %add_part.2.refs_0_ = bf16[128,2048]{1,0:T(8,128)(2,1)} custom-call(f32[128,1024]{1,0:T(8,128)S(1)} %project.6.mine_ref, bf16[128,1024]{1,0:T(8,128)(2,1)S(1)} %collective-permute-done.10.theirs_ref), custom_call_target="tpu_custom_call" | custom-call | tf_op jit(solution)/shard_map/add_part/pallas_call | solution.py:443
  42.7 4.1 %collective-permute-done.9.theirs_ref = bf16[128,1024]{1,0:T(8,128)(2,1)S(1)} collective-permute-done((bf16[128,1024]{1,0:T(8,128)(2,1)S(1)}, bf16[128,1024]{1,0:T(8,128)(2,1)S(1)}, u32[]{:S(2)}, u32[]{:S(2)}) %collective-permute-start.9) | collective-permute-done | bytes 262176 | tf_op jit(solution)/shard_map/ppermute | solution.py:457
  46.8 0.7 %add_part.3 = bf16[128,2048]{1,0:T(8,128)(2,1)} custom-call(f32[128,1024]{1,0:T(8,128)S(1)} %project.4.mine_ref, bf16[128,1024]{1,0:T(8,128)(2,1)S(1)} %collective-permute-done.9.theirs_ref, bf16[128,2048]{1,0:T(8,128)(2,1)} %add_part.2.refs_0_), custom_call_target="tpu_custom_call", output_to_operand_aliasing={{}: (2, {})} | custom-call | tf_op jit(solution)/shard_map/add_part/pallas_call | solution.py:443
  (13 shorter events, 2.1 us)
Async XLA Ops:
  0.0 32.3 %collective-permute-start.8 = (bf16[512,2048]{1,0:T(8,128)(2,1)}, bf16[512,2048]{1,0:T(8,128)(2,1)S(1)}, u32[]{:S(2)}, u32[]{:S(2)}) collective-permute-start(bf16[512,2048]{1,0:T(8,128)(2,1)} %w_ref.7), channel_id=1, source_target_pairs={{0,1},{1,0},{2,3},{3,2},{4,5},{5,4},{6,7},{7,6},{8,9},{9,8},{10,11... | collective-permute-start | bytes 6291464 | tf_op jit(solution)/shard_map/ppermute | solution.py:457
  7.9 5.8 %collective-permute-start = (bf16[128,256]{1,0:T(8,128)(2,1)S(1)}, bf16[128,256]{1,0:T(8,128)(2,1)S(1)}, u32[]{:S(2)}, u32[]{:S(2)}) collective-permute-start(bf16[128,256]{1,0:T(8,128)(2,1)S(1)} %get-tuple-element.40), channel_id=1, source_target_pairs={{0,4},{4,0},{8,12},{12,8},{16,20},{20,16},{24,28},{28,24},{1,5},{5... | collective-permute-start | bytes 196616 | tf_op jit(solution)/shard_map/ppermute | solution.py:457
  10.4 4.5 %collective-permute-start.1 = (bf16[128,256]{1,0:T(8,128)(2,1)S(1)}, bf16[128,256]{1,0:T(8,128)(2,1)S(1)}, u32[]{:S(2)}, u32[]{:S(2)}) collective-permute-start(bf16[128,256]{1,0:T(8,128)(2,1)S(1)} %get-tuple-element.41), channel_id=1, source_target_pairs={{0,8},{4,12},{8,0},{12,4},{16,24},{20,28},{24,16},{28,20},{1,9},{5... | collective-permute-start | bytes 196616 | tf_op jit(solution)/shard_map/ppermute | solution.py:457
  12.0 5.2 %collective-permute-start.2 = (bf16[128,256]{1,0:T(8,128)(2,1)S(1)}, bf16[128,256]{1,0:T(8,128)(2,1)S(1)}, u32[]{:S(2)}, u32[]{:S(2)}) collective-permute-start(bf16[128,256]{1,0:T(8,128)(2,1)S(1)} %get-tuple-element.42), channel_id=1, source_target_pairs={{0,12},{4,8},{8,4},{12,0},{16,28},{20,24},{24,20},{28,16},{1,13},{... | collective-permute-start | bytes 196616 | tf_op jit(solution)/shard_map/ppermute | solution.py:457
  17.7 5.1 %collective-permute-start.3 = (bf16[128,128]{1,0:T(8,128)(2,1)S(1)}, bf16[128,128]{1,0:T(8,128)(2,1)S(1)}, u32[]{:S(2)}, u32[]{:S(2)}) collective-permute-start(bf16[128,128]{1,0:T(8,128)(2,1)S(1)} %get-tuple-element.52), channel_id=1, source_target_pairs={{0,16},{4,20},{8,24},{12,28},{16,0},{20,4},{24,8},{28,12},{1,17},{... | collective-permute-start | bytes 98312 | tf_op jit(solution)/shard_map/ppermute | solution.py:457
  23.7 5.2 %collective-permute-start.4 = (bf16[128,128]{1,0:T(8,128)(2,1)S(1)}, bf16[128,128]{1,0:T(8,128)(2,1)S(1)}, u32[]{:S(2)}, u32[]{:S(2)}) collective-permute-start(bf16[128,128]{1,0:T(8,128)(2,1)S(1)} %get-tuple-element.58), channel_id=1, source_target_pairs={{0,4},{4,0},{8,12},{12,8},{16,20},{20,16},{24,28},{28,24},{1,5},{5... | collective-permute-start | bytes 98312 | tf_op jit(solution)/shard_map/ppermute | solution.py:457
  24.0 5.0 %collective-permute-start.5 = (bf16[128,128]{1,0:T(8,128)(2,1)S(1)}, bf16[128,128]{1,0:T(8,128)(2,1)S(1)}, u32[]{:S(2)}, u32[]{:S(2)}) collective-permute-start(bf16[128,128]{1,0:T(8,128)(2,1)S(1)} %get-tuple-element.59), channel_id=1, source_target_pairs={{0,8},{4,12},{8,0},{12,4},{16,24},{20,28},{24,16},{28,20},{1,9},{5... | collective-permute-start | bytes 98312 | tf_op jit(solution)/shard_map/ppermute | solution.py:457
  25.4 4.8 %collective-permute-start.6 = (bf16[128,128]{1,0:T(8,128)(2,1)S(1)}, bf16[128,128]{1,0:T(8,128)(2,1)S(1)}, u32[]{:S(2)}, u32[]{:S(2)}) collective-permute-start(bf16[128,128]{1,0:T(8,128)(2,1)S(1)} %get-tuple-element.60), channel_id=1, source_target_pairs={{0,12},{4,8},{8,4},{12,0},{16,28},{20,24},{24,20},{28,16},{1,13},{... | collective-permute-start | bytes 98312 | tf_op jit(solution)/shard_map/ppermute | solution.py:457
  28.9 3.3 %copy-start = (bf16[512,2048]{1,0:T(8,128)(2,1)S(1)}, bf16[512,2048]{1,0:T(8,128)(2,1)}, u32[]{:S(2)}) copy-start(bf16[512,2048]{1,0:T(8,128)(2,1)} %w_ref.7) | copy-start | bytes 6291460
  30.7 1.6 %collective-permute-start.7 = (bf16[2,128,512]{2,1,0:T(8,128)(2,1)S(1)}, bf16[2,128,512]{2,1,0:T(8,128)(2,1)S(1)}, u32[]{:S(2)}, u32[]{:S(2)}) collective-permute-start(bf16[2,128,512]{2,1,0:T(8,128)(2,1)S(1)} %get-tuple-element.62), channel_id=1, source_target_pairs={{0,1},{1,0},{2,3},{3,2},{4,5},{5,4},{6,7},{7,6},{8,9},{9,8},{10,11... | collective-permute-start | bytes 786440 | tf_op jit(solution)/shard_map/ppermute | solution.py:457
  32.7 9.2 %collective-permute-start.10 = (bf16[128,1024]{1,0:T(8,128)(2,1)S(1)}, bf16[128,1024]{1,0:T(8,128)(2,1)S(1)}, u32[]{:S(2)}, u32[]{:S(2)}) collective-permute-start(bf16[128,1024]{1,0:T(8,128)(2,1)S(1)} %project.7), channel_id=1, source_target_pairs={{0,2},{1,3},{2,0},{3,1},{4,6},{5,7},{6,4},{7,5},{8,10},{9,11},{10,... | collective-permute-start | bytes 786440 | tf_op jit(solution)/shard_map/ppermute | solution.py:457
  34.8 12.0 %collective-permute-start.9 = (bf16[128,1024]{1,0:T(8,128)(2,1)S(1)}, bf16[128,1024]{1,0:T(8,128)(2,1)S(1)}, u32[]{:S(2)}, u32[]{:S(2)}) collective-permute-start(bf16[128,1024]{1,0:T(8,128)(2,1)S(1)} %project.5), channel_id=1, source_target_pairs={{0,2},{1,3},{2,0},{3,1},{4,6},{5,7},{6,4},{7,5},{8,10},{9,11},{10,... | collective-permute-start | bytes 786440 | tf_op jit(solution)/shard_map/ppermute | solution.py:457

commit v11 on v9

v11 whole, which is shorter than its diff:
```python
import functools

import jax
import jax.numpy as jnp
from jax import lax
from jax.experimental import pallas as pl
from jax.experimental.pallas import tpu as pltpu
from jax.sharding import PartitionSpec as P

C = 128
B = 16
F32 = jnp.float32
BF16 = jnp.bfloat16
NN = (((1,), (0,)), ((), ()))
NT = (((1,), (1,)), ((), ()))
TN = (((0,), (0,)), ((), ()))
MIB = 1024 * 1024


def dot(a, b, dims=NN):
    return lax.dot_general(a, b, dims, preferred_element_type=F32)


def split(x):
    high = x.astype(BF16)
    return high, (x - high.astype(F32)).astype(BF16)


def twice(x):
    return jnp.concatenate([x, x], axis=0)


def dot3(a, b):
    (ah, al), (bh, bl) = a, b
    width = bh.shape[1]
    left = jnp.concatenate([ah, al], axis=1)
    if width > C:
        return dot(left, twice(bh)) + dot(ah, bl)
    both = dot(left, twice(jnp.concatenate([bh, bl], axis=1)))
    return both[:, :width] + both[:, width:]


def iotas():
    return (
        lax.broadcasted_iota(jnp.int32, (C, C), 0),
        lax.broadcasted_iota(jnp.int32, (C, C), 1),
    )


def to_column(row, eye):
    return jnp.sum(jnp.where(eye, row, 0.0), axis=1, keepdims=True)


def to_row(column, eye):
    return jnp.sum(jnp.where(eye, column, 0.0), axis=0, keepdims=True)


def inverse_scale(rows):
    return lax.rsqrt(jnp.sum(rows * rows, axis=1, keepdims=True) + 1e-06)


def three(x):
    high, rest = x.astype(BF16), x
    rest = rest - high.astype(F32)
    return (high,) + split(rest)


def running_sums(rows, upper):
    return sum(dot(x, upper) for x in reversed(three(rows)))


def spread_columns(row, eye, ones):
    parts = three(jnp.broadcast_to(row, (16, C)))
    high, middle, low = (
        jnp.where(eye, jnp.concatenate([x] * (C // 16), axis=0), jnp.zeros((), BF16)) for x in parts
    )
    return dot(jnp.concatenate([high, middle], axis=1), twice(ones)) + dot(low, ones)


def base_inverse(lower, row, col):
    on_block = (row // B) == (col // B)
    blocks = jnp.where(on_block, lower, 0.0)
    packed = sum(blocks[i * B : (i + 1) * B] for i in range(1, C // B)) + blocks[:B]
    r, c = row[:B], col[:B]
    found = jnp.where(r == c % B, 1.0, 0.0)
    first = (c // B) * B
    for j in range(B - 1):
        factor = jnp.take_along_axis(packed, first + j, axis=1)
        found = found - factor * found[j : j + 1]
    return jnp.where(on_block, jnp.concatenate([found] * (C // B), axis=0), 0.0)


def odd_rows(x, size):
    return jnp.concatenate([x[i : i + size] for i in range(size, C, 2 * size)], axis=0)


def weave(even, odd, size):
    parts = []
    for i in range(0, C // 2, size):
        parts += [even[i : i + size], odd[i : i + size]]
    return jnp.concatenate(parts, axis=0)


def even_rows(x, size):
    return jnp.concatenate([x[i : i + size] for i in range(0, C, 2 * size)], axis=0)


def inverses(lowers, row, col):
    found = [base_inverse(a, row, col) for a in lowers]
    parts = [split(a) for a in lowers]
    halves = [split(x) for x in found]
    size = B
    while size < C:
        r, c = odd_rows(row, size), odd_rows(col, size)
        mask = ((r // (2 * size)) == (c // (2 * size))) & ((r // size) != (c // size))
        nothing = jnp.zeros((C // 2, C), BF16)
        joins = [tuple(jnp.where(mask, odd_rows(x, size), nothing) for x in part) for part in parts]
        middle = [split(dot3(a, x)) for a, x in zip(joins, halves)]
        middle = [tuple(weave(nothing, x, size) for x in part) for part in middle]
        lows = [dot3(tuple(odd_rows(x, size) for x in h), y) for h, y in zip(halves, middle)]
        lows = [odd_rows(x, size) - y for x, y in zip(found, lows)]
        found = [weave(even_rows(x, size), y, size) for x, y in zip(found, lows)]
        if 2 * size < C:
            halves = [
                tuple(weave(even_rows(x, size), y, size) for x, y in zip(h, split(low)))
                for h, low in zip(halves, lows)
            ]
        size *= 2
    return found


def fetch(pairs, sems, late):
    copies = [pltpu.make_async_copy(x, y, sems.at[i]) for i, (x, y) in enumerate(pairs)]
    for copy in copies:
        copy.start()
    late.start()
    for copy in copies:
        copy.wait()


def in_hbm(*arrays):
    return [pltpu.with_memory_space_constraint(x, pltpu.HBM) for x in arrays]


def chunk_rows(heads, head, c):
    return pl.ds(c * C * heads + head, C, stride=heads)


def tokens_of(ref, head, c):
    return ref[head : head + 1, c * C : (c + 1) * C]


def per_chunk(ref):
    return jnp.concatenate([ref[:, i : i + C] for i in range(0, ref.shape[1], C)], axis=0)


def local_maps_kernel(
    heads, k_hbm, v_hbm, beta_hbm, log_hbm, q_hbm, q16, k32, sums_ref, mix_ref, wu_ref, n_ref, send_ref,
    k16, v16, v32, beta_ref, log_ref, sems,
):
    late = pltpu.make_async_copy(q_hbm, q16, sems.at[4])
    fetch(((k_hbm, k16), (log_hbm, log_ref), (beta_hbm, beta_ref), (v_hbm, v16)), sems, late)
    k32[...] = k16[...].astype(F32)
    v32[...] = v16[...].astype(F32)
    chunks = beta_ref.shape[1] // C
    row, col = iotas()
    eye = row == col
    within = row >= col
    strict = row > col
    one = jnp.ones((C, C), BF16)
    eye16 = jnp.where(eye, one, jnp.zeros((), BF16))
    sums = running_sums(per_chunk(log_ref), jnp.where(row <= col, one, jnp.zeros((), BF16)))
    sums_ref[...] = sums
    grown = jnp.exp(sums)
    faded = jnp.exp(sums[:, C - 1 :] - sums)
    betas = per_chunk(beta_ref)
    jobs = [(head, c) for head in range(heads) for c in range(chunks)]
    spots = [slice(c * heads + head, c * heads + head + 1) for head, c in jobs]
    lowers, raws, values, fades, lengths = [], [], [], [], []
    for i, (head, c) in enumerate(jobs):
        raw = k32[chunk_rows(heads, head, c), :].astype(BF16)
        raws.append(raw)
        values.append(v32[chunk_rows(heads, head, c), :].astype(BF16))
        both = dot(jnp.concatenate([raw, eye16], axis=0), raw, NT)
        gram, turned = both[:C], both[C:]
        square = to_row(gram, eye) + 1e-06
        scale = lax.rsqrt(square)
        lengths.append(square * scale)
        strength = betas[spots[i]] * (scale * scale)
        span = spread_columns(sums[spots[i]], eye, one) - sums[spots[i]]
        mix = jnp.where(within, jnp.exp(span), 0.0) * strength
        mix_ref[i] = mix
        lowers.append(jnp.where(strict, gram * mix, 0.0))
        fades.append(turned * (strength * faded[spots[i]]))
    solved = []
    for i, found in enumerate(inverses(lowers, row, col)):
        kept = dot(jnp.concatenate(split(found * grown[spots[i]]), axis=1), twice(raws[i]))
        fresh = dot(jnp.concatenate(split(found * lengths[i]), axis=1), twice(values[i]))
        solved.append(jnp.concatenate([kept, fresh], axis=1))
    maps = []
    for i in range(len(jobs)):
        wu_ref[i] = solved[i]
        both = dot3(split(fades[i]), split(solved[i]))
        maps.append((jnp.where(eye, grown[spots[i], C - 1 :], 0.0) - both[:, :C], both[:, C:]))
    place = lax.rem(lax.axis_index("seq"), heads)
    for head in range(heads):
        state = jnp.concatenate(maps[head * chunks], axis=1)
        for c in range(1, chunks):
            n_ref[head * chunks + c] = state
            moved, fresh = maps[head * chunks + c]
            state = dot3(split(moved), split(state))
            state = jnp.concatenate([state[:, :C], state[:, C:] + fresh], axis=1)
        send_ref[other_place(place, head, heads)] = state.astype(BF16)
    late.wait()


def other_place(place, r, heads):
    result = place
    for i in range(heads):
        result = jnp.where(place == i, i ^ r, result)
    return result


def local_maps(key, value, beta, log_decay, query):
    heads, tokens = beta.shape
    count = heads * (tokens // C)
    here = pl.BlockSpec(memory_space=pltpu.VMEM)
    return pl.pallas_call(
        functools.partial(local_maps_kernel, heads),
        in_specs=[pl.BlockSpec(memory_space=pltpu.HBM)] * 5,
        out_specs=[here] * 7,
        out_shape=[
            jax.ShapeDtypeStruct(query.shape, BF16),
            jax.ShapeDtypeStruct(key.shape, F32),
            jax.ShapeDtypeStruct((count, C), F32),
            jax.ShapeDtypeStruct((count, C, C), F32),
            jax.ShapeDtypeStruct((count, C, 2 * C), F32),
            jax.ShapeDtypeStruct((count, C, 2 * C), F32),
            jax.ShapeDtypeStruct((heads, C, 2 * C), BF16),
        ],
        scratch_shapes=[
            pltpu.VMEM(key.shape, BF16),
            pltpu.VMEM(key.shape, BF16),
            pltpu.VMEM(key.shape, F32),
            pltpu.VMEM(beta.shape, F32),
            pltpu.VMEM(beta.shape, F32),
            pltpu.SemaphoreType.DMA((5,)),
        ],
        compiler_params=pltpu.CompilerParams(vmem_limit_bytes=32 * MIB),
        name="local_maps",
    )(*in_hbm(key, value, beta, log_decay, query))


def on_core(core):
    return lax.rem(lax.axis_index("head"), 2) == core


def rows_kernel(heads, mine, q16, k32, sums_ref, mix_ref, wu_ref, n_ref, keep_ref, send_ref, q32):
    q32[...] = q16[...].astype(F32)
    chunks = q16.shape[0] // (heads * C)
    row, col = iotas()
    eye = row == col
    for j, head in enumerate(mine):
        for c in range(chunks):
            i = head * chunks + c
            query, raw = q32[chunk_rows(heads, head, c), :], k32[chunk_rows(heads, head, c), :]
            grown = to_column(jnp.exp(sums_ref[c * heads + head : c * heads + head + 1, :]), eye)
            pairs = dot(query.astype(BF16), raw.astype(BF16), NT) * mix_ref[i]
            both = dot3(split(pairs), split(wu_ref[i]))
            scale = inverse_scale(query)
            reach = (query * grown - both[:, :C]) * scale
            fresh = both[:, C:] * scale
            if c > 0:
                earlier = dot3(split(reach), split(n_ref[i]))
                reach = earlier[:, :C]
                fresh = fresh + earlier[:, C:]
            for ref, core in ((keep_ref, c % 2), (send_ref, 1 - c % 2)):

                @pl.when(on_core(core))
                def _(ref=ref, reach=reach, fresh=fresh):
                    ref[c // 2, j, :, :C] = reach
                    ref[c // 2, j, :, C:] = fresh


def row_maps(heads, mine, query, k32, sums, mix, wu, states):
    chunks = query.shape[0] // (heads * C)
    here = pl.BlockSpec(memory_space=pltpu.VMEM)
    out = jax.ShapeDtypeStruct((chunks // 2, len(mine), C, 2 * C), F32)
    return pl.pallas_call(
        functools.partial(rows_kernel, heads, mine),
        in_specs=[here] * 6,
        out_specs=[here] * 2,
        out_shape=[out, out],
        scratch_shapes=[pltpu.VMEM(query.shape, F32)],
        compiler_params=pltpu.CompilerParams(vmem_limit_bytes=16 * MIB),
        cost_estimate=pl.CostEstimate(flops=2000000000, bytes_accessed=8000000, transcendentals=0),
        name="row_maps",
    )(query, k32, sums, mix, wu, states)


def small_call(kernel, out_shape, *args):
    here = pl.BlockSpec(memory_space=pltpu.VMEM)
    return pl.pallas_call(
        kernel,
        in_specs=[here] * len(args),
        out_specs=[here] * len(out_shape),
        out_shape=out_shape,
        compiler_params=pltpu.CompilerParams(vmem_limit_bytes=8 * MIB),
        name=kernel.__name__,
    )(*args)


def moved_on(maps, state16, added):
    high, low = split(maps)
    return dot(jnp.concatenate([high, low], axis=1), twice(state16)) + added


def gather_cores(mine_ref, other_ref, *out_refs):
    for first, second, core in ((mine_ref, other_ref, 0), (other_ref, mine_ref, 1)):

        @pl.when(on_core(core))
        def _(first=first, second=second):
            for r, out_ref in enumerate(out_refs):
                out_ref[0] = first[r]
                out_ref[1] = second[r]


def times_parts(maps16, x):
    width = x.shape[1]
    both = dot(maps16, jnp.concatenate(split(x), axis=1))
    return both[:, :width] + both[:, width:]


def group_state(*refs):
    parts, (held, out_ref) = refs[:-2], refs[-2:]
    heads = len(parts)
    place = lax.rem(lax.axis_index("seq"), heads)
    for r, part in enumerate(parts):
        member = other_place(place, r, heads)
        for g in range(2):
            held[g * heads + member] = part[g]
    for g in range(2):
        state = held[g * heads, :, C:].astype(F32)
        for i in range(g * heads + 1, (g + 1) * heads):
            state = times_parts(held[i, :, :C], state) + held[i, :, C:].astype(F32)
        out_ref[g] = state.astype(BF16)


def group_prefix(held, high_ref, low_ref, added_ref, total_ref):
    heads = held.shape[0] // 2
    row, col = iotas()
    eye = jnp.where(row == col, 1.0, 0.0)
    for g in range(2):
        total = jnp.concatenate([eye, jnp.zeros((C, C), F32)], axis=1)
        for i in range(g * heads, (g + 1) * heads):
            high_ref[i], low_ref[i] = split(total[:, :C])
            added_ref[i] = total[:, C:]
            if i == g * heads:
                total = held[i].astype(F32)
            else:
                total = times_parts(held[i, :, :C], total)
                total = jnp.concatenate([total[:, :C], total[:, C:] + held[i, :, C:].astype(F32)], axis=1)
        total_ref[g] = total.astype(BF16)


def group_states(upper_only, high_ref, low_ref, added_ref, state_ref, *refs):
    outs, states = refs[:-1], refs[-1]
    heads = len(outs)
    for g in range(2):
        state = state_ref[g]
        if upper_only:
            state = jnp.where(lax.axis_index("seq") < heads, jnp.zeros_like(state), state)
        both = twice(state)
        for i in range(g * heads, (g + 1) * heads):
            maps = jnp.concatenate([high_ref[i], low_ref[i]], axis=1)
            states[i] = (dot(maps, both) + added_ref[i]).astype(BF16)
    place = lax.rem(lax.axis_index("seq"), heads)
    for r, out_ref in enumerate(outs):
        member = other_place(place, r, heads)
        for g in range(2):
            out_ref[g] = states[g * heads + member]


def states_of_upper(*refs):
    group_states(True, *refs)


def states_given(*refs):
    group_states(False, *refs)


def gather_heads(*refs):
    parts, out_ref = refs[:-1], refs[-1]
    heads = len(parts)
    place = lax.rem(lax.axis_index("seq"), heads)
    for r, part in enumerate(parts):
        head = other_place(place, r, heads)
        for g in range(2):
            out_ref[g * heads + head] = part[g]


def prefix(total, heads):
    count = lax.axis_size("seq")
    groups = [list(range(i, count, heads)) for i in range(heads)]
    me = lax.axis_index("seq") // heads
    totals = lax.all_gather(total, "seq", axis_index_groups=groups)

    def step(d, state):
        parts = jnp.stack(split(state))
        longer = jnp.einsum("gik,pgkw->giw", totals[d, :, :, :C], parts, preferred_element_type=F32)
        return jnp.where(d < me, longer + totals[d, :, :, C:].astype(F32), state)

    start = jnp.zeros((2, C, C), F32)
    return lax.fori_loop(0, count // heads - 1, step, start).astype(BF16)


def share_of(block, rows, st_ref, w_ref, w2_ref):
    heads = st_ref.shape[0] // 2
    core = lax.rem(lax.axis_index("head"), 2)
    sums = []
    for refs, first, weight in ((rows[:2], core, w_ref), (rows[2:], 1 - core, w2_ref)):
        attended = []
        for h in range(heads):
            ref = refs[h // (heads // 2)]
            state = st_ref[first * heads + h]
            j = h % (heads // 2)
            attended.append(moved_on(ref[block, j, :, :C], state, ref[block, j, :, C:]).astype(BF16))
        sums.append(dot(jnp.concatenate(attended, axis=1), weight[...]))
    return sums[0] + sums[1]


def share_out_kernel(core, rows0, rows1, rows2, rows3, st_ref, w_ref, w2_ref, *refs):
    @pl.when(on_core(core))
    def _():
        block = 1 - lax.axis_index("head") // 2
        refs[-1][...] = share_of(block, (rows0, rows1, rows2, rows3), st_ref, w_ref, w2_ref).astype(BF16)

    if len(refs) > 1:

        @pl.when(on_core(1 - core))
        def _():
            refs[-1][...] = refs[0][...]


def share_out(core, rows, states, weight, weight2, earlier):
    here = pl.BlockSpec(memory_space=pltpu.VMEM)
    width = weight.shape[1]
    return pl.pallas_call(
        functools.partial(share_out_kernel, core),
        in_specs=[here] * (7 + len(earlier)),
        out_specs=here,
        out_shape=jax.ShapeDtypeStruct((C, width), BF16),
        compiler_params=pltpu.CompilerParams(vmem_limit_bytes=16 * MIB),
        cost_estimate=pl.CostEstimate(
            flops=4 * C * weight.size, bytes_accessed=4 * weight.size, transcendentals=0
        ),
        name="share_out",
    )(*rows, states, weight, weight2, *earlier)


def share_here_kernel(rows0, rows1, rows2, rows3, st0_ref, st1_ref, w_ref, w2_ref, out_ref):
    for core, st_ref in ((0, st0_ref), (1, st1_ref)):

        @pl.when(on_core(core))
        def _(st_ref=st_ref):
            block = lax.axis_index("head") // 2
            out_ref[...] = share_of(block, (rows0, rows1, rows2, rows3), st_ref, w_ref, w2_ref)


def share_here(rows, states0, states1, weight, weight2):
    here = pl.BlockSpec(memory_space=pltpu.VMEM)
    return pl.pallas_call(
        share_here_kernel,
        in_specs=[here] * 8,
        out_specs=here,
        out_shape=jax.ShapeDtypeStruct((C, weight.shape[1]), F32),
        compiler_params=pltpu.CompilerParams(vmem_limit_bytes=16 * MIB),
        cost_estimate=pl.CostEstimate(
            flops=4 * C * weight.size, bytes_accessed=4 * weight.size, transcendentals=0
        ),
        name="share_here",
    )(*rows, states0, states1, weight, weight2)


def swap(x, axis, bit):
    count = lax.axis_size(axis)
    return lax.ppermute(x, axis, [(i, i ^ bit) for i in range(count)])


def swap_odd(x, bit):
    count, groups = lax.axis_size("seq"), lax.axis_size("head")
    pairs = [(i * groups + g, (i ^ bit) * groups + g) for i in range(count) for g in range(1, groups, 2)]
    return lax.ppermute(x, ("seq", "head"), pairs)


def hand_back(x):
    return lax.ppermute(x, "head", [(g, g - 1) for g in range(1, lax.axis_size("head"), 2)])


def body(query, key, value, beta, log_decay, out_weight):
    tokens, heads, _ = key.shape
    count = lax.axis_size("seq")
    flat = lambda x: x.reshape(tokens * heads, C)
    weight2 = swap(out_weight, "head", 1)
    q16, k32, *chunk_maps, send = local_maps(flat(key), flat(value), beta, log_decay, flat(query))
    other = swap(send, "head", 1)
    part = jax.ShapeDtypeStruct((2, C, 2 * C), BF16)
    square = jax.ShapeDtypeStruct((2, C, C), BF16)
    squares = jax.ShapeDtypeStruct((2 * heads, C, C), BF16)
    both = jax.ShapeDtypeStruct((2 * heads, C, 2 * C), BF16)
    parts = small_call(gather_cores, [part] * heads, send, other)
    got = [parts[0]] + [swap_odd(x, r) for r, x in enumerate(parts[1:], 1)]
    half = heads // 2
    keep0, away0 = row_maps(heads, range(half), q16, k32, *chunk_maps)
    keep1, away1 = row_maps(heads, range(half, heads), q16, k32, *chunk_maps)
    keep0, got = lax.optimization_barrier((keep0, got))
    held, state = small_call(group_state, [both, square], *got)
    *maps, total = small_call(
        group_prefix, [squares, squares, jax.ShapeDtypeStruct((2 * heads, C, C), F32), part], held
    )
    rows = (keep0, keep1, swap(away0, "head", 1), swap(away1, "head", 1))
    if count == 2 * heads:
        lower = swap_odd(state, heads)
        maps, lower, rows, weight2 = lax.optimization_barrier((maps, lower, rows, weight2))
        sends = small_call(states_of_upper, [square] * heads + [squares], *maps, lower)
    else:
        sends = small_call(states_given, [square] * heads + [squares], *maps, prefix(total, heads))
    got = [sends[0]] + [swap_odd(x, r) for r, x in enumerate(sends[1:heads], 1)]
    (states1,) = small_call(gather_heads, [squares], *got)
    states0 = hand_back(states1)
    theirs = share_out(1, rows, states1, out_weight, weight2, [])
    theirs = share_out(0, rows, states0, out_weight, weight2, [theirs])
    theirs = swap(theirs, "head", 2)
    mine = share_here(rows, states0, states1, out_weight, weight2)
    return (mine + theirs.astype(F32)).astype(BF16)


def solution(mesh):
    in_specs = (
        P("seq", "head", None),
        P("seq", "head", None),
        P("seq", "head", None),
        P("head", "seq"),
        P("head", "seq"),
        P("head", None),
    )
    out_specs = P(("seq", "head"), None)
    return jax.shard_map(body, mesh=mesh, in_specs=in_specs, out_specs=out_specs, check_vma=False)
```

time: 62.6 us -> 66.4 us (1.061)
  waiting for transfers between devices: 12.7 us -> 36.5 us
  local copies, waits for them, and re-layouts: 11.5 us -> 0.01 us
  blocking collectives: 11 us -> 0 us
  Pallas kernels: 18 us -> 19.6 us
  starting transfers between devices: 8.09 us -> 8.88 us
    ppermute x0 -> x8, waiting for transfers between devices: none -> 25.8 us  [the longest x1 25.8 us: hand_back(): lax.ppermute(x, 'head', [(g, g - 1) for g in range(1, lax.axis_size('head...]
    unnamed x22 -> x2, local copies, waits for them, and re-layouts: 11.5 us -> 0.01 us
    all_to_all x1 -> x0, blocking collectives: 11 us -> none  [share_out(): lax.all_to_all(parts, 'seq', 0, 0, axis_index_groups=groups, tiled=True)]
    ppermute x0 -> x8, starting transfers between devices: none -> 6.08 us  [the longest x7 4.79 us: swap_odd(): return lax.ppermute(x, ('seq', 'head'), pairs)]
    pallas_call x2, Pallas kernels: 3.26 us -> 7.35 us  [row_maps(): pl.pallas_call(functools.partial(rows_kernel, heads, mine), in_specs=[her...]
    all_to_all x1 -> x0, starting transfers between devices: 3.32 us -> none  [share_out(): lax.all_to_all(parts, 'seq', 0, 0, axis_index_groups=groups, tiled=True)]
    pallas_call x4, Pallas kernels: 12.1 us -> 8.95 us  [the longest x1 7.07 us: local_maps(): pl.pallas_call(functools.partial(local_maps_kernel, heads), in_specs=[pl....]
    ppermute x4 -> x5, waiting for transfers between devices: 12.6 us -> 10.7 us  [swap(): return lax.ppermute(x, axis, [(i, i ^ bit) for i in range(count)])]
  transfers between devices with their start and end apart: 5 -> 13, of which waited for: 3 -> 2; matrix products, arithmetic and copies ran while one was open for 0% -> 0% of each run, Pallas kernels for 25% -> 27%
where the time goes in v11:
time: 66.4 us; the launch traced here: 66.1 us
  waiting for transfers between devices  36.5 us (55%)
  Pallas kernels  19.6 us (30%)
  starting transfers between devices  8.88 us (13%)
  other arithmetic  0.9 us (1%)
    ppermute x1, waiting for transfers between devices, hand_back(): lax.ppermute(x, 'head', [(g, g - 1) for g in range(1, lax.axis_size('head...  25.8 us
    ppermute x5, waiting for transfers between devices, swap(): return lax.ppermute(x, axis, [(i, i ^ bit) for i in range(count)])  10.7 us
    pallas_call x2, Pallas kernels, row_maps(): pl.pallas_call(functools.partial(rows_kernel, heads, mine), in_specs=[her...  7.35 us
    pallas_call x1, Pallas kernels, local_maps(): pl.pallas_call(functools.partial(local_maps_kernel, heads), in_specs=[pl....  7.07 us
    ppermute x7, starting transfers between devices, swap_odd(): return lax.ppermute(x, ('seq', 'head'), pairs)  4.79 us
    pallas_call x5, Pallas kernels, small_call(): pl.pallas_call(kernel, in_specs=[here] * len(args), out_specs=[here] * le...  3.3 us
    ppermute x5, starting transfers between devices, swap(): return lax.ppermute(x, axis, [(i, i ^ bit) for i in range(count)])  2.8 us
  transfers between devices with their start and end apart: 13, of which 2 were waited for; matrix products, arithmetic and copies ran while one was open for 0% of the time, Pallas kernels for 27%

profile of v11, /device:TPU:0, one launch (start us, length us, event | category | flops | bytes accessed | tf_op | source)
XLA Modules:
  0.0 66.1 jit_solution(17743679349087079423)
XLA Ops:
  0.0 0.5 collective-permute-start.7
  0.5 7.1 %local_maps.1 = (bf16[2048,128]{1,0:T(8,128)(2,1)S(1)}, f32[2048,128]{1,0:T(8,128)S(1)}, f32[16,128]{1,0:T(8,128)S(1)}, f32[16,128,128]{2,1,0:T(8,128)S(1)}, f32...) custom-call(bf16[2048,128]{1,0:T(8,128)(2,1)} %bitcast.3, ...), custom_call_target="tpu_custom_call" | custom-call | tf_op jit(solution)/shard_map/local_maps/pallas_call | solution.py:228
  7.5 0.1 collective-permute-start
  7.6 3.7 %row_maps.3 = (f32[2,2,128,256]{3,2,1,0:T(8,128)S(1)}, f32[2,2,128,256]{3,2,1,0:T(8,128)S(1)}) custom-call(bf16[2048,128]{1,0:T(8,128)(2,1)S(1)} %get-tuple-element.43.q16, f32[2048,128]{1,0:T(8,128)S(1)} %get-tuple-element.44.k32, f32[16,128]{1,0:T(8,128)S(1)} %get-tuple-element.45.sums_ref, f32[16,128,128]{2,1,0:T(8,128)S(1)} %get-tuple-element.46.mix_ref, ...), custom_call_target="tpu_custom_call" | custom-call | flops 2000000000 | bytes 8000000 | tf_op jit(solution)/shard_map/row_maps/pallas_call | solution.py:289
  11.3 0.5 collective-permute-start.6
  11.9 3.7 %row_maps.2 = (f32[2,2,128,256]{3,2,1,0:T(8,128)S(1)}, f32[2,2,128,256]{3,2,1,0:T(8,128)S(1)}) custom-call(bf16[2048,128]{1,0:T(8,128)(2,1)S(1)} %get-tuple-element.43.q16, f32[2048,128]{1,0:T(8,128)S(1)} %get-tuple-element.44.k32, f32[16,128]{1,0:T(8,128)S(1)} %get-tuple-element.45.sums_ref, f32[16,128,128]{2,1,0:T(8,128)S(1)} %get-tuple-element.46.mix_ref, ...), custom_call_target="tpu_custom_call" | custom-call | flops 2000000000 | bytes 8000000 | tf_op jit(solution)/shard_map/row_maps/pallas_call | solution.py:289
  15.6 0.1 collective-permute-start.5
  15.7 0.8 %collective-permute-start.1 = (bf16[2,128,256]{2,1,0:T(8,128)(2,1)S(1)}, bf16[2,128,256]{2,1,0:T(8,128)(2,1)S(1)}, u32[]{:S(2)}, u32[]{:S(2)}) collective-permute-start(bf16[2,128,256]{2,1,0:T(8,128)(2,1)S(1)} %get-tuple-element.52), channel_id=1, source_target_pairs={{1,5},{3,7},{5,1},{7,3},{9,13},{11,15},{13,9},{15,11},{17,21},{19,... | collective-permute-start | bytes 393224 | tf_op jit(solution)/shard_map/ppermute | solution.py:493
  16.5 0.7 %collective-permute-start.2 = (bf16[2,128,256]{2,1,0:T(8,128)(2,1)S(1)}, bf16[2,128,256]{2,1,0:T(8,128)(2,1)S(1)}, u32[]{:S(2)}, u32[]{:S(2)}) collective-permute-start(bf16[2,128,256]{2,1,0:T(8,128)(2,1)S(1)} %get-tuple-element.53), channel_id=1, source_target_pairs={{1,9},{3,11},{5,13},{7,15},{9,1},{11,3},{13,5},{15,7},{17,25},{19,... | collective-permute-start | bytes 393224 | tf_op jit(solution)/shard_map/ppermute | solution.py:493
  17.2 0.7 %collective-permute-start.3 = (bf16[2,128,256]{2,1,0:T(8,128)(2,1)S(1)}, bf16[2,128,256]{2,1,0:T(8,128)(2,1)S(1)}, u32[]{:S(2)}, u32[]{:S(2)}) collective-permute-start(bf16[2,128,256]{2,1,0:T(8,128)(2,1)S(1)} %get-tuple-element.54), channel_id=1, source_target_pairs={{1,13},{3,15},{5,9},{7,11},{9,5},{11,7},{13,1},{15,3},{17,29},{19,... | collective-permute-start | bytes 393224 | tf_op jit(solution)/shard_map/ppermute | solution.py:493
  17.9 0.7 %group_state.1 = (bf16[8,128,256]{2,1,0:T(8,128)(2,1)S(1)}, bf16[2,128,128]{2,1,0:T(8,128)(2,1)S(1)}) custom-call(bf16[2,128,256]{2,1,0:T(8,128)(2,1)S(1)} %get-tuple-element.55.refs_0_, bf16[2,128,256]{2,1,0:T(8,128)(2,1)S(1)} %collective-permute-done.1.refs_1_, bf16[2,128,256]{2,1,0:T(8,128)(2,1)S(1)} %collective-permute-done.2.refs_2_, ...), custom_call_target="tpu_custom_call" | custom-call | tf_op jit(solution)/shard_map/group_state/pallas_call | solution.py:303
  18.6 0.7 %collective-permute-start.4 = (bf16[2,128,128]{2,1,0:T(8,128)(2,1)S(1)}, bf16[2,128,128]{2,1,0:T(8,128)(2,1)S(1)}, u32[]{:S(2)}, u32[]{:S(2)}) collective-permute-start(bf16[2,128,128]{2,1,0:T(8,128)(2,1)S(1)} %get-tuple-element.63), channel_id=1, source_target_pairs={{1,17},{3,19},{5,21},{7,23},{9,25},{11,27},{13,29},{15,31},{17,1},... | collective-permute-start | bytes 196616 | tf_op jit(solution)/shard_map/ppermute | solution.py:493
  19.3 1.5 %group_prefix.1 = (bf16[8,128,128]{2,1,0:T(8,128)(2,1)S(1)}, bf16[8,128,128]{2,1,0:T(8,128)(2,1)S(1)}, f32[8,128,128]{2,1,0:T(8,128)S(1)}, bf16[2,128,256]{2,1,0:T(8,128)(2,1)}) custom-call(bf16[8,128,256]{2,1,0:T(8,128)(2,1)S(1)} %get-tuple-element.59.held), custom_call_target="tpu_custom_call" | custom-call | tf_op jit(solution)/shard_map/group_prefix/pallas_call | solution.py:303
  20.8 1.0 %states_of_upper.1 = (bf16[2,128,128]{2,1,0:T(8,128)(2,1)S(1)}, bf16[2,128,128]{2,1,0:T(8,128)(2,1)S(1)}, bf16[2,128,128]{2,1,0:T(8,128)(2,1)S(1)}, bf16[2,128,128]{2,1,0:T(8,128)(2,1)S(1)}, bf16[8,128,128]{2,1,0:T(8,128)(2,1)}) custom-call(bf16[8,128,128]{2,1,0:T(8,128)(2,1)S(1)} %get-tuple-element.72.refs_0_, ...), custom_call_target="tpu_custom_call" | custom-call | tf_op jit(solution)/shard_map/states_of_upper/pallas_call | solution.py:303
  21.8 0.7 collective-permute-start.10
  22.5 0.7 %collective-permute-start.8 = (bf16[2,128,128]{2,1,0:T(8,128)(2,1)S(1)}, bf16[2,128,128]{2,1,0:T(8,128)(2,1)S(1)}, u32[]{:S(2)}, u32[]{:S(2)}) collective-permute-start(bf16[2,128,128]{2,1,0:T(8,128)(2,1)S(1)} %get-tuple-element.77), channel_id=1, source_target_pairs={{1,5},{3,7},{5,1},{7,3},{9,13},{11,15},{13,9},{15,11},{17,21},{19,... | collective-permute-start | bytes 196616 | tf_op jit(solution)/shard_map/ppermute | solution.py:493
  23.2 0.7 %collective-permute-start.9 = (bf16[2,128,128]{2,1,0:T(8,128)(2,1)S(1)}, bf16[2,128,128]{2,1,0:T(8,128)(2,1)S(1)}, u32[]{:S(2)}, u32[]{:S(2)}) collective-permute-start(bf16[2,128,128]{2,1,0:T(8,128)(2,1)S(1)} %get-tuple-element.78), channel_id=1, source_target_pairs={{1,9},{3,11},{5,13},{7,15},{9,1},{11,3},{13,5},{15,7},{17,25},{19,... | collective-permute-start | bytes 196616 | tf_op jit(solution)/shard_map/ppermute | solution.py:493
  23.9 1.3 %collective-permute-start.11 = (bf16[8,128,128]{2,1,0:T(8,128)(2,1)S(1)}, bf16[8,128,128]{2,1,0:T(8,128)(2,1)S(1)}, u32[]{:S(2)}, u32[]{:S(2)}) collective-permute-start(bf16[8,128,128]{2,1,0:T(8,128)(2,1)S(1)} %gather_heads.1.st1_ref.st_ref), channel_id=1, source_target_pairs={{1,0},{3,2},{5,4},{7,6},{9,8},{11,10},{13,12},{15,14},{17,16},{19,... | collective-permute-start | bytes 786440 | tf_op jit(solution)/shard_map/ppermute | solution.py:497
  25.3 25.8 %collective-permute-done.11.st0_ref.st_ref = bf16[8,128,128]{2,1,0:T(8,128)(2,1)S(1)} collective-permute-done((bf16[8,128,128]{2,1,0:T(8,128)(2,1)S(1)}, bf16[8,128,128]{2,1,0:T(8,128)(2,1)S(1)}, u32[]{:S(2)}, u32[]{:S(2)}) %collective-permute-start.11) | collective-permute-done | bytes 262176 | tf_op jit(solution)/shard_map/ppermute | solution.py:497
  51.1 0.9 %share_out.3 = bf16[128,2048]{1,0:T(8,128)(2,1)S(1)} custom-call(f32[2,2,128,256]{3,2,1,0:T(8,128)S(1)} %get-tuple-element.68.rows0, f32[2,2,128,256]{3,2,1,0:T(8,128)S(1)} %get-tuple-element.69.rows1, f32[2,2,128,256]{3,2,1,0:T(8,128)S(1)} %collective-permute-done.5.rows2, f32[2,2,128,256]{3,2,1,0:T(8,128)S(1)} %collective-permute-done.6.rows3, ...), custom_call_target="tpu_custom_call" | custom-call | flops 536870912 | bytes 4194304 | tf_op jit(solution)/shard_map/share_out/pallas_call | solution.py:448
  52.0 1.6 %collective-permute-start.12 = (bf16[128,2048]{1,0:T(8,128)(2,1)S(1)}, bf16[128,2048]{1,0:T(8,128)(2,1)S(1)}, u32[]{:S(2)}, u32[]{:S(2)}) collective-permute-start(bf16[128,2048]{1,0:T(8,128)(2,1)S(1)} %share_out.3), channel_id=1, source_target_pairs={{0,2},{1,3},{2,0},{3,1},{4,6},{5,7},{6,4},{7,5},{8,10},{9,11},{10,... | collective-permute-start | bytes 1572872 | tf_op jit(solution)/shard_map/ppermute | solution.py:487
  53.6 0.9 %share_here.1 = f32[128,2048]{1,0:T(8,128)S(1)} custom-call(f32[2,2,128,256]{3,2,1,0:T(8,128)S(1)} %get-tuple-element.68.rows0, f32[2,2,128,256]{3,2,1,0:T(8,128)S(1)} %get-tuple-element.69.rows1, f32[2,2,128,256]{3,2,1,0:T(8,128)S(1)} %collective-permute-done.5.rows2, f32[2,2,128,256]{3,2,1,0:T(8,128)S(1)} %collective-permute-done.6.rows3, ...), custom_call_target="tpu_custom_call" | custom-call | flops 536870912 | bytes 4194304 | tf_op jit(solution)/shard_map/share_here/pallas_call | solution.py:472
  54.6 10.6 %collective-permute-done.12 = bf16[128,2048]{1,0:T(8,128)(2,1)S(1)} collective-permute-done((bf16[128,2048]{1,0:T(8,128)(2,1)S(1)}, bf16[128,2048]{1,0:T(8,128)(2,1)S(1)}, u32[]{:S(2)}, u32[]{:S(2)}) %collective-permute-start.12) | collective-permute-done | bytes 524320 | tf_op jit(solution)/shard_map/ppermute | solution.py:487
  65.2 0.9 %add_convert_fusion = bf16[128,2048]{1,0:T(8,128)(2,1)} fusion(f32[128,2048]{1,0:T(8,128)S(1)} %share_here.1, bf16[128,2048]{1,0:T(8,128)(2,1)S(1)} %collective-permute-done.12), kind=kLoop, calls=%fused_computation | loop fusion | flops 786432 | bytes 2097152 | tf_op jit(solution)/shard_map/convert_element_type | solution.py:535
  (16 shorter events, 0.1 us)
Async XLA Ops:
  0.0 20.8 %collective-permute-start.7 = (bf16[512,2048]{1,0:T(8,128)(2,1)}, bf16[512,2048]{1,0:T(8,128)(2,1)S(1)}, u32[]{:S(2)}, u32[]{:S(2)}) collective-permute-start(bf16[512,2048]{1,0:T(8,128)(2,1)} %w_ref.5), channel_id=1, source_target_pairs={{0,1},{1,0},{2,3},{3,2},{4,5},{5,4},{6,7},{7,6},{8,9},{9,8},{10,11... | collective-permute-start | bytes 6291464 | tf_op jit(solution)/shard_map/ppermute | solution.py:487
  7.5 8.1 %collective-permute-start = (bf16[4,128,256]{2,1,0:T(8,128)(2,1)S(1)}, bf16[4,128,256]{2,1,0:T(8,128)(2,1)S(1)}, u32[]{:S(2)}, u32[]{:S(2)}) collective-permute-start(bf16[4,128,256]{2,1,0:T(8,128)(2,1)S(1)} %get-tuple-element.50.mine_ref), channel_id=1, source_target_pairs={{0,1},{1,0},{2,3},{3,2},{4,5},{5,4},{6,7},{7,6},{8,9},{9,8},{10,11... | collective-permute-start | bytes 786440 | tf_op jit(solution)/shard_map/ppermute | solution.py:487
  11.3 9.5 %collective-permute-start.6 = (f32[2,2,128,256]{3,2,1,0:T(8,128)S(1)}, f32[2,2,128,256]{3,2,1,0:T(8,128)S(1)}, u32[]{:S(2)}, u32[]{:S(2)}) collective-permute-start(f32[2,2,128,256]{3,2,1,0:T(8,128)S(1)} %get-tuple-element.67), channel_id=1, source_target_pairs={{0,1},{1,0},{2,3},{3,2},{4,5},{5,4},{6,7},{7,6},{8,9},{9,8},{10,11... | collective-permute-start | bytes 1572872 | tf_op jit(solution)/shard_map/ppermute | solution.py:487
  15.5 9.7 %copy-start = (bf16[512,2048]{1,0:T(8,128)(2,1)S(1)}, bf16[512,2048]{1,0:T(8,128)(2,1)}, u32[]{:S(2)}) copy-start(bf16[512,2048]{1,0:T(8,128)(2,1)} %w_ref.5) | copy-start | bytes 6291460
  15.6 5.2 %collective-permute-start.5 = (f32[2,2,128,256]{3,2,1,0:T(8,128)S(1)}, f32[2,2,128,256]{3,2,1,0:T(8,128)S(1)}, u32[]{:S(2)}, u32[]{:S(2)}) collective-permute-start(f32[2,2,128,256]{3,2,1,0:T(8,128)S(1)} %get-tuple-element.66), channel_id=1, source_target_pairs={{0,1},{1,0},{2,3},{3,2},{4,5},{5,4},{6,7},{7,6},{8,9},{9,8},{10,11... | collective-permute-start | bytes 1572872 | tf_op jit(solution)/shard_map/ppermute | solution.py:487
  15.7 1.5 %collective-permute-start.1 = (bf16[2,128,256]{2,1,0:T(8,128)(2,1)S(1)}, bf16[2,128,256]{2,1,0:T(8,128)(2,1)S(1)}, u32[]{:S(2)}, u32[]{:S(2)}) collective-permute-start(bf16[2,128,256]{2,1,0:T(8,128)(2,1)S(1)} %get-tuple-element.52), channel_id=1, source_target_pairs={{1,5},{3,7},{5,1},{7,3},{9,13},{11,15},{13,9},{15,11},{17,21},{19,... | collective-permute-start | bytes 393224 | tf_op jit(solution)/shard_map/ppermute | solution.py:493
  16.5 1.4 %collective-permute-start.2 = (bf16[2,128,256]{2,1,0:T(8,128)(2,1)S(1)}, bf16[2,128,256]{2,1,0:T(8,128)(2,1)S(1)}, u32[]{:S(2)}, u32[]{:S(2)}) collective-permute-start(bf16[2,128,256]{2,1,0:T(8,128)(2,1)S(1)} %get-tuple-element.53), channel_id=1, source_target_pairs={{1,9},{3,11},{5,13},{7,15},{9,1},{11,3},{13,5},{15,7},{17,25},{19,... | collective-permute-start | bytes 393224 | tf_op jit(solution)/shard_map/ppermute | solution.py:493
  17.2 0.7 %collective-permute-start.3 = (bf16[2,128,256]{2,1,0:T(8,128)(2,1)S(1)}, bf16[2,128,256]{2,1,0:T(8,128)(2,1)S(1)}, u32[]{:S(2)}, u32[]{:S(2)}) collective-permute-start(bf16[2,128,256]{2,1,0:T(8,128)(2,1)S(1)} %get-tuple-element.54), channel_id=1, source_target_pairs={{1,13},{3,15},{5,9},{7,11},{9,5},{11,7},{13,1},{15,3},{17,29},{19,... | collective-permute-start | bytes 393224 | tf_op jit(solution)/shard_map/ppermute | solution.py:493
  18.6 2.2 %collective-permute-start.4 = (bf16[2,128,128]{2,1,0:T(8,128)(2,1)S(1)}, bf16[2,128,128]{2,1,0:T(8,128)(2,1)S(1)}, u32[]{:S(2)}, u32[]{:S(2)}) collective-permute-start(bf16[2,128,128]{2,1,0:T(8,128)(2,1)S(1)} %get-tuple-element.63), channel_id=1, source_target_pairs={{1,17},{3,19},{5,21},{7,23},{9,25},{11,27},{13,29},{15,31},{17,1},... | collective-permute-start | bytes 196616 | tf_op jit(solution)/shard_map/ppermute | solution.py:493
  21.8 2.0 %collective-permute-start.10 = (bf16[2,128,128]{2,1,0:T(8,128)(2,1)S(1)}, bf16[2,128,128]{2,1,0:T(8,128)(2,1)S(1)}, u32[]{:S(2)}, u32[]{:S(2)}) collective-permute-start(bf16[2,128,128]{2,1,0:T(8,128)(2,1)S(1)} %get-tuple-element.79), channel_id=1, source_target_pairs={{1,13},{3,15},{5,9},{7,11},{9,5},{11,7},{13,1},{15,3},{17,29},{19,... | collective-permute-start | bytes 196616 | tf_op jit(solution)/shard_map/ppermute | solution.py:493
  22.5 1.4 %collective-permute-start.8 = (bf16[2,128,128]{2,1,0:T(8,128)(2,1)S(1)}, bf16[2,128,128]{2,1,0:T(8,128)(2,1)S(1)}, u32[]{:S(2)}, u32[]{:S(2)}) collective-permute-start(bf16[2,128,128]{2,1,0:T(8,128)(2,1)S(1)} %get-tuple-element.77), channel_id=1, source_target_pairs={{1,5},{3,7},{5,1},{7,3},{9,13},{11,15},{13,9},{15,11},{17,21},{19,... | collective-permute-start | bytes 196616 | tf_op jit(solution)/shard_map/ppermute | solution.py:493
  23.2 0.7 %collective-permute-start.9 = (bf16[2,128,128]{2,1,0:T(8,128)(2,1)S(1)}, bf16[2,128,128]{2,1,0:T(8,128)(2,1)S(1)}, u32[]{:S(2)}, u32[]{:S(2)}) collective-permute-start(bf16[2,128,128]{2,1,0:T(8,128)(2,1)S(1)} %get-tuple-element.78), channel_id=1, source_target_pairs={{1,9},{3,11},{5,13},{7,15},{9,1},{11,3},{13,5},{15,7},{17,25},{19,... | collective-permute-start | bytes 196616 | tf_op jit(solution)/shard_map/ppermute | solution.py:493
  23.9 27.2 %collective-permute-start.11 = (bf16[8,128,128]{2,1,0:T(8,128)(2,1)S(1)}, bf16[8,128,128]{2,1,0:T(8,128)(2,1)S(1)}, u32[]{:S(2)}, u32[]{:S(2)}) collective-permute-start(bf16[8,128,128]{2,1,0:T(8,128)(2,1)S(1)} %gather_heads.1.st1_ref.st_ref), channel_id=1, source_target_pairs={{1,0},{3,2},{5,4},{7,6},{9,8},{11,10},{13,12},{15,14},{17,16},{19,... | collective-permute-start | bytes 786440 | tf_op jit(solution)/shard_map/ppermute | solution.py:497
  52.0 13.2 %collective-permute-start.12 = (bf16[128,2048]{1,0:T(8,128)(2,1)S(1)}, bf16[128,2048]{1,0:T(8,128)(2,1)S(1)}, u32[]{:S(2)}, u32[]{:S(2)}) collective-permute-start(bf16[128,2048]{1,0:T(8,128)(2,1)S(1)} %share_out.3), channel_id=1, source_target_pairs={{0,2},{1,3},{2,0},{3,1},{4,6},{5,7},{6,4},{7,5},{8,10},{9,11},{10,... | collective-permute-start | bytes 1572872 | tf_op jit(solution)/shard_map/ppermute | solution.py:487

commit v12 on v10

--- a/solution.py
+++ b/solution.py
@@ -32,7 +32,12 @@
 
 def dot3(a, b):
     (ah, al), (bh, bl) = a, b
-    return dot(jnp.concatenate([ah, al, ah], axis=1), jnp.concatenate([bh, bh, bl], axis=0))
+    width = bh.shape[1]
+    left = jnp.concatenate([ah, al], axis=1)
+    if width > C:
+        return dot(left, twice(bh)) + dot(ah, bl)
+    both = dot(left, twice(jnp.concatenate([bh, bl], axis=1)))
+    return both[:, :width] + both[:, width:]
 
 
 def iotas():
@@ -62,14 +67,6 @@
 
 def running_sums(rows, upper):
     return sum(dot(x, upper) for x in reversed(three(rows)))
-
-
-def spread_columns(row, eye, ones):
-    parts = three(jnp.broadcast_to(row, (16, C)))
-    high, middle, low = (
-        jnp.where(eye, jnp.concatenate([x] * (C // 16), axis=0), jnp.zeros((), BF16)) for x in parts
-    )
-    return dot(jnp.concatenate([high, middle, low], axis=1), jnp.concatenate([ones] * 3, axis=0))
 
 
 def base_inverse(lower, row, col):
@@ -109,7 +106,8 @@
         r, c = odd_rows(row, size), odd_rows(col, size)
         mask = ((r // (2 * size)) == (c // (2 * size))) & ((r // size) != (c // size))
         nothing = jnp.zeros((C // 2, C), BF16)
-        joins = [tuple(jnp.where(mask, odd_rows(x, size), nothing) for x in part) for part in parts]
+        mask = jnp.where(mask, 1.0, 0.0).astype(BF16)
+        joins = [tuple(odd_rows(x, size) * mask for x in part) for part in parts]
         middle = [split(dot3(a, x)) for a, x in zip(joins, halves)]
         middle = [tuple(weave(nothing, x, size) for x in part) for part in middle]
         lows = [dot3(tuple(odd_rows(x, size) for x in h), y) for h, y in zip(halves, middle)]
@@ -143,6 +141,15 @@
 
 def tokens_of(ref, head, c):
     return ref[head : head + 1, c * C : (c + 1) * C]
+
+
+def join(moved, added):
+    return jnp.concatenate([moved, added], axis=1)
+
+
+def after(later, earlier):
+    total = dot3(split(later[:, :C]), split(earlier))
+    return join(total[:, :C], total[:, C:] + later[:, C:])
 
 
 def per_chunk(ref):
@@ -164,6 +171,7 @@
     eye16 = jnp.where(eye, one, jnp.zeros((), BF16))
     sums = running_sums(per_chunk(log_ref), jnp.where(row <= col, one, jnp.zeros((), BF16)))
     sums_ref[...] = sums
+    columns = jnp.concatenate([sums] * (C // sums.shape[0]), axis=0).T
     grown = jnp.exp(sums)
     faded = jnp.exp(sums[:, C - 1 :] - sums)
     betas = per_chunk(beta_ref)
@@ -181,7 +189,7 @@
             scale = lax.rsqrt(square)
             lengths.append(square * scale)
             strength = betas[at] * (scale * scale)
-            span = spread_columns(sums[at], eye, one) - sums[at]
+            span = columns[:, c * heads + head : c * heads + head + 1] - sums[at]
             mix = jnp.where(within, jnp.exp(span), 0.0) * strength
             mix_ref[head * chunks + c] = mix
             lowers.append(jnp.where(strict, gram * mix, 0.0))
@@ -199,13 +207,12 @@
             end = grown[c * heads + head : c * heads + head + 1, C - 1 :]
             maps.append((jnp.where(eye, end, 0.0) - both[:, :C], both[:, C:]))
         for j in range(batch):
-            state = jnp.concatenate(maps[j * chunks], axis=1)
-            for c in range(1, chunks):
-                n_ref[(start + j) * chunks + c] = state
-                moved, fresh = maps[j * chunks + c]
-                state = dot3(split(moved), split(state))
-                state = jnp.concatenate([state[:, :C], state[:, C:] + fresh], axis=1)
-            all_ref[start + j] = state
+            first, second, third, last = (join(*x) for x in maps[j * chunks : (j + 1) * chunks])
+            early = after(second, first)
+            n_ref[(start + j) * chunks + 1] = first
+            n_ref[(start + j) * chunks + 2] = early
+            n_ref[(start + j) * chunks + 3] = after(third, early)
+            all_ref[start + j] = after(after(last, third), early)
     place = lax.rem(lax.axis_index("seq"), heads)
     own_ref[...] = all_ref[place]
     for r in range(1, heads):

time: 47.7 us -> 47.1 us (0.987)
  Pallas kernels: 17.2 us -> 16.5 us
    pallas_call x1, Pallas kernels: 7.42 us -> 6.89 us  [local_maps(): pl.pallas_call(functools.partial(local_maps_kernel, heads, batch), in_spe...]
  transfers between devices with their start and end apart: 11 -> 11, of which waited for: 7 -> 7; matrix products, arithmetic and copies ran while one was open for 0% -> 0% of each run, Pallas kernels for 34% -> 33%
where the time goes in v12:
time: 47.1 us; the launch traced here: 47 us
  waiting for transfers between devices  17.4 us (37%)
  Pallas kernels  16.5 us (35%)
  starting transfers between devices  13 us (28%)
    ppermute x11, waiting for transfers between devices, swap(): return lax.ppermute(x, axis, [(i, i ^ bit) for i in range(count)])  17.4 us
    ppermute x11, starting transfers between devices, swap(): return lax.ppermute(x, axis, [(i, i ^ bit) for i in range(count)])  13 us
    pallas_call x1, Pallas kernels, local_maps(): pl.pallas_call(functools.partial(local_maps_kernel, heads, batch), in_spe...  6.89 us
    pallas_call x2, Pallas kernels, row_maps(): pl.pallas_call(functools.partial(rows_kernel, heads, mine), in_specs=[her...  3.27 us
    pallas_call x3, Pallas kernels, small_call(): pl.pallas_call(kernel, in_specs=[here] * len(args), out_specs=[here] * le...  2.61 us
    pallas_call x4, Pallas kernels, project(): pl.pallas_call(functools.partial(project_kernel, other, start), out_shape...  1.78 us
    pallas_call x2, Pallas kernels, add_part(): pl.pallas_call(add_kernel, grid=(1,), in_specs=[here, here] + [pl.BlockSp...  1.5 us
  transfers between devices with their start and end apart: 11, of which 7 were waited for; matrix products, arithmetic and copies ran while one was open for 0% of the time, Pallas kernels for 33%

profile of v12, /device:TPU:0, one launch (start us, length us, event | category | flops | bytes accessed | tf_op | source)
XLA Modules:
  0.0 47.0 jit_solution(16001294905069220390)
XLA Ops:
  0.0 0.5 collective-permute-start.8
  0.5 6.9 %local_maps.1 = (bf16[2048,128]{1,0:T(8,128)(2,1)S(1)}, f32[2048,128]{1,0:T(8,128)S(1)}, f32[16,128]{1,0:T(8,128)S(1)}, f32[16,128,128]{2,1,0:T(8,128)S(1)}, f32...) custom-call(bf16[2048,128]{1,0:T(8,128)(2,1)} %bitcast.3, ...), custom_call_target="tpu_custom_call" | custom-call | tf_op jit(solution)/shard_map/local_maps/pallas_call | solution.py:234
  7.4 2.5 %collective-permute-start = (bf16[128,256]{1,0:T(8,128)(2,1)S(1)}, bf16[128,256]{1,0:T(8,128)(2,1)S(1)}, u32[]{:S(2)}, u32[]{:S(2)}) collective-permute-start(bf16[128,256]{1,0:T(8,128)(2,1)S(1)} %get-tuple-element.40), channel_id=1, source_target_pairs={{0,4},{4,0},{8,12},{12,8},{16,20},{20,16},{24,28},{28,24},{1,5},{5... | collective-permute-start | bytes 196616 | tf_op jit(solution)/shard_map/ppermute | solution.py:464
  9.9 1.6 %collective-permute-start.1 = (bf16[128,256]{1,0:T(8,128)(2,1)S(1)}, bf16[128,256]{1,0:T(8,128)(2,1)S(1)}, u32[]{:S(2)}, u32[]{:S(2)}) collective-permute-start(bf16[128,256]{1,0:T(8,128)(2,1)S(1)} %get-tuple-element.41), channel_id=1, source_target_pairs={{0,8},{4,12},{8,0},{12,4},{16,24},{20,28},{24,16},{28,20},{1,9},{5... | collective-permute-start | bytes 196616 | tf_op jit(solution)/shard_map/ppermute | solution.py:464
  11.5 1.6 %row_maps.2.rows0_ref = f32[2,512,256]{2,1,0:T(8,128)S(1)} custom-call(bf16[2048,128]{1,0:T(8,128)(2,1)S(1)} %get-tuple-element.34.q16, f32[2048,128]{1,0:T(8,128)S(1)} %get-tuple-element.35.k32, f32[16,128]{1,0:T(8,128)S(1)} %get-tuple-element.36.sums_ref, f32[16,128,128]{2,1,0:T(8,128)S(1)} %get-tuple-element.37.mix_ref, ...), custom_call_target="tpu_custom_call" | custom-call | flops 2000000000 | bytes 8000000 | tf_op jit(solution)/shard_map/row_maps/pallas_call | solution.py:287
  13.1 1.3 %collective-permute-done.1.refs_1_ = bf16[128,256]{1,0:T(8,128)(2,1)S(1)} collective-permute-done((bf16[128,256]{1,0:T(8,128)(2,1)S(1)}, bf16[128,256]{1,0:T(8,128)(2,1)S(1)}, u32[]{:S(2)}, u32[]{:S(2)}) %collective-permute-start.1) | collective-permute-done | bytes 65568 | tf_op jit(solution)/shard_map/ppermute | solution.py:464
  14.4 2.2 %collective-permute-done.2.refs_2_ = bf16[128,256]{1,0:T(8,128)(2,1)S(1)} collective-permute-done((bf16[128,256]{1,0:T(8,128)(2,1)S(1)}, bf16[128,256]{1,0:T(8,128)(2,1)S(1)}, u32[]{:S(2)}, u32[]{:S(2)}) %collective-permute-start.2) | collective-permute-done | bytes 65568 | tf_op jit(solution)/shard_map/ppermute | solution.py:464
  16.6 0.5 %group_state.1 = (f32[4,128,256]{2,1,0:T(8,128)S(1)}, bf16[128,128]{1,0:T(8,128)(2,1)S(1)}) custom-call(f32[128,256]{1,0:T(8,128)S(1)} %get-tuple-element.44.own_ref, bf16[128,256]{1,0:T(8,128)(2,1)S(1)} %collective-permute-done.refs_0_, bf16[128,256]{1,0:T(8,128)(2,1)S(1)} %collective-permute-done.1.refs_1_, bf16[128,256]{1,0:T(8,128)(2,1)S(1)} %collective-permute-done.2.refs_2_), custom_call_target="tpu_custom_call" | custom-call | tf_op jit(solution)/shard_map/group_state/pallas_call | solution.py:301
  17.2 2.7 %collective-permute-start.3 = (bf16[128,128]{1,0:T(8,128)(2,1)S(1)}, bf16[128,128]{1,0:T(8,128)(2,1)S(1)}, u32[]{:S(2)}, u32[]{:S(2)}) collective-permute-start(bf16[128,128]{1,0:T(8,128)(2,1)S(1)} %get-tuple-element.52), channel_id=1, source_target_pairs={{0,16},{4,20},{8,24},{12,28},{16,0},{20,4},{24,8},{28,12},{1,17},{... | collective-permute-start | bytes 98312 | tf_op jit(solution)/shard_map/ppermute | solution.py:464
  19.8 1.2 %group_prefix.1 = (bf16[4,128,128]{2,1,0:T(8,128)(2,1)S(1)}, bf16[4,128,128]{2,1,0:T(8,128)(2,1)S(1)}, f32[4,128,128]{2,1,0:T(8,128)S(1)}, bf16[128,256]{1,0:T(8,128)(2,1)}) custom-call(f32[4,128,256]{2,1,0:T(8,128)S(1)} %get-tuple-element.48.held), custom_call_target="tpu_custom_call" | custom-call | tf_op jit(solution)/shard_map/group_prefix/pallas_call | solution.py:301
  21.0 1.3 %collective-permute-done.3.refs_3_ = bf16[128,128]{1,0:T(8,128)(2,1)S(1)} collective-permute-done((bf16[128,128]{1,0:T(8,128)(2,1)S(1)}, bf16[128,128]{1,0:T(8,128)(2,1)S(1)}, u32[]{:S(2)}, u32[]{:S(2)}) %collective-permute-start.3) | collective-permute-done | bytes 32800 | tf_op jit(solution)/shard_map/ppermute | solution.py:464
  22.3 0.9 %states_of_upper.1 = (bf16[128,128]{1,0:T(8,128)(2,1)S(1)}, bf16[128,128]{1,0:T(8,128)(2,1)S(1)}, bf16[128,128]{1,0:T(8,128)(2,1)S(1)}, bf16[128,128]{1,0:T(8,128)(2,1)S(1)}, bf16[4,128,128]{2,1,0:T(8,128)(2,1)}) custom-call(bf16[4,128,128]{2,1,0:T(8,128)(2,1)S(1)} %get-tuple-element.53.refs_0_, bf16[4,128,128]{2,1,0:T(8,128)(2,1)S(1)} %get-tuple-element.54.refs_1_, ...), custom_call_target="tpu_custom_call" | custom-call | tf_op jit(solution)/shard_map/states_of_upper/pallas_call | solution.py:301
  23.5 1.4 %collective-permute-start.5 = (bf16[128,128]{1,0:T(8,128)(2,1)S(1)}, bf16[128,128]{1,0:T(8,128)(2,1)S(1)}, u32[]{:S(2)}, u32[]{:S(2)}) collective-permute-start(bf16[128,128]{1,0:T(8,128)(2,1)S(1)} %get-tuple-element.59), channel_id=1, source_target_pairs={{0,8},{4,12},{8,0},{12,4},{16,24},{20,28},{24,16},{28,20},{1,9},{5... | collective-permute-start | bytes 98312 | tf_op jit(solution)/shard_map/ppermute | solution.py:464
  24.9 1.8 %collective-permute-start.6 = (bf16[128,128]{1,0:T(8,128)(2,1)S(1)}, bf16[128,128]{1,0:T(8,128)(2,1)S(1)}, u32[]{:S(2)}, u32[]{:S(2)}) collective-permute-start(bf16[128,128]{1,0:T(8,128)(2,1)S(1)} %get-tuple-element.60), channel_id=1, source_target_pairs={{0,12},{4,8},{8,4},{12,0},{16,28},{20,24},{24,20},{28,16},{1,13},{... | collective-permute-start | bytes 98312 | tf_op jit(solution)/shard_map/ppermute | solution.py:464
  26.7 1.6 %row_maps.3.rows1_ref = f32[2,512,256]{2,1,0:T(8,128)S(1)} custom-call(bf16[2048,128]{1,0:T(8,128)(2,1)S(1)} %get-tuple-element.34.q16, f32[2048,128]{1,0:T(8,128)S(1)} %get-tuple-element.35.k32, f32[16,128]{1,0:T(8,128)S(1)} %get-tuple-element.36.sums_ref, f32[16,128,128]{2,1,0:T(8,128)S(1)} %get-tuple-element.37.mix_ref, ...), custom_call_target="tpu_custom_call" | custom-call | flops 2000000000 | bytes 8000000 | tf_op jit(solution)/shard_map/row_maps/pallas_call | solution.py:287
  28.4 1.3 %collective-permute-done.6.refs_3_ = bf16[128,128]{1,0:T(8,128)(2,1)S(1)} collective-permute-done((bf16[128,128]{1,0:T(8,128)(2,1)S(1)}, bf16[128,128]{1,0:T(8,128)(2,1)S(1)}, u32[]{:S(2)}, u32[]{:S(2)}) %collective-permute-start.6) | collective-permute-done | bytes 32800 | tf_op jit(solution)/shard_map/ppermute | solution.py:464
  30.2 1.5 %collective-permute-done.7.got_ref = bf16[2,128,512]{2,1,0:T(8,128)(2,1)S(1)} collective-permute-done((bf16[2,128,512]{2,1,0:T(8,128)(2,1)S(1)}, bf16[2,128,512]{2,1,0:T(8,128)(2,1)S(1)}, u32[]{:S(2)}, u32[]{:S(2)}) %collective-permute-start.7) | collective-permute-done | bytes 262176 | tf_op jit(solution)/shard_map/ppermute | solution.py:464
  31.7 0.4 project.7
  32.2 1.6 %collective-permute-start.10 = (bf16[128,1024]{1,0:T(8,128)(2,1)S(1)}, bf16[128,1024]{1,0:T(8,128)(2,1)S(1)}, u32[]{:S(2)}, u32[]{:S(2)}) collective-permute-start(bf16[128,1024]{1,0:T(8,128)(2,1)S(1)} %project.7), channel_id=1, source_target_pairs={{0,2},{1,3},{2,0},{3,1},{4,6},{5,7},{6,4},{7,5},{8,10},{9,11},{10,... | collective-permute-start | bytes 786440 | tf_op jit(solution)/shard_map/ppermute | solution.py:464
  34.2 0.6 %collective-permute-start.9 = (bf16[128,1024]{1,0:T(8,128)(2,1)S(1)}, bf16[128,1024]{1,0:T(8,128)(2,1)S(1)}, u32[]{:S(2)}, u32[]{:S(2)}) collective-permute-start(bf16[128,1024]{1,0:T(8,128)(2,1)S(1)} %project.5), channel_id=1, source_target_pairs={{0,2},{1,3},{2,0},{3,1},{4,6},{5,7},{6,4},{7,5},{8,10},{9,11},{10,... | collective-permute-start | bytes 786440 | tf_op jit(solution)/shard_map/ppermute | solution.py:464
  35.7 5.7 %collective-permute-done.10.theirs_ref = bf16[128,1024]{1,0:T(8,128)(2,1)S(1)} collective-permute-done((bf16[128,1024]{1,0:T(8,128)(2,1)S(1)}, bf16[128,1024]{1,0:T(8,128)(2,1)S(1)}, u32[]{:S(2)}, u32[]{:S(2)}) %collective-permute-start.10) | collective-permute-done | bytes 262176 | tf_op jit(solution)/shard_map/ppermute | solution.py:464
  41.4 0.7 %add_part.2.refs_0_ = bf16[128,2048]{1,0:T(8,128)(2,1)} custom-call(f32[128,1024]{1,0:T(8,128)S(1)} %project.6.mine_ref, bf16[128,1024]{1,0:T(8,128)(2,1)S(1)} %collective-permute-done.10.theirs_ref), custom_call_target="tpu_custom_call" | custom-call | tf_op jit(solution)/shard_map/add_part/pallas_call | solution.py:450
  42.2 4.1 %collective-permute-done.9.theirs_ref = bf16[128,1024]{1,0:T(8,128)(2,1)S(1)} collective-permute-done((bf16[128,1024]{1,0:T(8,128)(2,1)S(1)}, bf16[128,1024]{1,0:T(8,128)(2,1)S(1)}, u32[]{:S(2)}, u32[]{:S(2)}) %collective-permute-start.9) | collective-permute-done | bytes 262176 | tf_op jit(solution)/shard_map/ppermute | solution.py:464
  46.2 0.7 %add_part.3 = bf16[128,2048]{1,0:T(8,128)(2,1)} custom-call(f32[128,1024]{1,0:T(8,128)S(1)} %project.4.mine_ref, bf16[128,1024]{1,0:T(8,128)(2,1)S(1)} %collective-permute-done.9.theirs_ref, bf16[128,2048]{1,0:T(8,128)(2,1)} %add_part.2.refs_0_), custom_call_target="tpu_custom_call", output_to_operand_aliasing={{}: (2, {})} | custom-call | tf_op jit(solution)/shard_map/add_part/pallas_call | solution.py:450
  (13 shorter events, 2.1 us)
Async XLA Ops:
  0.0 31.7 %collective-permute-start.8 = (bf16[512,2048]{1,0:T(8,128)(2,1)}, bf16[512,2048]{1,0:T(8,128)(2,1)S(1)}, u32[]{:S(2)}, u32[]{:S(2)}) collective-permute-start(bf16[512,2048]{1,0:T(8,128)(2,1)} %w_ref.7), channel_id=1, source_target_pairs={{0,1},{1,0},{2,3},{3,2},{4,5},{5,4},{6,7},{7,6},{8,9},{9,8},{10,11... | collective-permute-start | bytes 6291464 | tf_op jit(solution)/shard_map/ppermute | solution.py:464
  7.4 5.8 %collective-permute-start = (bf16[128,256]{1,0:T(8,128)(2,1)S(1)}, bf16[128,256]{1,0:T(8,128)(2,1)S(1)}, u32[]{:S(2)}, u32[]{:S(2)}) collective-permute-start(bf16[128,256]{1,0:T(8,128)(2,1)S(1)} %get-tuple-element.40), channel_id=1, source_target_pairs={{0,4},{4,0},{8,12},{12,8},{16,20},{20,16},{24,28},{28,24},{1,5},{5... | collective-permute-start | bytes 196616 | tf_op jit(solution)/shard_map/ppermute | solution.py:464
  9.9 4.5 %collective-permute-start.1 = (bf16[128,256]{1,0:T(8,128)(2,1)S(1)}, bf16[128,256]{1,0:T(8,128)(2,1)S(1)}, u32[]{:S(2)}, u32[]{:S(2)}) collective-permute-start(bf16[128,256]{1,0:T(8,128)(2,1)S(1)} %get-tuple-element.41), channel_id=1, source_target_pairs={{0,8},{4,12},{8,0},{12,4},{16,24},{20,28},{24,16},{28,20},{1,9},{5... | collective-permute-start | bytes 196616 | tf_op jit(solution)/shard_map/ppermute | solution.py:464
  11.5 5.2 %collective-permute-start.2 = (bf16[128,256]{1,0:T(8,128)(2,1)S(1)}, bf16[128,256]{1,0:T(8,128)(2,1)S(1)}, u32[]{:S(2)}, u32[]{:S(2)}) collective-permute-start(bf16[128,256]{1,0:T(8,128)(2,1)S(1)} %get-tuple-element.42), channel_id=1, source_target_pairs={{0,12},{4,8},{8,4},{12,0},{16,28},{20,24},{24,20},{28,16},{1,13},{... | collective-permute-start | bytes 196616 | tf_op jit(solution)/shard_map/ppermute | solution.py:464
  17.2 5.1 %collective-permute-start.3 = (bf16[128,128]{1,0:T(8,128)(2,1)S(1)}, bf16[128,128]{1,0:T(8,128)(2,1)S(1)}, u32[]{:S(2)}, u32[]{:S(2)}) collective-permute-start(bf16[128,128]{1,0:T(8,128)(2,1)S(1)} %get-tuple-element.52), channel_id=1, source_target_pairs={{0,16},{4,20},{8,24},{12,28},{16,0},{20,4},{24,8},{28,12},{1,17},{... | collective-permute-start | bytes 98312 | tf_op jit(solution)/shard_map/ppermute | solution.py:464
  23.2 5.1 %collective-permute-start.4 = (bf16[128,128]{1,0:T(8,128)(2,1)S(1)}, bf16[128,128]{1,0:T(8,128)(2,1)S(1)}, u32[]{:S(2)}, u32[]{:S(2)}) collective-permute-start(bf16[128,128]{1,0:T(8,128)(2,1)S(1)} %get-tuple-element.58), channel_id=1, source_target_pairs={{0,4},{4,0},{8,12},{12,8},{16,20},{20,16},{24,28},{28,24},{1,5},{5... | collective-permute-start | bytes 98312 | tf_op jit(solution)/shard_map/ppermute | solution.py:464
  23.5 4.9 %collective-permute-start.5 = (bf16[128,128]{1,0:T(8,128)(2,1)S(1)}, bf16[128,128]{1,0:T(8,128)(2,1)S(1)}, u32[]{:S(2)}, u32[]{:S(2)}) collective-permute-start(bf16[128,128]{1,0:T(8,128)(2,1)S(1)} %get-tuple-element.59), channel_id=1, source_target_pairs={{0,8},{4,12},{8,0},{12,4},{16,24},{20,28},{24,16},{28,20},{1,9},{5... | collective-permute-start | bytes 98312 | tf_op jit(solution)/shard_map/ppermute | solution.py:464
  24.9 4.8 %collective-permute-start.6 = (bf16[128,128]{1,0:T(8,128)(2,1)S(1)}, bf16[128,128]{1,0:T(8,128)(2,1)S(1)}, u32[]{:S(2)}, u32[]{:S(2)}) collective-permute-start(bf16[128,128]{1,0:T(8,128)(2,1)S(1)} %get-tuple-element.60), channel_id=1, source_target_pairs={{0,12},{4,8},{8,4},{12,0},{16,28},{20,24},{24,20},{28,16},{1,13},{... | collective-permute-start | bytes 98312 | tf_op jit(solution)/shard_map/ppermute | solution.py:464
  28.3 3.4 %copy-start = (bf16[512,2048]{1,0:T(8,128)(2,1)S(1)}, bf16[512,2048]{1,0:T(8,128)(2,1)}, u32[]{:S(2)}) copy-start(bf16[512,2048]{1,0:T(8,128)(2,1)} %w_ref.7) | copy-start | bytes 6291460
  30.1 1.6 %collective-permute-start.7 = (bf16[2,128,512]{2,1,0:T(8,128)(2,1)S(1)}, bf16[2,128,512]{2,1,0:T(8,128)(2,1)S(1)}, u32[]{:S(2)}, u32[]{:S(2)}) collective-permute-start(bf16[2,128,512]{2,1,0:T(8,128)(2,1)S(1)} %get-tuple-element.62), channel_id=1, source_target_pairs={{0,1},{1,0},{2,3},{3,2},{4,5},{5,4},{6,7},{7,6},{8,9},{9,8},{10,11... | collective-permute-start | bytes 786440 | tf_op jit(solution)/shard_map/ppermute | solution.py:464
  32.2 9.2 %collective-permute-start.10 = (bf16[128,1024]{1,0:T(8,128)(2,1)S(1)}, bf16[128,1024]{1,0:T(8,128)(2,1)S(1)}, u32[]{:S(2)}, u32[]{:S(2)}) collective-permute-start(bf16[128,1024]{1,0:T(8,128)(2,1)S(1)} %project.7), channel_id=1, source_target_pairs={{0,2},{1,3},{2,0},{3,1},{4,6},{5,7},{6,4},{7,5},{8,10},{9,11},{10,... | collective-permute-start | bytes 786440 | tf_op jit(solution)/shard_map/ppermute | solution.py:464
  34.2 12.0 %collective-permute-start.9 = (bf16[128,1024]{1,0:T(8,128)(2,1)S(1)}, bf16[128,1024]{1,0:T(8,128)(2,1)S(1)}, u32[]{:S(2)}, u32[]{:S(2)}) collective-permute-start(bf16[128,1024]{1,0:T(8,128)(2,1)S(1)} %project.5), channel_id=1, source_target_pairs={{0,2},{1,3},{2,0},{3,1},{4,6},{5,7},{6,4},{7,5},{8,10},{9,11},{10,... | collective-permute-start | bytes 786440 | tf_op jit(solution)/shard_map/ppermute | solution.py:464

commit v13 on v12

--- a/solution.py
+++ b/solution.py
@@ -33,11 +33,11 @@
 def dot3(a, b):
     (ah, al), (bh, bl) = a, b
     width = bh.shape[1]
-    left = jnp.concatenate([ah, al], axis=1)
     if width > C:
-        return dot(left, twice(bh)) + dot(ah, bl)
-    both = dot(left, twice(jnp.concatenate([bh, bl], axis=1)))
-    return both[:, :width] + both[:, width:]
+        return dot(jnp.concatenate([ah, al], axis=1), twice(bh)) + dot(ah, bl)
+    rows = ah.shape[0]
+    both = dot(jnp.concatenate([ah, al], axis=0), jnp.concatenate([bh, bl], axis=1))
+    return both[:rows, :width] + (both[:rows, width:] + both[rows:, :width])
 
 
 def iotas():
@@ -216,15 +216,12 @@
     place = lax.rem(lax.axis_index("seq"), heads)
     own_ref[...] = all_ref[place]
     for r in range(1, heads):
-        sends[r - 1][...] = all_ref[other_place(place, r, heads)].astype(BF16)
+        sends[r - 1][...] = all_ref[other_place(place, r)].astype(BF16)
     late.wait()
 
 
-def other_place(place, r, heads):
-    result = place
-    for i in range(heads):
-        result = jnp.where(place == i, i ^ r, result)
-    return result
+def other_place(place, r):
+    return lax.bitwise_xor(place, r)
 
 
 def local_maps(key, value, beta, log_decay, query, batch):
@@ -317,8 +314,8 @@
     heads = held.shape[0]
     place = lax.rem(lax.axis_index("seq"), heads)
     held[place] = own_ref[...]
-    for r, got in enumerate(got_refs, 1):
-        held[other_place(place, r, heads)] = got[...].astype(F32)
+    for r, got in zip(range(heads - 1, 0, -1), got_refs):
+        held[other_place(place, r)] = got[...].astype(F32)
     return place
 
 
@@ -360,7 +357,7 @@
     place = lax.rem(lax.axis_index("seq"), heads)
     keep_ref[...] = states[place]
     for r, send in enumerate(sends, 1):
-        send[...] = states[other_place(place, r, heads)]
+        send[...] = states[other_place(place, r)]
 
 
 def states_of_upper(*refs):
@@ -391,8 +388,8 @@
     half, tokens, _ = rows0_ref.shape
     block = tokens // groups
     place = lax.rem(lax.axis_index("seq"), heads)
-    for r in range(heads):
-        held[other_place(place, r, heads)] = states[r][...]
+    for r, state in zip(range(heads - 1, -1, -1), states):
+        held[other_place(place, r)] = state[...]
     core = lax.rem(lax.axis_index("head"), 2)
     for out_ref, parity in ((send_ref, 1 - core), (keep_ref, core)):
         for i in range(groups // 2):
@@ -464,6 +461,10 @@
     return lax.ppermute(x, axis, [(i, i ^ bit) for i in range(count)])
 
 
+def swap_all(parts):
+    return [swap(parts[r - 1], "seq", r) for r in range(len(parts), 0, -1)]
+
+
 def body(query, key, value, beta, log_decay, out_weight):
     tokens, heads, _ = key.shape
     count = lax.axis_size("seq")
@@ -472,7 +473,7 @@
     q16, k32, *chunk_maps, own, send1, send2, send3 = local_maps(
         flat(key), flat(value), beta, log_decay, flat(query), heads
     )
-    got = [swap(x, "seq", r) for r, x in enumerate((send1, send2, send3), 1)]
+    got = swap_all([send1, send2, send3])
     half = heads // 2
     rows0 = row_maps(heads, range(half), q16, k32, *chunk_maps)
     rows1 = row_maps(heads, range(half, heads), q16, k32, *chunk_maps)
@@ -492,7 +493,7 @@
         keep, *sends = small_call(states_of_upper, outs, *maps, lower)
     else:
         keep, *sends = small_call(states_given, outs, *maps, prefix(total, heads))
-    entering = [keep] + [swap(x, "seq", r) for r, x in enumerate(sends[: heads - 1], 1)]
+    entering = swap_all(sends[: heads - 1]) + [keep]
     keep, away = apply((rows0, rows1), entering, lax.axis_size("head"))
     got = swap(away, "head", 1)
     parts = 2

time: 47.1 us -> 46 us (0.977)
  waiting for transfers between devices: 17.4 us -> 16.3 us
    ppermute x11, waiting for transfers between devices: 17.4 us -> 16.3 us  [swap(): return lax.ppermute(x, axis, [(i, i ^ bit) for i in range(count)])]
  transfers between devices with their start and end apart: 11 -> 11, of which waited for: 7 -> 9; matrix products, arithmetic and copies ran while one was open for 0% -> 0% of each run, Pallas kernels for 33% -> 33%
where the time goes in v13:
time: 46 us; the launch traced here: 45.9 us
  Pallas kernels  16.4 us (36%)
  waiting for transfers between devices  16.3 us (35%)
  starting transfers between devices  13 us (28%)
    ppermute x11, waiting for transfers between devices, swap(): return lax.ppermute(x, axis, [(i, i ^ bit) for i in range(count)])  16.3 us
    ppermute x11, starting transfers between devices, swap(): return lax.ppermute(x, axis, [(i, i ^ bit) for i in range(count)])  13 us
    pallas_call x1, Pallas kernels, local_maps(): pl.pallas_call(functools.partial(local_maps_kernel, heads, batch), in_spe...  6.83 us
    pallas_call x2, Pallas kernels, row_maps(): pl.pallas_call(functools.partial(rows_kernel, heads, mine), in_specs=[her...  3.27 us
    pallas_call x3, Pallas kernels, small_call(): pl.pallas_call(kernel, in_specs=[here] * len(args), out_specs=[here] * le...  2.59 us
    pallas_call x4, Pallas kernels, project(): pl.pallas_call(functools.partial(project_kernel, other, start), out_shape...  1.78 us
    pallas_call x2, Pallas kernels, add_part(): pl.pallas_call(add_kernel, grid=(1,), in_specs=[here, here] + [pl.BlockSp...  1.5 us
  transfers between devices with their start and end apart: 11, of which 9 were waited for; matrix products, arithmetic and copies ran while one was open for 0% of the time, Pallas kernels for 33%

profile of v13, /device:TPU:0, one launch (start us, length us, event | category | flops | bytes accessed | tf_op | source)
XLA Modules:
  0.0 45.9 jit_solution(9418949338382341730)
XLA Ops:
  0.0 0.5 collective-permute-start.8
  0.5 6.8 %local_maps.1 = (bf16[2048,128]{1,0:T(8,128)(2,1)S(1)}, f32[2048,128]{1,0:T(8,128)S(1)}, f32[16,128]{1,0:T(8,128)S(1)}, f32[16,128,128]{2,1,0:T(8,128)S(1)}, f32...) custom-call(bf16[2048,128]{1,0:T(8,128)(2,1)} %bitcast.3, ...), custom_call_target="tpu_custom_call" | custom-call | tf_op jit(solution)/shard_map/local_maps/pallas_call | solution.py:231
  7.3 3.6 %collective-permute-start = (bf16[128,256]{1,0:T(8,128)(2,1)S(1)}, bf16[128,256]{1,0:T(8,128)(2,1)S(1)}, u32[]{:S(2)}, u32[]{:S(2)}) collective-permute-start(bf16[128,256]{1,0:T(8,128)(2,1)S(1)} %get-tuple-element.40), channel_id=1, source_target_pairs={{0,12},{4,8},{8,4},{12,0},{16,28},{20,24},{24,20},{28,16},{1,13},{... | collective-permute-start | bytes 196616 | tf_op jit(solution)/shard_map/ppermute | solution.py:461
  11.5 1.6 %row_maps.2.rows0_ref = f32[2,512,256]{2,1,0:T(8,128)S(1)} custom-call(bf16[2048,128]{1,0:T(8,128)(2,1)S(1)} %get-tuple-element.34.q16, f32[2048,128]{1,0:T(8,128)S(1)} %get-tuple-element.35.k32, f32[16,128]{1,0:T(8,128)S(1)} %get-tuple-element.36.sums_ref, f32[16,128,128]{2,1,0:T(8,128)S(1)} %get-tuple-element.37.mix_ref, ...), custom_call_target="tpu_custom_call" | custom-call | flops 2000000000 | bytes 8000000 | tf_op jit(solution)/shard_map/row_maps/pallas_call | solution.py:284
  13.2 0.5 %collective-permute-done.refs_0_ = bf16[128,256]{1,0:T(8,128)(2,1)S(1)} collective-permute-done((bf16[128,256]{1,0:T(8,128)(2,1)S(1)}, bf16[128,256]{1,0:T(8,128)(2,1)S(1)}, u32[]{:S(2)}, u32[]{:S(2)}) %collective-permute-start) | collective-permute-done | bytes 65568 | tf_op jit(solution)/shard_map/ppermute | solution.py:461
  13.6 1.6 %collective-permute-done.1.refs_1_ = bf16[128,256]{1,0:T(8,128)(2,1)S(1)} collective-permute-done((bf16[128,256]{1,0:T(8,128)(2,1)S(1)}, bf16[128,256]{1,0:T(8,128)(2,1)S(1)}, u32[]{:S(2)}, u32[]{:S(2)}) %collective-permute-start.1) | collective-permute-done | bytes 65568 | tf_op jit(solution)/shard_map/ppermute | solution.py:461
  15.6 0.5 %group_state.1 = (f32[4,128,256]{2,1,0:T(8,128)S(1)}, bf16[128,128]{1,0:T(8,128)(2,1)S(1)}) custom-call(f32[128,256]{1,0:T(8,128)S(1)} %get-tuple-element.44.own_ref, bf16[128,256]{1,0:T(8,128)(2,1)S(1)} %collective-permute-done.refs_0_, bf16[128,256]{1,0:T(8,128)(2,1)S(1)} %collective-permute-done.1.refs_1_, bf16[128,256]{1,0:T(8,128)(2,1)S(1)} %collective-permute-done.2.refs_2_), custom_call_target="tpu_custom_call" | custom-call | tf_op jit(solution)/shard_map/group_state/pallas_call | solution.py:298
  16.1 2.6 %collective-permute-start.3 = (bf16[128,128]{1,0:T(8,128)(2,1)S(1)}, bf16[128,128]{1,0:T(8,128)(2,1)S(1)}, u32[]{:S(2)}, u32[]{:S(2)}) collective-permute-start(bf16[128,128]{1,0:T(8,128)(2,1)S(1)} %get-tuple-element.52), channel_id=1, source_target_pairs={{0,16},{4,20},{8,24},{12,28},{16,0},{20,4},{24,8},{28,12},{1,17},{... | collective-permute-start | bytes 98312 | tf_op jit(solution)/shard_map/ppermute | solution.py:461
  18.7 1.2 %group_prefix.1 = (bf16[4,128,128]{2,1,0:T(8,128)(2,1)S(1)}, bf16[4,128,128]{2,1,0:T(8,128)(2,1)S(1)}, f32[4,128,128]{2,1,0:T(8,128)S(1)}, bf16[128,256]{1,0:T(8,128)(2,1)}) custom-call(f32[4,128,256]{2,1,0:T(8,128)S(1)} %get-tuple-element.48.held), custom_call_target="tpu_custom_call" | custom-call | tf_op jit(solution)/shard_map/group_prefix/pallas_call | solution.py:298
  20.0 1.0 %collective-permute-done.3.refs_3_ = bf16[128,128]{1,0:T(8,128)(2,1)S(1)} collective-permute-done((bf16[128,128]{1,0:T(8,128)(2,1)S(1)}, bf16[128,128]{1,0:T(8,128)(2,1)S(1)}, u32[]{:S(2)}, u32[]{:S(2)}) %collective-permute-start.3) | collective-permute-done | bytes 32800 | tf_op jit(solution)/shard_map/ppermute | solution.py:461
  21.0 0.9 %states_of_upper.1 = (bf16[128,128]{1,0:T(8,128)(2,1)S(1)}, bf16[128,128]{1,0:T(8,128)(2,1)S(1)}, bf16[128,128]{1,0:T(8,128)(2,1)S(1)}, bf16[128,128]{1,0:T(8,128)(2,1)S(1)}, bf16[4,128,128]{2,1,0:T(8,128)(2,1)}) custom-call(bf16[4,128,128]{2,1,0:T(8,128)(2,1)S(1)} %get-tuple-element.53.refs_0_, bf16[4,128,128]{2,1,0:T(8,128)(2,1)S(1)} %get-tuple-element.54.refs_1_, ...), custom_call_target="tpu_custom_call" | custom-call | tf_op jit(solution)/shard_map/states_of_upper/pallas_call | solution.py:298
  21.9 2.1 %collective-permute-start.4 = (bf16[128,128]{1,0:T(8,128)(2,1)S(1)}, bf16[128,128]{1,0:T(8,128)(2,1)S(1)}, u32[]{:S(2)}, u32[]{:S(2)}) collective-permute-start(bf16[128,128]{1,0:T(8,128)(2,1)S(1)} %get-tuple-element.57), channel_id=1, source_target_pairs={{0,12},{4,8},{8,4},{12,0},{16,28},{20,24},{24,20},{28,16},{1,13},{... | collective-permute-start | bytes 98312 | tf_op jit(solution)/shard_map/ppermute | solution.py:461
  24.0 0.7 %collective-permute-start.5 = (bf16[128,128]{1,0:T(8,128)(2,1)S(1)}, bf16[128,128]{1,0:T(8,128)(2,1)S(1)}, u32[]{:S(2)}, u32[]{:S(2)}) collective-permute-start(bf16[128,128]{1,0:T(8,128)(2,1)S(1)} %get-tuple-element.58), channel_id=1, source_target_pairs={{0,8},{4,12},{8,0},{12,4},{16,24},{20,28},{24,16},{28,20},{1,9},{5... | collective-permute-start | bytes 98312 | tf_op jit(solution)/shard_map/ppermute | solution.py:461
  24.6 0.7 %collective-permute-start.6 = (bf16[128,128]{1,0:T(8,128)(2,1)S(1)}, bf16[128,128]{1,0:T(8,128)(2,1)S(1)}, u32[]{:S(2)}, u32[]{:S(2)}) collective-permute-start(bf16[128,128]{1,0:T(8,128)(2,1)S(1)} %get-tuple-element.59), channel_id=1, source_target_pairs={{0,4},{4,0},{8,12},{12,8},{16,20},{20,16},{24,28},{28,24},{1,5},{5... | collective-permute-start | bytes 98312 | tf_op jit(solution)/shard_map/ppermute | solution.py:461
  25.3 1.6 %row_maps.3.rows1_ref = f32[2,512,256]{2,1,0:T(8,128)S(1)} custom-call(bf16[2048,128]{1,0:T(8,128)(2,1)S(1)} %get-tuple-element.34.q16, f32[2048,128]{1,0:T(8,128)S(1)} %get-tuple-element.35.k32, f32[16,128]{1,0:T(8,128)S(1)} %get-tuple-element.36.sums_ref, f32[16,128,128]{2,1,0:T(8,128)S(1)} %get-tuple-element.37.mix_ref, ...), custom_call_target="tpu_custom_call" | custom-call | flops 2000000000 | bytes 8000000 | tf_op jit(solution)/shard_map/row_maps/pallas_call | solution.py:284
  27.0 0.9 %collective-permute-done.5.refs_1_ = bf16[128,128]{1,0:T(8,128)(2,1)S(1)} collective-permute-done((bf16[128,128]{1,0:T(8,128)(2,1)S(1)}, bf16[128,128]{1,0:T(8,128)(2,1)S(1)}, u32[]{:S(2)}, u32[]{:S(2)}) %collective-permute-start.5) | collective-permute-done | bytes 32800 | tf_op jit(solution)/shard_map/ppermute | solution.py:461
  27.9 0.7 %collective-permute-done.6.refs_2_ = bf16[128,128]{1,0:T(8,128)(2,1)S(1)} collective-permute-done((bf16[128,128]{1,0:T(8,128)(2,1)S(1)}, bf16[128,128]{1,0:T(8,128)(2,1)S(1)}, u32[]{:S(2)}, u32[]{:S(2)}) %collective-permute-start.6) | collective-permute-done | bytes 32800 | tf_op jit(solution)/shard_map/ppermute | solution.py:461
  29.1 1.5 %collective-permute-done.7.got_ref = bf16[2,128,512]{2,1,0:T(8,128)(2,1)S(1)} collective-permute-done((bf16[2,128,512]{2,1,0:T(8,128)(2,1)S(1)}, bf16[2,128,512]{2,1,0:T(8,128)(2,1)S(1)}, u32[]{:S(2)}, u32[]{:S(2)}) %collective-permute-start.7) | collective-permute-done | bytes 262176 | tf_op jit(solution)/shard_map/ppermute | solution.py:461
  31.1 1.6 %collective-permute-start.10 = (bf16[128,1024]{1,0:T(8,128)(2,1)S(1)}, bf16[128,1024]{1,0:T(8,128)(2,1)S(1)}, u32[]{:S(2)}, u32[]{:S(2)}) collective-permute-start(bf16[128,1024]{1,0:T(8,128)(2,1)S(1)} %project.7), channel_id=1, source_target_pairs={{0,2},{1,3},{2,0},{3,1},{4,6},{5,7},{6,4},{7,5},{8,10},{9,11},{10,... | collective-permute-start | bytes 786440 | tf_op jit(solution)/shard_map/ppermute | solution.py:461
  33.1 0.6 %collective-permute-start.9 = (bf16[128,1024]{1,0:T(8,128)(2,1)S(1)}, bf16[128,1024]{1,0:T(8,128)(2,1)S(1)}, u32[]{:S(2)}, u32[]{:S(2)}) collective-permute-start(bf16[128,1024]{1,0:T(8,128)(2,1)S(1)} %project.5), channel_id=1, source_target_pairs={{0,2},{1,3},{2,0},{3,1},{4,6},{5,7},{6,4},{7,5},{8,10},{9,11},{10,... | collective-permute-start | bytes 786440 | tf_op jit(solution)/shard_map/ppermute | solution.py:461
  34.6 5.7 %collective-permute-done.10.theirs_ref = bf16[128,1024]{1,0:T(8,128)(2,1)S(1)} collective-permute-done((bf16[128,1024]{1,0:T(8,128)(2,1)S(1)}, bf16[128,1024]{1,0:T(8,128)(2,1)S(1)}, u32[]{:S(2)}, u32[]{:S(2)}) %collective-permute-start.10) | collective-permute-done | bytes 262176 | tf_op jit(solution)/shard_map/ppermute | solution.py:461
  40.3 0.7 %add_part.2.refs_0_ = bf16[128,2048]{1,0:T(8,128)(2,1)} custom-call(f32[128,1024]{1,0:T(8,128)S(1)} %project.6.mine_ref, bf16[128,1024]{1,0:T(8,128)(2,1)S(1)} %collective-permute-done.10.theirs_ref), custom_call_target="tpu_custom_call" | custom-call | tf_op jit(solution)/shard_map/add_part/pallas_call | solution.py:447
  41.0 4.1 %collective-permute-done.9.theirs_ref = bf16[128,1024]{1,0:T(8,128)(2,1)S(1)} collective-permute-done((bf16[128,1024]{1,0:T(8,128)(2,1)S(1)}, bf16[128,1024]{1,0:T(8,128)(2,1)S(1)}, u32[]{:S(2)}, u32[]{:S(2)}) %collective-permute-start.9) | collective-permute-done | bytes 262176 | tf_op jit(solution)/shard_map/ppermute | solution.py:461
  45.1 0.7 %add_part.3 = bf16[128,2048]{1,0:T(8,128)(2,1)} custom-call(f32[128,1024]{1,0:T(8,128)S(1)} %project.4.mine_ref, bf16[128,1024]{1,0:T(8,128)(2,1)S(1)} %collective-permute-done.9.theirs_ref, bf16[128,2048]{1,0:T(8,128)(2,1)} %add_part.2.refs_0_), custom_call_target="tpu_custom_call", output_to_operand_aliasing={{}: (2, {})} | custom-call | tf_op jit(solution)/shard_map/add_part/pallas_call | solution.py:447
  (13 shorter events, 3.3 us)
Async XLA Ops:
  0.0 30.6 %collective-permute-start.8 = (bf16[512,2048]{1,0:T(8,128)(2,1)}, bf16[512,2048]{1,0:T(8,128)(2,1)S(1)}, u32[]{:S(2)}, u32[]{:S(2)}) collective-permute-start(bf16[512,2048]{1,0:T(8,128)(2,1)} %w_ref.7), channel_id=1, source_target_pairs={{0,1},{1,0},{2,3},{3,2},{4,5},{5,4},{6,7},{7,6},{8,9},{9,8},{10,11... | collective-permute-start | bytes 6291464 | tf_op jit(solution)/shard_map/ppermute | solution.py:461
  7.3 6.3 %collective-permute-start = (bf16[128,256]{1,0:T(8,128)(2,1)S(1)}, bf16[128,256]{1,0:T(8,128)(2,1)S(1)}, u32[]{:S(2)}, u32[]{:S(2)}) collective-permute-start(bf16[128,256]{1,0:T(8,128)(2,1)S(1)} %get-tuple-element.40), channel_id=1, source_target_pairs={{0,12},{4,8},{8,4},{12,0},{16,28},{20,24},{24,20},{28,16},{1,13},{... | collective-permute-start | bytes 196616 | tf_op jit(solution)/shard_map/ppermute | solution.py:461
  10.9 4.3 %collective-permute-start.1 = (bf16[128,256]{1,0:T(8,128)(2,1)S(1)}, bf16[128,256]{1,0:T(8,128)(2,1)S(1)}, u32[]{:S(2)}, u32[]{:S(2)}) collective-permute-start(bf16[128,256]{1,0:T(8,128)(2,1)S(1)} %get-tuple-element.41), channel_id=1, source_target_pairs={{0,8},{4,12},{8,0},{12,4},{16,24},{20,28},{24,16},{28,20},{1,9},{5... | collective-permute-start | bytes 196616 | tf_op jit(solution)/shard_map/ppermute | solution.py:461
  11.3 4.3 %collective-permute-start.2 = (bf16[128,256]{1,0:T(8,128)(2,1)S(1)}, bf16[128,256]{1,0:T(8,128)(2,1)S(1)}, u32[]{:S(2)}, u32[]{:S(2)}) collective-permute-start(bf16[128,256]{1,0:T(8,128)(2,1)S(1)} %get-tuple-element.42), channel_id=1, source_target_pairs={{0,4},{4,0},{8,12},{12,8},{16,20},{20,16},{24,28},{28,24},{1,5},{5... | collective-permute-start | bytes 196616 | tf_op jit(solution)/shard_map/ppermute | solution.py:461
  16.1 4.9 %collective-permute-start.3 = (bf16[128,128]{1,0:T(8,128)(2,1)S(1)}, bf16[128,128]{1,0:T(8,128)(2,1)S(1)}, u32[]{:S(2)}, u32[]{:S(2)}) collective-permute-start(bf16[128,128]{1,0:T(8,128)(2,1)S(1)} %get-tuple-element.52), channel_id=1, source_target_pairs={{0,16},{4,20},{8,24},{12,28},{16,0},{20,4},{24,8},{28,12},{1,17},{... | collective-permute-start | bytes 98312 | tf_op jit(solution)/shard_map/ppermute | solution.py:461
  21.9 5.1 %collective-permute-start.4 = (bf16[128,128]{1,0:T(8,128)(2,1)S(1)}, bf16[128,128]{1,0:T(8,128)(2,1)S(1)}, u32[]{:S(2)}, u32[]{:S(2)}) collective-permute-start(bf16[128,128]{1,0:T(8,128)(2,1)S(1)} %get-tuple-element.57), channel_id=1, source_target_pairs={{0,12},{4,8},{8,4},{12,0},{16,28},{20,24},{24,20},{28,16},{1,13},{... | collective-permute-start | bytes 98312 | tf_op jit(solution)/shard_map/ppermute | solution.py:461
  24.0 3.9 %collective-permute-start.5 = (bf16[128,128]{1,0:T(8,128)(2,1)S(1)}, bf16[128,128]{1,0:T(8,128)(2,1)S(1)}, u32[]{:S(2)}, u32[]{:S(2)}) collective-permute-start(bf16[128,128]{1,0:T(8,128)(2,1)S(1)} %get-tuple-element.58), channel_id=1, source_target_pairs={{0,8},{4,12},{8,0},{12,4},{16,24},{20,28},{24,16},{28,20},{1,9},{5... | collective-permute-start | bytes 98312 | tf_op jit(solution)/shard_map/ppermute | solution.py:461
  24.6 3.9 %collective-permute-start.6 = (bf16[128,128]{1,0:T(8,128)(2,1)S(1)}, bf16[128,128]{1,0:T(8,128)(2,1)S(1)}, u32[]{:S(2)}, u32[]{:S(2)}) collective-permute-start(bf16[128,128]{1,0:T(8,128)(2,1)S(1)} %get-tuple-element.59), channel_id=1, source_target_pairs={{0,4},{4,0},{8,12},{12,8},{16,20},{20,16},{24,28},{28,24},{1,5},{5... | collective-permute-start | bytes 98312 | tf_op jit(solution)/shard_map/ppermute | solution.py:461
  27.0 3.6 %copy-start = (bf16[512,2048]{1,0:T(8,128)(2,1)S(1)}, bf16[512,2048]{1,0:T(8,128)(2,1)}, u32[]{:S(2)}) copy-start(bf16[512,2048]{1,0:T(8,128)(2,1)} %w_ref.7) | copy-start | bytes 6291460
  29.0 1.6 %collective-permute-start.7 = (bf16[2,128,512]{2,1,0:T(8,128)(2,1)S(1)}, bf16[2,128,512]{2,1,0:T(8,128)(2,1)S(1)}, u32[]{:S(2)}, u32[]{:S(2)}) collective-permute-start(bf16[2,128,512]{2,1,0:T(8,128)(2,1)S(1)} %get-tuple-element.62), channel_id=1, source_target_pairs={{0,1},{1,0},{2,3},{3,2},{4,5},{5,4},{6,7},{7,6},{8,9},{9,8},{10,11... | collective-permute-start | bytes 786440 | tf_op jit(solution)/shard_map/ppermute | solution.py:461
  31.1 9.2 %collective-permute-start.10 = (bf16[128,1024]{1,0:T(8,128)(2,1)S(1)}, bf16[128,1024]{1,0:T(8,128)(2,1)S(1)}, u32[]{:S(2)}, u32[]{:S(2)}) collective-permute-start(bf16[128,1024]{1,0:T(8,128)(2,1)S(1)} %project.7), channel_id=1, source_target_pairs={{0,2},{1,3},{2,0},{3,1},{4,6},{5,7},{6,4},{7,5},{8,10},{9,11},{10,... | collective-permute-start | bytes 786440 | tf_op jit(solution)/shard_map/ppermute | solution.py:461
  33.1 12.0 %collective-permute-start.9 = (bf16[128,1024]{1,0:T(8,128)(2,1)S(1)}, bf16[128,1024]{1,0:T(8,128)(2,1)S(1)}, u32[]{:S(2)}, u32[]{:S(2)}) collective-permute-start(bf16[128,1024]{1,0:T(8,128)(2,1)S(1)} %project.5), channel_id=1, source_target_pairs={{0,2},{1,3},{2,0},{3,1},{4,6},{5,7},{6,4},{7,5},{8,10},{9,11},{10,... | collective-permute-start | bytes 786440 | tf_op jit(solution)/shard_map/ppermute | solution.py:461

commit v14 on v13

v14 whole, which is shorter than its diff:
```python
import functools

import jax
import jax.numpy as jnp
from jax import lax
from jax.experimental import pallas as pl
from jax.experimental.pallas import tpu as pltpu
from jax.sharding import PartitionSpec as P

C = 128
B = 16
F32 = jnp.float32
BF16 = jnp.bfloat16
NN = (((1,), (0,)), ((), ()))
NT = (((1,), (1,)), ((), ()))
TN = (((0,), (0,)), ((), ()))
MIB = 1024 * 1024


def dot(a, b, dims=NN):
    return lax.dot_general(a, b, dims, preferred_element_type=F32)


def split(x):
    high = x.astype(BF16)
    return high, (x - high.astype(F32)).astype(BF16)


def twice(x):
    return jnp.concatenate([x, x], axis=0)


def dot3(a, b):
    (ah, al), (bh, bl) = a, b
    width = bh.shape[1]
    if width > C:
        return dot(jnp.concatenate([ah, al], axis=1), twice(bh)) + dot(ah, bl)
    rows = ah.shape[0]
    both = dot(jnp.concatenate([ah, al], axis=0), jnp.concatenate([bh, bl], axis=1))
    return both[:rows, :width] + (both[:rows, width:] + both[rows:, :width])


def iotas():
    return (
        lax.broadcasted_iota(jnp.int32, (C, C), 0),
        lax.broadcasted_iota(jnp.int32, (C, C), 1),
    )


def to_column(row, eye):
    return jnp.sum(jnp.where(eye, row, 0.0), axis=1, keepdims=True)


def to_row(column, eye):
    return jnp.sum(jnp.where(eye, column, 0.0), axis=0, keepdims=True)


def inverse_scale(rows):
    return lax.rsqrt(jnp.sum(rows * rows, axis=1, keepdims=True) + 1e-06)


def three(x):
    high, rest = x.astype(BF16), x
    rest = rest - high.astype(F32)
    return (high,) + split(rest)


def running_sums(rows, upper):
    return sum(dot(x, upper) for x in reversed(three(rows)))


def base_inverse(lower, row, col):
    on_block = (row // B) == (col // B)
    blocks = jnp.where(on_block, lower, 0.0)
    packed = sum(blocks[i * B : (i + 1) * B] for i in range(1, C // B)) + blocks[:B]
    r, c = row[:B], col[:B]
    found = jnp.where(r == c % B, 1.0, 0.0)
    first = (c // B) * B
    for j in range(B - 1):
        factor = jnp.take_along_axis(packed, first + j, axis=1)
        found = found - factor * found[j : j + 1]
    return jnp.where(on_block, jnp.concatenate([found] * (C // B), axis=0), 0.0)


def odd_rows(x, size):
    return jnp.concatenate([x[i : i + size] for i in range(size, C, 2 * size)], axis=0)


def weave(even, odd, size):
    parts = []
    for i in range(0, C // 2, size):
        parts += [even[i : i + size], odd[i : i + size]]
    return jnp.concatenate(parts, axis=0)


def even_rows(x, size):
    return jnp.concatenate([x[i : i + size] for i in range(0, C, 2 * size)], axis=0)


def inverses(lowers, row, col):
    found = [base_inverse(a, row, col) for a in lowers]
    parts = [split(a) for a in lowers]
    halves = [split(x) for x in found]
    size = B
    while size < C:
        r, c = odd_rows(row, size), odd_rows(col, size)
        mask = ((r // (2 * size)) == (c // (2 * size))) & ((r // size) != (c // size))
        nothing = jnp.zeros((C // 2, C), BF16)
        mask = jnp.where(mask, 1.0, 0.0).astype(BF16)
        joins = [tuple(odd_rows(x, size) * mask for x in part) for part in parts]
        middle = [split(dot3(a, x)) for a, x in zip(joins, halves)]
        middle = [tuple(weave(nothing, x, size) for x in part) for part in middle]
        lows = [dot3(tuple(odd_rows(x, size) for x in h), y) for h, y in zip(halves, middle)]
        lows = [odd_rows(x, size) - y for x, y in zip(found, lows)]
        found = [weave(even_rows(x, size), y, size) for x, y in zip(found, lows)]
        if 2 * size < C:
            halves = [
                tuple(weave(even_rows(x, size), y, size) for x, y in zip(h, split(low)))
                for h, low in zip(halves, lows)
            ]
        size *= 2
    return found


def fetch(pairs, sems):
    copies = [pltpu.make_async_copy(x, y, sems.at[i]) for i, (x, y) in enumerate(pairs)]
    for copy in copies:
        copy.start()
    return copies


def in_hbm(*arrays):
    return [pltpu.with_memory_space_constraint(x, pltpu.HBM) for x in arrays]


def join(moved, added):
    return jnp.concatenate([moved, added], axis=1)


def after(later, earlier):
    total = dot3(split(later[:, :C]), split(earlier))
    return join(total[:, :C], total[:, C:] + later[:, C:])


def per_chunk(ref):
    return jnp.concatenate([ref[:, i : i + C] for i in range(0, ref.shape[1], C)], axis=0)


def chunk_rows(heads, head, c):
    return pl.ds(c * C * heads + head, C, stride=heads)


def places(heads):
    place = lax.rem(lax.axis_index("seq"), heads)
    return place, [lax.bitwise_xor(place, r) for r in range(heads - 1, -1, -1)]


def local_heads(heads, mine, k32, v32, sums_ref, betas_ref, mix_ref, wu_ref, n_ref):
    chunks = sums_ref.shape[0] // heads
    row, col = iotas()
    eye = row == col
    within = row >= col
    strict = row > col
    eye16 = jnp.where(eye, 1.0, 0.0).astype(BF16)
    jobs = [(head, c) for head in mine for c in range(chunks)]
    sums = jnp.concatenate([sums_ref[pl.ds(head, chunks, stride=heads), :] for head in mine], axis=0)
    betas = jnp.concatenate([betas_ref[pl.ds(head, chunks, stride=heads), :] for head in mine], axis=0)
    filled = jnp.concatenate([sums, jnp.zeros((C - sums.shape[0], C), F32)], axis=0)
    columns = filled.T
    grown = jnp.exp(sums)
    faded = jnp.exp(sums[:, C - 1 :] - sums)
    lowers, raws, values, fades, lengths = [], [], [], [], []
    for i, (head, c) in enumerate(jobs):
        at = slice(i, i + 1)
        raw = k32[chunk_rows(heads, head, c), :].astype(BF16)
        raws.append(raw)
        values.append(v32[chunk_rows(heads, head, c), :].astype(BF16))
        both = dot(jnp.concatenate([raw, eye16], axis=0), raw, NT)
        gram, turned = both[:C], both[C:]
        square = to_row(gram, eye) + 1e-06
        scale = lax.rsqrt(square)
        lengths.append(square * scale)
        strength = betas[at] * (scale * scale)
        mix = jnp.where(within, jnp.exp(columns[:, at] - sums[at]), 0.0) * strength
        mix_ref[i] = mix
        lowers.append(jnp.where(strict, gram * mix, 0.0))
        fades.append(turned * (strength * faded[at]))
    solved = []
    for i, found in enumerate(inverses(lowers, row, col)):
        at = slice(i, i + 1)
        kept = dot(jnp.concatenate(split(found * grown[at]), axis=1), twice(raws[i]))
        fresh = dot(jnp.concatenate(split(found * lengths[i]), axis=1), twice(values[i]))
        solved.append(join(kept, fresh))
    maps = []
    for i in range(len(jobs)):
        wu_ref[i] = solved[i]
        both = dot3(split(fades[i]), split(solved[i]))
        maps.append(join(jnp.where(eye, grown[i : i + 1, C - 1 :], 0.0) - both[:, :C], both[:, C:]))
    totals = []
    for j in range(len(mine)):
        first, second, third, last = maps[j * chunks : (j + 1) * chunks]
        early = after(second, first)
        n_ref[j * chunks + 1] = first
        n_ref[j * chunks + 2] = early
        n_ref[j * chunks + 3] = after(third, early)
        totals.append(after(after(last, third), early))
    return totals


def first_kernel(
    heads, k_hbm, v_hbm, beta_hbm, log_hbm, q_hbm, q16, k32, v32, sums_ref, betas_ref, mix_ref, wu_ref, n_ref, *refs
):
    sends, (k16, v16, beta_ref, log_ref, sems) = refs[: heads - 1], refs[heads - 1 :]
    pairs = ((k_hbm, k16), (log_hbm, log_ref), (beta_hbm, beta_ref), (v_hbm, v16), (q_hbm, q16))
    *copies, late = fetch(pairs, sems)
    for copy in copies:
        copy.wait()
    k32[...] = k16[...].astype(F32)
    v32[...] = v16[...].astype(F32)
    row, col = iotas()
    sums_ref[...] = running_sums(per_chunk(log_ref), jnp.where(row <= col, 1.0, 0.0).astype(BF16))
    betas_ref[...] = per_chunk(beta_ref)
    mine = places(heads)[1][: heads - 1]
    totals = local_heads(heads, mine, k32, v32, sums_ref, betas_ref, mix_ref, wu_ref, n_ref)
    for send, total in zip(sends, totals):
        send[...] = total.astype(BF16)
    late.wait()


def maps_shapes(heads, chunks):
    return [
        jax.ShapeDtypeStruct((heads * chunks, C, C), F32),
        jax.ShapeDtypeStruct((heads * chunks, C, 2 * C), F32),
        jax.ShapeDtypeStruct((heads * chunks, C, 2 * C), F32),
    ] + [jax.ShapeDtypeStruct((C, 2 * C), BF16)] * heads


def first_maps(key, value, beta, log_decay, query):
    heads, tokens = beta.shape
    chunks = tokens // C
    here = pl.BlockSpec(memory_space=pltpu.VMEM)
    rows = jax.ShapeDtypeStruct((chunks * heads, C), F32)
    wide = jax.ShapeDtypeStruct(key.shape, F32)
    out_shape = [jax.ShapeDtypeStruct(query.shape, BF16), wide, wide, rows, rows] + maps_shapes(heads - 1, chunks)
    return pl.pallas_call(
        functools.partial(first_kernel, heads),
        in_specs=[pl.BlockSpec(memory_space=pltpu.HBM)] * 5,
        out_specs=[here] * len(out_shape),
        out_shape=out_shape,
        scratch_shapes=[
            pltpu.VMEM(key.shape, BF16),
            pltpu.VMEM(key.shape, BF16),
            pltpu.VMEM(beta.shape, F32),
            pltpu.VMEM(beta.shape, F32),
            pltpu.SemaphoreType.DMA((5,)),
        ],
        compiler_params=pltpu.CompilerParams(vmem_limit_bytes=32 * MIB),
        name="first_maps",
    )(*in_hbm(key, value, beta, log_decay, query))


def own_kernel(heads, k32, v32, sums_ref, betas_ref, mix_ref, wu_ref, n_ref, own_ref):
    mine = places(heads)[1][heads - 1 :]
    (total,) = local_heads(heads, mine, k32, v32, sums_ref, betas_ref, mix_ref, wu_ref, n_ref)
    own_ref[...] = total.astype(BF16)


def own_maps(heads, k32, v32, sums, betas):
    here = pl.BlockSpec(memory_space=pltpu.VMEM)
    out_shape = maps_shapes(1, sums.shape[0] // heads)
    return pl.pallas_call(
        functools.partial(own_kernel, heads),
        in_specs=[here] * 4,
        out_specs=[here] * len(out_shape),
        out_shape=out_shape,
        compiler_params=pltpu.CompilerParams(vmem_limit_bytes=16 * MIB),
        cost_estimate=pl.CostEstimate(flops=2000000000, bytes_accessed=8000000, transcendentals=0),
        name="own_maps",
    )(k32, v32, sums, betas)


def rows_kernel(heads, work, q16, k32, sums_ref, *refs):
    *maps, out_ref, q32 = refs
    q32[...] = q16[...].astype(F32)
    chunks = sums_ref.shape[0] // heads
    row, col = iotas()
    eye = row == col
    order = places(heads)[1]
    for j, (spot, source, slot) in enumerate(work):
        mix_ref, wu_ref, n_ref = maps[3 * source : 3 * source + 3]
        head = order[spot]
        grown = jnp.exp(sums_ref[pl.ds(head, chunks, stride=heads), :])
        for c in range(chunks):
            i = slot * chunks + c
            query, raw = q32[chunk_rows(heads, head, c), :], k32[chunk_rows(heads, head, c), :]
            pairs = dot(query.astype(BF16), raw.astype(BF16), NT) * mix_ref[i]
            both = dot3(split(pairs), split(wu_ref[i]))
            scale = inverse_scale(query)
            reach = (query * to_column(grown[c : c + 1], eye) - both[:, :C]) * scale
            fresh = both[:, C:] * scale
            if c > 0:
                earlier = dot3(split(reach), split(n_ref[i]))
                reach = earlier[:, :C]
                fresh = fresh + earlier[:, C:]
            out_ref[j, c * C : (c + 1) * C, :] = join(reach, fresh)


def row_maps(heads, work, query, k32, sums, *maps):
    tokens = query.shape[0] // heads
    here = pl.BlockSpec(memory_space=pltpu.VMEM)
    return pl.pallas_call(
        functools.partial(rows_kernel, heads, work),
        in_specs=[here] * (3 + len(maps)),
        out_specs=here,
        out_shape=jax.ShapeDtypeStruct((len(work), tokens, 2 * C), F32),
        scratch_shapes=[pltpu.VMEM(query.shape, F32)],
        compiler_params=pltpu.CompilerParams(vmem_limit_bytes=16 * MIB),
        cost_estimate=pl.CostEstimate(flops=2000000000, bytes_accessed=8000000, transcendentals=0),
        name="row_maps",
    )(query, k32, sums, *maps)


def small_call(kernel, out_shape, *args):
    here = pl.BlockSpec(memory_space=pltpu.VMEM)
    return pl.pallas_call(
        kernel,
        in_specs=[here] * len(args),
        out_specs=[here] * len(out_shape),
        out_shape=out_shape,
        compiler_params=pltpu.CompilerParams(vmem_limit_bytes=8 * MIB),
        name=kernel.__name__,
    )(*args)


def moved_on(maps, state16, added):
    high, low = split(maps)
    return dot(jnp.concatenate([high, low], axis=1), twice(state16)) + added


def times_parts(maps16, x):
    width = x.shape[1]
    both = dot(maps16, jnp.concatenate(split(x), axis=1))
    return both[:, :width] + both[:, width:]


def by_place(parts, work):
    heads = len(parts)
    place = places(heads)[0]
    for p in range(heads):

        @pl.when(place == p)
        def _(p=p):
            members = [i ^ p for i in range(heads)]
            work([parts[heads - 1 - r] for r in members], members)


def group_state(*refs):
    out_ref = refs[-1]

    def work(parts, _):
        state = parts[0][:, C:].astype(F32)
        for part in parts[1:]:
            state = times_parts(part[:, :C], state) + part[:, C:].astype(F32)
        out_ref[...] = state.astype(BF16)

    by_place(refs[:-1], work)


def group_prefix(*refs):
    parts, (maps_ref, added_ref, total_ref) = refs[:-3], refs[-3:]
    row, col = iotas()

    def work(parts, members):
        total = join(jnp.where(row == col, 1.0, 0.0), jnp.zeros((C, C), F32))
        for i, (part, r) in enumerate(zip(parts, members)):
            maps_ref[r] = jnp.concatenate(split(total[:, :C]), axis=1)
            added_ref[r] = total[:, C:]
            if i == 0:
                total = part[...].astype(F32)
            else:
                total = times_parts(part[:, :C], total)
                total = join(total[:, :C], total[:, C:] + part[:, C:].astype(F32))
        total_ref[...] = total.astype(BF16)

    by_place(parts, work)


def group_states(upper_only, maps_ref, added_ref, state_ref, *outs):
    state = state_ref[...]
    if upper_only:
        state = jnp.where(lax.axis_index("seq") < len(outs), jnp.zeros_like(state), state)
    both = twice(state)
    for r, out_ref in enumerate(outs):
        out_ref[...] = (dot(maps_ref[r], both) + added_ref[r]).astype(BF16)


def states_of_upper(*refs):
    group_states(True, *refs)


def states_given(*refs):
    group_states(False, *refs)


def prefix(total, heads):
    count = lax.axis_size("seq")
    groups = [list(range(i, count, heads)) for i in range(heads)]
    me = lax.axis_index("seq") // heads
    totals = lax.all_gather(total, "seq", axis_index_groups=groups)

    def step(d, state):
        longer = jnp.einsum("ik,pkw->iw", totals[d, :, :C], jnp.stack(split(state)), preferred_element_type=F32)
        return jnp.where(d < me, longer + totals[d, :, C:].astype(F32), state)

    start = jnp.zeros((C, C), F32)
    return lax.fori_loop(0, count // heads - 1, step, start).astype(BF16)


def apply_kernel(groups, rows0_ref, rows1_ref, *refs):
    states, (keep_ref, send_ref) = refs[:-2], refs[-2:]
    heads = len(states)
    half, tokens, _ = rows0_ref.shape
    block = tokens // groups
    order = places(heads)[1]
    core = lax.rem(lax.axis_index("head"), 2)
    for out_ref, parity in ((send_ref, 1 - core), (keep_ref, core)):
        for i in range(groups // 2):
            rows = pl.ds(pl.multiple_of((2 * i + parity) * block, block), block)
            for spot, state in enumerate(states):
                ref, j = (rows0_ref, rows1_ref)[spot // half], spot % half
                attended = moved_on(ref[j, rows, :C], state[...], ref[j, rows, C:])
                columns = pl.ds(pl.multiple_of(order[spot] * C, C), C)
                out_ref[i, :, columns] = attended.astype(BF16)


def apply(rows, states, groups):
    _, tokens, _ = rows[0].shape
    heads = len(states)
    here = pl.BlockSpec(memory_space=pltpu.VMEM)
    out = jax.ShapeDtypeStruct((groups // 2, tokens // groups, heads * C), BF16)
    return pl.pallas_call(
        functools.partial(apply_kernel, groups),
        in_specs=[here] * (2 + heads),
        out_specs=[here] * 2,
        out_shape=[out, out],
        compiler_params=pltpu.CompilerParams(vmem_limit_bytes=8 * MIB),
        name="apply",
    )(*rows, *states)


def project_kernel(other, start, keep_ref, got_ref, w_ref, w2_ref, out_ref):
    pair = lax.axis_index("head") // 2
    index = 1 - pair if other else pair
    columns = slice(start, start + out_ref.shape[1])
    shares = dot(keep_ref[index], w_ref[:, columns]) + dot(got_ref[index], w2_ref[:, columns])
    out_ref[...] = shares.astype(out_ref.dtype)


def project(other, start, width, keep, got, weight, weight2):
    _, block, depth = keep.shape
    return pl.pallas_call(
        functools.partial(project_kernel, other, start),
        out_shape=jax.ShapeDtypeStruct((block, width), BF16 if other else F32),
        compiler_params=pltpu.CompilerParams(vmem_limit_bytes=20 * MIB),
        cost_estimate=pl.CostEstimate(
            flops=4 * block * depth * width, bytes_accessed=4 * depth * width, transcendentals=0
        ),
        name="project",
    )(keep, got, weight, weight2)


def add_kernel(mine_ref, theirs_ref, *refs):
    refs[-1][...] = (mine_ref[...] + theirs_ref[...].astype(F32)).astype(BF16)


def add_part(index, parts, mine, theirs, earlier):
    block, width = mine.shape
    here = pl.BlockSpec(memory_space=pltpu.VMEM)
    return pl.pallas_call(
        add_kernel,
        grid=(1,),
        in_specs=[here, here] + [pl.BlockSpec(memory_space=pl.ANY)] * len(earlier),
        out_specs=pl.BlockSpec((block, width), lambda i: (0, index)),
        out_shape=jax.ShapeDtypeStruct((block, width * parts), BF16),
        input_output_aliases={2: 0} if earlier else {},
        compiler_params=pltpu.CompilerParams(vmem_limit_bytes=8 * MIB),
        name="add_part",
    )(mine, theirs, *earlier)


def swap(x, axis, bit):
    count = lax.axis_size(axis)
    return lax.ppermute(x, axis, [(i, i ^ bit) for i in range(count)])


def body(query, key, value, beta, log_decay, out_weight):
    tokens, heads, _ = key.shape
    count = lax.axis_size("seq")
    flat = lambda x: x.reshape(tokens * heads, C)
    weight2 = swap(out_weight, "head", 1)
    q16, k32, v32, sums, betas, mix, wu, states, *sends = first_maps(
        flat(key), flat(value), beta, log_decay, flat(query)
    )
    away = range(heads - 1, 0, -1)
    parts = [swap(x, "seq", r) for r, x in zip(away, sends)]
    *own_chunks, own = own_maps(heads, k32, v32, sums, betas)
    parts = lax.optimization_barrier(parts + [own])
    first = (mix, wu, states)
    rows0 = row_maps(heads, ((0, 0, 0), (1, 0, 1)), q16, k32, sums, *first)
    rows1 = row_maps(heads, ((2, 0, 2), (3, 1, 0)), q16, k32, sums, *first, *own_chunks)
    square = jax.ShapeDtypeStruct((C, C), BF16)
    both = jax.ShapeDtypeStruct((heads, C, 2 * C), BF16)
    added = jax.ShapeDtypeStruct((heads, C, C), F32)
    (state,) = small_call(group_state, [square], *parts)
    *maps, total = small_call(group_prefix, [both, added, jax.ShapeDtypeStruct((C, 2 * C), BF16)], *parts)
    if count == 2 * heads:
        lower = swap(state, "seq", heads)
        rows0, maps, lower = lax.optimization_barrier((rows0, maps, lower))
        keep, *sends = small_call(states_of_upper, [square] * heads, *maps, lower)
    else:
        keep, *sends = small_call(states_given, [square] * heads, *maps, prefix(total, heads))
    entering = [swap(sends[r - 1], "seq", r) for r in away] + [keep]
    keep, away = apply((rows0, rows1), entering, lax.axis_size("head"))
    got = swap(away, "head", 1)
    parts = 2
    width = out_weight.shape[1] // parts
    ranges = [(i * width, width) for i in range(parts)]
    args = (keep, got, out_weight, weight2)
    theirs = [swap(project(True, *x, *args), "head", 2) for x in ranges]
    mine = [project(False, *x, *args) for x in ranges]
    mixed = []
    for i in range(parts):
        mixed = [add_part(i, parts, mine[i], theirs[i], mixed)]
    return mixed[0]


def solution(mesh):
    in_specs = (
        P("seq", "head", None),
        P("seq", "head", None),
        P("seq", "head", None),
        P("head", "seq"),
        P("head", "seq"),
        P("head", None),
    )
    out_specs = P(("seq", "head"), None)
    return jax.shard_map(body, mesh=mesh, in_specs=in_specs, out_specs=out_specs, check_vma=False)
```

time: 46 us -> 44.9 us (0.976)
  waiting for transfers between devices: 16.3 us -> 14.2 us
  Pallas kernels: 16.4 us -> 17.3 us
    ppermute x11, waiting for transfers between devices: 16.3 us -> 14.2 us  [swap(): return lax.ppermute(x, axis, [(i, i ^ bit) for i in range(count)])]
    pallas_call x3 -> x4, Pallas kernels: 10.1 us -> 11.4 us  [the longest x1 5.69 us: first_maps(): pl.pallas_call(functools.partial(first_kernel, heads), in_specs=[pl.Block...]
    pallas_call x3, Pallas kernels: 2.59 us -> 2.1 us  [small_call(): pl.pallas_call(kernel, in_specs=[here] * len(args), out_specs=[here] * le...]
  transfers between devices with their start and end apart: 11 -> 11, of which waited for: 9 -> 7; matrix products, arithmetic and copies ran while one was open for 0% -> 0% of each run, Pallas kernels for 33% -> 36%
where the time goes in v14:
time: 44.9 us; the launch traced here: 44.7 us
  Pallas kernels  17.3 us (39%)
  waiting for transfers between devices  14.2 us (32%)
  starting transfers between devices  13.1 us (29%)
    ppermute x11, waiting for transfers between devices, swap(): return lax.ppermute(x, axis, [(i, i ^ bit) for i in range(count)])  14.2 us
    ppermute x11, starting transfers between devices, swap(): return lax.ppermute(x, axis, [(i, i ^ bit) for i in range(count)])  13.1 us
    pallas_call x1, Pallas kernels, first_maps(): pl.pallas_call(functools.partial(first_kernel, heads), in_specs=[pl.Block...  5.69 us
    pallas_call x2, Pallas kernels, row_maps(): pl.pallas_call(functools.partial(rows_kernel, heads, work), in_specs=[her...  3.36 us
    pallas_call x1, Pallas kernels, own_maps(): pl.pallas_call(functools.partial(own_kernel, heads), in_specs=[here] * 4,...  2.39 us
    pallas_call x3, Pallas kernels, small_call(): pl.pallas_call(kernel, in_specs=[here] * len(args), out_specs=[here] * le...  2.1 us
    pallas_call x4, Pallas kernels, project(): pl.pallas_call(functools.partial(project_kernel, other, start), out_shape...  1.77 us
    pallas_call x2, Pallas kernels, add_part(): pl.pallas_call(add_kernel, grid=(1,), in_specs=[here, here] + [pl.BlockSp...  1.5 us
  transfers between devices with their start and end apart: 11, of which 7 were waited for; matrix products, arithmetic and copies ran while one was open for 0% of the time, Pallas kernels for 36%

profile of v14, /device:TPU:0, one launch (start us, length us, event | category | flops | bytes accessed | tf_op | source)
XLA Modules:
  0.0 44.7 jit_solution(511261406071978487)
XLA Ops:
  0.0 0.5 %collective-permute-start.8 = (bf16[512,2048]{1,0:T(8,128)(2,1)}, bf16[512,2048]{1,0:T(8,128)(2,1)S(1)}, u32[]{:S(2)}, u32[]{:S(2)}) collective-permute-start(bf16[512,2048]{1,0:T(8,128)(2,1)} %w_ref.7), channel_id=1, source_target_pairs={{0,1},{1,0},{2,3},{3,2},{4,5},{5,4},{6,7},{7,6},{8,9},{9,8},{10,11... | collective-permute-start | bytes 6291464 | tf_op jit(solution)/shard_map/ppermute | solution.py:493
  0.5 5.7 %first_maps.1 = (bf16[2048,128]{1,0:T(8,128)(2,1)S(1)}, f32[2048,128]{1,0:T(8,128)S(1)}, f32[2048,128]{1,0:T(8,128)S(1)}, f32[16,128]{1,0:T(8,128)S(1)}, f32[16,...) custom-call(bf16[2048,128]{1,0:T(8,128)(2,1)} %bitcast.3, ...), custom_call_target="tpu_custom_call" | custom-call | tf_op jit(solution)/shard_map/first_maps/pallas_call | solution.py:245
  6.2 3.6 %collective-permute-start = (bf16[128,256]{1,0:T(8,128)(2,1)S(1)}, bf16[128,256]{1,0:T(8,128)(2,1)S(1)}, u32[]{:S(2)}, u32[]{:S(2)}) collective-permute-start(bf16[128,256]{1,0:T(8,128)(2,1)S(1)} %get-tuple-element.42), channel_id=1, source_target_pairs={{0,12},{4,8},{8,4},{12,0},{16,28},{20,24},{24,20},{28,16},{1,13},{... | collective-permute-start | bytes 196616 | tf_op jit(solution)/shard_map/ppermute | solution.py:493
  9.7 0.5 %collective-permute-start.1 = (bf16[128,256]{1,0:T(8,128)(2,1)S(1)}, bf16[128,256]{1,0:T(8,128)(2,1)S(1)}, u32[]{:S(2)}, u32[]{:S(2)}) collective-permute-start(bf16[128,256]{1,0:T(8,128)(2,1)S(1)} %get-tuple-element.43), channel_id=1, source_target_pairs={{0,8},{4,12},{8,0},{12,4},{16,24},{20,28},{24,16},{28,20},{1,9},{5... | collective-permute-start | bytes 196616 | tf_op jit(solution)/shard_map/ppermute | solution.py:493
  10.4 2.4 %own_maps.1 = (f32[4,128,128]{2,1,0:T(8,128)S(1)}, f32[4,128,256]{2,1,0:T(8,128)S(1)}, f32[4,128,256]{2,1,0:T(8,128)S(1)}, bf16[128,256]{1,0:T(8,128)(2,1)S(1)}) custom-call(f32[2048,128]{1,0:T(8,128)S(1)} %get-tuple-element.37.k32, f32[2048,128]{1,0:T(8,128)S(1)} %get-tuple-element.45.v32, f32[16,128]{1,0:T(8,128)S(1)} %get-tuple-element.38.sums_ref, ...), custom_call_target="tpu_custom_call" | custom-call | flops 2000000000 | bytes 8000000 | tf_op jit(solution)/shard_map/own_maps/pallas_call | solution.py:271
  12.8 1.3 %collective-permute-done.1.refs_1_ = bf16[128,256]{1,0:T(8,128)(2,1)S(1)} collective-permute-done((bf16[128,256]{1,0:T(8,128)(2,1)S(1)}, bf16[128,256]{1,0:T(8,128)(2,1)S(1)}, u32[]{:S(2)}, u32[]{:S(2)}) %collective-permute-start.1) | collective-permute-done | bytes 65568 | tf_op jit(solution)/shard_map/ppermute | solution.py:493
  14.4 0.5 %group_state.1 = bf16[128,128]{1,0:T(8,128)(2,1)S(1)} custom-call(bf16[128,256]{1,0:T(8,128)(2,1)S(1)} %collective-permute-done.refs_0_, bf16[128,256]{1,0:T(8,128)(2,1)S(1)} %collective-permute-done.1.refs_1_, bf16[128,256]{1,0:T(8,128)(2,1)S(1)} %collective-permute-done.2.refs_2_, bf16[128,256]{1,0:T(8,128)(2,1)S(1)} %get-tuple-element.51.refs_3_), custom_call_target="tpu_custom_call" | custom-call | tf_op jit(solution)/shard_map/group_state/pallas_call | solution.py:325
  14.9 2.6 %collective-permute-start.3 = (bf16[128,128]{1,0:T(8,128)(2,1)S(1)}, bf16[128,128]{1,0:T(8,128)(2,1)S(1)}, u32[]{:S(2)}, u32[]{:S(2)}) collective-permute-start(bf16[128,128]{1,0:T(8,128)(2,1)S(1)} %group_state.1), channel_id=1, source_target_pairs={{0,16},{4,20},{8,24},{12,28},{16,0},{20,4},{24,8},{28,12},{1,17},{... | collective-permute-start | bytes 98312 | tf_op jit(solution)/shard_map/ppermute | solution.py:493
  17.6 1.7 %row_maps.2.rows0_ref = f32[2,512,256]{2,1,0:T(8,128)S(1)} custom-call(bf16[2048,128]{1,0:T(8,128)(2,1)S(1)} %get-tuple-element.36.q16, f32[2048,128]{1,0:T(8,128)S(1)} %get-tuple-element.37.k32, f32[16,128]{1,0:T(8,128)S(1)} %get-tuple-element.38.sums_ref, f32[12,128,128]{2,1,0:T(8,128)S(1)} %get-tuple-element.39.refs_0_, ...), custom_call_target="tpu_custom_call" | custom-call | flops 2000000000 | bytes 8000000 | tf_op jit(solution)/shard_map/row_maps/pallas_call | solution.py:311
  19.3 1.4 %group_prefix.1 = (bf16[4,128,256]{2,1,0:T(8,128)(2,1)S(1)}, f32[4,128,128]{2,1,0:T(8,128)S(1)}, bf16[128,256]{1,0:T(8,128)(2,1)}) custom-call(bf16[128,256]{1,0:T(8,128)(2,1)S(1)} %collective-permute-done.refs_0_, bf16[128,256]{1,0:T(8,128)(2,1)S(1)} %collective-permute-done.1.refs_1_, bf16[128,256]{1,0:T(8,128)(2,1)S(1)} %collective-permute-done.2.refs_2_, ...), custom_call_target="tpu_custom_call" | custom-call | tf_op jit(solution)/shard_map/group_prefix/pallas_call | solution.py:325
  20.9 2.1 %collective-permute-start.4 = (bf16[128,128]{1,0:T(8,128)(2,1)S(1)}, bf16[128,128]{1,0:T(8,128)(2,1)S(1)}, u32[]{:S(2)}, u32[]{:S(2)}) collective-permute-start(bf16[128,128]{1,0:T(8,128)(2,1)S(1)} %get-tuple-element.61), channel_id=1, source_target_pairs={{0,12},{4,8},{8,4},{12,0},{16,28},{20,24},{24,20},{28,16},{1,13},{... | collective-permute-start | bytes 98312 | tf_op jit(solution)/shard_map/ppermute | solution.py:493
  23.0 0.5 %collective-permute-start.5 = (bf16[128,128]{1,0:T(8,128)(2,1)S(1)}, bf16[128,128]{1,0:T(8,128)(2,1)S(1)}, u32[]{:S(2)}, u32[]{:S(2)}) collective-permute-start(bf16[128,128]{1,0:T(8,128)(2,1)S(1)} %get-tuple-element.62), channel_id=1, source_target_pairs={{0,8},{4,12},{8,0},{12,4},{16,24},{20,28},{24,16},{28,20},{1,9},{5... | collective-permute-start | bytes 98312 | tf_op jit(solution)/shard_map/ppermute | solution.py:493
  23.5 0.9 %collective-permute-start.6 = (bf16[128,128]{1,0:T(8,128)(2,1)S(1)}, bf16[128,128]{1,0:T(8,128)(2,1)S(1)}, u32[]{:S(2)}, u32[]{:S(2)}) collective-permute-start(bf16[128,128]{1,0:T(8,128)(2,1)S(1)} %get-tuple-element.63), channel_id=1, source_target_pairs={{0,4},{4,0},{8,12},{12,8},{16,20},{20,16},{24,28},{28,24},{1,5},{5... | collective-permute-start | bytes 98312 | tf_op jit(solution)/shard_map/ppermute | solution.py:493
  24.4 1.7 %row_maps.3.rows1_ref = f32[2,512,256]{2,1,0:T(8,128)S(1)} custom-call(bf16[2048,128]{1,0:T(8,128)(2,1)S(1)} %get-tuple-element.36.q16, f32[2048,128]{1,0:T(8,128)S(1)} %get-tuple-element.37.k32, f32[16,128]{1,0:T(8,128)S(1)} %get-tuple-element.38.sums_ref, f32[12,128,128]{2,1,0:T(8,128)S(1)} %get-tuple-element.39.refs_0_, ...), custom_call_target="tpu_custom_call" | custom-call | flops 2000000000 | bytes 8000000 | tf_op jit(solution)/shard_map/row_maps/pallas_call | solution.py:311
  26.2 0.8 %collective-permute-done.5.refs_1_ = bf16[128,128]{1,0:T(8,128)(2,1)S(1)} collective-permute-done((bf16[128,128]{1,0:T(8,128)(2,1)S(1)}, bf16[128,128]{1,0:T(8,128)(2,1)S(1)}, u32[]{:S(2)}, u32[]{:S(2)}) %collective-permute-start.5) | collective-permute-done | bytes 32800 | tf_op jit(solution)/shard_map/ppermute | solution.py:493
  26.9 0.5 %collective-permute-done.6.refs_2_ = bf16[128,128]{1,0:T(8,128)(2,1)S(1)} collective-permute-done((bf16[128,128]{1,0:T(8,128)(2,1)S(1)}, bf16[128,128]{1,0:T(8,128)(2,1)S(1)}, u32[]{:S(2)}, u32[]{:S(2)}) %collective-permute-start.6) | collective-permute-done | bytes 32800 | tf_op jit(solution)/shard_map/ppermute | solution.py:493
  27.4 0.4 %apply.1 = (bf16[2,128,512]{2,1,0:T(8,128)(2,1)S(1)}, bf16[2,128,512]{2,1,0:T(8,128)(2,1)S(1)}) custom-call(f32[2,512,256]{2,1,0:T(8,128)S(1)} %row_maps.2.rows0_ref, f32[2,512,256]{2,1,0:T(8,128)S(1)} %row_maps.3.rows1_ref, bf16[128,128]{1,0:T(8,128)(2,1)S(1)} %collective-permute-done.4.refs_0_, bf16[128,128]{1,0:T(8,128)(2,1)S(1)} %collective-permute-done.5.refs_1_, ...), custom_call_target="tpu_custom_call" | custom-call | tf_op jit(solution)/shard_map/apply/pallas_call | solution.py:441
  28.0 1.5 %collective-permute-done.7.got_ref = bf16[2,128,512]{2,1,0:T(8,128)(2,1)S(1)} collective-permute-done((bf16[2,128,512]{2,1,0:T(8,128)(2,1)S(1)}, bf16[2,128,512]{2,1,0:T(8,128)(2,1)S(1)}, u32[]{:S(2)}, u32[]{:S(2)}) %collective-permute-start.7) | collective-permute-done | bytes 262176 | tf_op jit(solution)/shard_map/ppermute | solution.py:493
  29.9 1.6 %collective-permute-start.10 = (bf16[128,1024]{1,0:T(8,128)(2,1)S(1)}, bf16[128,1024]{1,0:T(8,128)(2,1)S(1)}, u32[]{:S(2)}, u32[]{:S(2)}) collective-permute-start(bf16[128,1024]{1,0:T(8,128)(2,1)S(1)} %project.7), channel_id=1, source_target_pairs={{0,2},{1,3},{2,0},{3,1},{4,6},{5,7},{6,4},{7,5},{8,10},{9,11},{10,... | collective-permute-start | bytes 786440 | tf_op jit(solution)/shard_map/ppermute | solution.py:493
  32.0 0.6 %collective-permute-start.9 = (bf16[128,1024]{1,0:T(8,128)(2,1)S(1)}, bf16[128,1024]{1,0:T(8,128)(2,1)S(1)}, u32[]{:S(2)}, u32[]{:S(2)}) collective-permute-start(bf16[128,1024]{1,0:T(8,128)(2,1)S(1)} %project.5), channel_id=1, source_target_pairs={{0,2},{1,3},{2,0},{3,1},{4,6},{5,7},{6,4},{7,5},{8,10},{9,11},{10,... | collective-permute-start | bytes 786440 | tf_op jit(solution)/shard_map/ppermute | solution.py:493
  33.4 5.7 %collective-permute-done.10.theirs_ref = bf16[128,1024]{1,0:T(8,128)(2,1)S(1)} collective-permute-done((bf16[128,1024]{1,0:T(8,128)(2,1)S(1)}, bf16[128,1024]{1,0:T(8,128)(2,1)S(1)}, u32[]{:S(2)}, u32[]{:S(2)}) %collective-permute-start.10) | collective-permute-done | bytes 262176 | tf_op jit(solution)/shard_map/ppermute | solution.py:493
  39.2 0.7 %add_part.2.refs_0_ = bf16[128,2048]{1,0:T(8,128)(2,1)} custom-call(f32[128,1024]{1,0:T(8,128)S(1)} %project.6.mine_ref, bf16[128,1024]{1,0:T(8,128)(2,1)S(1)} %collective-permute-done.10.theirs_ref), custom_call_target="tpu_custom_call" | custom-call | tf_op jit(solution)/shard_map/add_part/pallas_call | solution.py:479
  39.9 4.1 %collective-permute-done.9.theirs_ref = bf16[128,1024]{1,0:T(8,128)(2,1)S(1)} collective-permute-done((bf16[128,1024]{1,0:T(8,128)(2,1)S(1)}, bf16[128,1024]{1,0:T(8,128)(2,1)S(1)}, u32[]{:S(2)}, u32[]{:S(2)}) %collective-permute-start.9) | collective-permute-done | bytes 262176 | tf_op jit(solution)/shard_map/ppermute | solution.py:493
  44.0 0.7 %add_part.3 = bf16[128,2048]{1,0:T(8,128)(2,1)} custom-call(f32[128,1024]{1,0:T(8,128)S(1)} %project.4.mine_ref, bf16[128,1024]{1,0:T(8,128)(2,1)S(1)} %collective-permute-done.9.theirs_ref, bf16[128,2048]{1,0:T(8,128)(2,1)} %add_part.2.refs_0_), custom_call_target="tpu_custom_call", output_to_operand_aliasing={{}: (2, {})} | custom-call | tf_op jit(solution)/shard_map/add_part/pallas_call | solution.py:479
  (14 shorter events, 2.7 us)
Async XLA Ops:
  0.0 29.5 %collective-permute-start.8 = (bf16[512,2048]{1,0:T(8,128)(2,1)}, bf16[512,2048]{1,0:T(8,128)(2,1)S(1)}, u32[]{:S(2)}, u32[]{:S(2)}) collective-permute-start(bf16[512,2048]{1,0:T(8,128)(2,1)} %w_ref.7), channel_id=1, source_target_pairs={{0,1},{1,0},{2,3},{3,2},{4,5},{5,4},{6,7},{7,6},{8,9},{9,8},{10,11... | collective-permute-start | bytes 6291464 | tf_op jit(solution)/shard_map/ppermute | solution.py:493
  6.2 6.6 %collective-permute-start = (bf16[128,256]{1,0:T(8,128)(2,1)S(1)}, bf16[128,256]{1,0:T(8,128)(2,1)S(1)}, u32[]{:S(2)}, u32[]{:S(2)}) collective-permute-start(bf16[128,256]{1,0:T(8,128)(2,1)S(1)} %get-tuple-element.42), channel_id=1, source_target_pairs={{0,12},{4,8},{8,4},{12,0},{16,28},{20,24},{24,20},{28,16},{1,13},{... | collective-permute-start | bytes 196616 | tf_op jit(solution)/shard_map/ppermute | solution.py:493
  9.7 4.3 %collective-permute-start.1 = (bf16[128,256]{1,0:T(8,128)(2,1)S(1)}, bf16[128,256]{1,0:T(8,128)(2,1)S(1)}, u32[]{:S(2)}, u32[]{:S(2)}) collective-permute-start(bf16[128,256]{1,0:T(8,128)(2,1)S(1)} %get-tuple-element.43), channel_id=1, source_target_pairs={{0,8},{4,12},{8,0},{12,4},{16,24},{20,28},{24,16},{28,20},{1,9},{5... | collective-permute-start | bytes 196616 | tf_op jit(solution)/shard_map/ppermute | solution.py:493
  10.2 4.3 %collective-permute-start.2 = (bf16[128,256]{1,0:T(8,128)(2,1)S(1)}, bf16[128,256]{1,0:T(8,128)(2,1)S(1)}, u32[]{:S(2)}, u32[]{:S(2)}) collective-permute-start(bf16[128,256]{1,0:T(8,128)(2,1)S(1)} %get-tuple-element.44), channel_id=1, source_target_pairs={{0,4},{4,0},{8,12},{12,8},{16,20},{20,16},{24,28},{28,24},{1,5},{5... | collective-permute-start | bytes 196616 | tf_op jit(solution)/shard_map/ppermute | solution.py:493
  14.9 5.7 %collective-permute-start.3 = (bf16[128,128]{1,0:T(8,128)(2,1)S(1)}, bf16[128,128]{1,0:T(8,128)(2,1)S(1)}, u32[]{:S(2)}, u32[]{:S(2)}) collective-permute-start(bf16[128,128]{1,0:T(8,128)(2,1)S(1)} %group_state.1), channel_id=1, source_target_pairs={{0,16},{4,20},{8,24},{12,28},{16,0},{20,4},{24,8},{28,12},{1,17},{... | collective-permute-start | bytes 98312 | tf_op jit(solution)/shard_map/ppermute | solution.py:493
  20.9 5.3 %collective-permute-start.4 = (bf16[128,128]{1,0:T(8,128)(2,1)S(1)}, bf16[128,128]{1,0:T(8,128)(2,1)S(1)}, u32[]{:S(2)}, u32[]{:S(2)}) collective-permute-start(bf16[128,128]{1,0:T(8,128)(2,1)S(1)} %get-tuple-element.61), channel_id=1, source_target_pairs={{0,12},{4,8},{8,4},{12,0},{16,28},{20,24},{24,20},{28,16},{1,13},{... | collective-permute-start | bytes 98312 | tf_op jit(solution)/shard_map/ppermute | solution.py:493
  23.0 3.9 %collective-permute-start.5 = (bf16[128,128]{1,0:T(8,128)(2,1)S(1)}, bf16[128,128]{1,0:T(8,128)(2,1)S(1)}, u32[]{:S(2)}, u32[]{:S(2)}) collective-permute-start(bf16[128,128]{1,0:T(8,128)(2,1)S(1)} %get-tuple-element.62), channel_id=1, source_target_pairs={{0,8},{4,12},{8,0},{12,4},{16,24},{20,28},{24,16},{28,20},{1,9},{5... | collective-permute-start | bytes 98312 | tf_op jit(solution)/shard_map/ppermute | solution.py:493
  23.5 3.9 %collective-permute-start.6 = (bf16[128,128]{1,0:T(8,128)(2,1)S(1)}, bf16[128,128]{1,0:T(8,128)(2,1)S(1)}, u32[]{:S(2)}, u32[]{:S(2)}) collective-permute-start(bf16[128,128]{1,0:T(8,128)(2,1)S(1)} %get-tuple-element.63), channel_id=1, source_target_pairs={{0,4},{4,0},{8,12},{12,8},{16,20},{20,16},{24,28},{28,24},{1,5},{5... | collective-permute-start | bytes 98312 | tf_op jit(solution)/shard_map/ppermute | solution.py:493
  26.1 3.3 %copy-start = (bf16[512,2048]{1,0:T(8,128)(2,1)S(1)}, bf16[512,2048]{1,0:T(8,128)(2,1)}, u32[]{:S(2)}) copy-start(bf16[512,2048]{1,0:T(8,128)(2,1)} %w_ref.7) | copy-start | bytes 6291460
  27.9 1.6 %collective-permute-start.7 = (bf16[2,128,512]{2,1,0:T(8,128)(2,1)S(1)}, bf16[2,128,512]{2,1,0:T(8,128)(2,1)S(1)}, u32[]{:S(2)}, u32[]{:S(2)}) collective-permute-start(bf16[2,128,512]{2,1,0:T(8,128)(2,1)S(1)} %get-tuple-element.66), channel_id=1, source_target_pairs={{0,1},{1,0},{2,3},{3,2},{4,5},{5,4},{6,7},{7,6},{8,9},{9,8},{10,11... | collective-permute-start | bytes 786440 | tf_op jit(solution)/shard_map/ppermute | solution.py:493
  29.9 9.2 %collective-permute-start.10 = (bf16[128,1024]{1,0:T(8,128)(2,1)S(1)}, bf16[128,1024]{1,0:T(8,128)(2,1)S(1)}, u32[]{:S(2)}, u32[]{:S(2)}) collective-permute-start(bf16[128,1024]{1,0:T(8,128)(2,1)S(1)} %project.7), channel_id=1, source_target_pairs={{0,2},{1,3},{2,0},{3,1},{4,6},{5,7},{6,4},{7,5},{8,10},{9,11},{10,... | collective-permute-start | bytes 786440 | tf_op jit(solution)/shard_map/ppermute | solution.py:493
  32.0 12.0 %collective-permute-start.9 = (bf16[128,1024]{1,0:T(8,128)(2,1)S(1)}, bf16[128,1024]{1,0:T(8,128)(2,1)S(1)}, u32[]{:S(2)}, u32[]{:S(2)}) collective-permute-start(bf16[128,1024]{1,0:T(8,128)(2,1)S(1)} %project.5), channel_id=1, source_target_pairs={{0,2},{1,3},{2,0},{3,1},{4,6},{5,7},{6,4},{7,5},{8,10},{9,11},{10,... | collective-permute-start | bytes 786440 | tf_op jit(solution)/shard_map/ppermute | solution.py:493

commit v15 on v14

--- a/solution.py
+++ b/solution.py
@@ -120,13 +120,6 @@
             ]
         size *= 2
     return found
-
-
-def fetch(pairs, sems):
-    copies = [pltpu.make_async_copy(x, y, sems.at[i]) for i, (x, y) in enumerate(pairs)]
-    for copy in copies:
-        copy.start()
-    return copies
 
 
 def in_hbm(*arrays):
@@ -211,15 +204,21 @@
     heads, k_hbm, v_hbm, beta_hbm, log_hbm, q_hbm, q16, k32, v32, sums_ref, betas_ref, mix_ref, wu_ref, n_ref, *refs
 ):
     sends, (k16, v16, beta_ref, log_ref, sems) = refs[: heads - 1], refs[heads - 1 :]
-    pairs = ((k_hbm, k16), (log_hbm, log_ref), (beta_hbm, beta_ref), (v_hbm, v16), (q_hbm, q16))
-    *copies, late = fetch(pairs, sems)
-    for copy in copies:
+    pairs = ((log_hbm, log_ref), (beta_hbm, beta_ref), (k_hbm, k16), (v_hbm, v16), (q_hbm, q16))
+    copies = [pltpu.make_async_copy(x, y, sems.at[i]) for i, (x, y) in enumerate(pairs)]
+    *early, late = copies
+    for copy in early:
+        copy.start()
+    for copy in early[:2]:
         copy.wait()
-    k32[...] = k16[...].astype(F32)
-    v32[...] = v16[...].astype(F32)
     row, col = iotas()
     sums_ref[...] = running_sums(per_chunk(log_ref), jnp.where(row <= col, 1.0, 0.0).astype(BF16))
     betas_ref[...] = per_chunk(beta_ref)
+    early[2].wait()
+    k32[...] = k16[...].astype(F32)
+    early[3].wait()
+    late.start()
+    v32[...] = v16[...].astype(F32)
     mine = places(heads)[1][: heads - 1]
     totals = local_heads(heads, mine, k32, v32, sums_ref, betas_ref, mix_ref, wu_ref, n_ref)
     for send, total in zip(sends, totals):
@@ -279,45 +278,45 @@
     )(k32, v32, sums, betas)
 
 
-def rows_kernel(heads, work, q16, k32, sums_ref, *refs):
-    *maps, out_ref, q32 = refs
-    q32[...] = q16[...].astype(F32)
+def rows_kernel(heads, spot, slot, q_ref, k32, sums_ref, mix_ref, wu_ref, n_ref, out_ref, *wide):
+    if wide:
+        wide[0][...] = q_ref[...].astype(F32)
+    q32 = wide[0] if wide else q_ref
     chunks = sums_ref.shape[0] // heads
     row, col = iotas()
     eye = row == col
-    order = places(heads)[1]
-    for j, (spot, source, slot) in enumerate(work):
-        mix_ref, wu_ref, n_ref = maps[3 * source : 3 * source + 3]
-        head = order[spot]
-        grown = jnp.exp(sums_ref[pl.ds(head, chunks, stride=heads), :])
-        for c in range(chunks):
-            i = slot * chunks + c
-            query, raw = q32[chunk_rows(heads, head, c), :], k32[chunk_rows(heads, head, c), :]
-            pairs = dot(query.astype(BF16), raw.astype(BF16), NT) * mix_ref[i]
-            both = dot3(split(pairs), split(wu_ref[i]))
-            scale = inverse_scale(query)
-            reach = (query * to_column(grown[c : c + 1], eye) - both[:, :C]) * scale
-            fresh = both[:, C:] * scale
-            if c > 0:
-                earlier = dot3(split(reach), split(n_ref[i]))
-                reach = earlier[:, :C]
-                fresh = fresh + earlier[:, C:]
-            out_ref[j, c * C : (c + 1) * C, :] = join(reach, fresh)
-
-
-def row_maps(heads, work, query, k32, sums, *maps):
+    head = places(heads)[1][spot]
+    grown = jnp.exp(sums_ref[pl.ds(head, chunks, stride=heads), :])
+    for c in range(chunks):
+        i = slot * chunks + c
+        query, raw = q32[chunk_rows(heads, head, c), :], k32[chunk_rows(heads, head, c), :]
+        pairs = dot(query.astype(BF16), raw.astype(BF16), NT) * mix_ref[i]
+        both = dot3(split(pairs), split(wu_ref[i]))
+        scale = inverse_scale(query)
+        reach = (query * to_column(grown[c : c + 1], eye) - both[:, :C]) * scale
+        fresh = both[:, C:] * scale
+        if c > 0:
+            earlier = dot3(split(reach), split(n_ref[i]))
+            reach = earlier[:, :C]
+            fresh = fresh + earlier[:, C:]
+        out_ref[c * C : (c + 1) * C, :] = join(reach, fresh)
+
+
+def row_maps(heads, spot, slot, query, *maps):
     tokens = query.shape[0] // heads
     here = pl.BlockSpec(memory_space=pltpu.VMEM)
-    return pl.pallas_call(
-        functools.partial(rows_kernel, heads, work),
-        in_specs=[here] * (3 + len(maps)),
-        out_specs=here,
-        out_shape=jax.ShapeDtypeStruct((len(work), tokens, 2 * C), F32),
-        scratch_shapes=[pltpu.VMEM(query.shape, F32)],
+    out_shape = [jax.ShapeDtypeStruct((tokens, 2 * C), F32)]
+    if query.dtype == BF16:
+        out_shape.append(jax.ShapeDtypeStruct(query.shape, F32))
+    return pl.pallas_call(
+        functools.partial(rows_kernel, heads, spot, slot),
+        in_specs=[here] * (1 + len(maps)),
+        out_specs=[here] * len(out_shape),
+        out_shape=out_shape,
         compiler_params=pltpu.CompilerParams(vmem_limit_bytes=16 * MIB),
-        cost_estimate=pl.CostEstimate(flops=2000000000, bytes_accessed=8000000, transcendentals=0),
+        cost_estimate=pl.CostEstimate(flops=1000000000, bytes_accessed=4000000, transcendentals=0),
         name="row_maps",
-    )(query, k32, sums, *maps)
+    )(query, *maps)
 
 
 def small_call(kernel, out_shape, *args):
@@ -416,51 +415,47 @@
     return lax.fori_loop(0, count // heads - 1, step, start).astype(BF16)
 
 
-def apply_kernel(groups, rows0_ref, rows1_ref, *refs):
-    states, (keep_ref, send_ref) = refs[:-2], refs[-2:]
-    heads = len(states)
-    half, tokens, _ = rows0_ref.shape
-    block = tokens // groups
+def apply_kernel(groups, other, *refs):
+    heads = (len(refs) - 2) // 2
+    rows_refs, states, (keep_ref, send_ref) = refs[:heads], refs[heads : 2 * heads], refs[2 * heads :]
+    block = rows_refs[0].shape[0] // groups
     order = places(heads)[1]
-    core = lax.rem(lax.axis_index("head"), 2)
+    member = lax.axis_index("head")
+    pair, core = member // 2, lax.rem(member, 2)
+    pair = 1 - pair if other else pair
     for out_ref, parity in ((send_ref, 1 - core), (keep_ref, core)):
-        for i in range(groups // 2):
-            rows = pl.ds(pl.multiple_of((2 * i + parity) * block, block), block)
-            for spot, state in enumerate(states):
-                ref, j = (rows0_ref, rows1_ref)[spot // half], spot % half
-                attended = moved_on(ref[j, rows, :C], state[...], ref[j, rows, C:])
-                columns = pl.ds(pl.multiple_of(order[spot] * C, C), C)
-                out_ref[i, :, columns] = attended.astype(BF16)
-
-
-def apply(rows, states, groups):
-    _, tokens, _ = rows[0].shape
+        rows = pl.ds(pl.multiple_of((2 * pair + parity) * block, block), block)
+        for head, rows_ref, state in zip(order, rows_refs, states):
+            attended = moved_on(rows_ref[rows, :C], state[...], rows_ref[rows, C:])
+            out_ref[:, pl.ds(pl.multiple_of(head * C, C), C)] = attended.astype(BF16)
+
+
+def apply(other, rows, states, groups):
     heads = len(states)
     here = pl.BlockSpec(memory_space=pltpu.VMEM)
-    out = jax.ShapeDtypeStruct((groups // 2, tokens // groups, heads * C), BF16)
-    return pl.pallas_call(
-        functools.partial(apply_kernel, groups),
-        in_specs=[here] * (2 + heads),
+    out = jax.ShapeDtypeStruct((rows[0].shape[0] // groups, heads * C), BF16)
+    return pl.pallas_call(
+        functools.partial(apply_kernel, groups, other),
+        in_specs=[here] * (2 * heads),
         out_specs=[here] * 2,
         out_shape=[out, out],
         compiler_params=pltpu.CompilerParams(vmem_limit_bytes=8 * MIB),
+        cost_estimate=pl.CostEstimate(flops=200000000, bytes_accessed=1000000, transcendentals=0),
         name="apply",
     )(*rows, *states)
 
 
-def project_kernel(other, start, keep_ref, got_ref, w_ref, w2_ref, out_ref):
-    pair = lax.axis_index("head") // 2
-    index = 1 - pair if other else pair
+def project_kernel(start, keep_ref, got_ref, w_ref, w2_ref, out_ref):
     columns = slice(start, start + out_ref.shape[1])
-    shares = dot(keep_ref[index], w_ref[:, columns]) + dot(got_ref[index], w2_ref[:, columns])
+    shares = dot(keep_ref[...], w_ref[:, columns]) + dot(got_ref[...], w2_ref[:, columns])
     out_ref[...] = shares.astype(out_ref.dtype)
 
 
-def project(other, start, width, keep, got, weight, weight2):
-    _, block, depth = keep.shape
-    return pl.pallas_call(
-        functools.partial(project_kernel, other, start),
-        out_shape=jax.ShapeDtypeStruct((block, width), BF16 if other else F32),
+def project(dtype, start, width, keep, got, weight, weight2):
+    block, depth = keep.shape
+    return pl.pallas_call(
+        functools.partial(project_kernel, start),
+        out_shape=jax.ShapeDtypeStruct((block, width), dtype),
         compiler_params=pltpu.CompilerParams(vmem_limit_bytes=20 * MIB),
         cost_estimate=pl.CostEstimate(
             flops=4 * block * depth * width, bytes_accessed=4 * depth * width, transcendentals=0
@@ -504,30 +499,38 @@
     away = range(heads - 1, 0, -1)
     parts = [swap(x, "seq", r) for r, x in zip(away, sends)]
     *own_chunks, own = own_maps(heads, k32, v32, sums, betas)
-    parts = lax.optimization_barrier(parts + [own])
-    first = (mix, wu, states)
-    rows0 = row_maps(heads, ((0, 0, 0), (1, 0, 1)), q16, k32, sums, *first)
-    rows1 = row_maps(heads, ((2, 0, 2), (3, 1, 0)), q16, k32, sums, *first, *own_chunks)
+    first = (k32, sums, mix, wu, states)
+    own_maps_here = (k32, sums, *own_chunks)
+    rows3, q32 = row_maps(heads, 0, 0, q16, *first)
+    rows3, *parts = lax.optimization_barrier([rows3] + parts + [own])
     square = jax.ShapeDtypeStruct((C, C), BF16)
     both = jax.ShapeDtypeStruct((heads, C, 2 * C), BF16)
     added = jax.ShapeDtypeStruct((heads, C, C), F32)
     (state,) = small_call(group_state, [square], *parts)
+    state, q32 = lax.optimization_barrier((state, q32))
+    (rows2,) = row_maps(heads, 1, 1, q32, *first)
     *maps, total = small_call(group_prefix, [both, added, jax.ShapeDtypeStruct((C, 2 * C), BF16)], *parts)
     if count == 2 * heads:
         lower = swap(state, "seq", heads)
-        rows0, maps, lower = lax.optimization_barrier((rows0, maps, lower))
+        rows2, maps, lower = lax.optimization_barrier((rows2, maps, lower))
         keep, *sends = small_call(states_of_upper, [square] * heads, *maps, lower)
     else:
         keep, *sends = small_call(states_given, [square] * heads, *maps, prefix(total, heads))
+    keep, q32 = lax.optimization_barrier((keep, q32))
+    (rows1,) = row_maps(heads, 2, 2, q32, *first)
+    (rows0,) = row_maps(heads, 3, 0, q32, *own_maps_here)
     entering = [swap(sends[r - 1], "seq", r) for r in away] + [keep]
-    keep, away = apply((rows0, rows1), entering, lax.axis_size("head"))
-    got = swap(away, "head", 1)
+    rows = (rows3, rows2, rows1, rows0)
+    groups = lax.axis_size("head")
+    keep, send = apply(True, rows, entering, groups)
+    across = (keep, swap(send, "head", 1), out_weight, weight2)
+    keep, send = apply(False, rows, entering, groups)
+    here = (keep, swap(send, "head", 1), out_weight, weight2)
     parts = 2
     width = out_weight.shape[1] // parts
     ranges = [(i * width, width) for i in range(parts)]
-    args = (keep, got, out_weight, weight2)
-    theirs = [swap(project(True, *x, *args), "head", 2) for x in ranges]
-    mine = [project(False, *x, *args) for x in ranges]
+    theirs = [swap(project(BF16, *x, *across), "head", 2) for x in ranges]
+    mine = [project(F32, *x, *here) for x in ranges]
     mixed = []
     for i in range(parts):
         mixed = [add_part(i, parts, mine[i], theirs[i], mixed)]

time: 44.9 us -> 43.9 us (0.978)
  waiting for transfers between devices: 14.2 us -> 12.5 us
  Pallas kernels: 17.3 us -> 17.9 us
    ppermute x11 -> x12, waiting for transfers between devices: 14.2 us -> 12.5 us  [swap(): return lax.ppermute(x, axis, [(i, i ^ bit) for i in range(count)])]
    pallas_call x7 -> x10, Pallas kernels: 5.58 us -> 6.35 us  [the longest x4 3.98 us: row_maps(): pl.pallas_call(functools.partial(rows_kernel, heads, spot, slot), in_spec...]
    ppermute x11 -> x12, starting transfers between devices: 13.1 us -> 13.2 us  [swap(): return lax.ppermute(x, axis, [(i, i ^ bit) for i in range(count)])]
  transfers between devices with their start and end apart: 11 -> 12, of which waited for: 7 -> 8; matrix products, arithmetic and copies ran while one was open for 0% -> 0% of each run, Pallas kernels for 36% -> 38%
where the time goes in v15:
time: 43.9 us; the launch traced here: 43.7 us
  Pallas kernels  17.9 us (41%)
  starting transfers between devices  13.2 us (30%)
  waiting for transfers between devices  12.5 us (28%)
    ppermute x12, starting transfers between devices, swap(): return lax.ppermute(x, axis, [(i, i ^ bit) for i in range(count)])  13.2 us
    ppermute x12, waiting for transfers between devices, swap(): return lax.ppermute(x, axis, [(i, i ^ bit) for i in range(count)])  12.5 us
    pallas_call x1, Pallas kernels, first_maps(): pl.pallas_call(functools.partial(first_kernel, heads), in_specs=[pl.Block...  5.52 us
    pallas_call x4, Pallas kernels, row_maps(): pl.pallas_call(functools.partial(rows_kernel, heads, spot, slot), in_spec...  3.98 us
    pallas_call x1, Pallas kernels, own_maps(): pl.pallas_call(functools.partial(own_kernel, heads), in_specs=[here] * 4,...  2.39 us
    pallas_call x3, Pallas kernels, small_call(): pl.pallas_call(kernel, in_specs=[here] * len(args), out_specs=[here] * le...  2.1 us
    pallas_call x4, Pallas kernels, project(): pl.pallas_call(functools.partial(project_kernel, start), out_shape=jax.Sh...  1.76 us
    pallas_call x2, Pallas kernels, add_part(): pl.pallas_call(add_kernel, grid=(1,), in_specs=[here, here] + [pl.BlockSp...  1.53 us
  transfers between devices with their start and end apart: 12, of which 8 were waited for; matrix products, arithmetic and copies ran while one was open for 0% of the time, Pallas kernels for 38%

profile of v15, /device:TPU:0, one launch (start us, length us, event | category | flops | bytes accessed | tf_op | source)
XLA Modules:
  0.0 43.7 jit_solution(14412107241978947244)
XLA Ops:
  0.0 0.5 %collective-permute-start.8 = (bf16[512,2048]{1,0:T(8,128)(2,1)}, bf16[512,2048]{1,0:T(8,128)(2,1)S(1)}, u32[]{:S(2)}, u32[]{:S(2)}) collective-permute-start(bf16[512,2048]{1,0:T(8,128)(2,1)} %w_ref.7), channel_id=1, source_target_pairs={{0,1},{1,0},{2,3},{3,2},{4,5},{5,4},{6,7},{7,6},{8,9},{9,8},{10,11... | collective-permute-start | bytes 6291464 | tf_op jit(solution)/shard_map/ppermute | solution.py:488
  0.5 5.5 %first_maps.1 = (bf16[2048,128]{1,0:T(8,128)(2,1)S(1)}, f32[2048,128]{1,0:T(8,128)S(1)}, f32[2048,128]{1,0:T(8,128)S(1)}, f32[16,128]{1,0:T(8,128)S(1)}, f32[16,...) custom-call(bf16[2048,128]{1,0:T(8,128)(2,1)} %bitcast.3, ...), custom_call_target="tpu_custom_call" | custom-call | tf_op jit(solution)/shard_map/first_maps/pallas_call | solution.py:244
  6.0 3.6 %collective-permute-start = (bf16[128,256]{1,0:T(8,128)(2,1)S(1)}, bf16[128,256]{1,0:T(8,128)(2,1)S(1)}, u32[]{:S(2)}, u32[]{:S(2)}) collective-permute-start(bf16[128,256]{1,0:T(8,128)(2,1)S(1)} %get-tuple-element.52), channel_id=1, source_target_pairs={{0,12},{4,8},{8,4},{12,0},{16,28},{20,24},{24,20},{28,16},{1,13},{... | collective-permute-start | bytes 196616 | tf_op jit(solution)/shard_map/ppermute | solution.py:488
  9.6 0.4 %collective-permute-start.1 = (bf16[128,256]{1,0:T(8,128)(2,1)S(1)}, bf16[128,256]{1,0:T(8,128)(2,1)S(1)}, u32[]{:S(2)}, u32[]{:S(2)}) collective-permute-start(bf16[128,256]{1,0:T(8,128)(2,1)S(1)} %get-tuple-element.53), channel_id=1, source_target_pairs={{0,8},{4,12},{8,0},{12,4},{16,24},{20,28},{24,16},{28,20},{1,9},{5... | collective-permute-start | bytes 196616 | tf_op jit(solution)/shard_map/ppermute | solution.py:488
  10.2 2.4 %own_maps.1 = (f32[4,128,128]{2,1,0:T(8,128)S(1)}, f32[4,128,256]{2,1,0:T(8,128)S(1)}, f32[4,128,256]{2,1,0:T(8,128)S(1)}, bf16[128,256]{1,0:T(8,128)(2,1)S(1)}) custom-call(f32[2048,128]{1,0:T(8,128)S(1)} %get-tuple-element.46.k32, f32[2048,128]{1,0:T(8,128)S(1)} %get-tuple-element.55.v32, f32[16,128]{1,0:T(8,128)S(1)} %get-tuple-element.47.sums_ref, ...), custom_call_target="tpu_custom_call" | custom-call | flops 2000000000 | bytes 8000000 | tf_op jit(solution)/shard_map/own_maps/pallas_call | solution.py:270
  12.6 1.0 %row_maps.4 = (f32[512,256]{1,0:T(8,128)S(1)}, f32[2048,128]{1,0:T(8,128)S(1)}) custom-call(bf16[2048,128]{1,0:T(8,128)(2,1)S(1)} %get-tuple-element.45.q_ref, f32[2048,128]{1,0:T(8,128)S(1)} %get-tuple-element.46.k32, f32[16,128]{1,0:T(8,128)S(1)} %get-tuple-element.47.sums_ref, f32[12,128,128]{2,1,0:T(8,128)S(1)} %get-tuple-element.48.mix_ref, ...), custom_call_target="tpu_custom_call" | custom-call | flops 1000000000 | bytes 4000000 | tf_op jit(solution)/shard_map/row_maps/pallas_call | solution.py:311
  14.3 0.5 %group_state.1 = bf16[128,128]{1,0:T(8,128)(2,1)S(1)} custom-call(bf16[128,256]{1,0:T(8,128)(2,1)S(1)} %collective-permute-done.refs_0_, bf16[128,256]{1,0:T(8,128)(2,1)S(1)} %collective-permute-done.1.refs_1_, bf16[128,256]{1,0:T(8,128)(2,1)S(1)} %collective-permute-done.2.refs_2_, bf16[128,256]{1,0:T(8,128)(2,1)S(1)} %get-tuple-element.62.refs_3_), custom_call_target="tpu_custom_call" | custom-call | tf_op jit(solution)/shard_map/group_state/pallas_call | solution.py:324
  14.8 2.7 %collective-permute-start.3 = (bf16[128,128]{1,0:T(8,128)(2,1)S(1)}, bf16[128,128]{1,0:T(8,128)(2,1)S(1)}, u32[]{:S(2)}, u32[]{:S(2)}) collective-permute-start(bf16[128,128]{1,0:T(8,128)(2,1)S(1)} %group_state.1), channel_id=1, source_target_pairs={{0,16},{4,20},{8,24},{12,28},{16,0},{20,4},{24,8},{28,12},{1,17},{... | collective-permute-start | bytes 98312 | tf_op jit(solution)/shard_map/ppermute | solution.py:488
  17.4 1.0 %row_maps.5.refs_1_ = f32[512,256]{1,0:T(8,128)S(1)} custom-call(f32[2048,128]{1,0:T(8,128)S(1)} %get-tuple-element.73.q_ref, f32[2048,128]{1,0:T(8,128)S(1)} %get-tuple-element.46.k32, f32[16,128]{1,0:T(8,128)S(1)} %get-tuple-element.47.sums_ref, f32[12,128,128]{2,1,0:T(8,128)S(1)} %get-tuple-element.48.mix_ref, ...), custom_call_target="tpu_custom_call" | custom-call | flops 1000000000 | bytes 4000000 | tf_op jit(solution)/shard_map/row_maps/pallas_call | solution.py:311
  18.4 1.4 %group_prefix.1 = (bf16[4,128,256]{2,1,0:T(8,128)(2,1)S(1)}, f32[4,128,128]{2,1,0:T(8,128)S(1)}, bf16[128,256]{1,0:T(8,128)(2,1)}) custom-call(bf16[128,256]{1,0:T(8,128)(2,1)S(1)} %collective-permute-done.refs_0_, bf16[128,256]{1,0:T(8,128)(2,1)S(1)} %collective-permute-done.1.refs_1_, bf16[128,256]{1,0:T(8,128)(2,1)S(1)} %collective-permute-done.2.refs_2_, ...), custom_call_target="tpu_custom_call" | custom-call | tf_op jit(solution)/shard_map/group_prefix/pallas_call | solution.py:324
  20.0 2.3 %collective-permute-start.4 = (bf16[128,128]{1,0:T(8,128)(2,1)S(1)}, bf16[128,128]{1,0:T(8,128)(2,1)S(1)}, u32[]{:S(2)}, u32[]{:S(2)}) collective-permute-start(bf16[128,128]{1,0:T(8,128)(2,1)S(1)} %get-tuple-element.77), channel_id=1, source_target_pairs={{0,12},{4,8},{8,4},{12,0},{16,28},{20,24},{24,20},{28,16},{1,13},{... | collective-permute-start | bytes 98312 | tf_op jit(solution)/shard_map/ppermute | solution.py:488
  22.4 0.4 %collective-permute-start.5 = (bf16[128,128]{1,0:T(8,128)(2,1)S(1)}, bf16[128,128]{1,0:T(8,128)(2,1)S(1)}, u32[]{:S(2)}, u32[]{:S(2)}) collective-permute-start(bf16[128,128]{1,0:T(8,128)(2,1)S(1)} %get-tuple-element.78), channel_id=1, source_target_pairs={{0,8},{4,12},{8,0},{12,4},{16,24},{20,28},{24,16},{28,20},{1,9},{5... | collective-permute-start | bytes 98312 | tf_op jit(solution)/shard_map/ppermute | solution.py:488
  22.8 0.8 %collective-permute-start.6 = (bf16[128,128]{1,0:T(8,128)(2,1)S(1)}, bf16[128,128]{1,0:T(8,128)(2,1)S(1)}, u32[]{:S(2)}, u32[]{:S(2)}) collective-permute-start(bf16[128,128]{1,0:T(8,128)(2,1)S(1)} %get-tuple-element.79), channel_id=1, source_target_pairs={{0,4},{4,0},{8,12},{12,8},{16,20},{20,16},{24,28},{28,24},{1,5},{5... | collective-permute-start | bytes 98312 | tf_op jit(solution)/shard_map/ppermute | solution.py:488
  23.6 1.0 %row_maps.6.refs_2_ = f32[512,256]{1,0:T(8,128)S(1)} custom-call(f32[2048,128]{1,0:T(8,128)S(1)} %get-tuple-element.73.q_ref, f32[2048,128]{1,0:T(8,128)S(1)} %get-tuple-element.46.k32, f32[16,128]{1,0:T(8,128)S(1)} %get-tuple-element.47.sums_ref, f32[12,128,128]{2,1,0:T(8,128)S(1)} %get-tuple-element.48.mix_ref, ...), custom_call_target="tpu_custom_call" | custom-call | flops 1000000000 | bytes 4000000 | tf_op jit(solution)/shard_map/row_maps/pallas_call | solution.py:311
  24.6 1.0 %row_maps.7.refs_3_ = f32[512,256]{1,0:T(8,128)S(1)} custom-call(f32[2048,128]{1,0:T(8,128)S(1)} %get-tuple-element.73.q_ref, f32[2048,128]{1,0:T(8,128)S(1)} %get-tuple-element.46.k32, f32[16,128]{1,0:T(8,128)S(1)} %get-tuple-element.47.sums_ref, f32[4,128,128]{2,1,0:T(8,128)S(1)} %get-tuple-element.74.mix_ref, ...), custom_call_target="tpu_custom_call" | custom-call | flops 1000000000 | bytes 4000000 | tf_op jit(solution)/shard_map/row_maps/pallas_call | solution.py:311
  25.6 0.7 %collective-permute-done.5.refs_5_ = bf16[128,128]{1,0:T(8,128)(2,1)S(1)} collective-permute-done((bf16[128,128]{1,0:T(8,128)(2,1)S(1)}, bf16[128,128]{1,0:T(8,128)(2,1)S(1)}, u32[]{:S(2)}, u32[]{:S(2)}) %collective-permute-start.5) | collective-permute-done | bytes 32800 | tf_op jit(solution)/shard_map/ppermute | solution.py:488
  27.1 1.3 %collective-permute-done.9.got_ref = bf16[128,512]{1,0:T(8,128)(2,1)S(1)} collective-permute-done((bf16[128,512]{1,0:T(8,128)(2,1)S(1)}, bf16[128,512]{1,0:T(8,128)(2,1)S(1)}, u32[]{:S(2)}, u32[]{:S(2)}) %collective-permute-start.9) | collective-permute-done | bytes 131104 | tf_op jit(solution)/shard_map/ppermute | solution.py:488
  28.9 1.6 %collective-permute-start.11 = (bf16[128,1024]{1,0:T(8,128)(2,1)S(1)}, bf16[128,1024]{1,0:T(8,128)(2,1)S(1)}, u32[]{:S(2)}, u32[]{:S(2)}) collective-permute-start(bf16[128,1024]{1,0:T(8,128)(2,1)S(1)} %project.7), channel_id=1, source_target_pairs={{0,2},{1,3},{2,0},{3,1},{4,6},{5,7},{6,4},{7,5},{8,10},{9,11},{10,... | collective-permute-start | bytes 786440 | tf_op jit(solution)/shard_map/ppermute | solution.py:488
  30.9 0.6 %collective-permute-start.10 = (bf16[128,1024]{1,0:T(8,128)(2,1)S(1)}, bf16[128,1024]{1,0:T(8,128)(2,1)S(1)}, u32[]{:S(2)}, u32[]{:S(2)}) collective-permute-start(bf16[128,1024]{1,0:T(8,128)(2,1)S(1)} %project.5), channel_id=1, source_target_pairs={{0,2},{1,3},{2,0},{3,1},{4,6},{5,7},{6,4},{7,5},{8,10},{9,11},{10,... | collective-permute-start | bytes 786440 | tf_op jit(solution)/shard_map/ppermute | solution.py:488
  31.9 1.3 %collective-permute-done.7.got_ref = bf16[128,512]{1,0:T(8,128)(2,1)S(1)} collective-permute-done((bf16[128,512]{1,0:T(8,128)(2,1)S(1)}, bf16[128,512]{1,0:T(8,128)(2,1)S(1)}, u32[]{:S(2)}, u32[]{:S(2)}) %collective-permute-start.7) | collective-permute-done | bytes 131104 | tf_op jit(solution)/shard_map/ppermute | solution.py:488
  34.1 4.0 %collective-permute-done.11.theirs_ref = bf16[128,1024]{1,0:T(8,128)(2,1)S(1)} collective-permute-done((bf16[128,1024]{1,0:T(8,128)(2,1)S(1)}, bf16[128,1024]{1,0:T(8,128)(2,1)S(1)}, u32[]{:S(2)}, u32[]{:S(2)}) %collective-permute-start.11) | collective-permute-done | bytes 262176 | tf_op jit(solution)/shard_map/ppermute | solution.py:488
  38.1 0.8 %add_part.2.refs_0_ = bf16[128,2048]{1,0:T(8,128)(2,1)} custom-call(f32[128,1024]{1,0:T(8,128)S(1)} %project.6.mine_ref, bf16[128,1024]{1,0:T(8,128)(2,1)S(1)} %collective-permute-done.11.theirs_ref), custom_call_target="tpu_custom_call" | custom-call | tf_op jit(solution)/shard_map/add_part/pallas_call | solution.py:474
  38.9 4.1 %collective-permute-done.10.theirs_ref = bf16[128,1024]{1,0:T(8,128)(2,1)S(1)} collective-permute-done((bf16[128,1024]{1,0:T(8,128)(2,1)S(1)}, bf16[128,1024]{1,0:T(8,128)(2,1)S(1)}, u32[]{:S(2)}, u32[]{:S(2)}) %collective-permute-start.10) | collective-permute-done | bytes 262176 | tf_op jit(solution)/shard_map/ppermute | solution.py:488
  42.9 0.8 %add_part.3 = bf16[128,2048]{1,0:T(8,128)(2,1)} custom-call(f32[128,1024]{1,0:T(8,128)S(1)} %project.4.mine_ref, bf16[128,1024]{1,0:T(8,128)(2,1)S(1)} %collective-permute-done.10.theirs_ref, bf16[128,2048]{1,0:T(8,128)(2,1)} %add_part.2.refs_0_), custom_call_target="tpu_custom_call", output_to_operand_aliasing={{}: (2, {})} | custom-call | tf_op jit(solution)/shard_map/add_part/pallas_call | solution.py:474
  (19 shorter events, 4.0 us)
Async XLA Ops:
  0.0 28.4 %collective-permute-start.8 = (bf16[512,2048]{1,0:T(8,128)(2,1)}, bf16[512,2048]{1,0:T(8,128)(2,1)S(1)}, u32[]{:S(2)}, u32[]{:S(2)}) collective-permute-start(bf16[512,2048]{1,0:T(8,128)(2,1)} %w_ref.7), channel_id=1, source_target_pairs={{0,1},{1,0},{2,3},{3,2},{4,5},{5,4},{6,7},{7,6},{8,9},{9,8},{10,11... | collective-permute-start | bytes 6291464 | tf_op jit(solution)/shard_map/ppermute | solution.py:488
  6.0 7.6 %collective-permute-start = (bf16[128,256]{1,0:T(8,128)(2,1)S(1)}, bf16[128,256]{1,0:T(8,128)(2,1)S(1)}, u32[]{:S(2)}, u32[]{:S(2)}) collective-permute-start(bf16[128,256]{1,0:T(8,128)(2,1)S(1)} %get-tuple-element.52), channel_id=1, source_target_pairs={{0,12},{4,8},{8,4},{12,0},{16,28},{20,24},{24,20},{28,16},{1,13},{... | collective-permute-start | bytes 196616 | tf_op jit(solution)/shard_map/ppermute | solution.py:488
  9.6 4.3 %collective-permute-start.1 = (bf16[128,256]{1,0:T(8,128)(2,1)S(1)}, bf16[128,256]{1,0:T(8,128)(2,1)S(1)}, u32[]{:S(2)}, u32[]{:S(2)}) collective-permute-start(bf16[128,256]{1,0:T(8,128)(2,1)S(1)} %get-tuple-element.53), channel_id=1, source_target_pairs={{0,8},{4,12},{8,0},{12,4},{16,24},{20,28},{24,16},{28,20},{1,9},{5... | collective-permute-start | bytes 196616 | tf_op jit(solution)/shard_map/ppermute | solution.py:488
  10.0 4.3 %collective-permute-start.2 = (bf16[128,256]{1,0:T(8,128)(2,1)S(1)}, bf16[128,256]{1,0:T(8,128)(2,1)S(1)}, u32[]{:S(2)}, u32[]{:S(2)}) collective-permute-start(bf16[128,256]{1,0:T(8,128)(2,1)S(1)} %get-tuple-element.54), channel_id=1, source_target_pairs={{0,4},{4,0},{8,12},{12,8},{16,20},{20,16},{24,28},{28,24},{1,5},{5... | collective-permute-start | bytes 196616 | tf_op jit(solution)/shard_map/ppermute | solution.py:488
  14.8 5.0 %collective-permute-start.3 = (bf16[128,128]{1,0:T(8,128)(2,1)S(1)}, bf16[128,128]{1,0:T(8,128)(2,1)S(1)}, u32[]{:S(2)}, u32[]{:S(2)}) collective-permute-start(bf16[128,128]{1,0:T(8,128)(2,1)S(1)} %group_state.1), channel_id=1, source_target_pairs={{0,16},{4,20},{8,24},{12,28},{16,0},{20,4},{24,8},{28,12},{1,17},{... | collective-permute-start | bytes 98312 | tf_op jit(solution)/shard_map/ppermute | solution.py:488
  20.0 5.6 %collective-permute-start.4 = (bf16[128,128]{1,0:T(8,128)(2,1)S(1)}, bf16[128,128]{1,0:T(8,128)(2,1)S(1)}, u32[]{:S(2)}, u32[]{:S(2)}) collective-permute-start(bf16[128,128]{1,0:T(8,128)(2,1)S(1)} %get-tuple-element.77), channel_id=1, source_target_pairs={{0,12},{4,8},{8,4},{12,0},{16,28},{20,24},{24,20},{28,16},{1,13},{... | collective-permute-start | bytes 98312 | tf_op jit(solution)/shard_map/ppermute | solution.py:488
  22.4 3.9 %collective-permute-start.5 = (bf16[128,128]{1,0:T(8,128)(2,1)S(1)}, bf16[128,128]{1,0:T(8,128)(2,1)S(1)}, u32[]{:S(2)}, u32[]{:S(2)}) collective-permute-start(bf16[128,128]{1,0:T(8,128)(2,1)S(1)} %get-tuple-element.78), channel_id=1, source_target_pairs={{0,8},{4,12},{8,0},{12,4},{16,24},{20,28},{24,16},{28,20},{1,9},{5... | collective-permute-start | bytes 98312 | tf_op jit(solution)/shard_map/ppermute | solution.py:488
  22.8 3.9 %collective-permute-start.6 = (bf16[128,128]{1,0:T(8,128)(2,1)S(1)}, bf16[128,128]{1,0:T(8,128)(2,1)S(1)}, u32[]{:S(2)}, u32[]{:S(2)}) collective-permute-start(bf16[128,128]{1,0:T(8,128)(2,1)S(1)} %get-tuple-element.79), channel_id=1, source_target_pairs={{0,4},{4,0},{8,12},{12,8},{16,20},{20,16},{24,28},{28,24},{1,5},{5... | collective-permute-start | bytes 98312 | tf_op jit(solution)/shard_map/ppermute | solution.py:488
  25.6 2.9 %copy-start = (bf16[512,2048]{1,0:T(8,128)(2,1)S(1)}, bf16[512,2048]{1,0:T(8,128)(2,1)}, u32[]{:S(2)}) copy-start(bf16[512,2048]{1,0:T(8,128)(2,1)} %w_ref.7) | copy-start | bytes 6291460
  27.0 1.4 %collective-permute-start.9 = (bf16[128,512]{1,0:T(8,128)(2,1)S(1)}, bf16[128,512]{1,0:T(8,128)(2,1)S(1)}, u32[]{:S(2)}, u32[]{:S(2)}) collective-permute-start(bf16[128,512]{1,0:T(8,128)(2,1)S(1)} %get-tuple-element.84), channel_id=1, source_target_pairs={{0,1},{1,0},{2,3},{3,2},{4,5},{5,4},{6,7},{7,6},{8,9},{9,8},{10,11... | collective-permute-start | bytes 393224 | tf_op jit(solution)/shard_map/ppermute | solution.py:488
  28.9 9.2 %collective-permute-start.11 = (bf16[128,1024]{1,0:T(8,128)(2,1)S(1)}, bf16[128,1024]{1,0:T(8,128)(2,1)S(1)}, u32[]{:S(2)}, u32[]{:S(2)}) collective-permute-start(bf16[128,1024]{1,0:T(8,128)(2,1)S(1)} %project.7), channel_id=1, source_target_pairs={{0,2},{1,3},{2,0},{3,1},{4,6},{5,7},{6,4},{7,5},{8,10},{9,11},{10,... | collective-permute-start | bytes 786440 | tf_op jit(solution)/shard_map/ppermute | solution.py:488
  30.9 12.0 %collective-permute-start.10 = (bf16[128,1024]{1,0:T(8,128)(2,1)S(1)}, bf16[128,1024]{1,0:T(8,128)(2,1)S(1)}, u32[]{:S(2)}, u32[]{:S(2)}) collective-permute-start(bf16[128,1024]{1,0:T(8,128)(2,1)S(1)} %project.5), channel_id=1, source_target_pairs={{0,2},{1,3},{2,0},{3,1},{4,6},{5,7},{6,4},{7,5},{8,10},{9,11},{10,... | collective-permute-start | bytes 786440 | tf_op jit(solution)/shard_map/ppermute | solution.py:488
  31.8 1.4 %collective-permute-start.7 = (bf16[128,512]{1,0:T(8,128)(2,1)S(1)}, bf16[128,512]{1,0:T(8,128)(2,1)S(1)}, u32[]{:S(2)}, u32[]{:S(2)}) collective-permute-start(bf16[128,512]{1,0:T(8,128)(2,1)S(1)} %get-tuple-element.82), channel_id=1, source_target_pairs={{0,1},{1,0},{2,3},{3,2},{4,5},{5,4},{6,7},{7,6},{8,9},{9,8},{10,11... | collective-permute-start | bytes 393224 | tf_op jit(solution)/shard_map/ppermute | solution.py:488

commit v16 on v15

--- a/solution.py
+++ b/solution.py
@@ -148,7 +148,7 @@
     return place, [lax.bitwise_xor(place, r) for r in range(heads - 1, -1, -1)]
 
 
-def local_heads(heads, mine, k32, v32, sums_ref, betas_ref, mix_ref, wu_ref, n_ref):
+def local_heads(heads, mine, k32, v32, sums_ref, betas_ref, mix_ref, wu_ref, n_ref, fetch_values=lambda: None):
     chunks = sums_ref.shape[0] // heads
     row, col = iotas()
     eye = row == col
@@ -162,12 +162,11 @@
     columns = filled.T
     grown = jnp.exp(sums)
     faded = jnp.exp(sums[:, C - 1 :] - sums)
-    lowers, raws, values, fades, lengths = [], [], [], [], []
+    lowers, raws, fades, lengths = [], [], [], []
     for i, (head, c) in enumerate(jobs):
         at = slice(i, i + 1)
         raw = k32[chunk_rows(heads, head, c), :].astype(BF16)
         raws.append(raw)
-        values.append(v32[chunk_rows(heads, head, c), :].astype(BF16))
         both = dot(jnp.concatenate([raw, eye16], axis=0), raw, NT)
         gram, turned = both[:C], both[C:]
         square = to_row(gram, eye) + 1e-06
@@ -179,10 +178,13 @@
         lowers.append(jnp.where(strict, gram * mix, 0.0))
         fades.append(turned * (strength * faded[at]))
     solved = []
-    for i, found in enumerate(inverses(lowers, row, col)):
+    inverted = inverses(lowers, row, col)
+    fetch_values()
+    for i, found in enumerate(inverted):
         at = slice(i, i + 1)
+        value = v32[chunk_rows(heads, jobs[i][0], jobs[i][1]), :].astype(BF16)
         kept = dot(jnp.concatenate(split(found * grown[at]), axis=1), twice(raws[i]))
-        fresh = dot(jnp.concatenate(split(found * lengths[i]), axis=1), twice(values[i]))
+        fresh = dot(jnp.concatenate(split(found * lengths[i]), axis=1), twice(value))
         solved.append(join(kept, fresh))
     maps = []
     for i in range(len(jobs)):
@@ -216,11 +218,14 @@
     betas_ref[...] = per_chunk(beta_ref)
     early[2].wait()
     k32[...] = k16[...].astype(F32)
-    early[3].wait()
-    late.start()
-    v32[...] = v16[...].astype(F32)
+
+    def fetch_values():
+        early[3].wait()
+        late.start()
+        v32[...] = v16[...].astype(F32)
+
     mine = places(heads)[1][: heads - 1]
-    totals = local_heads(heads, mine, k32, v32, sums_ref, betas_ref, mix_ref, wu_ref, n_ref)
+    totals = local_heads(heads, mine, k32, v32, sums_ref, betas_ref, mix_ref, wu_ref, n_ref, fetch_values)
     for send, total in zip(sends, totals):
         send[...] = total.astype(BF16)
     late.wait()
@@ -526,7 +531,7 @@
     across = (keep, swap(send, "head", 1), out_weight, weight2)
     keep, send = apply(False, rows, entering, groups)
     here = (keep, swap(send, "head", 1), out_weight, weight2)
-    parts = 2
+    parts = 4
     width = out_weight.shape[1] // parts
     ranges = [(i * width, width) for i in range(parts)]
     theirs = [swap(project(BF16, *x, *across), "head", 2) for x in ranges]

time: 43.9 us -> 44.1 us (level)
  waiting for transfers between devices: 12.5 us -> 7.68 us
  starting transfers between devices: 13.2 us -> 15.8 us
  Pallas kernels: 17.9 us -> 20.2 us
    ppermute x12 -> x14, waiting for transfers between devices: 12.5 us -> 7.68 us  [swap(): return lax.ppermute(x, axis, [(i, i ^ bit) for i in range(count)])]
    ppermute x12 -> x14, starting transfers between devices: 13.2 us -> 15.8 us  [swap(): return lax.ppermute(x, axis, [(i, i ^ bit) for i in range(count)])]
    pallas_call x2 -> x4, Pallas kernels: 1.53 us -> 2.72 us  [add_part(): pl.pallas_call(add_kernel, grid=(1,), in_specs=[here, here] + [pl.BlockSp...]
    pallas_call x4 -> x8, Pallas kernels: 1.76 us -> 2.47 us  [project(): pl.pallas_call(functools.partial(project_kernel, start), out_shape=jax.Sh...]
  transfers between devices with their start and end apart: 12 -> 14, of which waited for: 8 -> 8; matrix products, arithmetic and copies ran while one was open for 0% -> 0% of each run, Pallas kernels for 38% -> 44%
where the time goes in v16:
time: 44.1 us; the launch traced here: 43.9 us
  Pallas kernels  20.2 us (46%)
  starting transfers between devices  15.8 us (36%)
  waiting for transfers between devices  7.68 us (17%)
    ppermute x14, starting transfers between devices, swap(): return lax.ppermute(x, axis, [(i, i ^ bit) for i in range(count)])  15.8 us
    ppermute x14, waiting for transfers between devices, swap(): return lax.ppermute(x, axis, [(i, i ^ bit) for i in range(count)])  7.68 us
    pallas_call x1, Pallas kernels, first_maps(): pl.pallas_call(functools.partial(first_kernel, heads), in_specs=[pl.Block...  5.94 us
    pallas_call x4, Pallas kernels, row_maps(): pl.pallas_call(functools.partial(rows_kernel, heads, spot, slot), in_spec...  3.98 us
    pallas_call x4, Pallas kernels, add_part(): pl.pallas_call(add_kernel, grid=(1,), in_specs=[here, here] + [pl.BlockSp...  2.72 us
    pallas_call x8, Pallas kernels, project(): pl.pallas_call(functools.partial(project_kernel, start), out_shape=jax.Sh...  2.47 us
    pallas_call x1, Pallas kernels, own_maps(): pl.pallas_call(functools.partial(own_kernel, heads), in_specs=[here] * 4,...  2.39 us
    pallas_call x3, Pallas kernels, small_call(): pl.pallas_call(kernel, in_specs=[here] * len(args), out_specs=[here] * le...  2.1 us
  transfers between devices with their start and end apart: 14, of which 8 were waited for; matrix products, arithmetic and copies ran while one was open for 0% of the time, Pallas kernels for 44%

profile of v16, /device:TPU:0, one launch (start us, length us, event | category | flops | bytes accessed | tf_op | source)
XLA Modules:
  0.0 43.9 jit_solution(10229940105744095658)
XLA Ops:
  0.5 5.9 %first_maps.1 = (bf16[2048,128]{1,0:T(8,128)(2,1)S(1)}, f32[2048,128]{1,0:T(8,128)S(1)}, f32[2048,128]{1,0:T(8,128)S(1)}, f32[16,128]{1,0:T(8,128)S(1)}, f32[16,...) custom-call(bf16[2048,128]{1,0:T(8,128)(2,1)} %bitcast.3, ...), custom_call_target="tpu_custom_call" | custom-call | tf_op jit(solution)/shard_map/first_maps/pallas_call | solution.py:249
  6.4 3.6 %collective-permute-start = (bf16[128,256]{1,0:T(8,128)(2,1)S(1)}, bf16[128,256]{1,0:T(8,128)(2,1)S(1)}, u32[]{:S(2)}, u32[]{:S(2)}) collective-permute-start(bf16[128,256]{1,0:T(8,128)(2,1)S(1)} %get-tuple-element.52), channel_id=1, source_target_pairs={{0,12},{4,8},{8,4},{12,0},{16,28},{20,24},{24,20},{28,16},{1,13},{... | collective-permute-start | bytes 196616 | tf_op jit(solution)/shard_map/ppermute | solution.py:493
  10.6 2.4 %own_maps.1 = (f32[4,128,128]{2,1,0:T(8,128)S(1)}, f32[4,128,256]{2,1,0:T(8,128)S(1)}, f32[4,128,256]{2,1,0:T(8,128)S(1)}, bf16[128,256]{1,0:T(8,128)(2,1)S(1)}) custom-call(f32[2048,128]{1,0:T(8,128)S(1)} %get-tuple-element.46.k32, f32[2048,128]{1,0:T(8,128)S(1)} %get-tuple-element.55.v32, f32[16,128]{1,0:T(8,128)S(1)} %get-tuple-element.47.sums_ref, ...), custom_call_target="tpu_custom_call" | custom-call | flops 2000000000 | bytes 8000000 | tf_op jit(solution)/shard_map/own_maps/pallas_call | solution.py:275
  13.0 1.0 %row_maps.4 = (f32[512,256]{1,0:T(8,128)S(1)}, f32[2048,128]{1,0:T(8,128)S(1)}) custom-call(bf16[2048,128]{1,0:T(8,128)(2,1)S(1)} %get-tuple-element.45.q_ref, f32[2048,128]{1,0:T(8,128)S(1)} %get-tuple-element.46.k32, f32[16,128]{1,0:T(8,128)S(1)} %get-tuple-element.47.sums_ref, f32[12,128,128]{2,1,0:T(8,128)S(1)} %get-tuple-element.48.mix_ref, ...), custom_call_target="tpu_custom_call" | custom-call | flops 1000000000 | bytes 4000000 | tf_op jit(solution)/shard_map/row_maps/pallas_call | solution.py:316
  15.2 2.7 %collective-permute-start.3 = (bf16[128,128]{1,0:T(8,128)(2,1)S(1)}, bf16[128,128]{1,0:T(8,128)(2,1)S(1)}, u32[]{:S(2)}, u32[]{:S(2)}) collective-permute-start(bf16[128,128]{1,0:T(8,128)(2,1)S(1)} %group_state.1), channel_id=1, source_target_pairs={{0,16},{4,20},{8,24},{12,28},{16,0},{20,4},{24,8},{28,12},{1,17},{... | collective-permute-start | bytes 98312 | tf_op jit(solution)/shard_map/ppermute | solution.py:493
  17.8 1.0 %row_maps.5.refs_1_ = f32[512,256]{1,0:T(8,128)S(1)} custom-call(f32[2048,128]{1,0:T(8,128)S(1)} %get-tuple-element.73.q_ref, f32[2048,128]{1,0:T(8,128)S(1)} %get-tuple-element.46.k32, f32[16,128]{1,0:T(8,128)S(1)} %get-tuple-element.47.sums_ref, f32[12,128,128]{2,1,0:T(8,128)S(1)} %get-tuple-element.48.mix_ref, ...), custom_call_target="tpu_custom_call" | custom-call | flops 1000000000 | bytes 4000000 | tf_op jit(solution)/shard_map/row_maps/pallas_call | solution.py:316
  18.8 1.4 %group_prefix.1 = (bf16[4,128,256]{2,1,0:T(8,128)(2,1)S(1)}, f32[4,128,128]{2,1,0:T(8,128)S(1)}, bf16[128,256]{1,0:T(8,128)(2,1)}) custom-call(bf16[128,256]{1,0:T(8,128)(2,1)S(1)} %collective-permute-done.refs_0_, bf16[128,256]{1,0:T(8,128)(2,1)S(1)} %collective-permute-done.1.refs_1_, bf16[128,256]{1,0:T(8,128)(2,1)S(1)} %collective-permute-done.2.refs_2_, ...), custom_call_target="tpu_custom_call" | custom-call | tf_op jit(solution)/shard_map/group_prefix/pallas_call | solution.py:329
  20.5 2.3 %collective-permute-start.4 = (bf16[128,128]{1,0:T(8,128)(2,1)S(1)}, bf16[128,128]{1,0:T(8,128)(2,1)S(1)}, u32[]{:S(2)}, u32[]{:S(2)}) collective-permute-start(bf16[128,128]{1,0:T(8,128)(2,1)S(1)} %get-tuple-element.77), channel_id=1, source_target_pairs={{0,12},{4,8},{8,4},{12,0},{16,28},{20,24},{24,20},{28,16},{1,13},{... | collective-permute-start | bytes 98312 | tf_op jit(solution)/shard_map/ppermute | solution.py:493
  23.2 0.8 %collective-permute-start.6 = (bf16[128,128]{1,0:T(8,128)(2,1)S(1)}, bf16[128,128]{1,0:T(8,128)(2,1)S(1)}, u32[]{:S(2)}, u32[]{:S(2)}) collective-permute-start(bf16[128,128]{1,0:T(8,128)(2,1)S(1)} %get-tuple-element.79), channel_id=1, source_target_pairs={{0,4},{4,0},{8,12},{12,8},{16,20},{20,16},{24,28},{28,24},{1,5},{5... | collective-permute-start | bytes 98312 | tf_op jit(solution)/shard_map/ppermute | solution.py:493
  24.0 1.0 %row_maps.6.refs_2_ = f32[512,256]{1,0:T(8,128)S(1)} custom-call(f32[2048,128]{1,0:T(8,128)S(1)} %get-tuple-element.73.q_ref, f32[2048,128]{1,0:T(8,128)S(1)} %get-tuple-element.46.k32, f32[16,128]{1,0:T(8,128)S(1)} %get-tuple-element.47.sums_ref, f32[12,128,128]{2,1,0:T(8,128)S(1)} %get-tuple-element.48.mix_ref, ...), custom_call_target="tpu_custom_call" | custom-call | flops 1000000000 | bytes 4000000 | tf_op jit(solution)/shard_map/row_maps/pallas_call | solution.py:316
  25.0 1.0 %row_maps.7.refs_3_ = f32[512,256]{1,0:T(8,128)S(1)} custom-call(f32[2048,128]{1,0:T(8,128)S(1)} %get-tuple-element.73.q_ref, f32[2048,128]{1,0:T(8,128)S(1)} %get-tuple-element.46.k32, f32[16,128]{1,0:T(8,128)S(1)} %get-tuple-element.47.sums_ref, f32[4,128,128]{2,1,0:T(8,128)S(1)} %get-tuple-element.74.mix_ref, ...), custom_call_target="tpu_custom_call" | custom-call | flops 1000000000 | bytes 4000000 | tf_op jit(solution)/shard_map/row_maps/pallas_call | solution.py:316
  26.0 0.6 %collective-permute-done.5.refs_5_ = bf16[128,128]{1,0:T(8,128)(2,1)S(1)} collective-permute-done((bf16[128,128]{1,0:T(8,128)(2,1)S(1)}, bf16[128,128]{1,0:T(8,128)(2,1)S(1)}, u32[]{:S(2)}, u32[]{:S(2)}) %collective-permute-start.5) | collective-permute-done | bytes 32800 | tf_op jit(solution)/shard_map/ppermute | solution.py:493
  27.8 0.6 %collective-permute-start.7 = (bf16[128,512]{1,0:T(8,128)(2,1)S(1)}, bf16[128,512]{1,0:T(8,128)(2,1)S(1)}, u32[]{:S(2)}, u32[]{:S(2)}) collective-permute-start(bf16[128,512]{1,0:T(8,128)(2,1)S(1)} %get-tuple-element.82), channel_id=1, source_target_pairs={{0,1},{1,0},{2,3},{3,2},{4,5},{5,4},{6,7},{7,6},{8,9},{9,8},{10,11... | collective-permute-start | bytes 393224 | tf_op jit(solution)/shard_map/ppermute | solution.py:493
  29.2 1.6 %collective-permute-start.13 = (bf16[128,512]{1,0:T(8,128)(2,1)S(1)}, bf16[128,512]{1,0:T(8,128)(2,1)S(1)}, u32[]{:S(2)}, u32[]{:S(2)}) collective-permute-start(bf16[128,512]{1,0:T(8,128)(2,1)S(1)} %project.15), channel_id=1, source_target_pairs={{0,2},{1,3},{2,0},{3,1},{4,6},{5,7},{6,4},{7,5},{8,10},{9,11},{10,... | collective-permute-start | bytes 393224 | tf_op jit(solution)/shard_map/ppermute | solution.py:493
  31.1 0.6 %collective-permute-start.12 = (bf16[128,512]{1,0:T(8,128)(2,1)S(1)}, bf16[128,512]{1,0:T(8,128)(2,1)S(1)}, u32[]{:S(2)}, u32[]{:S(2)}) collective-permute-start(bf16[128,512]{1,0:T(8,128)(2,1)S(1)} %project.13), channel_id=1, source_target_pairs={{0,2},{1,3},{2,0},{3,1},{4,6},{5,7},{6,4},{7,5},{8,10},{9,11},{10,... | collective-permute-start | bytes 393224 | tf_op jit(solution)/shard_map/ppermute | solution.py:493
  32.0 1.6 %collective-permute-start.11 = (bf16[128,512]{1,0:T(8,128)(2,1)S(1)}, bf16[128,512]{1,0:T(8,128)(2,1)S(1)}, u32[]{:S(2)}, u32[]{:S(2)}) collective-permute-start(bf16[128,512]{1,0:T(8,128)(2,1)S(1)} %project.11), channel_id=1, source_target_pairs={{0,2},{1,3},{2,0},{3,1},{4,6},{5,7},{6,4},{7,5},{8,10},{9,11},{10,... | collective-permute-start | bytes 393224 | tf_op jit(solution)/shard_map/ppermute | solution.py:493
  33.9 0.6 %collective-permute-start.10 = (bf16[128,512]{1,0:T(8,128)(2,1)S(1)}, bf16[128,512]{1,0:T(8,128)(2,1)S(1)}, u32[]{:S(2)}, u32[]{:S(2)}) collective-permute-start(bf16[128,512]{1,0:T(8,128)(2,1)S(1)} %project.9), channel_id=1, source_target_pairs={{0,2},{1,3},{2,0},{3,1},{4,6},{5,7},{6,4},{7,5},{8,10},{9,11},{10,... | collective-permute-start | bytes 393224 | tf_op jit(solution)/shard_map/ppermute | solution.py:493
  35.7 0.7 %add_part.4.refs_0_ = bf16[128,2048]{1,0:T(8,128)(2,1)} custom-call(f32[128,512]{1,0:T(8,128)S(1)} %project.14.mine_ref, bf16[128,512]{1,0:T(8,128)(2,1)S(1)} %collective-permute-done.13.theirs_ref), custom_call_target="tpu_custom_call" | custom-call | tf_op jit(solution)/shard_map/add_part/pallas_call | solution.py:479
  36.4 2.0 %collective-permute-done.12.theirs_ref = bf16[128,512]{1,0:T(8,128)(2,1)S(1)} collective-permute-done((bf16[128,512]{1,0:T(8,128)(2,1)S(1)}, bf16[128,512]{1,0:T(8,128)(2,1)S(1)}, u32[]{:S(2)}, u32[]{:S(2)}) %collective-permute-start.12) | collective-permute-done | bytes 131104 | tf_op jit(solution)/shard_map/ppermute | solution.py:493
  38.4 0.7 %add_part.5.refs_0_ = bf16[128,2048]{1,0:T(8,128)(2,1)} custom-call(f32[128,512]{1,0:T(8,128)S(1)} %project.12.mine_ref, bf16[128,512]{1,0:T(8,128)(2,1)S(1)} %collective-permute-done.12.theirs_ref, bf16[128,2048]{1,0:T(8,128)(2,1)} %add_part.4.refs_0_), custom_call_target="tpu_custom_call", output_to_operand_aliasing={{}: (2, {})} | custom-call | tf_op jit(solution)/shard_map/add_part/pallas_call | solution.py:479
  39.1 2.1 %collective-permute-done.11.theirs_ref = bf16[128,512]{1,0:T(8,128)(2,1)S(1)} collective-permute-done((bf16[128,512]{1,0:T(8,128)(2,1)S(1)}, bf16[128,512]{1,0:T(8,128)(2,1)S(1)}, u32[]{:S(2)}, u32[]{:S(2)}) %collective-permute-start.11) | collective-permute-done | bytes 131104 | tf_op jit(solution)/shard_map/ppermute | solution.py:493
  41.2 0.7 %add_part.6.refs_0_ = bf16[128,2048]{1,0:T(8,128)(2,1)} custom-call(f32[128,512]{1,0:T(8,128)S(1)} %project.10.mine_ref, bf16[128,512]{1,0:T(8,128)(2,1)S(1)} %collective-permute-done.11.theirs_ref, bf16[128,2048]{1,0:T(8,128)(2,1)} %add_part.5.refs_0_), custom_call_target="tpu_custom_call", output_to_operand_aliasing={{}: (2, {})} | custom-call | tf_op jit(solution)/shard_map/add_part/pallas_call | solution.py:479
  41.9 1.3 %collective-permute-done.10.theirs_ref = bf16[128,512]{1,0:T(8,128)(2,1)S(1)} collective-permute-done((bf16[128,512]{1,0:T(8,128)(2,1)S(1)}, bf16[128,512]{1,0:T(8,128)(2,1)S(1)}, u32[]{:S(2)}, u32[]{:S(2)}) %collective-permute-start.10) | collective-permute-done | bytes 131104 | tf_op jit(solution)/shard_map/ppermute | solution.py:493
  43.2 0.7 %add_part.7 = bf16[128,2048]{1,0:T(8,128)(2,1)} custom-call(f32[128,512]{1,0:T(8,128)S(1)} %project.8.mine_ref, bf16[128,512]{1,0:T(8,128)(2,1)S(1)} %collective-permute-done.10.theirs_ref, bf16[128,2048]{1,0:T(8,128)(2,1)} %add_part.6.refs_0_), custom_call_target="tpu_custom_call", output_to_operand_aliasing={{}: (2, {})} | custom-call | tf_op jit(solution)/shard_map/add_part/pallas_call | solution.py:479
  (29 shorter events, 7.0 us)
Async XLA Ops:
  0.0 28.8 %collective-permute-start.8 = (bf16[512,2048]{1,0:T(8,128)(2,1)}, bf16[512,2048]{1,0:T(8,128)(2,1)S(1)}, u32[]{:S(2)}, u32[]{:S(2)}) collective-permute-start(bf16[512,2048]{1,0:T(8,128)(2,1)} %w_ref.15), channel_id=1, source_target_pairs={{0,1},{1,0},{2,3},{3,2},{4,5},{5,4},{6,7},{7,6},{8,9},{9,8},{10,11... | collective-permute-start | bytes 6291464 | tf_op jit(solution)/shard_map/ppermute | solution.py:493
  6.4 7.6 %collective-permute-start = (bf16[128,256]{1,0:T(8,128)(2,1)S(1)}, bf16[128,256]{1,0:T(8,128)(2,1)S(1)}, u32[]{:S(2)}, u32[]{:S(2)}) collective-permute-start(bf16[128,256]{1,0:T(8,128)(2,1)S(1)} %get-tuple-element.52), channel_id=1, source_target_pairs={{0,12},{4,8},{8,4},{12,0},{16,28},{20,24},{24,20},{28,16},{1,13},{... | collective-permute-start | bytes 196616 | tf_op jit(solution)/shard_map/ppermute | solution.py:493
  10.0 4.3 %collective-permute-start.1 = (bf16[128,256]{1,0:T(8,128)(2,1)S(1)}, bf16[128,256]{1,0:T(8,128)(2,1)S(1)}, u32[]{:S(2)}, u32[]{:S(2)}) collective-permute-start(bf16[128,256]{1,0:T(8,128)(2,1)S(1)} %get-tuple-element.53), channel_id=1, source_target_pairs={{0,8},{4,12},{8,0},{12,4},{16,24},{20,28},{24,16},{28,20},{1,9},{5... | collective-permute-start | bytes 196616 | tf_op jit(solution)/shard_map/ppermute | solution.py:493
  10.4 4.3 %collective-permute-start.2 = (bf16[128,256]{1,0:T(8,128)(2,1)S(1)}, bf16[128,256]{1,0:T(8,128)(2,1)S(1)}, u32[]{:S(2)}, u32[]{:S(2)}) collective-permute-start(bf16[128,256]{1,0:T(8,128)(2,1)S(1)} %get-tuple-element.54), channel_id=1, source_target_pairs={{0,4},{4,0},{8,12},{12,8},{16,20},{20,16},{24,28},{28,24},{1,5},{5... | collective-permute-start | bytes 196616 | tf_op jit(solution)/shard_map/ppermute | solution.py:493
  15.2 5.0 %collective-permute-start.3 = (bf16[128,128]{1,0:T(8,128)(2,1)S(1)}, bf16[128,128]{1,0:T(8,128)(2,1)S(1)}, u32[]{:S(2)}, u32[]{:S(2)}) collective-permute-start(bf16[128,128]{1,0:T(8,128)(2,1)S(1)} %group_state.1), channel_id=1, source_target_pairs={{0,16},{4,20},{8,24},{12,28},{16,0},{20,4},{24,8},{28,12},{1,17},{... | collective-permute-start | bytes 98312 | tf_op jit(solution)/shard_map/ppermute | solution.py:493
  20.5 5.6 %collective-permute-start.4 = (bf16[128,128]{1,0:T(8,128)(2,1)S(1)}, bf16[128,128]{1,0:T(8,128)(2,1)S(1)}, u32[]{:S(2)}, u32[]{:S(2)}) collective-permute-start(bf16[128,128]{1,0:T(8,128)(2,1)S(1)} %get-tuple-element.77), channel_id=1, source_target_pairs={{0,12},{4,8},{8,4},{12,0},{16,28},{20,24},{24,20},{28,16},{1,13},{... | collective-permute-start | bytes 98312 | tf_op jit(solution)/shard_map/ppermute | solution.py:493
  22.7 3.9 %collective-permute-start.5 = (bf16[128,128]{1,0:T(8,128)(2,1)S(1)}, bf16[128,128]{1,0:T(8,128)(2,1)S(1)}, u32[]{:S(2)}, u32[]{:S(2)}) collective-permute-start(bf16[128,128]{1,0:T(8,128)(2,1)S(1)} %get-tuple-element.78), channel_id=1, source_target_pairs={{0,8},{4,12},{8,0},{12,4},{16,24},{20,28},{24,16},{28,20},{1,9},{5... | collective-permute-start | bytes 98312 | tf_op jit(solution)/shard_map/ppermute | solution.py:493
  23.2 3.9 %collective-permute-start.6 = (bf16[128,128]{1,0:T(8,128)(2,1)S(1)}, bf16[128,128]{1,0:T(8,128)(2,1)S(1)}, u32[]{:S(2)}, u32[]{:S(2)}) collective-permute-start(bf16[128,128]{1,0:T(8,128)(2,1)S(1)} %get-tuple-element.79), channel_id=1, source_target_pairs={{0,4},{4,0},{8,12},{12,8},{16,20},{20,16},{24,28},{28,24},{1,5},{5... | collective-permute-start | bytes 98312 | tf_op jit(solution)/shard_map/ppermute | solution.py:493
  26.0 2.8 %copy-start = (bf16[512,2048]{1,0:T(8,128)(2,1)S(1)}, bf16[512,2048]{1,0:T(8,128)(2,1)}, u32[]{:S(2)}) copy-start(bf16[512,2048]{1,0:T(8,128)(2,1)} %w_ref.15) | copy-start | bytes 6291460
  27.4 1.4 %collective-permute-start.9 = (bf16[128,512]{1,0:T(8,128)(2,1)S(1)}, bf16[128,512]{1,0:T(8,128)(2,1)S(1)}, u32[]{:S(2)}, u32[]{:S(2)}) collective-permute-start(bf16[128,512]{1,0:T(8,128)(2,1)S(1)} %get-tuple-element.84), channel_id=1, source_target_pairs={{0,1},{1,0},{2,3},{3,2},{4,5},{5,4},{6,7},{7,6},{8,9},{9,8},{10,11... | collective-permute-start | bytes 393224 | tf_op jit(solution)/shard_map/ppermute | solution.py:493
  27.8 6.6 %collective-permute-start.7 = (bf16[128,512]{1,0:T(8,128)(2,1)S(1)}, bf16[128,512]{1,0:T(8,128)(2,1)S(1)}, u32[]{:S(2)}, u32[]{:S(2)}) collective-permute-start(bf16[128,512]{1,0:T(8,128)(2,1)S(1)} %get-tuple-element.82), channel_id=1, source_target_pairs={{0,1},{1,0},{2,3},{3,2},{4,5},{5,4},{6,7},{7,6},{8,9},{9,8},{10,11... | collective-permute-start | bytes 393224 | tf_op jit(solution)/shard_map/ppermute | solution.py:493
  29.2 6.5 %collective-permute-start.13 = (bf16[128,512]{1,0:T(8,128)(2,1)S(1)}, bf16[128,512]{1,0:T(8,128)(2,1)S(1)}, u32[]{:S(2)}, u32[]{:S(2)}) collective-permute-start(bf16[128,512]{1,0:T(8,128)(2,1)S(1)} %project.15), channel_id=1, source_target_pairs={{0,2},{1,3},{2,0},{3,1},{4,6},{5,7},{6,4},{7,5},{8,10},{9,11},{10,... | collective-permute-start | bytes 393224 | tf_op jit(solution)/shard_map/ppermute | solution.py:493
  31.1 7.3 %collective-permute-start.12 = (bf16[128,512]{1,0:T(8,128)(2,1)S(1)}, bf16[128,512]{1,0:T(8,128)(2,1)S(1)}, u32[]{:S(2)}, u32[]{:S(2)}) collective-permute-start(bf16[128,512]{1,0:T(8,128)(2,1)S(1)} %project.13), channel_id=1, source_target_pairs={{0,2},{1,3},{2,0},{3,1},{4,6},{5,7},{6,4},{7,5},{8,10},{9,11},{10,... | collective-permute-start | bytes 393224 | tf_op jit(solution)/shard_map/ppermute | solution.py:493
  32.0 9.2 %collective-permute-start.11 = (bf16[128,512]{1,0:T(8,128)(2,1)S(1)}, bf16[128,512]{1,0:T(8,128)(2,1)S(1)}, u32[]{:S(2)}, u32[]{:S(2)}) collective-permute-start(bf16[128,512]{1,0:T(8,128)(2,1)S(1)} %project.11), channel_id=1, source_target_pairs={{0,2},{1,3},{2,0},{3,1},{4,6},{5,7},{6,4},{7,5},{8,10},{9,11},{10,... | collective-permute-start | bytes 393224 | tf_op jit(solution)/shard_map/ppermute | solution.py:493
  33.9 9.3 %collective-permute-start.10 = (bf16[128,512]{1,0:T(8,128)(2,1)S(1)}, bf16[128,512]{1,0:T(8,128)(2,1)S(1)}, u32[]{:S(2)}, u32[]{:S(2)}) collective-permute-start(bf16[128,512]{1,0:T(8,128)(2,1)S(1)} %project.9), channel_id=1, source_target_pairs={{0,2},{1,3},{2,0},{3,1},{4,6},{5,7},{6,4},{7,5},{8,10},{9,11},{10,... | collective-permute-start | bytes 393224 | tf_op jit(solution)/shard_map/ppermute | solution.py:493

commit v17 on v15

--- a/solution.py
+++ b/solution.py
@@ -162,7 +162,7 @@
     columns = filled.T
     grown = jnp.exp(sums)
     faded = jnp.exp(sums[:, C - 1 :] - sums)
-    lowers, raws, values, fades, lengths = [], [], [], [], []
+    lowers, raws, values, turns, fades, lengths = [], [], [], [], [], []
     for i, (head, c) in enumerate(jobs):
         at = slice(i, i + 1)
         raw = k32[chunk_rows(heads, head, c), :].astype(BF16)
@@ -177,17 +177,19 @@
         mix = jnp.where(within, jnp.exp(columns[:, at] - sums[at]), 0.0) * strength
         mix_ref[i] = mix
         lowers.append(jnp.where(strict, gram * mix, 0.0))
-        fades.append(turned * (strength * faded[at]))
+        turns.append(turned.astype(BF16))
+        fades.append(strength * faded[at])
     solved = []
     for i, found in enumerate(inverses(lowers, row, col)):
         at = slice(i, i + 1)
         kept = dot(jnp.concatenate(split(found * grown[at]), axis=1), twice(raws[i]))
         fresh = dot(jnp.concatenate(split(found * lengths[i]), axis=1), twice(values[i]))
         solved.append(join(kept, fresh))
+    weights = jnp.concatenate(fades + [jnp.zeros((C - len(jobs), C), F32)], axis=0).T
     maps = []
     for i in range(len(jobs)):
         wu_ref[i] = solved[i]
-        both = dot3(split(fades[i]), split(solved[i]))
+        both = times_parts(turns[i], solved[i] * weights[:, i : i + 1])
         maps.append(join(jnp.where(eye, grown[i : i + 1, C - 1 :], 0.0) - both[:, :C], both[:, C:]))
     totals = []
     for j in range(len(mine)):
@@ -526,7 +528,7 @@
     across = (keep, swap(send, "head", 1), out_weight, weight2)
     keep, send = apply(False, rows, entering, groups)
     here = (keep, swap(send, "head", 1), out_weight, weight2)
-    parts = 2
+    parts = 4
     width = out_weight.shape[1] // parts
     ranges = [(i * width, width) for i in range(parts)]
     theirs = [swap(project(BF16, *x, *across), "head", 2) for x in ranges]

time: 43.9 us -> 44.2 us (level)
  waiting for transfers between devices: 12.5 us -> 7.67 us
  starting transfers between devices: 13.2 us -> 15.8 us
  Pallas kernels: 17.9 us -> 20.3 us
    ppermute x12 -> x14, waiting for transfers between devices: 12.5 us -> 7.67 us  [swap(): return lax.ppermute(x, axis, [(i, i ^ bit) for i in range(count)])]
    ppermute x12 -> x14, starting transfers between devices: 13.2 us -> 15.8 us  [swap(): return lax.ppermute(x, axis, [(i, i ^ bit) for i in range(count)])]
    pallas_call x2 -> x4, Pallas kernels: 1.53 us -> 2.72 us  [add_part(): pl.pallas_call(add_kernel, grid=(1,), in_specs=[here, here] + [pl.BlockSp...]
    pallas_call x4 -> x8, Pallas kernels: 1.76 us -> 2.47 us  [project(): pl.pallas_call(functools.partial(project_kernel, start), out_shape=jax.Sh...]
    pallas_call x1, Pallas kernels: 5.52 us -> 6 us  [first_maps(): pl.pallas_call(functools.partial(first_kernel, heads), in_specs=[pl.Block...]
  transfers between devices with their start and end apart: 12 -> 14, of which waited for: 8 -> 8; matrix products, arithmetic and copies ran while one was open for 0% -> 0% of each run, Pallas kernels for 38% -> 45%
where the time goes in v17:
time: 44.2 us; the launch traced here: 43.9 us
  Pallas kernels  20.3 us (46%)
  starting transfers between devices  15.8 us (36%)
  waiting for transfers between devices  7.67 us (17%)
    ppermute x14, starting transfers between devices, swap(): return lax.ppermute(x, axis, [(i, i ^ bit) for i in range(count)])  15.8 us
    ppermute x14, waiting for transfers between devices, swap(): return lax.ppermute(x, axis, [(i, i ^ bit) for i in range(count)])  7.67 us
    pallas_call x1, Pallas kernels, first_maps(): pl.pallas_call(functools.partial(first_kernel, heads), in_specs=[pl.Block...  6 us
    pallas_call x4, Pallas kernels, row_maps(): pl.pallas_call(functools.partial(rows_kernel, heads, spot, slot), in_spec...  3.98 us
    pallas_call x4, Pallas kernels, add_part(): pl.pallas_call(add_kernel, grid=(1,), in_specs=[here, here] + [pl.BlockSp...  2.72 us
    pallas_call x8, Pallas kernels, project(): pl.pallas_call(functools.partial(project_kernel, start), out_shape=jax.Sh...  2.47 us
    pallas_call x1, Pallas kernels, own_maps(): pl.pallas_call(functools.partial(own_kernel, heads), in_specs=[here] * 4,...  2.39 us
    pallas_call x3, Pallas kernels, small_call(): pl.pallas_call(kernel, in_specs=[here] * len(args), out_specs=[here] * le...  2.1 us
  transfers between devices with their start and end apart: 14, of which 8 were waited for; matrix products, arithmetic and copies ran while one was open for 0% of the time, Pallas kernels for 45%

profile of v17, /device:TPU:0, one launch (start us, length us, event | category | flops | bytes accessed | tf_op | source)
XLA Modules:
  0.0 43.9 jit_solution(6120941319341981483)
XLA Ops:
  0.5 6.0 %first_maps.1 = (bf16[2048,128]{1,0:T(8,128)(2,1)S(1)}, f32[2048,128]{1,0:T(8,128)S(1)}, f32[2048,128]{1,0:T(8,128)S(1)}, f32[16,128]{1,0:T(8,128)S(1)}, f32[16,...) custom-call(bf16[2048,128]{1,0:T(8,128)(2,1)} %bitcast.3, ...), custom_call_target="tpu_custom_call" | custom-call | tf_op jit(solution)/shard_map/first_maps/pallas_call | solution.py:246
  6.5 3.6 %collective-permute-start = (bf16[128,256]{1,0:T(8,128)(2,1)S(1)}, bf16[128,256]{1,0:T(8,128)(2,1)S(1)}, u32[]{:S(2)}, u32[]{:S(2)}) collective-permute-start(bf16[128,256]{1,0:T(8,128)(2,1)S(1)} %get-tuple-element.52), channel_id=1, source_target_pairs={{0,12},{4,8},{8,4},{12,0},{16,28},{20,24},{24,20},{28,16},{1,13},{... | collective-permute-start | bytes 196616 | tf_op jit(solution)/shard_map/ppermute | solution.py:490
  10.7 2.4 %own_maps.1 = (f32[4,128,128]{2,1,0:T(8,128)S(1)}, f32[4,128,256]{2,1,0:T(8,128)S(1)}, f32[4,128,256]{2,1,0:T(8,128)S(1)}, bf16[128,256]{1,0:T(8,128)(2,1)S(1)}) custom-call(f32[2048,128]{1,0:T(8,128)S(1)} %get-tuple-element.46.k32, f32[2048,128]{1,0:T(8,128)S(1)} %get-tuple-element.55.v32, f32[16,128]{1,0:T(8,128)S(1)} %get-tuple-element.47.sums_ref, ...), custom_call_target="tpu_custom_call" | custom-call | flops 2000000000 | bytes 8000000 | tf_op jit(solution)/shard_map/own_maps/pallas_call | solution.py:272
  13.1 1.0 %row_maps.4 = (f32[512,256]{1,0:T(8,128)S(1)}, f32[2048,128]{1,0:T(8,128)S(1)}) custom-call(bf16[2048,128]{1,0:T(8,128)(2,1)S(1)} %get-tuple-element.45.q_ref, f32[2048,128]{1,0:T(8,128)S(1)} %get-tuple-element.46.k32, f32[16,128]{1,0:T(8,128)S(1)} %get-tuple-element.47.sums_ref, f32[12,128,128]{2,1,0:T(8,128)S(1)} %get-tuple-element.48.mix_ref, ...), custom_call_target="tpu_custom_call" | custom-call | flops 1000000000 | bytes 4000000 | tf_op jit(solution)/shard_map/row_maps/pallas_call | solution.py:313
  15.2 2.7 %collective-permute-start.3 = (bf16[128,128]{1,0:T(8,128)(2,1)S(1)}, bf16[128,128]{1,0:T(8,128)(2,1)S(1)}, u32[]{:S(2)}, u32[]{:S(2)}) collective-permute-start(bf16[128,128]{1,0:T(8,128)(2,1)S(1)} %group_state.1), channel_id=1, source_target_pairs={{0,16},{4,20},{8,24},{12,28},{16,0},{20,4},{24,8},{28,12},{1,17},{... | collective-permute-start | bytes 98312 | tf_op jit(solution)/shard_map/ppermute | solution.py:490
  17.9 1.0 %row_maps.5.refs_1_ = f32[512,256]{1,0:T(8,128)S(1)} custom-call(f32[2048,128]{1,0:T(8,128)S(1)} %get-tuple-element.73.q_ref, f32[2048,128]{1,0:T(8,128)S(1)} %get-tuple-element.46.k32, f32[16,128]{1,0:T(8,128)S(1)} %get-tuple-element.47.sums_ref, f32[12,128,128]{2,1,0:T(8,128)S(1)} %get-tuple-element.48.mix_ref, ...), custom_call_target="tpu_custom_call" | custom-call | flops 1000000000 | bytes 4000000 | tf_op jit(solution)/shard_map/row_maps/pallas_call | solution.py:313
  18.9 1.4 %group_prefix.1 = (bf16[4,128,256]{2,1,0:T(8,128)(2,1)S(1)}, f32[4,128,128]{2,1,0:T(8,128)S(1)}, bf16[128,256]{1,0:T(8,128)(2,1)}) custom-call(bf16[128,256]{1,0:T(8,128)(2,1)S(1)} %collective-permute-done.refs_0_, bf16[128,256]{1,0:T(8,128)(2,1)S(1)} %collective-permute-done.1.refs_1_, bf16[128,256]{1,0:T(8,128)(2,1)S(1)} %collective-permute-done.2.refs_2_, ...), custom_call_target="tpu_custom_call" | custom-call | tf_op jit(solution)/shard_map/group_prefix/pallas_call | solution.py:326
  20.5 2.3 %collective-permute-start.4 = (bf16[128,128]{1,0:T(8,128)(2,1)S(1)}, bf16[128,128]{1,0:T(8,128)(2,1)S(1)}, u32[]{:S(2)}, u32[]{:S(2)}) collective-permute-start(bf16[128,128]{1,0:T(8,128)(2,1)S(1)} %get-tuple-element.77), channel_id=1, source_target_pairs={{0,12},{4,8},{8,4},{12,0},{16,28},{20,24},{24,20},{28,16},{1,13},{... | collective-permute-start | bytes 98312 | tf_op jit(solution)/shard_map/ppermute | solution.py:490
  23.3 0.8 %collective-permute-start.6 = (bf16[128,128]{1,0:T(8,128)(2,1)S(1)}, bf16[128,128]{1,0:T(8,128)(2,1)S(1)}, u32[]{:S(2)}, u32[]{:S(2)}) collective-permute-start(bf16[128,128]{1,0:T(8,128)(2,1)S(1)} %get-tuple-element.79), channel_id=1, source_target_pairs={{0,4},{4,0},{8,12},{12,8},{16,20},{20,16},{24,28},{28,24},{1,5},{5... | collective-permute-start | bytes 98312 | tf_op jit(solution)/shard_map/ppermute | solution.py:490
  24.1 1.0 %row_maps.6.refs_2_ = f32[512,256]{1,0:T(8,128)S(1)} custom-call(f32[2048,128]{1,0:T(8,128)S(1)} %get-tuple-element.73.q_ref, f32[2048,128]{1,0:T(8,128)S(1)} %get-tuple-element.46.k32, f32[16,128]{1,0:T(8,128)S(1)} %get-tuple-element.47.sums_ref, f32[12,128,128]{2,1,0:T(8,128)S(1)} %get-tuple-element.48.mix_ref, ...), custom_call_target="tpu_custom_call" | custom-call | flops 1000000000 | bytes 4000000 | tf_op jit(solution)/shard_map/row_maps/pallas_call | solution.py:313
  25.0 1.0 %row_maps.7.refs_3_ = f32[512,256]{1,0:T(8,128)S(1)} custom-call(f32[2048,128]{1,0:T(8,128)S(1)} %get-tuple-element.73.q_ref, f32[2048,128]{1,0:T(8,128)S(1)} %get-tuple-element.46.k32, f32[16,128]{1,0:T(8,128)S(1)} %get-tuple-element.47.sums_ref, f32[4,128,128]{2,1,0:T(8,128)S(1)} %get-tuple-element.74.mix_ref, ...), custom_call_target="tpu_custom_call" | custom-call | flops 1000000000 | bytes 4000000 | tf_op jit(solution)/shard_map/row_maps/pallas_call | solution.py:313
  26.1 0.7 %collective-permute-done.5.refs_5_ = bf16[128,128]{1,0:T(8,128)(2,1)S(1)} collective-permute-done((bf16[128,128]{1,0:T(8,128)(2,1)S(1)}, bf16[128,128]{1,0:T(8,128)(2,1)S(1)}, u32[]{:S(2)}, u32[]{:S(2)}) %collective-permute-start.5) | collective-permute-done | bytes 32800 | tf_op jit(solution)/shard_map/ppermute | solution.py:490
  27.9 0.6 %collective-permute-start.7 = (bf16[128,512]{1,0:T(8,128)(2,1)S(1)}, bf16[128,512]{1,0:T(8,128)(2,1)S(1)}, u32[]{:S(2)}, u32[]{:S(2)}) collective-permute-start(bf16[128,512]{1,0:T(8,128)(2,1)S(1)} %get-tuple-element.82), channel_id=1, source_target_pairs={{0,1},{1,0},{2,3},{3,2},{4,5},{5,4},{6,7},{7,6},{8,9},{9,8},{10,11... | collective-permute-start | bytes 393224 | tf_op jit(solution)/shard_map/ppermute | solution.py:490
  29.2 1.6 %collective-permute-start.13 = (bf16[128,512]{1,0:T(8,128)(2,1)S(1)}, bf16[128,512]{1,0:T(8,128)(2,1)S(1)}, u32[]{:S(2)}, u32[]{:S(2)}) collective-permute-start(bf16[128,512]{1,0:T(8,128)(2,1)S(1)} %project.15), channel_id=1, source_target_pairs={{0,2},{1,3},{2,0},{3,1},{4,6},{5,7},{6,4},{7,5},{8,10},{9,11},{10,... | collective-permute-start | bytes 393224 | tf_op jit(solution)/shard_map/ppermute | solution.py:490
  31.1 0.6 %collective-permute-start.12 = (bf16[128,512]{1,0:T(8,128)(2,1)S(1)}, bf16[128,512]{1,0:T(8,128)(2,1)S(1)}, u32[]{:S(2)}, u32[]{:S(2)}) collective-permute-start(bf16[128,512]{1,0:T(8,128)(2,1)S(1)} %project.13), channel_id=1, source_target_pairs={{0,2},{1,3},{2,0},{3,1},{4,6},{5,7},{6,4},{7,5},{8,10},{9,11},{10,... | collective-permute-start | bytes 393224 | tf_op jit(solution)/shard_map/ppermute | solution.py:490
  32.0 1.6 %collective-permute-start.11 = (bf16[128,512]{1,0:T(8,128)(2,1)S(1)}, bf16[128,512]{1,0:T(8,128)(2,1)S(1)}, u32[]{:S(2)}, u32[]{:S(2)}) collective-permute-start(bf16[128,512]{1,0:T(8,128)(2,1)S(1)} %project.11), channel_id=1, source_target_pairs={{0,2},{1,3},{2,0},{3,1},{4,6},{5,7},{6,4},{7,5},{8,10},{9,11},{10,... | collective-permute-start | bytes 393224 | tf_op jit(solution)/shard_map/ppermute | solution.py:490
  33.9 0.6 %collective-permute-start.10 = (bf16[128,512]{1,0:T(8,128)(2,1)S(1)}, bf16[128,512]{1,0:T(8,128)(2,1)S(1)}, u32[]{:S(2)}, u32[]{:S(2)}) collective-permute-start(bf16[128,512]{1,0:T(8,128)(2,1)S(1)} %project.9), channel_id=1, source_target_pairs={{0,2},{1,3},{2,0},{3,1},{4,6},{5,7},{6,4},{7,5},{8,10},{9,11},{10,... | collective-permute-start | bytes 393224 | tf_op jit(solution)/shard_map/ppermute | solution.py:490
  35.8 0.7 %add_part.4.refs_0_ = bf16[128,2048]{1,0:T(8,128)(2,1)} custom-call(f32[128,512]{1,0:T(8,128)S(1)} %project.14.mine_ref, bf16[128,512]{1,0:T(8,128)(2,1)S(1)} %collective-permute-done.13.theirs_ref), custom_call_target="tpu_custom_call" | custom-call | tf_op jit(solution)/shard_map/add_part/pallas_call | solution.py:476
  36.4 2.0 %collective-permute-done.12.theirs_ref = bf16[128,512]{1,0:T(8,128)(2,1)S(1)} collective-permute-done((bf16[128,512]{1,0:T(8,128)(2,1)S(1)}, bf16[128,512]{1,0:T(8,128)(2,1)S(1)}, u32[]{:S(2)}, u32[]{:S(2)}) %collective-permute-start.12) | collective-permute-done | bytes 131104 | tf_op jit(solution)/shard_map/ppermute | solution.py:490
  38.4 0.7 %add_part.5.refs_0_ = bf16[128,2048]{1,0:T(8,128)(2,1)} custom-call(f32[128,512]{1,0:T(8,128)S(1)} %project.12.mine_ref, bf16[128,512]{1,0:T(8,128)(2,1)S(1)} %collective-permute-done.12.theirs_ref, bf16[128,2048]{1,0:T(8,128)(2,1)} %add_part.4.refs_0_), custom_call_target="tpu_custom_call", output_to_operand_aliasing={{}: (2, {})} | custom-call | tf_op jit(solution)/shard_map/add_part/pallas_call | solution.py:476
  39.1 2.1 %collective-permute-done.11.theirs_ref = bf16[128,512]{1,0:T(8,128)(2,1)S(1)} collective-permute-done((bf16[128,512]{1,0:T(8,128)(2,1)S(1)}, bf16[128,512]{1,0:T(8,128)(2,1)S(1)}, u32[]{:S(2)}, u32[]{:S(2)}) %collective-permute-start.11) | collective-permute-done | bytes 131104 | tf_op jit(solution)/shard_map/ppermute | solution.py:490
  41.2 0.7 %add_part.6.refs_0_ = bf16[128,2048]{1,0:T(8,128)(2,1)} custom-call(f32[128,512]{1,0:T(8,128)S(1)} %project.10.mine_ref, bf16[128,512]{1,0:T(8,128)(2,1)S(1)} %collective-permute-done.11.theirs_ref, bf16[128,2048]{1,0:T(8,128)(2,1)} %add_part.5.refs_0_), custom_call_target="tpu_custom_call", output_to_operand_aliasing={{}: (2, {})} | custom-call | tf_op jit(solution)/shard_map/add_part/pallas_call | solution.py:476
  41.9 1.3 %collective-permute-done.10.theirs_ref = bf16[128,512]{1,0:T(8,128)(2,1)S(1)} collective-permute-done((bf16[128,512]{1,0:T(8,128)(2,1)S(1)}, bf16[128,512]{1,0:T(8,128)(2,1)S(1)}, u32[]{:S(2)}, u32[]{:S(2)}) %collective-permute-start.10) | collective-permute-done | bytes 131104 | tf_op jit(solution)/shard_map/ppermute | solution.py:490
  43.3 0.7 %add_part.7 = bf16[128,2048]{1,0:T(8,128)(2,1)} custom-call(f32[128,512]{1,0:T(8,128)S(1)} %project.8.mine_ref, bf16[128,512]{1,0:T(8,128)(2,1)S(1)} %collective-permute-done.10.theirs_ref, bf16[128,2048]{1,0:T(8,128)(2,1)} %add_part.6.refs_0_), custom_call_target="tpu_custom_call", output_to_operand_aliasing={{}: (2, {})} | custom-call | tf_op jit(solution)/shard_map/add_part/pallas_call | solution.py:476
  (29 shorter events, 7.0 us)
Async XLA Ops:
  0.0 28.9 %collective-permute-start.8 = (bf16[512,2048]{1,0:T(8,128)(2,1)}, bf16[512,2048]{1,0:T(8,128)(2,1)S(1)}, u32[]{:S(2)}, u32[]{:S(2)}) collective-permute-start(bf16[512,2048]{1,0:T(8,128)(2,1)} %w_ref.15), channel_id=1, source_target_pairs={{0,1},{1,0},{2,3},{3,2},{4,5},{5,4},{6,7},{7,6},{8,9},{9,8},{10,11... | collective-permute-start | bytes 6291464 | tf_op jit(solution)/shard_map/ppermute | solution.py:490
  6.5 7.6 %collective-permute-start = (bf16[128,256]{1,0:T(8,128)(2,1)S(1)}, bf16[128,256]{1,0:T(8,128)(2,1)S(1)}, u32[]{:S(2)}, u32[]{:S(2)}) collective-permute-start(bf16[128,256]{1,0:T(8,128)(2,1)S(1)} %get-tuple-element.52), channel_id=1, source_target_pairs={{0,12},{4,8},{8,4},{12,0},{16,28},{20,24},{24,20},{28,16},{1,13},{... | collective-permute-start | bytes 196616 | tf_op jit(solution)/shard_map/ppermute | solution.py:490
  10.0 4.3 %collective-permute-start.1 = (bf16[128,256]{1,0:T(8,128)(2,1)S(1)}, bf16[128,256]{1,0:T(8,128)(2,1)S(1)}, u32[]{:S(2)}, u32[]{:S(2)}) collective-permute-start(bf16[128,256]{1,0:T(8,128)(2,1)S(1)} %get-tuple-element.53), channel_id=1, source_target_pairs={{0,8},{4,12},{8,0},{12,4},{16,24},{20,28},{24,16},{28,20},{1,9},{5... | collective-permute-start | bytes 196616 | tf_op jit(solution)/shard_map/ppermute | solution.py:490
  10.5 4.3 %collective-permute-start.2 = (bf16[128,256]{1,0:T(8,128)(2,1)S(1)}, bf16[128,256]{1,0:T(8,128)(2,1)S(1)}, u32[]{:S(2)}, u32[]{:S(2)}) collective-permute-start(bf16[128,256]{1,0:T(8,128)(2,1)S(1)} %get-tuple-element.54), channel_id=1, source_target_pairs={{0,4},{4,0},{8,12},{12,8},{16,20},{20,16},{24,28},{28,24},{1,5},{5... | collective-permute-start | bytes 196616 | tf_op jit(solution)/shard_map/ppermute | solution.py:490
  15.2 5.0 %collective-permute-start.3 = (bf16[128,128]{1,0:T(8,128)(2,1)S(1)}, bf16[128,128]{1,0:T(8,128)(2,1)S(1)}, u32[]{:S(2)}, u32[]{:S(2)}) collective-permute-start(bf16[128,128]{1,0:T(8,128)(2,1)S(1)} %group_state.1), channel_id=1, source_target_pairs={{0,16},{4,20},{8,24},{12,28},{16,0},{20,4},{24,8},{28,12},{1,17},{... | collective-permute-start | bytes 98312 | tf_op jit(solution)/shard_map/ppermute | solution.py:490
  20.5 5.6 %collective-permute-start.4 = (bf16[128,128]{1,0:T(8,128)(2,1)S(1)}, bf16[128,128]{1,0:T(8,128)(2,1)S(1)}, u32[]{:S(2)}, u32[]{:S(2)}) collective-permute-start(bf16[128,128]{1,0:T(8,128)(2,1)S(1)} %get-tuple-element.77), channel_id=1, source_target_pairs={{0,12},{4,8},{8,4},{12,0},{16,28},{20,24},{24,20},{28,16},{1,13},{... | collective-permute-start | bytes 98312 | tf_op jit(solution)/shard_map/ppermute | solution.py:490
  22.8 3.9 %collective-permute-start.5 = (bf16[128,128]{1,0:T(8,128)(2,1)S(1)}, bf16[128,128]{1,0:T(8,128)(2,1)S(1)}, u32[]{:S(2)}, u32[]{:S(2)}) collective-permute-start(bf16[128,128]{1,0:T(8,128)(2,1)S(1)} %get-tuple-element.78), channel_id=1, source_target_pairs={{0,8},{4,12},{8,0},{12,4},{16,24},{20,28},{24,16},{28,20},{1,9},{5... | collective-permute-start | bytes 98312 | tf_op jit(solution)/shard_map/ppermute | solution.py:490
  23.3 3.9 %collective-permute-start.6 = (bf16[128,128]{1,0:T(8,128)(2,1)S(1)}, bf16[128,128]{1,0:T(8,128)(2,1)S(1)}, u32[]{:S(2)}, u32[]{:S(2)}) collective-permute-start(bf16[128,128]{1,0:T(8,128)(2,1)S(1)} %get-tuple-element.79), channel_id=1, source_target_pairs={{0,4},{4,0},{8,12},{12,8},{16,20},{20,16},{24,28},{28,24},{1,5},{5... | collective-permute-start | bytes 98312 | tf_op jit(solution)/shard_map/ppermute | solution.py:490
  26.0 2.9 %copy-start = (bf16[512,2048]{1,0:T(8,128)(2,1)S(1)}, bf16[512,2048]{1,0:T(8,128)(2,1)}, u32[]{:S(2)}) copy-start(bf16[512,2048]{1,0:T(8,128)(2,1)} %w_ref.15) | copy-start | bytes 6291460
  27.5 1.4 %collective-permute-start.9 = (bf16[128,512]{1,0:T(8,128)(2,1)S(1)}, bf16[128,512]{1,0:T(8,128)(2,1)S(1)}, u32[]{:S(2)}, u32[]{:S(2)}) collective-permute-start(bf16[128,512]{1,0:T(8,128)(2,1)S(1)} %get-tuple-element.84), channel_id=1, source_target_pairs={{0,1},{1,0},{2,3},{3,2},{4,5},{5,4},{6,7},{7,6},{8,9},{9,8},{10,11... | collective-permute-start | bytes 393224 | tf_op jit(solution)/shard_map/ppermute | solution.py:490
  27.9 6.6 %collective-permute-start.7 = (bf16[128,512]{1,0:T(8,128)(2,1)S(1)}, bf16[128,512]{1,0:T(8,128)(2,1)S(1)}, u32[]{:S(2)}, u32[]{:S(2)}) collective-permute-start(bf16[128,512]{1,0:T(8,128)(2,1)S(1)} %get-tuple-element.82), channel_id=1, source_target_pairs={{0,1},{1,0},{2,3},{3,2},{4,5},{5,4},{6,7},{7,6},{8,9},{9,8},{10,11... | collective-permute-start | bytes 393224 | tf_op jit(solution)/shard_map/ppermute | solution.py:490
  29.2 6.5 %collective-permute-start.13 = (bf16[128,512]{1,0:T(8,128)(2,1)S(1)}, bf16[128,512]{1,0:T(8,128)(2,1)S(1)}, u32[]{:S(2)}, u32[]{:S(2)}) collective-permute-start(bf16[128,512]{1,0:T(8,128)(2,1)S(1)} %project.15), channel_id=1, source_target_pairs={{0,2},{1,3},{2,0},{3,1},{4,6},{5,7},{6,4},{7,5},{8,10},{9,11},{10,... | collective-permute-start | bytes 393224 | tf_op jit(solution)/shard_map/ppermute | solution.py:490
  31.1 7.3 %collective-permute-start.12 = (bf16[128,512]{1,0:T(8,128)(2,1)S(1)}, bf16[128,512]{1,0:T(8,128)(2,1)S(1)}, u32[]{:S(2)}, u32[]{:S(2)}) collective-permute-start(bf16[128,512]{1,0:T(8,128)(2,1)S(1)} %project.13), channel_id=1, source_target_pairs={{0,2},{1,3},{2,0},{3,1},{4,6},{5,7},{6,4},{7,5},{8,10},{9,11},{10,... | collective-permute-start | bytes 393224 | tf_op jit(solution)/shard_map/ppermute | solution.py:490
  32.0 9.2 %collective-permute-start.11 = (bf16[128,512]{1,0:T(8,128)(2,1)S(1)}, bf16[128,512]{1,0:T(8,128)(2,1)S(1)}, u32[]{:S(2)}, u32[]{:S(2)}) collective-permute-start(bf16[128,512]{1,0:T(8,128)(2,1)S(1)} %project.11), channel_id=1, source_target_pairs={{0,2},{1,3},{2,0},{3,1},{4,6},{5,7},{6,4},{7,5},{8,10},{9,11},{10,... | collective-permute-start | bytes 393224 | tf_op jit(solution)/shard_map/ppermute | solution.py:490
  33.9 9.3 %collective-permute-start.10 = (bf16[128,512]{1,0:T(8,128)(2,1)S(1)}, bf16[128,512]{1,0:T(8,128)(2,1)S(1)}, u32[]{:S(2)}, u32[]{:S(2)}) collective-permute-start(bf16[128,512]{1,0:T(8,128)(2,1)S(1)} %project.9), channel_id=1, source_target_pairs={{0,2},{1,3},{2,0},{3,1},{4,6},{5,7},{6,4},{7,5},{8,10},{9,11},{10,... | collective-permute-start | bytes 393224 | tf_op jit(solution)/shard_map/ppermute | solution.py:490

commit v18 on v15

--- a/solution.py
+++ b/solution.py
@@ -526,7 +526,7 @@
     across = (keep, swap(send, "head", 1), out_weight, weight2)
     keep, send = apply(False, rows, entering, groups)
     here = (keep, swap(send, "head", 1), out_weight, weight2)
-    parts = 2
+    parts = 4
     width = out_weight.shape[1] // parts
     ranges = [(i * width, width) for i in range(parts)]
     theirs = [swap(project(BF16, *x, *across), "head", 2) for x in ranges]

time: 43.9 us -> 43.7 us (level)
  waiting for transfers between devices: 12.5 us -> 7.68 us
  starting transfers between devices: 13.2 us -> 15.8 us
  Pallas kernels: 17.9 us -> 19.8 us
    ppermute x12 -> x14, waiting for transfers between devices: 12.5 us -> 7.68 us  [swap(): return lax.ppermute(x, axis, [(i, i ^ bit) for i in range(count)])]
    ppermute x12 -> x14, starting transfers between devices: 13.2 us -> 15.8 us  [swap(): return lax.ppermute(x, axis, [(i, i ^ bit) for i in range(count)])]
    pallas_call x2 -> x4, Pallas kernels: 1.53 us -> 2.72 us  [add_part(): pl.pallas_call(add_kernel, grid=(1,), in_specs=[here, here] + [pl.BlockSp...]
    pallas_call x4 -> x8, Pallas kernels: 1.76 us -> 2.47 us  [project(): pl.pallas_call(functools.partial(project_kernel, start), out_shape=jax.Sh...]
  transfers between devices with their start and end apart: 12 -> 14, of which waited for: 8 -> 8; matrix products, arithmetic and copies ran while one was open for 0% -> 0% of each run, Pallas kernels for 38% -> 44%
where the time goes in v18:
time: 43.7 us; the launch traced here: 43.5 us
  Pallas kernels  19.8 us (45%)
  starting transfers between devices  15.8 us (36%)
  waiting for transfers between devices  7.68 us (18%)
    ppermute x14, starting transfers between devices, swap(): return lax.ppermute(x, axis, [(i, i ^ bit) for i in range(count)])  15.8 us
    ppermute x14, waiting for transfers between devices, swap(): return lax.ppermute(x, axis, [(i, i ^ bit) for i in range(count)])  7.68 us
    pallas_call x1, Pallas kernels, first_maps(): pl.pallas_call(functools.partial(first_kernel, heads), in_specs=[pl.Block...  5.52 us
    pallas_call x4, Pallas kernels, row_maps(): pl.pallas_call(functools.partial(rows_kernel, heads, spot, slot), in_spec...  3.98 us
    pallas_call x4, Pallas kernels, add_part(): pl.pallas_call(add_kernel, grid=(1,), in_specs=[here, here] + [pl.BlockSp...  2.72 us
    pallas_call x8, Pallas kernels, project(): pl.pallas_call(functools.partial(project_kernel, start), out_shape=jax.Sh...  2.47 us
    pallas_call x1, Pallas kernels, own_maps(): pl.pallas_call(functools.partial(own_kernel, heads), in_specs=[here] * 4,...  2.39 us
    pallas_call x3, Pallas kernels, small_call(): pl.pallas_call(kernel, in_specs=[here] * len(args), out_specs=[here] * le...  2.1 us
  transfers between devices with their start and end apart: 14, of which 8 were waited for; matrix products, arithmetic and copies ran while one was open for 0% of the time, Pallas kernels for 44%

profile of v18, /device:TPU:0, one launch (start us, length us, event | category | flops | bytes accessed | tf_op | source)
XLA Modules:
  0.0 43.5 jit_solution(4863620278889942740)
XLA Ops:
  0.5 5.5 %first_maps.1 = (bf16[2048,128]{1,0:T(8,128)(2,1)S(1)}, f32[2048,128]{1,0:T(8,128)S(1)}, f32[2048,128]{1,0:T(8,128)S(1)}, f32[16,128]{1,0:T(8,128)S(1)}, f32[16,...) custom-call(bf16[2048,128]{1,0:T(8,128)(2,1)} %bitcast.3, ...), custom_call_target="tpu_custom_call" | custom-call | tf_op jit(solution)/shard_map/first_maps/pallas_call | solution.py:244
  6.0 3.6 %collective-permute-start = (bf16[128,256]{1,0:T(8,128)(2,1)S(1)}, bf16[128,256]{1,0:T(8,128)(2,1)S(1)}, u32[]{:S(2)}, u32[]{:S(2)}) collective-permute-start(bf16[128,256]{1,0:T(8,128)(2,1)S(1)} %get-tuple-element.52), channel_id=1, source_target_pairs={{0,12},{4,8},{8,4},{12,0},{16,28},{20,24},{24,20},{28,16},{1,13},{... | collective-permute-start | bytes 196616 | tf_op jit(solution)/shard_map/ppermute | solution.py:488
  10.2 2.4 %own_maps.1 = (f32[4,128,128]{2,1,0:T(8,128)S(1)}, f32[4,128,256]{2,1,0:T(8,128)S(1)}, f32[4,128,256]{2,1,0:T(8,128)S(1)}, bf16[128,256]{1,0:T(8,128)(2,1)S(1)}) custom-call(f32[2048,128]{1,0:T(8,128)S(1)} %get-tuple-element.46.k32, f32[2048,128]{1,0:T(8,128)S(1)} %get-tuple-element.55.v32, f32[16,128]{1,0:T(8,128)S(1)} %get-tuple-element.47.sums_ref, ...), custom_call_target="tpu_custom_call" | custom-call | flops 2000000000 | bytes 8000000 | tf_op jit(solution)/shard_map/own_maps/pallas_call | solution.py:270
  12.6 1.0 %row_maps.4 = (f32[512,256]{1,0:T(8,128)S(1)}, f32[2048,128]{1,0:T(8,128)S(1)}) custom-call(bf16[2048,128]{1,0:T(8,128)(2,1)S(1)} %get-tuple-element.45.q_ref, f32[2048,128]{1,0:T(8,128)S(1)} %get-tuple-element.46.k32, f32[16,128]{1,0:T(8,128)S(1)} %get-tuple-element.47.sums_ref, f32[12,128,128]{2,1,0:T(8,128)S(1)} %get-tuple-element.48.mix_ref, ...), custom_call_target="tpu_custom_call" | custom-call | flops 1000000000 | bytes 4000000 | tf_op jit(solution)/shard_map/row_maps/pallas_call | solution.py:311
  14.8 2.7 %collective-permute-start.3 = (bf16[128,128]{1,0:T(8,128)(2,1)S(1)}, bf16[128,128]{1,0:T(8,128)(2,1)S(1)}, u32[]{:S(2)}, u32[]{:S(2)}) collective-permute-start(bf16[128,128]{1,0:T(8,128)(2,1)S(1)} %group_state.1), channel_id=1, source_target_pairs={{0,16},{4,20},{8,24},{12,28},{16,0},{20,4},{24,8},{28,12},{1,17},{... | collective-permute-start | bytes 98312 | tf_op jit(solution)/shard_map/ppermute | solution.py:488
  17.4 1.0 %row_maps.5.refs_1_ = f32[512,256]{1,0:T(8,128)S(1)} custom-call(f32[2048,128]{1,0:T(8,128)S(1)} %get-tuple-element.73.q_ref, f32[2048,128]{1,0:T(8,128)S(1)} %get-tuple-element.46.k32, f32[16,128]{1,0:T(8,128)S(1)} %get-tuple-element.47.sums_ref, f32[12,128,128]{2,1,0:T(8,128)S(1)} %get-tuple-element.48.mix_ref, ...), custom_call_target="tpu_custom_call" | custom-call | flops 1000000000 | bytes 4000000 | tf_op jit(solution)/shard_map/row_maps/pallas_call | solution.py:311
  18.4 1.4 %group_prefix.1 = (bf16[4,128,256]{2,1,0:T(8,128)(2,1)S(1)}, f32[4,128,128]{2,1,0:T(8,128)S(1)}, bf16[128,256]{1,0:T(8,128)(2,1)}) custom-call(bf16[128,256]{1,0:T(8,128)(2,1)S(1)} %collective-permute-done.refs_0_, bf16[128,256]{1,0:T(8,128)(2,1)S(1)} %collective-permute-done.1.refs_1_, bf16[128,256]{1,0:T(8,128)(2,1)S(1)} %collective-permute-done.2.refs_2_, ...), custom_call_target="tpu_custom_call" | custom-call | tf_op jit(solution)/shard_map/group_prefix/pallas_call | solution.py:324
  20.0 2.3 %collective-permute-start.4 = (bf16[128,128]{1,0:T(8,128)(2,1)S(1)}, bf16[128,128]{1,0:T(8,128)(2,1)S(1)}, u32[]{:S(2)}, u32[]{:S(2)}) collective-permute-start(bf16[128,128]{1,0:T(8,128)(2,1)S(1)} %get-tuple-element.77), channel_id=1, source_target_pairs={{0,12},{4,8},{8,4},{12,0},{16,28},{20,24},{24,20},{28,16},{1,13},{... | collective-permute-start | bytes 98312 | tf_op jit(solution)/shard_map/ppermute | solution.py:488
  22.8 0.8 %collective-permute-start.6 = (bf16[128,128]{1,0:T(8,128)(2,1)S(1)}, bf16[128,128]{1,0:T(8,128)(2,1)S(1)}, u32[]{:S(2)}, u32[]{:S(2)}) collective-permute-start(bf16[128,128]{1,0:T(8,128)(2,1)S(1)} %get-tuple-element.79), channel_id=1, source_target_pairs={{0,4},{4,0},{8,12},{12,8},{16,20},{20,16},{24,28},{28,24},{1,5},{5... | collective-permute-start | bytes 98312 | tf_op jit(solution)/shard_map/ppermute | solution.py:488
  23.6 1.0 %row_maps.6.refs_2_ = f32[512,256]{1,0:T(8,128)S(1)} custom-call(f32[2048,128]{1,0:T(8,128)S(1)} %get-tuple-element.73.q_ref, f32[2048,128]{1,0:T(8,128)S(1)} %get-tuple-element.46.k32, f32[16,128]{1,0:T(8,128)S(1)} %get-tuple-element.47.sums_ref, f32[12,128,128]{2,1,0:T(8,128)S(1)} %get-tuple-element.48.mix_ref, ...), custom_call_target="tpu_custom_call" | custom-call | flops 1000000000 | bytes 4000000 | tf_op jit(solution)/shard_map/row_maps/pallas_call | solution.py:311
  24.6 1.0 %row_maps.7.refs_3_ = f32[512,256]{1,0:T(8,128)S(1)} custom-call(f32[2048,128]{1,0:T(8,128)S(1)} %get-tuple-element.73.q_ref, f32[2048,128]{1,0:T(8,128)S(1)} %get-tuple-element.46.k32, f32[16,128]{1,0:T(8,128)S(1)} %get-tuple-element.47.sums_ref, f32[4,128,128]{2,1,0:T(8,128)S(1)} %get-tuple-element.74.mix_ref, ...), custom_call_target="tpu_custom_call" | custom-call | flops 1000000000 | bytes 4000000 | tf_op jit(solution)/shard_map/row_maps/pallas_call | solution.py:311
  25.6 0.7 %collective-permute-done.5.refs_5_ = bf16[128,128]{1,0:T(8,128)(2,1)S(1)} collective-permute-done((bf16[128,128]{1,0:T(8,128)(2,1)S(1)}, bf16[128,128]{1,0:T(8,128)(2,1)S(1)}, u32[]{:S(2)}, u32[]{:S(2)}) %collective-permute-start.5) | collective-permute-done | bytes 32800 | tf_op jit(solution)/shard_map/ppermute | solution.py:488
  27.4 0.6 %collective-permute-start.7 = (bf16[128,512]{1,0:T(8,128)(2,1)S(1)}, bf16[128,512]{1,0:T(8,128)(2,1)S(1)}, u32[]{:S(2)}, u32[]{:S(2)}) collective-permute-start(bf16[128,512]{1,0:T(8,128)(2,1)S(1)} %get-tuple-element.82), channel_id=1, source_target_pairs={{0,1},{1,0},{2,3},{3,2},{4,5},{5,4},{6,7},{7,6},{8,9},{9,8},{10,11... | collective-permute-start | bytes 393224 | tf_op jit(solution)/shard_map/ppermute | solution.py:488
  28.8 1.6 %collective-permute-start.13 = (bf16[128,512]{1,0:T(8,128)(2,1)S(1)}, bf16[128,512]{1,0:T(8,128)(2,1)S(1)}, u32[]{:S(2)}, u32[]{:S(2)}) collective-permute-start(bf16[128,512]{1,0:T(8,128)(2,1)S(1)} %project.15), channel_id=1, source_target_pairs={{0,2},{1,3},{2,0},{3,1},{4,6},{5,7},{6,4},{7,5},{8,10},{9,11},{10,... | collective-permute-start | bytes 393224 | tf_op jit(solution)/shard_map/ppermute | solution.py:488
  30.7 0.6 %collective-permute-start.12 = (bf16[128,512]{1,0:T(8,128)(2,1)S(1)}, bf16[128,512]{1,0:T(8,128)(2,1)S(1)}, u32[]{:S(2)}, u32[]{:S(2)}) collective-permute-start(bf16[128,512]{1,0:T(8,128)(2,1)S(1)} %project.13), channel_id=1, source_target_pairs={{0,2},{1,3},{2,0},{3,1},{4,6},{5,7},{6,4},{7,5},{8,10},{9,11},{10,... | collective-permute-start | bytes 393224 | tf_op jit(solution)/shard_map/ppermute | solution.py:488
  31.6 1.6 %collective-permute-start.11 = (bf16[128,512]{1,0:T(8,128)(2,1)S(1)}, bf16[128,512]{1,0:T(8,128)(2,1)S(1)}, u32[]{:S(2)}, u32[]{:S(2)}) collective-permute-start(bf16[128,512]{1,0:T(8,128)(2,1)S(1)} %project.11), channel_id=1, source_target_pairs={{0,2},{1,3},{2,0},{3,1},{4,6},{5,7},{6,4},{7,5},{8,10},{9,11},{10,... | collective-permute-start | bytes 393224 | tf_op jit(solution)/shard_map/ppermute | solution.py:488
  33.5 0.6 %collective-permute-start.10 = (bf16[128,512]{1,0:T(8,128)(2,1)S(1)}, bf16[128,512]{1,0:T(8,128)(2,1)S(1)}, u32[]{:S(2)}, u32[]{:S(2)}) collective-permute-start(bf16[128,512]{1,0:T(8,128)(2,1)S(1)} %project.9), channel_id=1, source_target_pairs={{0,2},{1,3},{2,0},{3,1},{4,6},{5,7},{6,4},{7,5},{8,10},{9,11},{10,... | collective-permute-start | bytes 393224 | tf_op jit(solution)/shard_map/ppermute | solution.py:488
  35.3 0.7 %add_part.4.refs_0_ = bf16[128,2048]{1,0:T(8,128)(2,1)} custom-call(f32[128,512]{1,0:T(8,128)S(1)} %project.14.mine_ref, bf16[128,512]{1,0:T(8,128)(2,1)S(1)} %collective-permute-done.13.theirs_ref), custom_call_target="tpu_custom_call" | custom-call | tf_op jit(solution)/shard_map/add_part/pallas_call | solution.py:474
  36.0 2.0 %collective-permute-done.12.theirs_ref = bf16[128,512]{1,0:T(8,128)(2,1)S(1)} collective-permute-done((bf16[128,512]{1,0:T(8,128)(2,1)S(1)}, bf16[128,512]{1,0:T(8,128)(2,1)S(1)}, u32[]{:S(2)}, u32[]{:S(2)}) %collective-permute-start.12) | collective-permute-done | bytes 131104 | tf_op jit(solution)/shard_map/ppermute | solution.py:488
  38.0 0.7 %add_part.5.refs_0_ = bf16[128,2048]{1,0:T(8,128)(2,1)} custom-call(f32[128,512]{1,0:T(8,128)S(1)} %project.12.mine_ref, bf16[128,512]{1,0:T(8,128)(2,1)S(1)} %collective-permute-done.12.theirs_ref, bf16[128,2048]{1,0:T(8,128)(2,1)} %add_part.4.refs_0_), custom_call_target="tpu_custom_call", output_to_operand_aliasing={{}: (2, {})} | custom-call | tf_op jit(solution)/shard_map/add_part/pallas_call | solution.py:474
  38.7 2.1 %collective-permute-done.11.theirs_ref = bf16[128,512]{1,0:T(8,128)(2,1)S(1)} collective-permute-done((bf16[128,512]{1,0:T(8,128)(2,1)S(1)}, bf16[128,512]{1,0:T(8,128)(2,1)S(1)}, u32[]{:S(2)}, u32[]{:S(2)}) %collective-permute-start.11) | collective-permute-done | bytes 131104 | tf_op jit(solution)/shard_map/ppermute | solution.py:488
  40.8 0.7 %add_part.6.refs_0_ = bf16[128,2048]{1,0:T(8,128)(2,1)} custom-call(f32[128,512]{1,0:T(8,128)S(1)} %project.10.mine_ref, bf16[128,512]{1,0:T(8,128)(2,1)S(1)} %collective-permute-done.11.theirs_ref, bf16[128,2048]{1,0:T(8,128)(2,1)} %add_part.5.refs_0_), custom_call_target="tpu_custom_call", output_to_operand_aliasing={{}: (2, {})} | custom-call | tf_op jit(solution)/shard_map/add_part/pallas_call | solution.py:474
  41.5 1.3 %collective-permute-done.10.theirs_ref = bf16[128,512]{1,0:T(8,128)(2,1)S(1)} collective-permute-done((bf16[128,512]{1,0:T(8,128)(2,1)S(1)}, bf16[128,512]{1,0:T(8,128)(2,1)S(1)}, u32[]{:S(2)}, u32[]{:S(2)}) %collective-permute-start.10) | collective-permute-done | bytes 131104 | tf_op jit(solution)/shard_map/ppermute | solution.py:488
  42.8 0.7 %add_part.7 = bf16[128,2048]{1,0:T(8,128)(2,1)} custom-call(f32[128,512]{1,0:T(8,128)S(1)} %project.8.mine_ref, bf16[128,512]{1,0:T(8,128)(2,1)S(1)} %collective-permute-done.10.theirs_ref, bf16[128,2048]{1,0:T(8,128)(2,1)} %add_part.6.refs_0_), custom_call_target="tpu_custom_call", output_to_operand_aliasing={{}: (2, {})} | custom-call | tf_op jit(solution)/shard_map/add_part/pallas_call | solution.py:474
  (29 shorter events, 7.0 us)
Async XLA Ops:
  0.0 28.4 %collective-permute-start.8 = (bf16[512,2048]{1,0:T(8,128)(2,1)}, bf16[512,2048]{1,0:T(8,128)(2,1)S(1)}, u32[]{:S(2)}, u32[]{:S(2)}) collective-permute-start(bf16[512,2048]{1,0:T(8,128)(2,1)} %w_ref.15), channel_id=1, source_target_pairs={{0,1},{1,0},{2,3},{3,2},{4,5},{5,4},{6,7},{7,6},{8,9},{9,8},{10,11... | collective-permute-start | bytes 6291464 | tf_op jit(solution)/shard_map/ppermute | solution.py:488
  6.0 7.6 %collective-permute-start = (bf16[128,256]{1,0:T(8,128)(2,1)S(1)}, bf16[128,256]{1,0:T(8,128)(2,1)S(1)}, u32[]{:S(2)}, u32[]{:S(2)}) collective-permute-start(bf16[128,256]{1,0:T(8,128)(2,1)S(1)} %get-tuple-element.52), channel_id=1, source_target_pairs={{0,12},{4,8},{8,4},{12,0},{16,28},{20,24},{24,20},{28,16},{1,13},{... | collective-permute-start | bytes 196616 | tf_op jit(solution)/shard_map/ppermute | solution.py:488
  9.6 4.3 %collective-permute-start.1 = (bf16[128,256]{1,0:T(8,128)(2,1)S(1)}, bf16[128,256]{1,0:T(8,128)(2,1)S(1)}, u32[]{:S(2)}, u32[]{:S(2)}) collective-permute-start(bf16[128,256]{1,0:T(8,128)(2,1)S(1)} %get-tuple-element.53), channel_id=1, source_target_pairs={{0,8},{4,12},{8,0},{12,4},{16,24},{20,28},{24,16},{28,20},{1,9},{5... | collective-permute-start | bytes 196616 | tf_op jit(solution)/shard_map/ppermute | solution.py:488
  10.0 4.3 %collective-permute-start.2 = (bf16[128,256]{1,0:T(8,128)(2,1)S(1)}, bf16[128,256]{1,0:T(8,128)(2,1)S(1)}, u32[]{:S(2)}, u32[]{:S(2)}) collective-permute-start(bf16[128,256]{1,0:T(8,128)(2,1)S(1)} %get-tuple-element.54), channel_id=1, source_target_pairs={{0,4},{4,0},{8,12},{12,8},{16,20},{20,16},{24,28},{28,24},{1,5},{5... | collective-permute-start | bytes 196616 | tf_op jit(solution)/shard_map/ppermute | solution.py:488
  14.8 5.0 %collective-permute-start.3 = (bf16[128,128]{1,0:T(8,128)(2,1)S(1)}, bf16[128,128]{1,0:T(8,128)(2,1)S(1)}, u32[]{:S(2)}, u32[]{:S(2)}) collective-permute-start(bf16[128,128]{1,0:T(8,128)(2,1)S(1)} %group_state.1), channel_id=1, source_target_pairs={{0,16},{4,20},{8,24},{12,28},{16,0},{20,4},{24,8},{28,12},{1,17},{... | collective-permute-start | bytes 98312 | tf_op jit(solution)/shard_map/ppermute | solution.py:488
  20.0 5.6 %collective-permute-start.4 = (bf16[128,128]{1,0:T(8,128)(2,1)S(1)}, bf16[128,128]{1,0:T(8,128)(2,1)S(1)}, u32[]{:S(2)}, u32[]{:S(2)}) collective-permute-start(bf16[128,128]{1,0:T(8,128)(2,1)S(1)} %get-tuple-element.77), channel_id=1, source_target_pairs={{0,12},{4,8},{8,4},{12,0},{16,28},{20,24},{24,20},{28,16},{1,13},{... | collective-permute-start | bytes 98312 | tf_op jit(solution)/shard_map/ppermute | solution.py:488
  22.4 3.9 %collective-permute-start.5 = (bf16[128,128]{1,0:T(8,128)(2,1)S(1)}, bf16[128,128]{1,0:T(8,128)(2,1)S(1)}, u32[]{:S(2)}, u32[]{:S(2)}) collective-permute-start(bf16[128,128]{1,0:T(8,128)(2,1)S(1)} %get-tuple-element.78), channel_id=1, source_target_pairs={{0,8},{4,12},{8,0},{12,4},{16,24},{20,28},{24,16},{28,20},{1,9},{5... | collective-permute-start | bytes 98312 | tf_op jit(solution)/shard_map/ppermute | solution.py:488
  22.8 3.9 %collective-permute-start.6 = (bf16[128,128]{1,0:T(8,128)(2,1)S(1)}, bf16[128,128]{1,0:T(8,128)(2,1)S(1)}, u32[]{:S(2)}, u32[]{:S(2)}) collective-permute-start(bf16[128,128]{1,0:T(8,128)(2,1)S(1)} %get-tuple-element.79), channel_id=1, source_target_pairs={{0,4},{4,0},{8,12},{12,8},{16,20},{20,16},{24,28},{28,24},{1,5},{5... | collective-permute-start | bytes 98312 | tf_op jit(solution)/shard_map/ppermute | solution.py:488
  25.6 2.9 %copy-start = (bf16[512,2048]{1,0:T(8,128)(2,1)S(1)}, bf16[512,2048]{1,0:T(8,128)(2,1)}, u32[]{:S(2)}) copy-start(bf16[512,2048]{1,0:T(8,128)(2,1)} %w_ref.15) | copy-start | bytes 6291460
  27.0 1.4 %collective-permute-start.9 = (bf16[128,512]{1,0:T(8,128)(2,1)S(1)}, bf16[128,512]{1,0:T(8,128)(2,1)S(1)}, u32[]{:S(2)}, u32[]{:S(2)}) collective-permute-start(bf16[128,512]{1,0:T(8,128)(2,1)S(1)} %get-tuple-element.84), channel_id=1, source_target_pairs={{0,1},{1,0},{2,3},{3,2},{4,5},{5,4},{6,7},{7,6},{8,9},{9,8},{10,11... | collective-permute-start | bytes 393224 | tf_op jit(solution)/shard_map/ppermute | solution.py:488
  27.4 6.6 %collective-permute-start.7 = (bf16[128,512]{1,0:T(8,128)(2,1)S(1)}, bf16[128,512]{1,0:T(8,128)(2,1)S(1)}, u32[]{:S(2)}, u32[]{:S(2)}) collective-permute-start(bf16[128,512]{1,0:T(8,128)(2,1)S(1)} %get-tuple-element.82), channel_id=1, source_target_pairs={{0,1},{1,0},{2,3},{3,2},{4,5},{5,4},{6,7},{7,6},{8,9},{9,8},{10,11... | collective-permute-start | bytes 393224 | tf_op jit(solution)/shard_map/ppermute | solution.py:488
  28.8 6.5 %collective-permute-start.13 = (bf16[128,512]{1,0:T(8,128)(2,1)S(1)}, bf16[128,512]{1,0:T(8,128)(2,1)S(1)}, u32[]{:S(2)}, u32[]{:S(2)}) collective-permute-start(bf16[128,512]{1,0:T(8,128)(2,1)S(1)} %project.15), channel_id=1, source_target_pairs={{0,2},{1,3},{2,0},{3,1},{4,6},{5,7},{6,4},{7,5},{8,10},{9,11},{10,... | collective-permute-start | bytes 393224 | tf_op jit(solution)/shard_map/ppermute | solution.py:488
  30.7 7.3 %collective-permute-start.12 = (bf16[128,512]{1,0:T(8,128)(2,1)S(1)}, bf16[128,512]{1,0:T(8,128)(2,1)S(1)}, u32[]{:S(2)}, u32[]{:S(2)}) collective-permute-start(bf16[128,512]{1,0:T(8,128)(2,1)S(1)} %project.13), channel_id=1, source_target_pairs={{0,2},{1,3},{2,0},{3,1},{4,6},{5,7},{6,4},{7,5},{8,10},{9,11},{10,... | collective-permute-start | bytes 393224 | tf_op jit(solution)/shard_map/ppermute | solution.py:488
  31.6 9.2 %collective-permute-start.11 = (bf16[128,512]{1,0:T(8,128)(2,1)S(1)}, bf16[128,512]{1,0:T(8,128)(2,1)S(1)}, u32[]{:S(2)}, u32[]{:S(2)}) collective-permute-start(bf16[128,512]{1,0:T(8,128)(2,1)S(1)} %project.11), channel_id=1, source_target_pairs={{0,2},{1,3},{2,0},{3,1},{4,6},{5,7},{6,4},{7,5},{8,10},{9,11},{10,... | collective-permute-start | bytes 393224 | tf_op jit(solution)/shard_map/ppermute | solution.py:488
  33.5 9.3 %collective-permute-start.10 = (bf16[128,512]{1,0:T(8,128)(2,1)S(1)}, bf16[128,512]{1,0:T(8,128)(2,1)S(1)}, u32[]{:S(2)}, u32[]{:S(2)}) collective-permute-start(bf16[128,512]{1,0:T(8,128)(2,1)S(1)} %project.9), channel_id=1, source_target_pairs={{0,2},{1,3},{2,0},{3,1},{4,6},{5,7},{6,4},{7,5},{8,10},{9,11},{10,... | collective-permute-start | bytes 393224 | tf_op jit(solution)/shard_map/ppermute | solution.py:488

commit v19 on v18

--- a/solution.py
+++ b/solution.py
@@ -69,17 +69,33 @@
     return sum(dot(x, upper) for x in reversed(three(rows)))
 
 
-def base_inverse(lower, row, col):
+LANES = lax.GatherDimensionNumbers(
+    offset_dims=(),
+    collapsed_slice_dims=(1,),
+    start_index_map=(1,),
+    operand_batching_dims=(0,),
+    start_indices_batching_dims=(0,),
+)
+
+
+def pick_lanes(x, index):
+    return lax.gather(x, index, LANES, (1, 1), mode=lax.GatherScatterMode.PROMISE_IN_BOUNDS)
+
+
+def base_inverses(lowers, row, col):
     on_block = (row // B) == (col // B)
-    blocks = jnp.where(on_block, lower, 0.0)
-    packed = sum(blocks[i * B : (i + 1) * B] for i in range(1, C // B)) + blocks[:B]
     r, c = row[:B], col[:B]
-    found = jnp.where(r == c % B, 1.0, 0.0)
-    first = (c // B) * B
-    for j in range(B - 1):
-        factor = jnp.take_along_axis(packed, first + j, axis=1)
-        found = found - factor * found[j : j + 1]
-    return jnp.where(on_block, jnp.concatenate([found] * (C // B), axis=0), 0.0)
+    identity = jnp.where(r == c % B, 1.0, 0.0)
+    columns = [((c // B) * B + j)[..., None] for j in range(B - 1)]
+    inverses = []
+    for lower in lowers:
+        blocks = jnp.where(on_block, lower, 0.0)
+        packed = sum(blocks[i * B : (i + 1) * B] for i in range(1, C // B)) + blocks[:B]
+        found = identity
+        for j, column in enumerate(columns):
+            found = found - pick_lanes(packed, column) * found[j : j + 1]
+        inverses.append(jnp.where(on_block, jnp.concatenate([found] * (C // B), axis=0), 0.0))
+    return inverses
 
 
 def odd_rows(x, size):
@@ -98,7 +114,7 @@
 
 
 def inverses(lowers, row, col):
-    found = [base_inverse(a, row, col) for a in lowers]
+    found = base_inverses(lowers, row, col)
     parts = [split(a) for a in lowers]
     halves = [split(x) for x in found]
     size = B
@@ -357,9 +373,10 @@
     out_ref = refs[-1]
 
     def work(parts, _):
-        state = parts[0][:, C:].astype(F32)
-        for part in parts[1:]:
-            state = times_parts(part[:, :C], state) + part[:, C:].astype(F32)
+        first, second, third, last = parts
+        state = dot(second[:, :C], first[:, C:]) + second[:, C:].astype(F32)
+        both = dot(last[:, :C], third[...])
+        state = dot3(split(both[:, :C]), split(state)) + (both[:, C:] + last[:, C:].astype(F32))
         out_ref[...] = state.astype(BF16)
 
     by_place(refs[:-1], work)

time: 43.7 us -> 43.9 us (level)
  no operation moved by 1% of the time
where the time goes in v19:
time: 43.9 us; the launch traced here: 43.7 us
  Pallas kernels  20 us (46%)
  starting transfers between devices  15.8 us (36%)
  waiting for transfers between devices  7.67 us (17%)
    ppermute x14, starting transfers between devices, swap(): return lax.ppermute(x, axis, [(i, i ^ bit) for i in range(count)])  15.8 us
    ppermute x14, waiting for transfers between devices, swap(): return lax.ppermute(x, axis, [(i, i ^ bit) for i in range(count)])  7.67 us
    pallas_call x1, Pallas kernels, first_maps(): pl.pallas_call(functools.partial(first_kernel, heads), in_specs=[pl.Block...  5.86 us
    pallas_call x4, Pallas kernels, row_maps(): pl.pallas_call(functools.partial(rows_kernel, heads, spot, slot), in_spec...  3.98 us
    pallas_call x4, Pallas kernels, add_part(): pl.pallas_call(add_kernel, grid=(1,), in_specs=[here, here] + [pl.BlockSp...  2.72 us
    pallas_call x8, Pallas kernels, project(): pl.pallas_call(functools.partial(project_kernel, start), out_shape=jax.Sh...  2.47 us
    pallas_call x1, Pallas kernels, own_maps(): pl.pallas_call(functools.partial(own_kernel, heads), in_specs=[here] * 4,...  2.4 us
    pallas_call x3, Pallas kernels, small_call(): pl.pallas_call(kernel, in_specs=[here] * len(args), out_specs=[here] * le...  1.95 us
  transfers between devices with their start and end apart: 14, of which 8 were waited for; matrix products, arithmetic and copies ran while one was open for 0% of the time, Pallas kernels for 44%

profile of v19, /device:TPU:0, one launch (start us, length us, event | category | flops | bytes accessed | tf_op | source)
XLA Modules:
  0.0 43.7 jit_solution(3172673038517865401)
XLA Ops:
  0.5 5.9 %first_maps.1 = (bf16[2048,128]{1,0:T(8,128)(2,1)S(1)}, f32[2048,128]{1,0:T(8,128)S(1)}, f32[2048,128]{1,0:T(8,128)S(1)}, f32[16,128]{1,0:T(8,128)S(1)}, f32[16,...) custom-call(bf16[2048,128]{1,0:T(8,128)(2,1)} %bitcast.3, ...), custom_call_target="tpu_custom_call" | custom-call | tf_op jit(solution)/shard_map/first_maps/pallas_call | solution.py:260
  6.3 3.6 %collective-permute-start = (bf16[128,256]{1,0:T(8,128)(2,1)S(1)}, bf16[128,256]{1,0:T(8,128)(2,1)S(1)}, u32[]{:S(2)}, u32[]{:S(2)}) collective-permute-start(bf16[128,256]{1,0:T(8,128)(2,1)S(1)} %get-tuple-element.52), channel_id=1, source_target_pairs={{0,12},{4,8},{8,4},{12,0},{16,28},{20,24},{24,20},{28,16},{1,13},{... | collective-permute-start | bytes 196616 | tf_op jit(solution)/shard_map/ppermute | solution.py:505
  10.5 2.4 %own_maps.1 = (f32[4,128,128]{2,1,0:T(8,128)S(1)}, f32[4,128,256]{2,1,0:T(8,128)S(1)}, f32[4,128,256]{2,1,0:T(8,128)S(1)}, bf16[128,256]{1,0:T(8,128)(2,1)S(1)}) custom-call(f32[2048,128]{1,0:T(8,128)S(1)} %get-tuple-element.46.k32, f32[2048,128]{1,0:T(8,128)S(1)} %get-tuple-element.55.v32, f32[16,128]{1,0:T(8,128)S(1)} %get-tuple-element.47.sums_ref, ...), custom_call_target="tpu_custom_call" | custom-call | flops 2000000000 | bytes 8000000 | tf_op jit(solution)/shard_map/own_maps/pallas_call | solution.py:286
  12.9 1.0 %row_maps.4 = (f32[512,256]{1,0:T(8,128)S(1)}, f32[2048,128]{1,0:T(8,128)S(1)}) custom-call(bf16[2048,128]{1,0:T(8,128)(2,1)S(1)} %get-tuple-element.45.q_ref, f32[2048,128]{1,0:T(8,128)S(1)} %get-tuple-element.46.k32, f32[16,128]{1,0:T(8,128)S(1)} %get-tuple-element.47.sums_ref, f32[12,128,128]{2,1,0:T(8,128)S(1)} %get-tuple-element.48.mix_ref, ...), custom_call_target="tpu_custom_call" | custom-call | flops 1000000000 | bytes 4000000 | tf_op jit(solution)/shard_map/row_maps/pallas_call | solution.py:327
  15.0 2.7 %collective-permute-start.3 = (bf16[128,128]{1,0:T(8,128)(2,1)S(1)}, bf16[128,128]{1,0:T(8,128)(2,1)S(1)}, u32[]{:S(2)}, u32[]{:S(2)}) collective-permute-start(bf16[128,128]{1,0:T(8,128)(2,1)S(1)} %group_state.1), channel_id=1, source_target_pairs={{0,16},{4,20},{8,24},{12,28},{16,0},{20,4},{24,8},{28,12},{1,17},{... | collective-permute-start | bytes 98312 | tf_op jit(solution)/shard_map/ppermute | solution.py:505
  17.6 1.0 %row_maps.5.refs_1_ = f32[512,256]{1,0:T(8,128)S(1)} custom-call(f32[2048,128]{1,0:T(8,128)S(1)} %get-tuple-element.73.q_ref, f32[2048,128]{1,0:T(8,128)S(1)} %get-tuple-element.46.k32, f32[16,128]{1,0:T(8,128)S(1)} %get-tuple-element.47.sums_ref, f32[12,128,128]{2,1,0:T(8,128)S(1)} %get-tuple-element.48.mix_ref, ...), custom_call_target="tpu_custom_call" | custom-call | flops 1000000000 | bytes 4000000 | tf_op jit(solution)/shard_map/row_maps/pallas_call | solution.py:327
  18.6 1.4 %group_prefix.1 = (bf16[4,128,256]{2,1,0:T(8,128)(2,1)S(1)}, f32[4,128,128]{2,1,0:T(8,128)S(1)}, bf16[128,256]{1,0:T(8,128)(2,1)}) custom-call(bf16[128,256]{1,0:T(8,128)(2,1)S(1)} %collective-permute-done.refs_0_, bf16[128,256]{1,0:T(8,128)(2,1)S(1)} %collective-permute-done.1.refs_1_, bf16[128,256]{1,0:T(8,128)(2,1)S(1)} %collective-permute-done.2.refs_2_, ...), custom_call_target="tpu_custom_call" | custom-call | tf_op jit(solution)/shard_map/group_prefix/pallas_call | solution.py:340
  20.2 2.3 %collective-permute-start.4 = (bf16[128,128]{1,0:T(8,128)(2,1)S(1)}, bf16[128,128]{1,0:T(8,128)(2,1)S(1)}, u32[]{:S(2)}, u32[]{:S(2)}) collective-permute-start(bf16[128,128]{1,0:T(8,128)(2,1)S(1)} %get-tuple-element.77), channel_id=1, source_target_pairs={{0,12},{4,8},{8,4},{12,0},{16,28},{20,24},{24,20},{28,16},{1,13},{... | collective-permute-start | bytes 98312 | tf_op jit(solution)/shard_map/ppermute | solution.py:505
  23.0 0.8 %collective-permute-start.6 = (bf16[128,128]{1,0:T(8,128)(2,1)S(1)}, bf16[128,128]{1,0:T(8,128)(2,1)S(1)}, u32[]{:S(2)}, u32[]{:S(2)}) collective-permute-start(bf16[128,128]{1,0:T(8,128)(2,1)S(1)} %get-tuple-element.79), channel_id=1, source_target_pairs={{0,4},{4,0},{8,12},{12,8},{16,20},{20,16},{24,28},{28,24},{1,5},{5... | collective-permute-start | bytes 98312 | tf_op jit(solution)/shard_map/ppermute | solution.py:505
  23.8 1.0 %row_maps.6.refs_2_ = f32[512,256]{1,0:T(8,128)S(1)} custom-call(f32[2048,128]{1,0:T(8,128)S(1)} %get-tuple-element.73.q_ref, f32[2048,128]{1,0:T(8,128)S(1)} %get-tuple-element.46.k32, f32[16,128]{1,0:T(8,128)S(1)} %get-tuple-element.47.sums_ref, f32[12,128,128]{2,1,0:T(8,128)S(1)} %get-tuple-element.48.mix_ref, ...), custom_call_target="tpu_custom_call" | custom-call | flops 1000000000 | bytes 4000000 | tf_op jit(solution)/shard_map/row_maps/pallas_call | solution.py:327
  24.8 1.0 %row_maps.7.refs_3_ = f32[512,256]{1,0:T(8,128)S(1)} custom-call(f32[2048,128]{1,0:T(8,128)S(1)} %get-tuple-element.73.q_ref, f32[2048,128]{1,0:T(8,128)S(1)} %get-tuple-element.46.k32, f32[16,128]{1,0:T(8,128)S(1)} %get-tuple-element.47.sums_ref, f32[4,128,128]{2,1,0:T(8,128)S(1)} %get-tuple-element.74.mix_ref, ...), custom_call_target="tpu_custom_call" | custom-call | flops 1000000000 | bytes 4000000 | tf_op jit(solution)/shard_map/row_maps/pallas_call | solution.py:327
  25.8 0.7 %collective-permute-done.5.refs_5_ = bf16[128,128]{1,0:T(8,128)(2,1)S(1)} collective-permute-done((bf16[128,128]{1,0:T(8,128)(2,1)S(1)}, bf16[128,128]{1,0:T(8,128)(2,1)S(1)}, u32[]{:S(2)}, u32[]{:S(2)}) %collective-permute-start.5) | collective-permute-done | bytes 32800 | tf_op jit(solution)/shard_map/ppermute | solution.py:505
  27.6 0.6 %collective-permute-start.7 = (bf16[128,512]{1,0:T(8,128)(2,1)S(1)}, bf16[128,512]{1,0:T(8,128)(2,1)S(1)}, u32[]{:S(2)}, u32[]{:S(2)}) collective-permute-start(bf16[128,512]{1,0:T(8,128)(2,1)S(1)} %get-tuple-element.82), channel_id=1, source_target_pairs={{0,1},{1,0},{2,3},{3,2},{4,5},{5,4},{6,7},{7,6},{8,9},{9,8},{10,11... | collective-permute-start | bytes 393224 | tf_op jit(solution)/shard_map/ppermute | solution.py:505
  29.0 1.6 %collective-permute-start.13 = (bf16[128,512]{1,0:T(8,128)(2,1)S(1)}, bf16[128,512]{1,0:T(8,128)(2,1)S(1)}, u32[]{:S(2)}, u32[]{:S(2)}) collective-permute-start(bf16[128,512]{1,0:T(8,128)(2,1)S(1)} %project.15), channel_id=1, source_target_pairs={{0,2},{1,3},{2,0},{3,1},{4,6},{5,7},{6,4},{7,5},{8,10},{9,11},{10,... | collective-permute-start | bytes 393224 | tf_op jit(solution)/shard_map/ppermute | solution.py:505
  30.9 0.6 %collective-permute-start.12 = (bf16[128,512]{1,0:T(8,128)(2,1)S(1)}, bf16[128,512]{1,0:T(8,128)(2,1)S(1)}, u32[]{:S(2)}, u32[]{:S(2)}) collective-permute-start(bf16[128,512]{1,0:T(8,128)(2,1)S(1)} %project.13), channel_id=1, source_target_pairs={{0,2},{1,3},{2,0},{3,1},{4,6},{5,7},{6,4},{7,5},{8,10},{9,11},{10,... | collective-permute-start | bytes 393224 | tf_op jit(solution)/shard_map/ppermute | solution.py:505
  31.7 1.6 %collective-permute-start.11 = (bf16[128,512]{1,0:T(8,128)(2,1)S(1)}, bf16[128,512]{1,0:T(8,128)(2,1)S(1)}, u32[]{:S(2)}, u32[]{:S(2)}) collective-permute-start(bf16[128,512]{1,0:T(8,128)(2,1)S(1)} %project.11), channel_id=1, source_target_pairs={{0,2},{1,3},{2,0},{3,1},{4,6},{5,7},{6,4},{7,5},{8,10},{9,11},{10,... | collective-permute-start | bytes 393224 | tf_op jit(solution)/shard_map/ppermute | solution.py:505
  33.6 0.6 %collective-permute-start.10 = (bf16[128,512]{1,0:T(8,128)(2,1)S(1)}, bf16[128,512]{1,0:T(8,128)(2,1)S(1)}, u32[]{:S(2)}, u32[]{:S(2)}) collective-permute-start(bf16[128,512]{1,0:T(8,128)(2,1)S(1)} %project.9), channel_id=1, source_target_pairs={{0,2},{1,3},{2,0},{3,1},{4,6},{5,7},{6,4},{7,5},{8,10},{9,11},{10,... | collective-permute-start | bytes 393224 | tf_op jit(solution)/shard_map/ppermute | solution.py:505
  35.5 0.7 %add_part.4.refs_0_ = bf16[128,2048]{1,0:T(8,128)(2,1)} custom-call(f32[128,512]{1,0:T(8,128)S(1)} %project.14.mine_ref, bf16[128,512]{1,0:T(8,128)(2,1)S(1)} %collective-permute-done.13.theirs_ref), custom_call_target="tpu_custom_call" | custom-call | tf_op jit(solution)/shard_map/add_part/pallas_call | solution.py:491
  36.2 2.0 %collective-permute-done.12.theirs_ref = bf16[128,512]{1,0:T(8,128)(2,1)S(1)} collective-permute-done((bf16[128,512]{1,0:T(8,128)(2,1)S(1)}, bf16[128,512]{1,0:T(8,128)(2,1)S(1)}, u32[]{:S(2)}, u32[]{:S(2)}) %collective-permute-start.12) | collective-permute-done | bytes 131104 | tf_op jit(solution)/shard_map/ppermute | solution.py:505
  38.2 0.7 %add_part.5.refs_0_ = bf16[128,2048]{1,0:T(8,128)(2,1)} custom-call(f32[128,512]{1,0:T(8,128)S(1)} %project.12.mine_ref, bf16[128,512]{1,0:T(8,128)(2,1)S(1)} %collective-permute-done.12.theirs_ref, bf16[128,2048]{1,0:T(8,128)(2,1)} %add_part.4.refs_0_), custom_call_target="tpu_custom_call", output_to_operand_aliasing={{}: (2, {})} | custom-call | tf_op jit(solution)/shard_map/add_part/pallas_call | solution.py:491
  38.8 2.1 %collective-permute-done.11.theirs_ref = bf16[128,512]{1,0:T(8,128)(2,1)S(1)} collective-permute-done((bf16[128,512]{1,0:T(8,128)(2,1)S(1)}, bf16[128,512]{1,0:T(8,128)(2,1)S(1)}, u32[]{:S(2)}, u32[]{:S(2)}) %collective-permute-start.11) | collective-permute-done | bytes 131104 | tf_op jit(solution)/shard_map/ppermute | solution.py:505
  41.0 0.7 %add_part.6.refs_0_ = bf16[128,2048]{1,0:T(8,128)(2,1)} custom-call(f32[128,512]{1,0:T(8,128)S(1)} %project.10.mine_ref, bf16[128,512]{1,0:T(8,128)(2,1)S(1)} %collective-permute-done.11.theirs_ref, bf16[128,2048]{1,0:T(8,128)(2,1)} %add_part.5.refs_0_), custom_call_target="tpu_custom_call", output_to_operand_aliasing={{}: (2, {})} | custom-call | tf_op jit(solution)/shard_map/add_part/pallas_call | solution.py:491
  41.7 1.3 %collective-permute-done.10.theirs_ref = bf16[128,512]{1,0:T(8,128)(2,1)S(1)} collective-permute-done((bf16[128,512]{1,0:T(8,128)(2,1)S(1)}, bf16[128,512]{1,0:T(8,128)(2,1)S(1)}, u32[]{:S(2)}, u32[]{:S(2)}) %collective-permute-start.10) | collective-permute-done | bytes 131104 | tf_op jit(solution)/shard_map/ppermute | solution.py:505
  43.0 0.7 %add_part.7 = bf16[128,2048]{1,0:T(8,128)(2,1)} custom-call(f32[128,512]{1,0:T(8,128)S(1)} %project.8.mine_ref, bf16[128,512]{1,0:T(8,128)(2,1)S(1)} %collective-permute-done.10.theirs_ref, bf16[128,2048]{1,0:T(8,128)(2,1)} %add_part.6.refs_0_), custom_call_target="tpu_custom_call", output_to_operand_aliasing={{}: (2, {})} | custom-call | tf_op jit(solution)/shard_map/add_part/pallas_call | solution.py:491
  (29 shorter events, 6.8 us)
Async XLA Ops:
  0.0 28.6 %collective-permute-start.8 = (bf16[512,2048]{1,0:T(8,128)(2,1)}, bf16[512,2048]{1,0:T(8,128)(2,1)S(1)}, u32[]{:S(2)}, u32[]{:S(2)}) collective-permute-start(bf16[512,2048]{1,0:T(8,128)(2,1)} %w_ref.15), channel_id=1, source_target_pairs={{0,1},{1,0},{2,3},{3,2},{4,5},{5,4},{6,7},{7,6},{8,9},{9,8},{10,11... | collective-permute-start | bytes 6291464 | tf_op jit(solution)/shard_map/ppermute | solution.py:505
  6.3 7.7 %collective-permute-start = (bf16[128,256]{1,0:T(8,128)(2,1)S(1)}, bf16[128,256]{1,0:T(8,128)(2,1)S(1)}, u32[]{:S(2)}, u32[]{:S(2)}) collective-permute-start(bf16[128,256]{1,0:T(8,128)(2,1)S(1)} %get-tuple-element.52), channel_id=1, source_target_pairs={{0,12},{4,8},{8,4},{12,0},{16,28},{20,24},{24,20},{28,16},{1,13},{... | collective-permute-start | bytes 196616 | tf_op jit(solution)/shard_map/ppermute | solution.py:505
  9.9 4.3 %collective-permute-start.1 = (bf16[128,256]{1,0:T(8,128)(2,1)S(1)}, bf16[128,256]{1,0:T(8,128)(2,1)S(1)}, u32[]{:S(2)}, u32[]{:S(2)}) collective-permute-start(bf16[128,256]{1,0:T(8,128)(2,1)S(1)} %get-tuple-element.53), channel_id=1, source_target_pairs={{0,8},{4,12},{8,0},{12,4},{16,24},{20,28},{24,16},{28,20},{1,9},{5... | collective-permute-start | bytes 196616 | tf_op jit(solution)/shard_map/ppermute | solution.py:505
  10.3 4.3 %collective-permute-start.2 = (bf16[128,256]{1,0:T(8,128)(2,1)S(1)}, bf16[128,256]{1,0:T(8,128)(2,1)S(1)}, u32[]{:S(2)}, u32[]{:S(2)}) collective-permute-start(bf16[128,256]{1,0:T(8,128)(2,1)S(1)} %get-tuple-element.54), channel_id=1, source_target_pairs={{0,4},{4,0},{8,12},{12,8},{16,20},{20,16},{24,28},{28,24},{1,5},{5... | collective-permute-start | bytes 196616 | tf_op jit(solution)/shard_map/ppermute | solution.py:505
  15.0 5.0 %collective-permute-start.3 = (bf16[128,128]{1,0:T(8,128)(2,1)S(1)}, bf16[128,128]{1,0:T(8,128)(2,1)S(1)}, u32[]{:S(2)}, u32[]{:S(2)}) collective-permute-start(bf16[128,128]{1,0:T(8,128)(2,1)S(1)} %group_state.1), channel_id=1, source_target_pairs={{0,16},{4,20},{8,24},{12,28},{16,0},{20,4},{24,8},{28,12},{1,17},{... | collective-permute-start | bytes 98312 | tf_op jit(solution)/shard_map/ppermute | solution.py:505
  20.2 5.6 %collective-permute-start.4 = (bf16[128,128]{1,0:T(8,128)(2,1)S(1)}, bf16[128,128]{1,0:T(8,128)(2,1)S(1)}, u32[]{:S(2)}, u32[]{:S(2)}) collective-permute-start(bf16[128,128]{1,0:T(8,128)(2,1)S(1)} %get-tuple-element.77), channel_id=1, source_target_pairs={{0,12},{4,8},{8,4},{12,0},{16,28},{20,24},{24,20},{28,16},{1,13},{... | collective-permute-start | bytes 98312 | tf_op jit(solution)/shard_map/ppermute | solution.py:505
  22.5 3.9 %collective-permute-start.5 = (bf16[128,128]{1,0:T(8,128)(2,1)S(1)}, bf16[128,128]{1,0:T(8,128)(2,1)S(1)}, u32[]{:S(2)}, u32[]{:S(2)}) collective-permute-start(bf16[128,128]{1,0:T(8,128)(2,1)S(1)} %get-tuple-element.78), channel_id=1, source_target_pairs={{0,8},{4,12},{8,0},{12,4},{16,24},{20,28},{24,16},{28,20},{1,9},{5... | collective-permute-start | bytes 98312 | tf_op jit(solution)/shard_map/ppermute | solution.py:505
  23.0 3.9 %collective-permute-start.6 = (bf16[128,128]{1,0:T(8,128)(2,1)S(1)}, bf16[128,128]{1,0:T(8,128)(2,1)S(1)}, u32[]{:S(2)}, u32[]{:S(2)}) collective-permute-start(bf16[128,128]{1,0:T(8,128)(2,1)S(1)} %get-tuple-element.79), channel_id=1, source_target_pairs={{0,4},{4,0},{8,12},{12,8},{16,20},{20,16},{24,28},{28,24},{1,5},{5... | collective-permute-start | bytes 98312 | tf_op jit(solution)/shard_map/ppermute | solution.py:505
  25.8 2.9 %copy-start = (bf16[512,2048]{1,0:T(8,128)(2,1)S(1)}, bf16[512,2048]{1,0:T(8,128)(2,1)}, u32[]{:S(2)}) copy-start(bf16[512,2048]{1,0:T(8,128)(2,1)} %w_ref.15) | copy-start | bytes 6291460
  27.2 1.4 %collective-permute-start.9 = (bf16[128,512]{1,0:T(8,128)(2,1)S(1)}, bf16[128,512]{1,0:T(8,128)(2,1)S(1)}, u32[]{:S(2)}, u32[]{:S(2)}) collective-permute-start(bf16[128,512]{1,0:T(8,128)(2,1)S(1)} %get-tuple-element.84), channel_id=1, source_target_pairs={{0,1},{1,0},{2,3},{3,2},{4,5},{5,4},{6,7},{7,6},{8,9},{9,8},{10,11... | collective-permute-start | bytes 393224 | tf_op jit(solution)/shard_map/ppermute | solution.py:505
  27.6 6.6 %collective-permute-start.7 = (bf16[128,512]{1,0:T(8,128)(2,1)S(1)}, bf16[128,512]{1,0:T(8,128)(2,1)S(1)}, u32[]{:S(2)}, u32[]{:S(2)}) collective-permute-start(bf16[128,512]{1,0:T(8,128)(2,1)S(1)} %get-tuple-element.82), channel_id=1, source_target_pairs={{0,1},{1,0},{2,3},{3,2},{4,5},{5,4},{6,7},{7,6},{8,9},{9,8},{10,11... | collective-permute-start | bytes 393224 | tf_op jit(solution)/shard_map/ppermute | solution.py:505
  29.0 6.5 %collective-permute-start.13 = (bf16[128,512]{1,0:T(8,128)(2,1)S(1)}, bf16[128,512]{1,0:T(8,128)(2,1)S(1)}, u32[]{:S(2)}, u32[]{:S(2)}) collective-permute-start(bf16[128,512]{1,0:T(8,128)(2,1)S(1)} %project.15), channel_id=1, source_target_pairs={{0,2},{1,3},{2,0},{3,1},{4,6},{5,7},{6,4},{7,5},{8,10},{9,11},{10,... | collective-permute-start | bytes 393224 | tf_op jit(solution)/shard_map/ppermute | solution.py:505
  30.9 7.3 %collective-permute-start.12 = (bf16[128,512]{1,0:T(8,128)(2,1)S(1)}, bf16[128,512]{1,0:T(8,128)(2,1)S(1)}, u32[]{:S(2)}, u32[]{:S(2)}) collective-permute-start(bf16[128,512]{1,0:T(8,128)(2,1)S(1)} %project.13), channel_id=1, source_target_pairs={{0,2},{1,3},{2,0},{3,1},{4,6},{5,7},{6,4},{7,5},{8,10},{9,11},{10,... | collective-permute-start | bytes 393224 | tf_op jit(solution)/shard_map/ppermute | solution.py:505
  31.7 9.2 %collective-permute-start.11 = (bf16[128,512]{1,0:T(8,128)(2,1)S(1)}, bf16[128,512]{1,0:T(8,128)(2,1)S(1)}, u32[]{:S(2)}, u32[]{:S(2)}) collective-permute-start(bf16[128,512]{1,0:T(8,128)(2,1)S(1)} %project.11), channel_id=1, source_target_pairs={{0,2},{1,3},{2,0},{3,1},{4,6},{5,7},{6,4},{7,5},{8,10},{9,11},{10,... | collective-permute-start | bytes 393224 | tf_op jit(solution)/shard_map/ppermute | solution.py:505
  33.6 9.3 %collective-permute-start.10 = (bf16[128,512]{1,0:T(8,128)(2,1)S(1)}, bf16[128,512]{1,0:T(8,128)(2,1)S(1)}, u32[]{:S(2)}, u32[]{:S(2)}) collective-permute-start(bf16[128,512]{1,0:T(8,128)(2,1)S(1)} %project.9), channel_id=1, source_target_pairs={{0,2},{1,3},{2,0},{3,1},{4,6},{5,7},{6,4},{7,5},{8,10},{9,11},{10,... | collective-permute-start | bytes 393224 | tf_op jit(solution)/shard_map/ppermute | solution.py:505

commit v20 on v18

--- a/solution.py
+++ b/solution.py
@@ -69,6 +69,19 @@
     return sum(dot(x, upper) for x in reversed(three(rows)))
 
 
+LANES = lax.GatherDimensionNumbers(
+    offset_dims=(),
+    collapsed_slice_dims=(1,),
+    start_index_map=(1,),
+    operand_batching_dims=(0,),
+    start_indices_batching_dims=(0,),
+)
+
+
+def pick_lanes(x, index):
+    return lax.gather(x, index, LANES, (1, 1), mode=lax.GatherScatterMode.PROMISE_IN_BOUNDS)
+
+
 def base_inverse(lower, row, col):
     on_block = (row // B) == (col // B)
     blocks = jnp.where(on_block, lower, 0.0)
@@ -77,8 +90,7 @@
     found = jnp.where(r == c % B, 1.0, 0.0)
     first = (c // B) * B
     for j in range(B - 1):
-        factor = jnp.take_along_axis(packed, first + j, axis=1)
-        found = found - factor * found[j : j + 1]
+        found = found - pick_lanes(packed, (first + j)[..., None]) * found[j : j + 1]
     return jnp.where(on_block, jnp.concatenate([found] * (C // B), axis=0), 0.0)
 
 
@@ -357,9 +369,10 @@
     out_ref = refs[-1]
 
     def work(parts, _):
-        state = parts[0][:, C:].astype(F32)
-        for part in parts[1:]:
-            state = times_parts(part[:, :C], state) + part[:, C:].astype(F32)
+        first, second, third, last = parts
+        state = dot(second[:, :C], first[:, C:]) + second[:, C:].astype(F32)
+        both = dot(last[:, :C], third[...])
+        state = dot3(split(both[:, :C]), split(state)) + (both[:, C:] + last[:, C:].astype(F32))
         out_ref[...] = state.astype(BF16)
 
     by_place(refs[:-1], work)

time: 43.7 us -> 43.9 us (level)
  no operation moved by 1% of the time
where the time goes in v20:
time: 43.9 us; the launch traced here: 43.7 us
  Pallas kernels  20 us (46%)
  starting transfers between devices  15.8 us (36%)
  waiting for transfers between devices  7.67 us (17%)
    ppermute x14, starting transfers between devices, swap(): return lax.ppermute(x, axis, [(i, i ^ bit) for i in range(count)])  15.8 us
    ppermute x14, waiting for transfers between devices, swap(): return lax.ppermute(x, axis, [(i, i ^ bit) for i in range(count)])  7.67 us
    pallas_call x1, Pallas kernels, first_maps(): pl.pallas_call(functools.partial(first_kernel, heads), in_specs=[pl.Block...  5.86 us
    pallas_call x4, Pallas kernels, row_maps(): pl.pallas_call(functools.partial(rows_kernel, heads, spot, slot), in_spec...  3.98 us
    pallas_call x4, Pallas kernels, add_part(): pl.pallas_call(add_kernel, grid=(1,), in_specs=[here, here] + [pl.BlockSp...  2.72 us
    pallas_call x8, Pallas kernels, project(): pl.pallas_call(functools.partial(project_kernel, start), out_shape=jax.Sh...  2.47 us
    pallas_call x1, Pallas kernels, own_maps(): pl.pallas_call(functools.partial(own_kernel, heads), in_specs=[here] * 4,...  2.4 us
    pallas_call x3, Pallas kernels, small_call(): pl.pallas_call(kernel, in_specs=[here] * len(args), out_specs=[here] * le...  1.95 us
  transfers between devices with their start and end apart: 14, of which 8 were waited for; matrix products, arithmetic and copies ran while one was open for 0% of the time, Pallas kernels for 44%

profile of v20, /device:TPU:0, one launch (start us, length us, event | category | flops | bytes accessed | tf_op | source)
XLA Modules:
  0.0 43.7 jit_solution(3172673038517865401)
XLA Ops:
  0.5 5.9 %first_maps.1 = (bf16[2048,128]{1,0:T(8,128)(2,1)S(1)}, f32[2048,128]{1,0:T(8,128)S(1)}, f32[2048,128]{1,0:T(8,128)S(1)}, f32[16,128]{1,0:T(8,128)S(1)}, f32[16,...) custom-call(bf16[2048,128]{1,0:T(8,128)(2,1)} %bitcast.3, ...), custom_call_target="tpu_custom_call" | custom-call | tf_op jit(solution)/shard_map/first_maps/pallas_call | solution.py:256
  6.3 3.6 %collective-permute-start = (bf16[128,256]{1,0:T(8,128)(2,1)S(1)}, bf16[128,256]{1,0:T(8,128)(2,1)S(1)}, u32[]{:S(2)}, u32[]{:S(2)}) collective-permute-start(bf16[128,256]{1,0:T(8,128)(2,1)S(1)} %get-tuple-element.52), channel_id=1, source_target_pairs={{0,12},{4,8},{8,4},{12,0},{16,28},{20,24},{24,20},{28,16},{1,13},{... | collective-permute-start | bytes 196616 | tf_op jit(solution)/shard_map/ppermute | solution.py:501
  10.5 2.4 %own_maps.1 = (f32[4,128,128]{2,1,0:T(8,128)S(1)}, f32[4,128,256]{2,1,0:T(8,128)S(1)}, f32[4,128,256]{2,1,0:T(8,128)S(1)}, bf16[128,256]{1,0:T(8,128)(2,1)S(1)}) custom-call(f32[2048,128]{1,0:T(8,128)S(1)} %get-tuple-element.46.k32, f32[2048,128]{1,0:T(8,128)S(1)} %get-tuple-element.55.v32, f32[16,128]{1,0:T(8,128)S(1)} %get-tuple-element.47.sums_ref, ...), custom_call_target="tpu_custom_call" | custom-call | flops 2000000000 | bytes 8000000 | tf_op jit(solution)/shard_map/own_maps/pallas_call | solution.py:282
  12.9 1.0 %row_maps.4 = (f32[512,256]{1,0:T(8,128)S(1)}, f32[2048,128]{1,0:T(8,128)S(1)}) custom-call(bf16[2048,128]{1,0:T(8,128)(2,1)S(1)} %get-tuple-element.45.q_ref, f32[2048,128]{1,0:T(8,128)S(1)} %get-tuple-element.46.k32, f32[16,128]{1,0:T(8,128)S(1)} %get-tuple-element.47.sums_ref, f32[12,128,128]{2,1,0:T(8,128)S(1)} %get-tuple-element.48.mix_ref, ...), custom_call_target="tpu_custom_call" | custom-call | flops 1000000000 | bytes 4000000 | tf_op jit(solution)/shard_map/row_maps/pallas_call | solution.py:323
  15.0 2.7 %collective-permute-start.3 = (bf16[128,128]{1,0:T(8,128)(2,1)S(1)}, bf16[128,128]{1,0:T(8,128)(2,1)S(1)}, u32[]{:S(2)}, u32[]{:S(2)}) collective-permute-start(bf16[128,128]{1,0:T(8,128)(2,1)S(1)} %group_state.1), channel_id=1, source_target_pairs={{0,16},{4,20},{8,24},{12,28},{16,0},{20,4},{24,8},{28,12},{1,17},{... | collective-permute-start | bytes 98312 | tf_op jit(solution)/shard_map/ppermute | solution.py:501
  17.6 1.0 %row_maps.5.refs_1_ = f32[512,256]{1,0:T(8,128)S(1)} custom-call(f32[2048,128]{1,0:T(8,128)S(1)} %get-tuple-element.73.q_ref, f32[2048,128]{1,0:T(8,128)S(1)} %get-tuple-element.46.k32, f32[16,128]{1,0:T(8,128)S(1)} %get-tuple-element.47.sums_ref, f32[12,128,128]{2,1,0:T(8,128)S(1)} %get-tuple-element.48.mix_ref, ...), custom_call_target="tpu_custom_call" | custom-call | flops 1000000000 | bytes 4000000 | tf_op jit(solution)/shard_map/row_maps/pallas_call | solution.py:323
  18.6 1.4 %group_prefix.1 = (bf16[4,128,256]{2,1,0:T(8,128)(2,1)S(1)}, f32[4,128,128]{2,1,0:T(8,128)S(1)}, bf16[128,256]{1,0:T(8,128)(2,1)}) custom-call(bf16[128,256]{1,0:T(8,128)(2,1)S(1)} %collective-permute-done.refs_0_, bf16[128,256]{1,0:T(8,128)(2,1)S(1)} %collective-permute-done.1.refs_1_, bf16[128,256]{1,0:T(8,128)(2,1)S(1)} %collective-permute-done.2.refs_2_, ...), custom_call_target="tpu_custom_call" | custom-call | tf_op jit(solution)/shard_map/group_prefix/pallas_call | solution.py:336
  20.2 2.3 %collective-permute-start.4 = (bf16[128,128]{1,0:T(8,128)(2,1)S(1)}, bf16[128,128]{1,0:T(8,128)(2,1)S(1)}, u32[]{:S(2)}, u32[]{:S(2)}) collective-permute-start(bf16[128,128]{1,0:T(8,128)(2,1)S(1)} %get-tuple-element.77), channel_id=1, source_target_pairs={{0,12},{4,8},{8,4},{12,0},{16,28},{20,24},{24,20},{28,16},{1,13},{... | collective-permute-start | bytes 98312 | tf_op jit(solution)/shard_map/ppermute | solution.py:501
  23.0 0.8 %collective-permute-start.6 = (bf16[128,128]{1,0:T(8,128)(2,1)S(1)}, bf16[128,128]{1,0:T(8,128)(2,1)S(1)}, u32[]{:S(2)}, u32[]{:S(2)}) collective-permute-start(bf16[128,128]{1,0:T(8,128)(2,1)S(1)} %get-tuple-element.79), channel_id=1, source_target_pairs={{0,4},{4,0},{8,12},{12,8},{16,20},{20,16},{24,28},{28,24},{1,5},{5... | collective-permute-start | bytes 98312 | tf_op jit(solution)/shard_map/ppermute | solution.py:501
  23.8 1.0 %row_maps.6.refs_2_ = f32[512,256]{1,0:T(8,128)S(1)} custom-call(f32[2048,128]{1,0:T(8,128)S(1)} %get-tuple-element.73.q_ref, f32[2048,128]{1,0:T(8,128)S(1)} %get-tuple-element.46.k32, f32[16,128]{1,0:T(8,128)S(1)} %get-tuple-element.47.sums_ref, f32[12,128,128]{2,1,0:T(8,128)S(1)} %get-tuple-element.48.mix_ref, ...), custom_call_target="tpu_custom_call" | custom-call | flops 1000000000 | bytes 4000000 | tf_op jit(solution)/shard_map/row_maps/pallas_call | solution.py:323
  24.8 1.0 %row_maps.7.refs_3_ = f32[512,256]{1,0:T(8,128)S(1)} custom-call(f32[2048,128]{1,0:T(8,128)S(1)} %get-tuple-element.73.q_ref, f32[2048,128]{1,0:T(8,128)S(1)} %get-tuple-element.46.k32, f32[16,128]{1,0:T(8,128)S(1)} %get-tuple-element.47.sums_ref, f32[4,128,128]{2,1,0:T(8,128)S(1)} %get-tuple-element.74.mix_ref, ...), custom_call_target="tpu_custom_call" | custom-call | flops 1000000000 | bytes 4000000 | tf_op jit(solution)/shard_map/row_maps/pallas_call | solution.py:323
  25.8 0.7 %collective-permute-done.5.refs_5_ = bf16[128,128]{1,0:T(8,128)(2,1)S(1)} collective-permute-done((bf16[128,128]{1,0:T(8,128)(2,1)S(1)}, bf16[128,128]{1,0:T(8,128)(2,1)S(1)}, u32[]{:S(2)}, u32[]{:S(2)}) %collective-permute-start.5) | collective-permute-done | bytes 32800 | tf_op jit(solution)/shard_map/ppermute | solution.py:501
  27.6 0.6 %collective-permute-start.7 = (bf16[128,512]{1,0:T(8,128)(2,1)S(1)}, bf16[128,512]{1,0:T(8,128)(2,1)S(1)}, u32[]{:S(2)}, u32[]{:S(2)}) collective-permute-start(bf16[128,512]{1,0:T(8,128)(2,1)S(1)} %get-tuple-element.82), channel_id=1, source_target_pairs={{0,1},{1,0},{2,3},{3,2},{4,5},{5,4},{6,7},{7,6},{8,9},{9,8},{10,11... | collective-permute-start | bytes 393224 | tf_op jit(solution)/shard_map/ppermute | solution.py:501
  29.0 1.6 %collective-permute-start.13 = (bf16[128,512]{1,0:T(8,128)(2,1)S(1)}, bf16[128,512]{1,0:T(8,128)(2,1)S(1)}, u32[]{:S(2)}, u32[]{:S(2)}) collective-permute-start(bf16[128,512]{1,0:T(8,128)(2,1)S(1)} %project.15), channel_id=1, source_target_pairs={{0,2},{1,3},{2,0},{3,1},{4,6},{5,7},{6,4},{7,5},{8,10},{9,11},{10,... | collective-permute-start | bytes 393224 | tf_op jit(solution)/shard_map/ppermute | solution.py:501
  30.9 0.6 %collective-permute-start.12 = (bf16[128,512]{1,0:T(8,128)(2,1)S(1)}, bf16[128,512]{1,0:T(8,128)(2,1)S(1)}, u32[]{:S(2)}, u32[]{:S(2)}) collective-permute-start(bf16[128,512]{1,0:T(8,128)(2,1)S(1)} %project.13), channel_id=1, source_target_pairs={{0,2},{1,3},{2,0},{3,1},{4,6},{5,7},{6,4},{7,5},{8,10},{9,11},{10,... | collective-permute-start | bytes 393224 | tf_op jit(solution)/shard_map/ppermute | solution.py:501
  31.7 1.6 %collective-permute-start.11 = (bf16[128,512]{1,0:T(8,128)(2,1)S(1)}, bf16[128,512]{1,0:T(8,128)(2,1)S(1)}, u32[]{:S(2)}, u32[]{:S(2)}) collective-permute-start(bf16[128,512]{1,0:T(8,128)(2,1)S(1)} %project.11), channel_id=1, source_target_pairs={{0,2},{1,3},{2,0},{3,1},{4,6},{5,7},{6,4},{7,5},{8,10},{9,11},{10,... | collective-permute-start | bytes 393224 | tf_op jit(solution)/shard_map/ppermute | solution.py:501
  33.6 0.6 %collective-permute-start.10 = (bf16[128,512]{1,0:T(8,128)(2,1)S(1)}, bf16[128,512]{1,0:T(8,128)(2,1)S(1)}, u32[]{:S(2)}, u32[]{:S(2)}) collective-permute-start(bf16[128,512]{1,0:T(8,128)(2,1)S(1)} %project.9), channel_id=1, source_target_pairs={{0,2},{1,3},{2,0},{3,1},{4,6},{5,7},{6,4},{7,5},{8,10},{9,11},{10,... | collective-permute-start | bytes 393224 | tf_op jit(solution)/shard_map/ppermute | solution.py:501
  35.5 0.7 %add_part.4.refs_0_ = bf16[128,2048]{1,0:T(8,128)(2,1)} custom-call(f32[128,512]{1,0:T(8,128)S(1)} %project.14.mine_ref, bf16[128,512]{1,0:T(8,128)(2,1)S(1)} %collective-permute-done.13.theirs_ref), custom_call_target="tpu_custom_call" | custom-call | tf_op jit(solution)/shard_map/add_part/pallas_call | solution.py:487
  36.2 2.0 %collective-permute-done.12.theirs_ref = bf16[128,512]{1,0:T(8,128)(2,1)S(1)} collective-permute-done((bf16[128,512]{1,0:T(8,128)(2,1)S(1)}, bf16[128,512]{1,0:T(8,128)(2,1)S(1)}, u32[]{:S(2)}, u32[]{:S(2)}) %collective-permute-start.12) | collective-permute-done | bytes 131104 | tf_op jit(solution)/shard_map/ppermute | solution.py:501
  38.2 0.7 %add_part.5.refs_0_ = bf16[128,2048]{1,0:T(8,128)(2,1)} custom-call(f32[128,512]{1,0:T(8,128)S(1)} %project.12.mine_ref, bf16[128,512]{1,0:T(8,128)(2,1)S(1)} %collective-permute-done.12.theirs_ref, bf16[128,2048]{1,0:T(8,128)(2,1)} %add_part.4.refs_0_), custom_call_target="tpu_custom_call", output_to_operand_aliasing={{}: (2, {})} | custom-call | tf_op jit(solution)/shard_map/add_part/pallas_call | solution.py:487
  38.8 2.1 %collective-permute-done.11.theirs_ref = bf16[128,512]{1,0:T(8,128)(2,1)S(1)} collective-permute-done((bf16[128,512]{1,0:T(8,128)(2,1)S(1)}, bf16[128,512]{1,0:T(8,128)(2,1)S(1)}, u32[]{:S(2)}, u32[]{:S(2)}) %collective-permute-start.11) | collective-permute-done | bytes 131104 | tf_op jit(solution)/shard_map/ppermute | solution.py:501
  41.0 0.7 %add_part.6.refs_0_ = bf16[128,2048]{1,0:T(8,128)(2,1)} custom-call(f32[128,512]{1,0:T(8,128)S(1)} %project.10.mine_ref, bf16[128,512]{1,0:T(8,128)(2,1)S(1)} %collective-permute-done.11.theirs_ref, bf16[128,2048]{1,0:T(8,128)(2,1)} %add_part.5.refs_0_), custom_call_target="tpu_custom_call", output_to_operand_aliasing={{}: (2, {})} | custom-call | tf_op jit(solution)/shard_map/add_part/pallas_call | solution.py:487
  41.7 1.3 %collective-permute-done.10.theirs_ref = bf16[128,512]{1,0:T(8,128)(2,1)S(1)} collective-permute-done((bf16[128,512]{1,0:T(8,128)(2,1)S(1)}, bf16[128,512]{1,0:T(8,128)(2,1)S(1)}, u32[]{:S(2)}, u32[]{:S(2)}) %collective-permute-start.10) | collective-permute-done | bytes 131104 | tf_op jit(solution)/shard_map/ppermute | solution.py:501
  43.0 0.7 %add_part.7 = bf16[128,2048]{1,0:T(8,128)(2,1)} custom-call(f32[128,512]{1,0:T(8,128)S(1)} %project.8.mine_ref, bf16[128,512]{1,0:T(8,128)(2,1)S(1)} %collective-permute-done.10.theirs_ref, bf16[128,2048]{1,0:T(8,128)(2,1)} %add_part.6.refs_0_), custom_call_target="tpu_custom_call", output_to_operand_aliasing={{}: (2, {})} | custom-call | tf_op jit(solution)/shard_map/add_part/pallas_call | solution.py:487
  (29 shorter events, 6.8 us)
Async XLA Ops:
  0.0 28.6 %collective-permute-start.8 = (bf16[512,2048]{1,0:T(8,128)(2,1)}, bf16[512,2048]{1,0:T(8,128)(2,1)S(1)}, u32[]{:S(2)}, u32[]{:S(2)}) collective-permute-start(bf16[512,2048]{1,0:T(8,128)(2,1)} %w_ref.15), channel_id=1, source_target_pairs={{0,1},{1,0},{2,3},{3,2},{4,5},{5,4},{6,7},{7,6},{8,9},{9,8},{10,11... | collective-permute-start | bytes 6291464 | tf_op jit(solution)/shard_map/ppermute | solution.py:501
  6.3 7.7 %collective-permute-start = (bf16[128,256]{1,0:T(8,128)(2,1)S(1)}, bf16[128,256]{1,0:T(8,128)(2,1)S(1)}, u32[]{:S(2)}, u32[]{:S(2)}) collective-permute-start(bf16[128,256]{1,0:T(8,128)(2,1)S(1)} %get-tuple-element.52), channel_id=1, source_target_pairs={{0,12},{4,8},{8,4},{12,0},{16,28},{20,24},{24,20},{28,16},{1,13},{... | collective-permute-start | bytes 196616 | tf_op jit(solution)/shard_map/ppermute | solution.py:501
  9.9 4.3 %collective-permute-start.1 = (bf16[128,256]{1,0:T(8,128)(2,1)S(1)}, bf16[128,256]{1,0:T(8,128)(2,1)S(1)}, u32[]{:S(2)}, u32[]{:S(2)}) collective-permute-start(bf16[128,256]{1,0:T(8,128)(2,1)S(1)} %get-tuple-element.53), channel_id=1, source_target_pairs={{0,8},{4,12},{8,0},{12,4},{16,24},{20,28},{24,16},{28,20},{1,9},{5... | collective-permute-start | bytes 196616 | tf_op jit(solution)/shard_map/ppermute | solution.py:501
  10.3 4.3 %collective-permute-start.2 = (bf16[128,256]{1,0:T(8,128)(2,1)S(1)}, bf16[128,256]{1,0:T(8,128)(2,1)S(1)}, u32[]{:S(2)}, u32[]{:S(2)}) collective-permute-start(bf16[128,256]{1,0:T(8,128)(2,1)S(1)} %get-tuple-element.54), channel_id=1, source_target_pairs={{0,4},{4,0},{8,12},{12,8},{16,20},{20,16},{24,28},{28,24},{1,5},{5... | collective-permute-start | bytes 196616 | tf_op jit(solution)/shard_map/ppermute | solution.py:501
  15.0 5.0 %collective-permute-start.3 = (bf16[128,128]{1,0:T(8,128)(2,1)S(1)}, bf16[128,128]{1,0:T(8,128)(2,1)S(1)}, u32[]{:S(2)}, u32[]{:S(2)}) collective-permute-start(bf16[128,128]{1,0:T(8,128)(2,1)S(1)} %group_state.1), channel_id=1, source_target_pairs={{0,16},{4,20},{8,24},{12,28},{16,0},{20,4},{24,8},{28,12},{1,17},{... | collective-permute-start | bytes 98312 | tf_op jit(solution)/shard_map/ppermute | solution.py:501
  20.2 5.6 %collective-permute-start.4 = (bf16[128,128]{1,0:T(8,128)(2,1)S(1)}, bf16[128,128]{1,0:T(8,128)(2,1)S(1)}, u32[]{:S(2)}, u32[]{:S(2)}) collective-permute-start(bf16[128,128]{1,0:T(8,128)(2,1)S(1)} %get-tuple-element.77), channel_id=1, source_target_pairs={{0,12},{4,8},{8,4},{12,0},{16,28},{20,24},{24,20},{28,16},{1,13},{... | collective-permute-start | bytes 98312 | tf_op jit(solution)/shard_map/ppermute | solution.py:501
  22.5 3.9 %collective-permute-start.5 = (bf16[128,128]{1,0:T(8,128)(2,1)S(1)}, bf16[128,128]{1,0:T(8,128)(2,1)S(1)}, u32[]{:S(2)}, u32[]{:S(2)}) collective-permute-start(bf16[128,128]{1,0:T(8,128)(2,1)S(1)} %get-tuple-element.78), channel_id=1, source_target_pairs={{0,8},{4,12},{8,0},{12,4},{16,24},{20,28},{24,16},{28,20},{1,9},{5... | collective-permute-start | bytes 98312 | tf_op jit(solution)/shard_map/ppermute | solution.py:501
  23.0 3.9 %collective-permute-start.6 = (bf16[128,128]{1,0:T(8,128)(2,1)S(1)}, bf16[128,128]{1,0:T(8,128)(2,1)S(1)}, u32[]{:S(2)}, u32[]{:S(2)}) collective-permute-start(bf16[128,128]{1,0:T(8,128)(2,1)S(1)} %get-tuple-element.79), channel_id=1, source_target_pairs={{0,4},{4,0},{8,12},{12,8},{16,20},{20,16},{24,28},{28,24},{1,5},{5... | collective-permute-start | bytes 98312 | tf_op jit(solution)/shard_map/ppermute | solution.py:501
  25.8 2.9 %copy-start = (bf16[512,2048]{1,0:T(8,128)(2,1)S(1)}, bf16[512,2048]{1,0:T(8,128)(2,1)}, u32[]{:S(2)}) copy-start(bf16[512,2048]{1,0:T(8,128)(2,1)} %w_ref.15) | copy-start | bytes 6291460
  27.2 1.4 %collective-permute-start.9 = (bf16[128,512]{1,0:T(8,128)(2,1)S(1)}, bf16[128,512]{1,0:T(8,128)(2,1)S(1)}, u32[]{:S(2)}, u32[]{:S(2)}) collective-permute-start(bf16[128,512]{1,0:T(8,128)(2,1)S(1)} %get-tuple-element.84), channel_id=1, source_target_pairs={{0,1},{1,0},{2,3},{3,2},{4,5},{5,4},{6,7},{7,6},{8,9},{9,8},{10,11... | collective-permute-start | bytes 393224 | tf_op jit(solution)/shard_map/ppermute | solution.py:501
  27.6 6.6 %collective-permute-start.7 = (bf16[128,512]{1,0:T(8,128)(2,1)S(1)}, bf16[128,512]{1,0:T(8,128)(2,1)S(1)}, u32[]{:S(2)}, u32[]{:S(2)}) collective-permute-start(bf16[128,512]{1,0:T(8,128)(2,1)S(1)} %get-tuple-element.82), channel_id=1, source_target_pairs={{0,1},{1,0},{2,3},{3,2},{4,5},{5,4},{6,7},{7,6},{8,9},{9,8},{10,11... | collective-permute-start | bytes 393224 | tf_op jit(solution)/shard_map/ppermute | solution.py:501
  29.0 6.5 %collective-permute-start.13 = (bf16[128,512]{1,0:T(8,128)(2,1)S(1)}, bf16[128,512]{1,0:T(8,128)(2,1)S(1)}, u32[]{:S(2)}, u32[]{:S(2)}) collective-permute-start(bf16[128,512]{1,0:T(8,128)(2,1)S(1)} %project.15), channel_id=1, source_target_pairs={{0,2},{1,3},{2,0},{3,1},{4,6},{5,7},{6,4},{7,5},{8,10},{9,11},{10,... | collective-permute-start | bytes 393224 | tf_op jit(solution)/shard_map/ppermute | solution.py:501
  30.9 7.3 %collective-permute-start.12 = (bf16[128,512]{1,0:T(8,128)(2,1)S(1)}, bf16[128,512]{1,0:T(8,128)(2,1)S(1)}, u32[]{:S(2)}, u32[]{:S(2)}) collective-permute-start(bf16[128,512]{1,0:T(8,128)(2,1)S(1)} %project.13), channel_id=1, source_target_pairs={{0,2},{1,3},{2,0},{3,1},{4,6},{5,7},{6,4},{7,5},{8,10},{9,11},{10,... | collective-permute-start | bytes 393224 | tf_op jit(solution)/shard_map/ppermute | solution.py:501
  31.7 9.2 %collective-permute-start.11 = (bf16[128,512]{1,0:T(8,128)(2,1)S(1)}, bf16[128,512]{1,0:T(8,128)(2,1)S(1)}, u32[]{:S(2)}, u32[]{:S(2)}) collective-permute-start(bf16[128,512]{1,0:T(8,128)(2,1)S(1)} %project.11), channel_id=1, source_target_pairs={{0,2},{1,3},{2,0},{3,1},{4,6},{5,7},{6,4},{7,5},{8,10},{9,11},{10,... | collective-permute-start | bytes 393224 | tf_op jit(solution)/shard_map/ppermute | solution.py:501
  33.6 9.3 %collective-permute-start.10 = (bf16[128,512]{1,0:T(8,128)(2,1)S(1)}, bf16[128,512]{1,0:T(8,128)(2,1)S(1)}, u32[]{:S(2)}, u32[]{:S(2)}) collective-permute-start(bf16[128,512]{1,0:T(8,128)(2,1)S(1)} %project.9), channel_id=1, source_target_pairs={{0,2},{1,3},{2,0},{3,1},{4,6},{5,7},{6,4},{7,5},{8,10},{9,11},{10,... | collective-permute-start | bytes 393224 | tf_op jit(solution)/shard_map/ppermute | solution.py:501

commit v21 on v18

--- a/solution.py
+++ b/solution.py
@@ -357,9 +357,10 @@
     out_ref = refs[-1]
 
     def work(parts, _):
-        state = parts[0][:, C:].astype(F32)
-        for part in parts[1:]:
-            state = times_parts(part[:, :C], state) + part[:, C:].astype(F32)
+        first, second, third, last = parts
+        state = dot(second[:, :C], first[:, C:]) + second[:, C:].astype(F32)
+        both = dot(last[:, :C], third[...])
+        state = dot3(split(both[:, :C]), split(state)) + (both[:, C:] + last[:, C:].astype(F32))
         out_ref[...] = state.astype(BF16)
 
     by_place(refs[:-1], work)

time: 43.7 us -> 43.6 us (level)
  no operation moved by 1% of the time
where the time goes in v21:
time: 43.6 us; the launch traced here: 43.3 us
  Pallas kernels  19.6 us (45%)
  starting transfers between devices  15.8 us (36%)
  waiting for transfers between devices  7.68 us (18%)
    ppermute x14, starting transfers between devices, swap(): return lax.ppermute(x, axis, [(i, i ^ bit) for i in range(count)])  15.8 us
    ppermute x14, waiting for transfers between devices, swap(): return lax.ppermute(x, axis, [(i, i ^ bit) for i in range(count)])  7.68 us
    pallas_call x1, Pallas kernels, first_maps(): pl.pallas_call(functools.partial(first_kernel, heads), in_specs=[pl.Block...  5.52 us
    pallas_call x4, Pallas kernels, row_maps(): pl.pallas_call(functools.partial(rows_kernel, heads, spot, slot), in_spec...  3.98 us
    pallas_call x4, Pallas kernels, add_part(): pl.pallas_call(add_kernel, grid=(1,), in_specs=[here, here] + [pl.BlockSp...  2.72 us
    pallas_call x8, Pallas kernels, project(): pl.pallas_call(functools.partial(project_kernel, start), out_shape=jax.Sh...  2.47 us
    pallas_call x1, Pallas kernels, own_maps(): pl.pallas_call(functools.partial(own_kernel, heads), in_specs=[here] * 4,...  2.39 us
    pallas_call x3, Pallas kernels, small_call(): pl.pallas_call(kernel, in_specs=[here] * len(args), out_specs=[here] * le...  1.96 us
  transfers between devices with their start and end apart: 14, of which 8 were waited for; matrix products, arithmetic and copies ran while one was open for 0% of the time, Pallas kernels for 44%

profile of v21, /device:TPU:0, one launch (start us, length us, event | category | flops | bytes accessed | tf_op | source)
XLA Modules:
  0.0 43.3 jit_solution(10225264042268480891)
XLA Ops:
  0.5 5.5 %first_maps.1 = (bf16[2048,128]{1,0:T(8,128)(2,1)S(1)}, f32[2048,128]{1,0:T(8,128)S(1)}, f32[2048,128]{1,0:T(8,128)S(1)}, f32[16,128]{1,0:T(8,128)S(1)}, f32[16,...) custom-call(bf16[2048,128]{1,0:T(8,128)(2,1)} %bitcast.3, ...), custom_call_target="tpu_custom_call" | custom-call | tf_op jit(solution)/shard_map/first_maps/pallas_call | solution.py:244
  6.0 3.6 %collective-permute-start = (bf16[128,256]{1,0:T(8,128)(2,1)S(1)}, bf16[128,256]{1,0:T(8,128)(2,1)S(1)}, u32[]{:S(2)}, u32[]{:S(2)}) collective-permute-start(bf16[128,256]{1,0:T(8,128)(2,1)S(1)} %get-tuple-element.52), channel_id=1, source_target_pairs={{0,12},{4,8},{8,4},{12,0},{16,28},{20,24},{24,20},{28,16},{1,13},{... | collective-permute-start | bytes 196616 | tf_op jit(solution)/shard_map/ppermute | solution.py:489
  10.2 2.4 %own_maps.1 = (f32[4,128,128]{2,1,0:T(8,128)S(1)}, f32[4,128,256]{2,1,0:T(8,128)S(1)}, f32[4,128,256]{2,1,0:T(8,128)S(1)}, bf16[128,256]{1,0:T(8,128)(2,1)S(1)}) custom-call(f32[2048,128]{1,0:T(8,128)S(1)} %get-tuple-element.46.k32, f32[2048,128]{1,0:T(8,128)S(1)} %get-tuple-element.55.v32, f32[16,128]{1,0:T(8,128)S(1)} %get-tuple-element.47.sums_ref, ...), custom_call_target="tpu_custom_call" | custom-call | flops 2000000000 | bytes 8000000 | tf_op jit(solution)/shard_map/own_maps/pallas_call | solution.py:270
  12.6 1.0 %row_maps.4 = (f32[512,256]{1,0:T(8,128)S(1)}, f32[2048,128]{1,0:T(8,128)S(1)}) custom-call(bf16[2048,128]{1,0:T(8,128)(2,1)S(1)} %get-tuple-element.45.q_ref, f32[2048,128]{1,0:T(8,128)S(1)} %get-tuple-element.46.k32, f32[16,128]{1,0:T(8,128)S(1)} %get-tuple-element.47.sums_ref, f32[12,128,128]{2,1,0:T(8,128)S(1)} %get-tuple-element.48.mix_ref, ...), custom_call_target="tpu_custom_call" | custom-call | flops 1000000000 | bytes 4000000 | tf_op jit(solution)/shard_map/row_maps/pallas_call | solution.py:311
  14.6 2.7 %collective-permute-start.3 = (bf16[128,128]{1,0:T(8,128)(2,1)S(1)}, bf16[128,128]{1,0:T(8,128)(2,1)S(1)}, u32[]{:S(2)}, u32[]{:S(2)}) collective-permute-start(bf16[128,128]{1,0:T(8,128)(2,1)S(1)} %group_state.1), channel_id=1, source_target_pairs={{0,16},{4,20},{8,24},{12,28},{16,0},{20,4},{24,8},{28,12},{1,17},{... | collective-permute-start | bytes 98312 | tf_op jit(solution)/shard_map/ppermute | solution.py:489
  17.3 1.0 %row_maps.5.refs_1_ = f32[512,256]{1,0:T(8,128)S(1)} custom-call(f32[2048,128]{1,0:T(8,128)S(1)} %get-tuple-element.73.q_ref, f32[2048,128]{1,0:T(8,128)S(1)} %get-tuple-element.46.k32, f32[16,128]{1,0:T(8,128)S(1)} %get-tuple-element.47.sums_ref, f32[12,128,128]{2,1,0:T(8,128)S(1)} %get-tuple-element.48.mix_ref, ...), custom_call_target="tpu_custom_call" | custom-call | flops 1000000000 | bytes 4000000 | tf_op jit(solution)/shard_map/row_maps/pallas_call | solution.py:311
  18.3 1.4 %group_prefix.1 = (bf16[4,128,256]{2,1,0:T(8,128)(2,1)S(1)}, f32[4,128,128]{2,1,0:T(8,128)S(1)}, bf16[128,256]{1,0:T(8,128)(2,1)}) custom-call(bf16[128,256]{1,0:T(8,128)(2,1)S(1)} %collective-permute-done.refs_0_, bf16[128,256]{1,0:T(8,128)(2,1)S(1)} %collective-permute-done.1.refs_1_, bf16[128,256]{1,0:T(8,128)(2,1)S(1)} %collective-permute-done.2.refs_2_, ...), custom_call_target="tpu_custom_call" | custom-call | tf_op jit(solution)/shard_map/group_prefix/pallas_call | solution.py:324
  19.9 2.3 %collective-permute-start.4 = (bf16[128,128]{1,0:T(8,128)(2,1)S(1)}, bf16[128,128]{1,0:T(8,128)(2,1)S(1)}, u32[]{:S(2)}, u32[]{:S(2)}) collective-permute-start(bf16[128,128]{1,0:T(8,128)(2,1)S(1)} %get-tuple-element.77), channel_id=1, source_target_pairs={{0,12},{4,8},{8,4},{12,0},{16,28},{20,24},{24,20},{28,16},{1,13},{... | collective-permute-start | bytes 98312 | tf_op jit(solution)/shard_map/ppermute | solution.py:489
  22.7 0.8 %collective-permute-start.6 = (bf16[128,128]{1,0:T(8,128)(2,1)S(1)}, bf16[128,128]{1,0:T(8,128)(2,1)S(1)}, u32[]{:S(2)}, u32[]{:S(2)}) collective-permute-start(bf16[128,128]{1,0:T(8,128)(2,1)S(1)} %get-tuple-element.79), channel_id=1, source_target_pairs={{0,4},{4,0},{8,12},{12,8},{16,20},{20,16},{24,28},{28,24},{1,5},{5... | collective-permute-start | bytes 98312 | tf_op jit(solution)/shard_map/ppermute | solution.py:489
  23.5 1.0 %row_maps.6.refs_2_ = f32[512,256]{1,0:T(8,128)S(1)} custom-call(f32[2048,128]{1,0:T(8,128)S(1)} %get-tuple-element.73.q_ref, f32[2048,128]{1,0:T(8,128)S(1)} %get-tuple-element.46.k32, f32[16,128]{1,0:T(8,128)S(1)} %get-tuple-element.47.sums_ref, f32[12,128,128]{2,1,0:T(8,128)S(1)} %get-tuple-element.48.mix_ref, ...), custom_call_target="tpu_custom_call" | custom-call | flops 1000000000 | bytes 4000000 | tf_op jit(solution)/shard_map/row_maps/pallas_call | solution.py:311
  24.4 1.0 %row_maps.7.refs_3_ = f32[512,256]{1,0:T(8,128)S(1)} custom-call(f32[2048,128]{1,0:T(8,128)S(1)} %get-tuple-element.73.q_ref, f32[2048,128]{1,0:T(8,128)S(1)} %get-tuple-element.46.k32, f32[16,128]{1,0:T(8,128)S(1)} %get-tuple-element.47.sums_ref, f32[4,128,128]{2,1,0:T(8,128)S(1)} %get-tuple-element.74.mix_ref, ...), custom_call_target="tpu_custom_call" | custom-call | flops 1000000000 | bytes 4000000 | tf_op jit(solution)/shard_map/row_maps/pallas_call | solution.py:311
  25.5 0.7 %collective-permute-done.5.refs_5_ = bf16[128,128]{1,0:T(8,128)(2,1)S(1)} collective-permute-done((bf16[128,128]{1,0:T(8,128)(2,1)S(1)}, bf16[128,128]{1,0:T(8,128)(2,1)S(1)}, u32[]{:S(2)}, u32[]{:S(2)}) %collective-permute-start.5) | collective-permute-done | bytes 32800 | tf_op jit(solution)/shard_map/ppermute | solution.py:489
  27.3 0.6 %collective-permute-start.7 = (bf16[128,512]{1,0:T(8,128)(2,1)S(1)}, bf16[128,512]{1,0:T(8,128)(2,1)S(1)}, u32[]{:S(2)}, u32[]{:S(2)}) collective-permute-start(bf16[128,512]{1,0:T(8,128)(2,1)S(1)} %get-tuple-element.82), channel_id=1, source_target_pairs={{0,1},{1,0},{2,3},{3,2},{4,5},{5,4},{6,7},{7,6},{8,9},{9,8},{10,11... | collective-permute-start | bytes 393224 | tf_op jit(solution)/shard_map/ppermute | solution.py:489
  28.6 1.6 %collective-permute-start.13 = (bf16[128,512]{1,0:T(8,128)(2,1)S(1)}, bf16[128,512]{1,0:T(8,128)(2,1)S(1)}, u32[]{:S(2)}, u32[]{:S(2)}) collective-permute-start(bf16[128,512]{1,0:T(8,128)(2,1)S(1)} %project.15), channel_id=1, source_target_pairs={{0,2},{1,3},{2,0},{3,1},{4,6},{5,7},{6,4},{7,5},{8,10},{9,11},{10,... | collective-permute-start | bytes 393224 | tf_op jit(solution)/shard_map/ppermute | solution.py:489
  30.5 0.6 %collective-permute-start.12 = (bf16[128,512]{1,0:T(8,128)(2,1)S(1)}, bf16[128,512]{1,0:T(8,128)(2,1)S(1)}, u32[]{:S(2)}, u32[]{:S(2)}) collective-permute-start(bf16[128,512]{1,0:T(8,128)(2,1)S(1)} %project.13), channel_id=1, source_target_pairs={{0,2},{1,3},{2,0},{3,1},{4,6},{5,7},{6,4},{7,5},{8,10},{9,11},{10,... | collective-permute-start | bytes 393224 | tf_op jit(solution)/shard_map/ppermute | solution.py:489
  31.4 1.6 %collective-permute-start.11 = (bf16[128,512]{1,0:T(8,128)(2,1)S(1)}, bf16[128,512]{1,0:T(8,128)(2,1)S(1)}, u32[]{:S(2)}, u32[]{:S(2)}) collective-permute-start(bf16[128,512]{1,0:T(8,128)(2,1)S(1)} %project.11), channel_id=1, source_target_pairs={{0,2},{1,3},{2,0},{3,1},{4,6},{5,7},{6,4},{7,5},{8,10},{9,11},{10,... | collective-permute-start | bytes 393224 | tf_op jit(solution)/shard_map/ppermute | solution.py:489
  33.3 0.6 %collective-permute-start.10 = (bf16[128,512]{1,0:T(8,128)(2,1)S(1)}, bf16[128,512]{1,0:T(8,128)(2,1)S(1)}, u32[]{:S(2)}, u32[]{:S(2)}) collective-permute-start(bf16[128,512]{1,0:T(8,128)(2,1)S(1)} %project.9), channel_id=1, source_target_pairs={{0,2},{1,3},{2,0},{3,1},{4,6},{5,7},{6,4},{7,5},{8,10},{9,11},{10,... | collective-permute-start | bytes 393224 | tf_op jit(solution)/shard_map/ppermute | solution.py:489
  35.2 0.7 %add_part.4.refs_0_ = bf16[128,2048]{1,0:T(8,128)(2,1)} custom-call(f32[128,512]{1,0:T(8,128)S(1)} %project.14.mine_ref, bf16[128,512]{1,0:T(8,128)(2,1)S(1)} %collective-permute-done.13.theirs_ref), custom_call_target="tpu_custom_call" | custom-call | tf_op jit(solution)/shard_map/add_part/pallas_call | solution.py:475
  35.8 2.0 %collective-permute-done.12.theirs_ref = bf16[128,512]{1,0:T(8,128)(2,1)S(1)} collective-permute-done((bf16[128,512]{1,0:T(8,128)(2,1)S(1)}, bf16[128,512]{1,0:T(8,128)(2,1)S(1)}, u32[]{:S(2)}, u32[]{:S(2)}) %collective-permute-start.12) | collective-permute-done | bytes 131104 | tf_op jit(solution)/shard_map/ppermute | solution.py:489
  37.8 0.7 %add_part.5.refs_0_ = bf16[128,2048]{1,0:T(8,128)(2,1)} custom-call(f32[128,512]{1,0:T(8,128)S(1)} %project.12.mine_ref, bf16[128,512]{1,0:T(8,128)(2,1)S(1)} %collective-permute-done.12.theirs_ref, bf16[128,2048]{1,0:T(8,128)(2,1)} %add_part.4.refs_0_), custom_call_target="tpu_custom_call", output_to_operand_aliasing={{}: (2, {})} | custom-call | tf_op jit(solution)/shard_map/add_part/pallas_call | solution.py:475
  38.5 2.1 %collective-permute-done.11.theirs_ref = bf16[128,512]{1,0:T(8,128)(2,1)S(1)} collective-permute-done((bf16[128,512]{1,0:T(8,128)(2,1)S(1)}, bf16[128,512]{1,0:T(8,128)(2,1)S(1)}, u32[]{:S(2)}, u32[]{:S(2)}) %collective-permute-start.11) | collective-permute-done | bytes 131104 | tf_op jit(solution)/shard_map/ppermute | solution.py:489
  40.6 0.7 %add_part.6.refs_0_ = bf16[128,2048]{1,0:T(8,128)(2,1)} custom-call(f32[128,512]{1,0:T(8,128)S(1)} %project.10.mine_ref, bf16[128,512]{1,0:T(8,128)(2,1)S(1)} %collective-permute-done.11.theirs_ref, bf16[128,2048]{1,0:T(8,128)(2,1)} %add_part.5.refs_0_), custom_call_target="tpu_custom_call", output_to_operand_aliasing={{}: (2, {})} | custom-call | tf_op jit(solution)/shard_map/add_part/pallas_call | solution.py:475
  41.3 1.3 %collective-permute-done.10.theirs_ref = bf16[128,512]{1,0:T(8,128)(2,1)S(1)} collective-permute-done((bf16[128,512]{1,0:T(8,128)(2,1)S(1)}, bf16[128,512]{1,0:T(8,128)(2,1)S(1)}, u32[]{:S(2)}, u32[]{:S(2)}) %collective-permute-start.10) | collective-permute-done | bytes 131104 | tf_op jit(solution)/shard_map/ppermute | solution.py:489
  42.7 0.7 %add_part.7 = bf16[128,2048]{1,0:T(8,128)(2,1)} custom-call(f32[128,512]{1,0:T(8,128)S(1)} %project.8.mine_ref, bf16[128,512]{1,0:T(8,128)(2,1)S(1)} %collective-permute-done.10.theirs_ref, bf16[128,2048]{1,0:T(8,128)(2,1)} %add_part.6.refs_0_), custom_call_target="tpu_custom_call", output_to_operand_aliasing={{}: (2, {})} | custom-call | tf_op jit(solution)/shard_map/add_part/pallas_call | solution.py:475
  (29 shorter events, 6.8 us)
Async XLA Ops:
  0.0 28.3 %collective-permute-start.8 = (bf16[512,2048]{1,0:T(8,128)(2,1)}, bf16[512,2048]{1,0:T(8,128)(2,1)S(1)}, u32[]{:S(2)}, u32[]{:S(2)}) collective-permute-start(bf16[512,2048]{1,0:T(8,128)(2,1)} %w_ref.15), channel_id=1, source_target_pairs={{0,1},{1,0},{2,3},{3,2},{4,5},{5,4},{6,7},{7,6},{8,9},{9,8},{10,11... | collective-permute-start | bytes 6291464 | tf_op jit(solution)/shard_map/ppermute | solution.py:489
  6.0 7.6 %collective-permute-start = (bf16[128,256]{1,0:T(8,128)(2,1)S(1)}, bf16[128,256]{1,0:T(8,128)(2,1)S(1)}, u32[]{:S(2)}, u32[]{:S(2)}) collective-permute-start(bf16[128,256]{1,0:T(8,128)(2,1)S(1)} %get-tuple-element.52), channel_id=1, source_target_pairs={{0,12},{4,8},{8,4},{12,0},{16,28},{20,24},{24,20},{28,16},{1,13},{... | collective-permute-start | bytes 196616 | tf_op jit(solution)/shard_map/ppermute | solution.py:489
  9.6 4.3 %collective-permute-start.1 = (bf16[128,256]{1,0:T(8,128)(2,1)S(1)}, bf16[128,256]{1,0:T(8,128)(2,1)S(1)}, u32[]{:S(2)}, u32[]{:S(2)}) collective-permute-start(bf16[128,256]{1,0:T(8,128)(2,1)S(1)} %get-tuple-element.53), channel_id=1, source_target_pairs={{0,8},{4,12},{8,0},{12,4},{16,24},{20,28},{24,16},{28,20},{1,9},{5... | collective-permute-start | bytes 196616 | tf_op jit(solution)/shard_map/ppermute | solution.py:489
  10.0 4.3 %collective-permute-start.2 = (bf16[128,256]{1,0:T(8,128)(2,1)S(1)}, bf16[128,256]{1,0:T(8,128)(2,1)S(1)}, u32[]{:S(2)}, u32[]{:S(2)}) collective-permute-start(bf16[128,256]{1,0:T(8,128)(2,1)S(1)} %get-tuple-element.54), channel_id=1, source_target_pairs={{0,4},{4,0},{8,12},{12,8},{16,20},{20,16},{24,28},{28,24},{1,5},{5... | collective-permute-start | bytes 196616 | tf_op jit(solution)/shard_map/ppermute | solution.py:489
  14.6 5.0 %collective-permute-start.3 = (bf16[128,128]{1,0:T(8,128)(2,1)S(1)}, bf16[128,128]{1,0:T(8,128)(2,1)S(1)}, u32[]{:S(2)}, u32[]{:S(2)}) collective-permute-start(bf16[128,128]{1,0:T(8,128)(2,1)S(1)} %group_state.1), channel_id=1, source_target_pairs={{0,16},{4,20},{8,24},{12,28},{16,0},{20,4},{24,8},{28,12},{1,17},{... | collective-permute-start | bytes 98312 | tf_op jit(solution)/shard_map/ppermute | solution.py:489
  19.9 5.6 %collective-permute-start.4 = (bf16[128,128]{1,0:T(8,128)(2,1)S(1)}, bf16[128,128]{1,0:T(8,128)(2,1)S(1)}, u32[]{:S(2)}, u32[]{:S(2)}) collective-permute-start(bf16[128,128]{1,0:T(8,128)(2,1)S(1)} %get-tuple-element.77), channel_id=1, source_target_pairs={{0,12},{4,8},{8,4},{12,0},{16,28},{20,24},{24,20},{28,16},{1,13},{... | collective-permute-start | bytes 98312 | tf_op jit(solution)/shard_map/ppermute | solution.py:489
  22.2 3.9 %collective-permute-start.5 = (bf16[128,128]{1,0:T(8,128)(2,1)S(1)}, bf16[128,128]{1,0:T(8,128)(2,1)S(1)}, u32[]{:S(2)}, u32[]{:S(2)}) collective-permute-start(bf16[128,128]{1,0:T(8,128)(2,1)S(1)} %get-tuple-element.78), channel_id=1, source_target_pairs={{0,8},{4,12},{8,0},{12,4},{16,24},{20,28},{24,16},{28,20},{1,9},{5... | collective-permute-start | bytes 98312 | tf_op jit(solution)/shard_map/ppermute | solution.py:489
  22.7 3.9 %collective-permute-start.6 = (bf16[128,128]{1,0:T(8,128)(2,1)S(1)}, bf16[128,128]{1,0:T(8,128)(2,1)S(1)}, u32[]{:S(2)}, u32[]{:S(2)}) collective-permute-start(bf16[128,128]{1,0:T(8,128)(2,1)S(1)} %get-tuple-element.79), channel_id=1, source_target_pairs={{0,4},{4,0},{8,12},{12,8},{16,20},{20,16},{24,28},{28,24},{1,5},{5... | collective-permute-start | bytes 98312 | tf_op jit(solution)/shard_map/ppermute | solution.py:489
  25.4 2.9 %copy-start = (bf16[512,2048]{1,0:T(8,128)(2,1)S(1)}, bf16[512,2048]{1,0:T(8,128)(2,1)}, u32[]{:S(2)}) copy-start(bf16[512,2048]{1,0:T(8,128)(2,1)} %w_ref.15) | copy-start | bytes 6291460
  26.9 1.4 %collective-permute-start.9 = (bf16[128,512]{1,0:T(8,128)(2,1)S(1)}, bf16[128,512]{1,0:T(8,128)(2,1)S(1)}, u32[]{:S(2)}, u32[]{:S(2)}) collective-permute-start(bf16[128,512]{1,0:T(8,128)(2,1)S(1)} %get-tuple-element.84), channel_id=1, source_target_pairs={{0,1},{1,0},{2,3},{3,2},{4,5},{5,4},{6,7},{7,6},{8,9},{9,8},{10,11... | collective-permute-start | bytes 393224 | tf_op jit(solution)/shard_map/ppermute | solution.py:489
  27.3 6.6 %collective-permute-start.7 = (bf16[128,512]{1,0:T(8,128)(2,1)S(1)}, bf16[128,512]{1,0:T(8,128)(2,1)S(1)}, u32[]{:S(2)}, u32[]{:S(2)}) collective-permute-start(bf16[128,512]{1,0:T(8,128)(2,1)S(1)} %get-tuple-element.82), channel_id=1, source_target_pairs={{0,1},{1,0},{2,3},{3,2},{4,5},{5,4},{6,7},{7,6},{8,9},{9,8},{10,11... | collective-permute-start | bytes 393224 | tf_op jit(solution)/shard_map/ppermute | solution.py:489
  28.6 6.5 %collective-permute-start.13 = (bf16[128,512]{1,0:T(8,128)(2,1)S(1)}, bf16[128,512]{1,0:T(8,128)(2,1)S(1)}, u32[]{:S(2)}, u32[]{:S(2)}) collective-permute-start(bf16[128,512]{1,0:T(8,128)(2,1)S(1)} %project.15), channel_id=1, source_target_pairs={{0,2},{1,3},{2,0},{3,1},{4,6},{5,7},{6,4},{7,5},{8,10},{9,11},{10,... | collective-permute-start | bytes 393224 | tf_op jit(solution)/shard_map/ppermute | solution.py:489
  30.5 7.3 %collective-permute-start.12 = (bf16[128,512]{1,0:T(8,128)(2,1)S(1)}, bf16[128,512]{1,0:T(8,128)(2,1)S(1)}, u32[]{:S(2)}, u32[]{:S(2)}) collective-permute-start(bf16[128,512]{1,0:T(8,128)(2,1)S(1)} %project.13), channel_id=1, source_target_pairs={{0,2},{1,3},{2,0},{3,1},{4,6},{5,7},{6,4},{7,5},{8,10},{9,11},{10,... | collective-permute-start | bytes 393224 | tf_op jit(solution)/shard_map/ppermute | solution.py:489
  31.4 9.2 %collective-permute-start.11 = (bf16[128,512]{1,0:T(8,128)(2,1)S(1)}, bf16[128,512]{1,0:T(8,128)(2,1)S(1)}, u32[]{:S(2)}, u32[]{:S(2)}) collective-permute-start(bf16[128,512]{1,0:T(8,128)(2,1)S(1)} %project.11), channel_id=1, source_target_pairs={{0,2},{1,3},{2,0},{3,1},{4,6},{5,7},{6,4},{7,5},{8,10},{9,11},{10,... | collective-permute-start | bytes 393224 | tf_op jit(solution)/shard_map/ppermute | solution.py:489
  33.3 9.3 %collective-permute-start.10 = (bf16[128,512]{1,0:T(8,128)(2,1)S(1)}, bf16[128,512]{1,0:T(8,128)(2,1)S(1)}, u32[]{:S(2)}, u32[]{:S(2)}) collective-permute-start(bf16[128,512]{1,0:T(8,128)(2,1)S(1)} %project.9), channel_id=1, source_target_pairs={{0,2},{1,3},{2,0},{3,1},{4,6},{5,7},{6,4},{7,5},{8,10},{9,11},{10,... | collective-permute-start | bytes 393224 | tf_op jit(solution)/shard_map/ppermute | solution.py:489

commit v22 on v21

--- a/solution.py
+++ b/solution.py
@@ -508,16 +508,15 @@
     both = jax.ShapeDtypeStruct((heads, C, 2 * C), BF16)
     added = jax.ShapeDtypeStruct((heads, C, C), F32)
     (state,) = small_call(group_state, [square], *parts)
-    state, q32 = lax.optimization_barrier((state, q32))
-    (rows2,) = row_maps(heads, 1, 1, q32, *first)
     *maps, total = small_call(group_prefix, [both, added, jax.ShapeDtypeStruct((C, 2 * C), BF16)], *parts)
     if count == 2 * heads:
         lower = swap(state, "seq", heads)
-        rows2, maps, lower = lax.optimization_barrier((rows2, maps, lower))
+        maps, lower = lax.optimization_barrier((maps, lower))
         keep, *sends = small_call(states_of_upper, [square] * heads, *maps, lower)
     else:
         keep, *sends = small_call(states_given, [square] * heads, *maps, prefix(total, heads))
     keep, q32 = lax.optimization_barrier((keep, q32))
+    (rows2,) = row_maps(heads, 1, 1, q32, *first)
     (rows1,) = row_maps(heads, 2, 2, q32, *first)
     (rows0,) = row_maps(heads, 3, 0, q32, *own_maps_here)
     entering = [swap(sends[r - 1], "seq", r) for r in away] + [keep]

time: 43.6 us -> 43.5 us (level)
  transfers between devices with their start and end apart: 14 -> 14, of which waited for: 8 -> 6; matrix products, arithmetic and copies ran while one was open for 0% -> 0% of each run, Pallas kernels for 44% -> 44%
where the time goes in v22:
time: 43.5 us; the launch traced here: 43.3 us
  Pallas kernels  19.6 us (45%)
  starting transfers between devices  15.8 us (36%)
  waiting for transfers between devices  7.63 us (18%)
    ppermute x14, starting transfers between devices, swap(): return lax.ppermute(x, axis, [(i, i ^ bit) for i in range(count)])  15.8 us
    ppermute x14, waiting for transfers between devices, swap(): return lax.ppermute(x, axis, [(i, i ^ bit) for i in range(count)])  7.63 us
    pallas_call x1, Pallas kernels, first_maps(): pl.pallas_call(functools.partial(first_kernel, heads), in_specs=[pl.Block...  5.52 us
    pallas_call x4, Pallas kernels, row_maps(): pl.pallas_call(functools.partial(rows_kernel, heads, spot, slot), in_spec...  3.99 us
    pallas_call x4, Pallas kernels, add_part(): pl.pallas_call(add_kernel, grid=(1,), in_specs=[here, here] + [pl.BlockSp...  2.72 us
    pallas_call x8, Pallas kernels, project(): pl.pallas_call(functools.partial(project_kernel, start), out_shape=jax.Sh...  2.47 us
    pallas_call x1, Pallas kernels, own_maps(): pl.pallas_call(functools.partial(own_kernel, heads), in_specs=[here] * 4,...  2.39 us
    pallas_call x3, Pallas kernels, small_call(): pl.pallas_call(kernel, in_specs=[here] * len(args), out_specs=[here] * le...  1.94 us
  transfers between devices with their start and end apart: 14, of which 6 were waited for; matrix products, arithmetic and copies ran while one was open for 0% of the time, Pallas kernels for 44%

profile of v22, /device:TPU:0, one launch (start us, length us, event | category | flops | bytes accessed | tf_op | source)
XLA Modules:
  0.0 43.3 jit_solution(2406401918785034223)
XLA Ops:
  0.5 5.5 %first_maps.1 = (bf16[2048,128]{1,0:T(8,128)(2,1)S(1)}, f32[2048,128]{1,0:T(8,128)S(1)}, f32[2048,128]{1,0:T(8,128)S(1)}, f32[16,128]{1,0:T(8,128)S(1)}, f32[16,...) custom-call(bf16[2048,128]{1,0:T(8,128)(2,1)} %bitcast.3, ...), custom_call_target="tpu_custom_call" | custom-call | tf_op jit(solution)/shard_map/first_maps/pallas_call | solution.py:244
  6.0 3.6 %collective-permute-start = (bf16[128,256]{1,0:T(8,128)(2,1)S(1)}, bf16[128,256]{1,0:T(8,128)(2,1)S(1)}, u32[]{:S(2)}, u32[]{:S(2)}) collective-permute-start(bf16[128,256]{1,0:T(8,128)(2,1)S(1)} %get-tuple-element.49), channel_id=1, source_target_pairs={{0,12},{4,8},{8,4},{12,0},{16,28},{20,24},{24,20},{28,16},{1,13},{... | collective-permute-start | bytes 196616 | tf_op jit(solution)/shard_map/ppermute | solution.py:489
  10.2 2.4 %own_maps.1 = (f32[4,128,128]{2,1,0:T(8,128)S(1)}, f32[4,128,256]{2,1,0:T(8,128)S(1)}, f32[4,128,256]{2,1,0:T(8,128)S(1)}, bf16[128,256]{1,0:T(8,128)(2,1)S(1)}) custom-call(f32[2048,128]{1,0:T(8,128)S(1)} %get-tuple-element.43.k32, f32[2048,128]{1,0:T(8,128)S(1)} %get-tuple-element.52.v32, f32[16,128]{1,0:T(8,128)S(1)} %get-tuple-element.44.sums_ref, ...), custom_call_target="tpu_custom_call" | custom-call | flops 2000000000 | bytes 8000000 | tf_op jit(solution)/shard_map/own_maps/pallas_call | solution.py:270
  12.6 1.0 %row_maps.4 = (f32[512,256]{1,0:T(8,128)S(1)}, f32[2048,128]{1,0:T(8,128)S(1)}) custom-call(bf16[2048,128]{1,0:T(8,128)(2,1)S(1)} %get-tuple-element.42.q_ref, f32[2048,128]{1,0:T(8,128)S(1)} %get-tuple-element.43.k32, f32[16,128]{1,0:T(8,128)S(1)} %get-tuple-element.44.sums_ref, f32[12,128,128]{2,1,0:T(8,128)S(1)} %get-tuple-element.45.mix_ref, ...), custom_call_target="tpu_custom_call" | custom-call | flops 1000000000 | bytes 4000000 | tf_op jit(solution)/shard_map/row_maps/pallas_call | solution.py:311
  14.6 2.7 %collective-permute-start.3 = (bf16[128,128]{1,0:T(8,128)(2,1)S(1)}, bf16[128,128]{1,0:T(8,128)(2,1)S(1)}, u32[]{:S(2)}, u32[]{:S(2)}) collective-permute-start(bf16[128,128]{1,0:T(8,128)(2,1)S(1)} %group_state.1), channel_id=1, source_target_pairs={{0,16},{4,20},{8,24},{12,28},{16,0},{20,4},{24,8},{28,12},{1,17},{... | collective-permute-start | bytes 98312 | tf_op jit(solution)/shard_map/ppermute | solution.py:489
  17.3 1.4 %group_prefix.1 = (bf16[4,128,256]{2,1,0:T(8,128)(2,1)S(1)}, f32[4,128,128]{2,1,0:T(8,128)S(1)}, bf16[128,256]{1,0:T(8,128)(2,1)}) custom-call(bf16[128,256]{1,0:T(8,128)(2,1)S(1)} %collective-permute-done.refs_0_, bf16[128,256]{1,0:T(8,128)(2,1)S(1)} %collective-permute-done.1.refs_1_, bf16[128,256]{1,0:T(8,128)(2,1)S(1)} %collective-permute-done.2.refs_2_, ...), custom_call_target="tpu_custom_call" | custom-call | tf_op jit(solution)/shard_map/group_prefix/pallas_call | solution.py:324
  18.7 0.8 %collective-permute-done.3.refs_2_ = bf16[128,128]{1,0:T(8,128)(2,1)S(1)} collective-permute-done((bf16[128,128]{1,0:T(8,128)(2,1)S(1)}, bf16[128,128]{1,0:T(8,128)(2,1)S(1)}, u32[]{:S(2)}, u32[]{:S(2)}) %collective-permute-start.3) | collective-permute-done | bytes 32800 | tf_op jit(solution)/shard_map/ppermute | solution.py:489
  19.7 2.3 %collective-permute-start.4 = (bf16[128,128]{1,0:T(8,128)(2,1)S(1)}, bf16[128,128]{1,0:T(8,128)(2,1)S(1)}, u32[]{:S(2)}, u32[]{:S(2)}) collective-permute-start(bf16[128,128]{1,0:T(8,128)(2,1)S(1)} %get-tuple-element.71), channel_id=1, source_target_pairs={{0,12},{4,8},{8,4},{12,0},{16,28},{20,24},{24,20},{28,16},{1,13},{... | collective-permute-start | bytes 98312 | tf_op jit(solution)/shard_map/ppermute | solution.py:489
  22.1 0.5 %collective-permute-start.5 = (bf16[128,128]{1,0:T(8,128)(2,1)S(1)}, bf16[128,128]{1,0:T(8,128)(2,1)S(1)}, u32[]{:S(2)}, u32[]{:S(2)}) collective-permute-start(bf16[128,128]{1,0:T(8,128)(2,1)S(1)} %get-tuple-element.72), channel_id=1, source_target_pairs={{0,8},{4,12},{8,0},{12,4},{16,24},{20,28},{24,16},{28,20},{1,9},{5... | collective-permute-start | bytes 98312 | tf_op jit(solution)/shard_map/ppermute | solution.py:489
  22.6 0.7 %collective-permute-start.6 = (bf16[128,128]{1,0:T(8,128)(2,1)S(1)}, bf16[128,128]{1,0:T(8,128)(2,1)S(1)}, u32[]{:S(2)}, u32[]{:S(2)}) collective-permute-start(bf16[128,128]{1,0:T(8,128)(2,1)S(1)} %get-tuple-element.73), channel_id=1, source_target_pairs={{0,4},{4,0},{8,12},{12,8},{16,20},{20,16},{24,28},{28,24},{1,5},{5... | collective-permute-start | bytes 98312 | tf_op jit(solution)/shard_map/ppermute | solution.py:489
  23.3 1.0 %row_maps.5.refs_1_ = f32[512,256]{1,0:T(8,128)S(1)} custom-call(f32[2048,128]{1,0:T(8,128)S(1)} %get-tuple-element.67.q_ref, f32[2048,128]{1,0:T(8,128)S(1)} %get-tuple-element.43.k32, f32[16,128]{1,0:T(8,128)S(1)} %get-tuple-element.44.sums_ref, f32[12,128,128]{2,1,0:T(8,128)S(1)} %get-tuple-element.45.mix_ref, ...), custom_call_target="tpu_custom_call" | custom-call | flops 1000000000 | bytes 4000000 | tf_op jit(solution)/shard_map/row_maps/pallas_call | solution.py:311
  24.3 1.0 %row_maps.6.refs_2_ = f32[512,256]{1,0:T(8,128)S(1)} custom-call(f32[2048,128]{1,0:T(8,128)S(1)} %get-tuple-element.67.q_ref, f32[2048,128]{1,0:T(8,128)S(1)} %get-tuple-element.43.k32, f32[16,128]{1,0:T(8,128)S(1)} %get-tuple-element.44.sums_ref, f32[12,128,128]{2,1,0:T(8,128)S(1)} %get-tuple-element.45.mix_ref, ...), custom_call_target="tpu_custom_call" | custom-call | flops 1000000000 | bytes 4000000 | tf_op jit(solution)/shard_map/row_maps/pallas_call | solution.py:311
  25.3 1.0 %row_maps.7.refs_3_ = f32[512,256]{1,0:T(8,128)S(1)} custom-call(f32[2048,128]{1,0:T(8,128)S(1)} %get-tuple-element.67.q_ref, f32[2048,128]{1,0:T(8,128)S(1)} %get-tuple-element.43.k32, f32[16,128]{1,0:T(8,128)S(1)} %get-tuple-element.44.sums_ref, f32[4,128,128]{2,1,0:T(8,128)S(1)} %get-tuple-element.68.mix_ref, ...), custom_call_target="tpu_custom_call" | custom-call | flops 1000000000 | bytes 4000000 | tf_op jit(solution)/shard_map/row_maps/pallas_call | solution.py:311
  27.2 0.6 %collective-permute-start.7 = (bf16[128,512]{1,0:T(8,128)(2,1)S(1)}, bf16[128,512]{1,0:T(8,128)(2,1)S(1)}, u32[]{:S(2)}, u32[]{:S(2)}) collective-permute-start(bf16[128,512]{1,0:T(8,128)(2,1)S(1)} %get-tuple-element.76), channel_id=1, source_target_pairs={{0,1},{1,0},{2,3},{3,2},{4,5},{5,4},{6,7},{7,6},{8,9},{9,8},{10,11... | collective-permute-start | bytes 393224 | tf_op jit(solution)/shard_map/ppermute | solution.py:489
  27.7 0.5 %collective-permute-done.9.got_ref = bf16[128,512]{1,0:T(8,128)(2,1)S(1)} collective-permute-done((bf16[128,512]{1,0:T(8,128)(2,1)S(1)}, bf16[128,512]{1,0:T(8,128)(2,1)S(1)}, u32[]{:S(2)}, u32[]{:S(2)}) %collective-permute-start.9) | collective-permute-done | bytes 131104 | tf_op jit(solution)/shard_map/ppermute | solution.py:489
  28.5 1.6 %collective-permute-start.11 = (bf16[128,512]{1,0:T(8,128)(2,1)S(1)}, bf16[128,512]{1,0:T(8,128)(2,1)S(1)}, u32[]{:S(2)}, u32[]{:S(2)}) collective-permute-start(bf16[128,512]{1,0:T(8,128)(2,1)S(1)} %project.11), channel_id=1, source_target_pairs={{0,2},{1,3},{2,0},{3,1},{4,6},{5,7},{6,4},{7,5},{8,10},{9,11},{10,... | collective-permute-start | bytes 393224 | tf_op jit(solution)/shard_map/ppermute | solution.py:489
  30.4 0.6 %collective-permute-start.12 = (bf16[128,512]{1,0:T(8,128)(2,1)S(1)}, bf16[128,512]{1,0:T(8,128)(2,1)S(1)}, u32[]{:S(2)}, u32[]{:S(2)}) collective-permute-start(bf16[128,512]{1,0:T(8,128)(2,1)S(1)} %project.13), channel_id=1, source_target_pairs={{0,2},{1,3},{2,0},{3,1},{4,6},{5,7},{6,4},{7,5},{8,10},{9,11},{10,... | collective-permute-start | bytes 393224 | tf_op jit(solution)/shard_map/ppermute | solution.py:489
  31.3 1.6 %collective-permute-start.13 = (bf16[128,512]{1,0:T(8,128)(2,1)S(1)}, bf16[128,512]{1,0:T(8,128)(2,1)S(1)}, u32[]{:S(2)}, u32[]{:S(2)}) collective-permute-start(bf16[128,512]{1,0:T(8,128)(2,1)S(1)} %project.15), channel_id=1, source_target_pairs={{0,2},{1,3},{2,0},{3,1},{4,6},{5,7},{6,4},{7,5},{8,10},{9,11},{10,... | collective-permute-start | bytes 393224 | tf_op jit(solution)/shard_map/ppermute | solution.py:489
  33.2 0.6 %collective-permute-start.10 = (bf16[128,512]{1,0:T(8,128)(2,1)S(1)}, bf16[128,512]{1,0:T(8,128)(2,1)S(1)}, u32[]{:S(2)}, u32[]{:S(2)}) collective-permute-start(bf16[128,512]{1,0:T(8,128)(2,1)S(1)} %project.9), channel_id=1, source_target_pairs={{0,2},{1,3},{2,0},{3,1},{4,6},{5,7},{6,4},{7,5},{8,10},{9,11},{10,... | collective-permute-start | bytes 393224 | tf_op jit(solution)/shard_map/ppermute | solution.py:489
  35.1 5.5 %collective-permute-done.13.theirs_ref = bf16[128,512]{1,0:T(8,128)(2,1)S(1)} collective-permute-done((bf16[128,512]{1,0:T(8,128)(2,1)S(1)}, bf16[128,512]{1,0:T(8,128)(2,1)S(1)}, u32[]{:S(2)}, u32[]{:S(2)}) %collective-permute-start.13) | collective-permute-done | bytes 131104 | tf_op jit(solution)/shard_map/ppermute | solution.py:489
  40.6 0.7 %add_part.4.refs_0_ = bf16[128,2048]{1,0:T(8,128)(2,1)} custom-call(f32[128,512]{1,0:T(8,128)S(1)} %project.14.mine_ref, bf16[128,512]{1,0:T(8,128)(2,1)S(1)} %collective-permute-done.13.theirs_ref), custom_call_target="tpu_custom_call" | custom-call | tf_op jit(solution)/shard_map/add_part/pallas_call | solution.py:475
  41.2 0.7 %add_part.5.refs_0_ = bf16[128,2048]{1,0:T(8,128)(2,1)} custom-call(f32[128,512]{1,0:T(8,128)S(1)} %project.12.mine_ref, bf16[128,512]{1,0:T(8,128)(2,1)S(1)} %collective-permute-done.12.theirs_ref, bf16[128,2048]{1,0:T(8,128)(2,1)} %add_part.4.refs_0_), custom_call_target="tpu_custom_call", output_to_operand_aliasing={{}: (2, {})} | custom-call | tf_op jit(solution)/shard_map/add_part/pallas_call | solution.py:475
  41.9 0.7 %add_part.6.refs_0_ = bf16[128,2048]{1,0:T(8,128)(2,1)} custom-call(f32[128,512]{1,0:T(8,128)S(1)} %project.10.mine_ref, bf16[128,512]{1,0:T(8,128)(2,1)S(1)} %collective-permute-done.11.theirs_ref, bf16[128,2048]{1,0:T(8,128)(2,1)} %add_part.5.refs_0_), custom_call_target="tpu_custom_call", output_to_operand_aliasing={{}: (2, {})} | custom-call | tf_op jit(solution)/shard_map/add_part/pallas_call | solution.py:475
  42.6 0.7 %add_part.7 = bf16[128,2048]{1,0:T(8,128)(2,1)} custom-call(f32[128,512]{1,0:T(8,128)S(1)} %project.8.mine_ref, bf16[128,512]{1,0:T(8,128)(2,1)S(1)} %collective-permute-done.10.theirs_ref, bf16[128,2048]{1,0:T(8,128)(2,1)} %add_part.6.refs_0_), custom_call_target="tpu_custom_call", output_to_operand_aliasing={{}: (2, {})} | custom-call | tf_op jit(solution)/shard_map/add_part/pallas_call | solution.py:475
  (29 shorter events, 5.6 us)
Async XLA Ops:
  0.0 28.2 %collective-permute-start.8 = (bf16[512,2048]{1,0:T(8,128)(2,1)}, bf16[512,2048]{1,0:T(8,128)(2,1)S(1)}, u32[]{:S(2)}, u32[]{:S(2)}) collective-permute-start(bf16[512,2048]{1,0:T(8,128)(2,1)} %w_ref.15), channel_id=1, source_target_pairs={{0,1},{1,0},{2,3},{3,2},{4,5},{5,4},{6,7},{7,6},{8,9},{9,8},{10,11... | collective-permute-start | bytes 6291464 | tf_op jit(solution)/shard_map/ppermute | solution.py:489
  6.0 7.6 %collective-permute-start = (bf16[128,256]{1,0:T(8,128)(2,1)S(1)}, bf16[128,256]{1,0:T(8,128)(2,1)S(1)}, u32[]{:S(2)}, u32[]{:S(2)}) collective-permute-start(bf16[128,256]{1,0:T(8,128)(2,1)S(1)} %get-tuple-element.49), channel_id=1, source_target_pairs={{0,12},{4,8},{8,4},{12,0},{16,28},{20,24},{24,20},{28,16},{1,13},{... | collective-permute-start | bytes 196616 | tf_op jit(solution)/shard_map/ppermute | solution.py:489
  9.6 4.3 %collective-permute-start.1 = (bf16[128,256]{1,0:T(8,128)(2,1)S(1)}, bf16[128,256]{1,0:T(8,128)(2,1)S(1)}, u32[]{:S(2)}, u32[]{:S(2)}) collective-permute-start(bf16[128,256]{1,0:T(8,128)(2,1)S(1)} %get-tuple-element.50), channel_id=1, source_target_pairs={{0,8},{4,12},{8,0},{12,4},{16,24},{20,28},{24,16},{28,20},{1,9},{5... | collective-permute-start | bytes 196616 | tf_op jit(solution)/shard_map/ppermute | solution.py:489
  10.0 4.3 %collective-permute-start.2 = (bf16[128,256]{1,0:T(8,128)(2,1)S(1)}, bf16[128,256]{1,0:T(8,128)(2,1)S(1)}, u32[]{:S(2)}, u32[]{:S(2)}) collective-permute-start(bf16[128,256]{1,0:T(8,128)(2,1)S(1)} %get-tuple-element.51), channel_id=1, source_target_pairs={{0,4},{4,0},{8,12},{12,8},{16,20},{20,16},{24,28},{28,24},{1,5},{5... | collective-permute-start | bytes 196616 | tf_op jit(solution)/shard_map/ppermute | solution.py:489
  14.6 4.9 %collective-permute-start.3 = (bf16[128,128]{1,0:T(8,128)(2,1)S(1)}, bf16[128,128]{1,0:T(8,128)(2,1)S(1)}, u32[]{:S(2)}, u32[]{:S(2)}) collective-permute-start(bf16[128,128]{1,0:T(8,128)(2,1)S(1)} %group_state.1), channel_id=1, source_target_pairs={{0,16},{4,20},{8,24},{12,28},{16,0},{20,4},{24,8},{28,12},{1,17},{... | collective-permute-start | bytes 98312 | tf_op jit(solution)/shard_map/ppermute | solution.py:489
  19.7 6.6 %collective-permute-start.4 = (bf16[128,128]{1,0:T(8,128)(2,1)S(1)}, bf16[128,128]{1,0:T(8,128)(2,1)S(1)}, u32[]{:S(2)}, u32[]{:S(2)}) collective-permute-start(bf16[128,128]{1,0:T(8,128)(2,1)S(1)} %get-tuple-element.71), channel_id=1, source_target_pairs={{0,12},{4,8},{8,4},{12,0},{16,28},{20,24},{24,20},{28,16},{1,13},{... | collective-permute-start | bytes 98312 | tf_op jit(solution)/shard_map/ppermute | solution.py:489
  22.1 4.2 %collective-permute-start.5 = (bf16[128,128]{1,0:T(8,128)(2,1)S(1)}, bf16[128,128]{1,0:T(8,128)(2,1)S(1)}, u32[]{:S(2)}, u32[]{:S(2)}) collective-permute-start(bf16[128,128]{1,0:T(8,128)(2,1)S(1)} %get-tuple-element.72), channel_id=1, source_target_pairs={{0,8},{4,12},{8,0},{12,4},{16,24},{20,28},{24,16},{28,20},{1,9},{5... | collective-permute-start | bytes 98312 | tf_op jit(solution)/shard_map/ppermute | solution.py:489
  22.6 3.9 %collective-permute-start.6 = (bf16[128,128]{1,0:T(8,128)(2,1)S(1)}, bf16[128,128]{1,0:T(8,128)(2,1)S(1)}, u32[]{:S(2)}, u32[]{:S(2)}) collective-permute-start(bf16[128,128]{1,0:T(8,128)(2,1)S(1)} %get-tuple-element.73), channel_id=1, source_target_pairs={{0,4},{4,0},{8,12},{12,8},{16,20},{20,16},{24,28},{28,24},{1,5},{5... | collective-permute-start | bytes 98312 | tf_op jit(solution)/shard_map/ppermute | solution.py:489
  26.3 1.9 %copy-start = (bf16[512,2048]{1,0:T(8,128)(2,1)S(1)}, bf16[512,2048]{1,0:T(8,128)(2,1)}, u32[]{:S(2)}) copy-start(bf16[512,2048]{1,0:T(8,128)(2,1)} %w_ref.15) | copy-start | bytes 6291460
  26.8 1.4 %collective-permute-start.9 = (bf16[128,512]{1,0:T(8,128)(2,1)S(1)}, bf16[128,512]{1,0:T(8,128)(2,1)S(1)}, u32[]{:S(2)}, u32[]{:S(2)}) collective-permute-start(bf16[128,512]{1,0:T(8,128)(2,1)S(1)} %get-tuple-element.78), channel_id=1, source_target_pairs={{0,1},{1,0},{2,3},{3,2},{4,5},{5,4},{6,7},{7,6},{8,9},{9,8},{10,11... | collective-permute-start | bytes 393224 | tf_op jit(solution)/shard_map/ppermute | solution.py:489
  27.2 6.6 %collective-permute-start.7 = (bf16[128,512]{1,0:T(8,128)(2,1)S(1)}, bf16[128,512]{1,0:T(8,128)(2,1)S(1)}, u32[]{:S(2)}, u32[]{:S(2)}) collective-permute-start(bf16[128,512]{1,0:T(8,128)(2,1)S(1)} %get-tuple-element.76), channel_id=1, source_target_pairs={{0,1},{1,0},{2,3},{3,2},{4,5},{5,4},{6,7},{7,6},{8,9},{9,8},{10,11... | collective-permute-start | bytes 393224 | tf_op jit(solution)/shard_map/ppermute | solution.py:489
  28.5 13.4 %collective-permute-start.11 = (bf16[128,512]{1,0:T(8,128)(2,1)S(1)}, bf16[128,512]{1,0:T(8,128)(2,1)S(1)}, u32[]{:S(2)}, u32[]{:S(2)}) collective-permute-start(bf16[128,512]{1,0:T(8,128)(2,1)S(1)} %project.11), channel_id=1, source_target_pairs={{0,2},{1,3},{2,0},{3,1},{4,6},{5,7},{6,4},{7,5},{8,10},{9,11},{10,... | collective-permute-start | bytes 393224 | tf_op jit(solution)/shard_map/ppermute | solution.py:489
  30.4 10.8 %collective-permute-start.12 = (bf16[128,512]{1,0:T(8,128)(2,1)S(1)}, bf16[128,512]{1,0:T(8,128)(2,1)S(1)}, u32[]{:S(2)}, u32[]{:S(2)}) collective-permute-start(bf16[128,512]{1,0:T(8,128)(2,1)S(1)} %project.13), channel_id=1, source_target_pairs={{0,2},{1,3},{2,0},{3,1},{4,6},{5,7},{6,4},{7,5},{8,10},{9,11},{10,... | collective-permute-start | bytes 393224 | tf_op jit(solution)/shard_map/ppermute | solution.py:489
  31.3 9.2 %collective-permute-start.13 = (bf16[128,512]{1,0:T(8,128)(2,1)S(1)}, bf16[128,512]{1,0:T(8,128)(2,1)S(1)}, u32[]{:S(2)}, u32[]{:S(2)}) collective-permute-start(bf16[128,512]{1,0:T(8,128)(2,1)S(1)} %project.15), channel_id=1, source_target_pairs={{0,2},{1,3},{2,0},{3,1},{4,6},{5,7},{6,4},{7,5},{8,10},{9,11},{10,... | collective-permute-start | bytes 393224 | tf_op jit(solution)/shard_map/ppermute | solution.py:489
  33.2 9.4 %collective-permute-start.10 = (bf16[128,512]{1,0:T(8,128)(2,1)S(1)}, bf16[128,512]{1,0:T(8,128)(2,1)S(1)}, u32[]{:S(2)}, u32[]{:S(2)}) collective-permute-start(bf16[128,512]{1,0:T(8,128)(2,1)S(1)} %project.9), channel_id=1, source_target_pairs={{0,2},{1,3},{2,0},{3,1},{4,6},{5,7},{6,4},{7,5},{8,10},{9,11},{10,... | collective-permute-start | bytes 393224 | tf_op jit(solution)/shard_map/ppermute | solution.py:489

commit v23 on v21

--- a/solution.py
+++ b/solution.py
@@ -35,9 +35,8 @@
     width = bh.shape[1]
     if width > C:
         return dot(jnp.concatenate([ah, al], axis=1), twice(bh)) + dot(ah, bl)
-    rows = ah.shape[0]
-    both = dot(jnp.concatenate([ah, al], axis=0), jnp.concatenate([bh, bl], axis=1))
-    return both[:rows, :width] + (both[:rows, width:] + both[rows:, :width])
+    both = dot(jnp.concatenate([ah, al], axis=1), twice(jnp.concatenate([bh, bl], axis=1)))
+    return both[:, :width] + both[:, width:]
 
 
 def iotas():

time: 43.6 us -> 43.7 us (level)
  no operation moved by 1% of the time
where the time goes in v23:
time: 43.7 us; the launch traced here: 43.5 us
  Pallas kernels  19.8 us (45%)
  starting transfers between devices  15.8 us (36%)
  waiting for transfers between devices  7.67 us (18%)
    ppermute x14, starting transfers between devices, swap(): return lax.ppermute(x, axis, [(i, i ^ bit) for i in range(count)])  15.8 us
    ppermute x14, waiting for transfers between devices, swap(): return lax.ppermute(x, axis, [(i, i ^ bit) for i in range(count)])  7.67 us
    pallas_call x1, Pallas kernels, first_maps(): pl.pallas_call(functools.partial(first_kernel, heads), in_specs=[pl.Block...  5.7 us
    pallas_call x4, Pallas kernels, row_maps(): pl.pallas_call(functools.partial(rows_kernel, heads, spot, slot), in_spec...  3.98 us
    pallas_call x4, Pallas kernels, add_part(): pl.pallas_call(add_kernel, grid=(1,), in_specs=[here, here] + [pl.BlockSp...  2.72 us
    pallas_call x8, Pallas kernels, project(): pl.pallas_call(functools.partial(project_kernel, start), out_shape=jax.Sh...  2.47 us
    pallas_call x1, Pallas kernels, own_maps(): pl.pallas_call(functools.partial(own_kernel, heads), in_specs=[here] * 4,...  2.39 us
    pallas_call x3, Pallas kernels, small_call(): pl.pallas_call(kernel, in_specs=[here] * len(args), out_specs=[here] * le...  1.94 us
  transfers between devices with their start and end apart: 14, of which 8 were waited for; matrix products, arithmetic and copies ran while one was open for 0% of the time, Pallas kernels for 44%

profile of v23, /device:TPU:0, one launch (start us, length us, event | category | flops | bytes accessed | tf_op | source)
XLA Modules:
  0.0 43.5 jit_solution(18170677287491480871)
XLA Ops:
  0.5 5.7 %first_maps.1 = (bf16[2048,128]{1,0:T(8,128)(2,1)S(1)}, f32[2048,128]{1,0:T(8,128)S(1)}, f32[2048,128]{1,0:T(8,128)S(1)}, f32[16,128]{1,0:T(8,128)S(1)}, f32[16,...) custom-call(bf16[2048,128]{1,0:T(8,128)(2,1)} %bitcast.3, ...), custom_call_target="tpu_custom_call" | custom-call | tf_op jit(solution)/shard_map/first_maps/pallas_call | solution.py:243
  6.2 3.6 %collective-permute-start = (bf16[128,256]{1,0:T(8,128)(2,1)S(1)}, bf16[128,256]{1,0:T(8,128)(2,1)S(1)}, u32[]{:S(2)}, u32[]{:S(2)}) collective-permute-start(bf16[128,256]{1,0:T(8,128)(2,1)S(1)} %get-tuple-element.52), channel_id=1, source_target_pairs={{0,12},{4,8},{8,4},{12,0},{16,28},{20,24},{24,20},{28,16},{1,13},{... | collective-permute-start | bytes 196616 | tf_op jit(solution)/shard_map/ppermute | solution.py:488
  10.4 2.4 %own_maps.1 = (f32[4,128,128]{2,1,0:T(8,128)S(1)}, f32[4,128,256]{2,1,0:T(8,128)S(1)}, f32[4,128,256]{2,1,0:T(8,128)S(1)}, bf16[128,256]{1,0:T(8,128)(2,1)S(1)}) custom-call(f32[2048,128]{1,0:T(8,128)S(1)} %get-tuple-element.46.k32, f32[2048,128]{1,0:T(8,128)S(1)} %get-tuple-element.55.v32, f32[16,128]{1,0:T(8,128)S(1)} %get-tuple-element.47.sums_ref, ...), custom_call_target="tpu_custom_call" | custom-call | flops 2000000000 | bytes 8000000 | tf_op jit(solution)/shard_map/own_maps/pallas_call | solution.py:269
  12.8 1.0 %row_maps.4 = (f32[512,256]{1,0:T(8,128)S(1)}, f32[2048,128]{1,0:T(8,128)S(1)}) custom-call(bf16[2048,128]{1,0:T(8,128)(2,1)S(1)} %get-tuple-element.45.q_ref, f32[2048,128]{1,0:T(8,128)S(1)} %get-tuple-element.46.k32, f32[16,128]{1,0:T(8,128)S(1)} %get-tuple-element.47.sums_ref, f32[12,128,128]{2,1,0:T(8,128)S(1)} %get-tuple-element.48.mix_ref, ...), custom_call_target="tpu_custom_call" | custom-call | flops 1000000000 | bytes 4000000 | tf_op jit(solution)/shard_map/row_maps/pallas_call | solution.py:310
  14.8 2.7 %collective-permute-start.3 = (bf16[128,128]{1,0:T(8,128)(2,1)S(1)}, bf16[128,128]{1,0:T(8,128)(2,1)S(1)}, u32[]{:S(2)}, u32[]{:S(2)}) collective-permute-start(bf16[128,128]{1,0:T(8,128)(2,1)S(1)} %group_state.1), channel_id=1, source_target_pairs={{0,16},{4,20},{8,24},{12,28},{16,0},{20,4},{24,8},{28,12},{1,17},{... | collective-permute-start | bytes 98312 | tf_op jit(solution)/shard_map/ppermute | solution.py:488
  17.4 1.0 %row_maps.5.refs_1_ = f32[512,256]{1,0:T(8,128)S(1)} custom-call(f32[2048,128]{1,0:T(8,128)S(1)} %get-tuple-element.73.q_ref, f32[2048,128]{1,0:T(8,128)S(1)} %get-tuple-element.46.k32, f32[16,128]{1,0:T(8,128)S(1)} %get-tuple-element.47.sums_ref, f32[12,128,128]{2,1,0:T(8,128)S(1)} %get-tuple-element.48.mix_ref, ...), custom_call_target="tpu_custom_call" | custom-call | flops 1000000000 | bytes 4000000 | tf_op jit(solution)/shard_map/row_maps/pallas_call | solution.py:310
  18.4 1.4 %group_prefix.1 = (bf16[4,128,256]{2,1,0:T(8,128)(2,1)S(1)}, f32[4,128,128]{2,1,0:T(8,128)S(1)}, bf16[128,256]{1,0:T(8,128)(2,1)}) custom-call(bf16[128,256]{1,0:T(8,128)(2,1)S(1)} %collective-permute-done.refs_0_, bf16[128,256]{1,0:T(8,128)(2,1)S(1)} %collective-permute-done.1.refs_1_, bf16[128,256]{1,0:T(8,128)(2,1)S(1)} %collective-permute-done.2.refs_2_, ...), custom_call_target="tpu_custom_call" | custom-call | tf_op jit(solution)/shard_map/group_prefix/pallas_call | solution.py:323
  20.1 2.3 %collective-permute-start.4 = (bf16[128,128]{1,0:T(8,128)(2,1)S(1)}, bf16[128,128]{1,0:T(8,128)(2,1)S(1)}, u32[]{:S(2)}, u32[]{:S(2)}) collective-permute-start(bf16[128,128]{1,0:T(8,128)(2,1)S(1)} %get-tuple-element.77), channel_id=1, source_target_pairs={{0,12},{4,8},{8,4},{12,0},{16,28},{20,24},{24,20},{28,16},{1,13},{... | collective-permute-start | bytes 98312 | tf_op jit(solution)/shard_map/ppermute | solution.py:488
  22.8 0.8 %collective-permute-start.6 = (bf16[128,128]{1,0:T(8,128)(2,1)S(1)}, bf16[128,128]{1,0:T(8,128)(2,1)S(1)}, u32[]{:S(2)}, u32[]{:S(2)}) collective-permute-start(bf16[128,128]{1,0:T(8,128)(2,1)S(1)} %get-tuple-element.79), channel_id=1, source_target_pairs={{0,4},{4,0},{8,12},{12,8},{16,20},{20,16},{24,28},{28,24},{1,5},{5... | collective-permute-start | bytes 98312 | tf_op jit(solution)/shard_map/ppermute | solution.py:488
  23.6 1.0 %row_maps.6.refs_2_ = f32[512,256]{1,0:T(8,128)S(1)} custom-call(f32[2048,128]{1,0:T(8,128)S(1)} %get-tuple-element.73.q_ref, f32[2048,128]{1,0:T(8,128)S(1)} %get-tuple-element.46.k32, f32[16,128]{1,0:T(8,128)S(1)} %get-tuple-element.47.sums_ref, f32[12,128,128]{2,1,0:T(8,128)S(1)} %get-tuple-element.48.mix_ref, ...), custom_call_target="tpu_custom_call" | custom-call | flops 1000000000 | bytes 4000000 | tf_op jit(solution)/shard_map/row_maps/pallas_call | solution.py:310
  24.6 1.0 %row_maps.7.refs_3_ = f32[512,256]{1,0:T(8,128)S(1)} custom-call(f32[2048,128]{1,0:T(8,128)S(1)} %get-tuple-element.73.q_ref, f32[2048,128]{1,0:T(8,128)S(1)} %get-tuple-element.46.k32, f32[16,128]{1,0:T(8,128)S(1)} %get-tuple-element.47.sums_ref, f32[4,128,128]{2,1,0:T(8,128)S(1)} %get-tuple-element.74.mix_ref, ...), custom_call_target="tpu_custom_call" | custom-call | flops 1000000000 | bytes 4000000 | tf_op jit(solution)/shard_map/row_maps/pallas_call | solution.py:310
  25.6 0.7 %collective-permute-done.5.refs_5_ = bf16[128,128]{1,0:T(8,128)(2,1)S(1)} collective-permute-done((bf16[128,128]{1,0:T(8,128)(2,1)S(1)}, bf16[128,128]{1,0:T(8,128)(2,1)S(1)}, u32[]{:S(2)}, u32[]{:S(2)}) %collective-permute-start.5) | collective-permute-done | bytes 32800 | tf_op jit(solution)/shard_map/ppermute | solution.py:488
  27.4 0.6 %collective-permute-start.7 = (bf16[128,512]{1,0:T(8,128)(2,1)S(1)}, bf16[128,512]{1,0:T(8,128)(2,1)S(1)}, u32[]{:S(2)}, u32[]{:S(2)}) collective-permute-start(bf16[128,512]{1,0:T(8,128)(2,1)S(1)} %get-tuple-element.82), channel_id=1, source_target_pairs={{0,1},{1,0},{2,3},{3,2},{4,5},{5,4},{6,7},{7,6},{8,9},{9,8},{10,11... | collective-permute-start | bytes 393224 | tf_op jit(solution)/shard_map/ppermute | solution.py:488
  28.8 1.6 %collective-permute-start.13 = (bf16[128,512]{1,0:T(8,128)(2,1)S(1)}, bf16[128,512]{1,0:T(8,128)(2,1)S(1)}, u32[]{:S(2)}, u32[]{:S(2)}) collective-permute-start(bf16[128,512]{1,0:T(8,128)(2,1)S(1)} %project.15), channel_id=1, source_target_pairs={{0,2},{1,3},{2,0},{3,1},{4,6},{5,7},{6,4},{7,5},{8,10},{9,11},{10,... | collective-permute-start | bytes 393224 | tf_op jit(solution)/shard_map/ppermute | solution.py:488
  30.7 0.6 %collective-permute-start.12 = (bf16[128,512]{1,0:T(8,128)(2,1)S(1)}, bf16[128,512]{1,0:T(8,128)(2,1)S(1)}, u32[]{:S(2)}, u32[]{:S(2)}) collective-permute-start(bf16[128,512]{1,0:T(8,128)(2,1)S(1)} %project.13), channel_id=1, source_target_pairs={{0,2},{1,3},{2,0},{3,1},{4,6},{5,7},{6,4},{7,5},{8,10},{9,11},{10,... | collective-permute-start | bytes 393224 | tf_op jit(solution)/shard_map/ppermute | solution.py:488
  31.6 1.6 %collective-permute-start.11 = (bf16[128,512]{1,0:T(8,128)(2,1)S(1)}, bf16[128,512]{1,0:T(8,128)(2,1)S(1)}, u32[]{:S(2)}, u32[]{:S(2)}) collective-permute-start(bf16[128,512]{1,0:T(8,128)(2,1)S(1)} %project.11), channel_id=1, source_target_pairs={{0,2},{1,3},{2,0},{3,1},{4,6},{5,7},{6,4},{7,5},{8,10},{9,11},{10,... | collective-permute-start | bytes 393224 | tf_op jit(solution)/shard_map/ppermute | solution.py:488
  33.5 0.6 %collective-permute-start.10 = (bf16[128,512]{1,0:T(8,128)(2,1)S(1)}, bf16[128,512]{1,0:T(8,128)(2,1)S(1)}, u32[]{:S(2)}, u32[]{:S(2)}) collective-permute-start(bf16[128,512]{1,0:T(8,128)(2,1)S(1)} %project.9), channel_id=1, source_target_pairs={{0,2},{1,3},{2,0},{3,1},{4,6},{5,7},{6,4},{7,5},{8,10},{9,11},{10,... | collective-permute-start | bytes 393224 | tf_op jit(solution)/shard_map/ppermute | solution.py:488
  35.3 0.7 %add_part.4.refs_0_ = bf16[128,2048]{1,0:T(8,128)(2,1)} custom-call(f32[128,512]{1,0:T(8,128)S(1)} %project.14.mine_ref, bf16[128,512]{1,0:T(8,128)(2,1)S(1)} %collective-permute-done.13.theirs_ref), custom_call_target="tpu_custom_call" | custom-call | tf_op jit(solution)/shard_map/add_part/pallas_call | solution.py:474
  36.0 2.0 %collective-permute-done.12.theirs_ref = bf16[128,512]{1,0:T(8,128)(2,1)S(1)} collective-permute-done((bf16[128,512]{1,0:T(8,128)(2,1)S(1)}, bf16[128,512]{1,0:T(8,128)(2,1)S(1)}, u32[]{:S(2)}, u32[]{:S(2)}) %collective-permute-start.12) | collective-permute-done | bytes 131104 | tf_op jit(solution)/shard_map/ppermute | solution.py:488
  38.0 0.7 %add_part.5.refs_0_ = bf16[128,2048]{1,0:T(8,128)(2,1)} custom-call(f32[128,512]{1,0:T(8,128)S(1)} %project.12.mine_ref, bf16[128,512]{1,0:T(8,128)(2,1)S(1)} %collective-permute-done.12.theirs_ref, bf16[128,2048]{1,0:T(8,128)(2,1)} %add_part.4.refs_0_), custom_call_target="tpu_custom_call", output_to_operand_aliasing={{}: (2, {})} | custom-call | tf_op jit(solution)/shard_map/add_part/pallas_call | solution.py:474
  38.7 2.1 %collective-permute-done.11.theirs_ref = bf16[128,512]{1,0:T(8,128)(2,1)S(1)} collective-permute-done((bf16[128,512]{1,0:T(8,128)(2,1)S(1)}, bf16[128,512]{1,0:T(8,128)(2,1)S(1)}, u32[]{:S(2)}, u32[]{:S(2)}) %collective-permute-start.11) | collective-permute-done | bytes 131104 | tf_op jit(solution)/shard_map/ppermute | solution.py:488
  40.8 0.7 %add_part.6.refs_0_ = bf16[128,2048]{1,0:T(8,128)(2,1)} custom-call(f32[128,512]{1,0:T(8,128)S(1)} %project.10.mine_ref, bf16[128,512]{1,0:T(8,128)(2,1)S(1)} %collective-permute-done.11.theirs_ref, bf16[128,2048]{1,0:T(8,128)(2,1)} %add_part.5.refs_0_), custom_call_target="tpu_custom_call", output_to_operand_aliasing={{}: (2, {})} | custom-call | tf_op jit(solution)/shard_map/add_part/pallas_call | solution.py:474
  41.5 1.3 %collective-permute-done.10.theirs_ref = bf16[128,512]{1,0:T(8,128)(2,1)S(1)} collective-permute-done((bf16[128,512]{1,0:T(8,128)(2,1)S(1)}, bf16[128,512]{1,0:T(8,128)(2,1)S(1)}, u32[]{:S(2)}, u32[]{:S(2)}) %collective-permute-start.10) | collective-permute-done | bytes 131104 | tf_op jit(solution)/shard_map/ppermute | solution.py:488
  42.8 0.7 %add_part.7 = bf16[128,2048]{1,0:T(8,128)(2,1)} custom-call(f32[128,512]{1,0:T(8,128)S(1)} %project.8.mine_ref, bf16[128,512]{1,0:T(8,128)(2,1)S(1)} %collective-permute-done.10.theirs_ref, bf16[128,2048]{1,0:T(8,128)(2,1)} %add_part.6.refs_0_), custom_call_target="tpu_custom_call", output_to_operand_aliasing={{}: (2, {})} | custom-call | tf_op jit(solution)/shard_map/add_part/pallas_call | solution.py:474
  (29 shorter events, 6.8 us)
Async XLA Ops:
  0.0 28.5 %collective-permute-start.8 = (bf16[512,2048]{1,0:T(8,128)(2,1)}, bf16[512,2048]{1,0:T(8,128)(2,1)S(1)}, u32[]{:S(2)}, u32[]{:S(2)}) collective-permute-start(bf16[512,2048]{1,0:T(8,128)(2,1)} %w_ref.15), channel_id=1, source_target_pairs={{0,1},{1,0},{2,3},{3,2},{4,5},{5,4},{6,7},{7,6},{8,9},{9,8},{10,11... | collective-permute-start | bytes 6291464 | tf_op jit(solution)/shard_map/ppermute | solution.py:488
  6.2 7.6 %collective-permute-start = (bf16[128,256]{1,0:T(8,128)(2,1)S(1)}, bf16[128,256]{1,0:T(8,128)(2,1)S(1)}, u32[]{:S(2)}, u32[]{:S(2)}) collective-permute-start(bf16[128,256]{1,0:T(8,128)(2,1)S(1)} %get-tuple-element.52), channel_id=1, source_target_pairs={{0,12},{4,8},{8,4},{12,0},{16,28},{20,24},{24,20},{28,16},{1,13},{... | collective-permute-start | bytes 196616 | tf_op jit(solution)/shard_map/ppermute | solution.py:488
  9.7 4.3 %collective-permute-start.1 = (bf16[128,256]{1,0:T(8,128)(2,1)S(1)}, bf16[128,256]{1,0:T(8,128)(2,1)S(1)}, u32[]{:S(2)}, u32[]{:S(2)}) collective-permute-start(bf16[128,256]{1,0:T(8,128)(2,1)S(1)} %get-tuple-element.53), channel_id=1, source_target_pairs={{0,8},{4,12},{8,0},{12,4},{16,24},{20,28},{24,16},{28,20},{1,9},{5... | collective-permute-start | bytes 196616 | tf_op jit(solution)/shard_map/ppermute | solution.py:488
  10.2 4.3 %collective-permute-start.2 = (bf16[128,256]{1,0:T(8,128)(2,1)S(1)}, bf16[128,256]{1,0:T(8,128)(2,1)S(1)}, u32[]{:S(2)}, u32[]{:S(2)}) collective-permute-start(bf16[128,256]{1,0:T(8,128)(2,1)S(1)} %get-tuple-element.54), channel_id=1, source_target_pairs={{0,4},{4,0},{8,12},{12,8},{16,20},{20,16},{24,28},{28,24},{1,5},{5... | collective-permute-start | bytes 196616 | tf_op jit(solution)/shard_map/ppermute | solution.py:488
  14.8 5.0 %collective-permute-start.3 = (bf16[128,128]{1,0:T(8,128)(2,1)S(1)}, bf16[128,128]{1,0:T(8,128)(2,1)S(1)}, u32[]{:S(2)}, u32[]{:S(2)}) collective-permute-start(bf16[128,128]{1,0:T(8,128)(2,1)S(1)} %group_state.1), channel_id=1, source_target_pairs={{0,16},{4,20},{8,24},{12,28},{16,0},{20,4},{24,8},{28,12},{1,17},{... | collective-permute-start | bytes 98312 | tf_op jit(solution)/shard_map/ppermute | solution.py:488
  20.1 5.6 %collective-permute-start.4 = (bf16[128,128]{1,0:T(8,128)(2,1)S(1)}, bf16[128,128]{1,0:T(8,128)(2,1)S(1)}, u32[]{:S(2)}, u32[]{:S(2)}) collective-permute-start(bf16[128,128]{1,0:T(8,128)(2,1)S(1)} %get-tuple-element.77), channel_id=1, source_target_pairs={{0,12},{4,8},{8,4},{12,0},{16,28},{20,24},{24,20},{28,16},{1,13},{... | collective-permute-start | bytes 98312 | tf_op jit(solution)/shard_map/ppermute | solution.py:488
  22.4 3.9 %collective-permute-start.5 = (bf16[128,128]{1,0:T(8,128)(2,1)S(1)}, bf16[128,128]{1,0:T(8,128)(2,1)S(1)}, u32[]{:S(2)}, u32[]{:S(2)}) collective-permute-start(bf16[128,128]{1,0:T(8,128)(2,1)S(1)} %get-tuple-element.78), channel_id=1, source_target_pairs={{0,8},{4,12},{8,0},{12,4},{16,24},{20,28},{24,16},{28,20},{1,9},{5... | collective-permute-start | bytes 98312 | tf_op jit(solution)/shard_map/ppermute | solution.py:488
  22.8 3.9 %collective-permute-start.6 = (bf16[128,128]{1,0:T(8,128)(2,1)S(1)}, bf16[128,128]{1,0:T(8,128)(2,1)S(1)}, u32[]{:S(2)}, u32[]{:S(2)}) collective-permute-start(bf16[128,128]{1,0:T(8,128)(2,1)S(1)} %get-tuple-element.79), channel_id=1, source_target_pairs={{0,4},{4,0},{8,12},{12,8},{16,20},{20,16},{24,28},{28,24},{1,5},{5... | collective-permute-start | bytes 98312 | tf_op jit(solution)/shard_map/ppermute | solution.py:488
  25.6 2.9 %copy-start = (bf16[512,2048]{1,0:T(8,128)(2,1)S(1)}, bf16[512,2048]{1,0:T(8,128)(2,1)}, u32[]{:S(2)}) copy-start(bf16[512,2048]{1,0:T(8,128)(2,1)} %w_ref.15) | copy-start | bytes 6291460
  27.0 1.4 %collective-permute-start.9 = (bf16[128,512]{1,0:T(8,128)(2,1)S(1)}, bf16[128,512]{1,0:T(8,128)(2,1)S(1)}, u32[]{:S(2)}, u32[]{:S(2)}) collective-permute-start(bf16[128,512]{1,0:T(8,128)(2,1)S(1)} %get-tuple-element.84), channel_id=1, source_target_pairs={{0,1},{1,0},{2,3},{3,2},{4,5},{5,4},{6,7},{7,6},{8,9},{9,8},{10,11... | collective-permute-start | bytes 393224 | tf_op jit(solution)/shard_map/ppermute | solution.py:488
  27.4 6.6 %collective-permute-start.7 = (bf16[128,512]{1,0:T(8,128)(2,1)S(1)}, bf16[128,512]{1,0:T(8,128)(2,1)S(1)}, u32[]{:S(2)}, u32[]{:S(2)}) collective-permute-start(bf16[128,512]{1,0:T(8,128)(2,1)S(1)} %get-tuple-element.82), channel_id=1, source_target_pairs={{0,1},{1,0},{2,3},{3,2},{4,5},{5,4},{6,7},{7,6},{8,9},{9,8},{10,11... | collective-permute-start | bytes 393224 | tf_op jit(solution)/shard_map/ppermute | solution.py:488
  28.8 6.5 %collective-permute-start.13 = (bf16[128,512]{1,0:T(8,128)(2,1)S(1)}, bf16[128,512]{1,0:T(8,128)(2,1)S(1)}, u32[]{:S(2)}, u32[]{:S(2)}) collective-permute-start(bf16[128,512]{1,0:T(8,128)(2,1)S(1)} %project.15), channel_id=1, source_target_pairs={{0,2},{1,3},{2,0},{3,1},{4,6},{5,7},{6,4},{7,5},{8,10},{9,11},{10,... | collective-permute-start | bytes 393224 | tf_op jit(solution)/shard_map/ppermute | solution.py:488
  30.7 7.3 %collective-permute-start.12 = (bf16[128,512]{1,0:T(8,128)(2,1)S(1)}, bf16[128,512]{1,0:T(8,128)(2,1)S(1)}, u32[]{:S(2)}, u32[]{:S(2)}) collective-permute-start(bf16[128,512]{1,0:T(8,128)(2,1)S(1)} %project.13), channel_id=1, source_target_pairs={{0,2},{1,3},{2,0},{3,1},{4,6},{5,7},{6,4},{7,5},{8,10},{9,11},{10,... | collective-permute-start | bytes 393224 | tf_op jit(solution)/shard_map/ppermute | solution.py:488
  31.6 9.2 %collective-permute-start.11 = (bf16[128,512]{1,0:T(8,128)(2,1)S(1)}, bf16[128,512]{1,0:T(8,128)(2,1)S(1)}, u32[]{:S(2)}, u32[]{:S(2)}) collective-permute-start(bf16[128,512]{1,0:T(8,128)(2,1)S(1)} %project.11), channel_id=1, source_target_pairs={{0,2},{1,3},{2,0},{3,1},{4,6},{5,7},{6,4},{7,5},{8,10},{9,11},{10,... | collective-permute-start | bytes 393224 | tf_op jit(solution)/shard_map/ppermute | solution.py:488
  33.5 9.4 %collective-permute-start.10 = (bf16[128,512]{1,0:T(8,128)(2,1)S(1)}, bf16[128,512]{1,0:T(8,128)(2,1)S(1)}, u32[]{:S(2)}, u32[]{:S(2)}) collective-permute-start(bf16[128,512]{1,0:T(8,128)(2,1)S(1)} %project.9), channel_id=1, source_target_pairs={{0,2},{1,3},{2,0},{3,1},{4,6},{5,7},{6,4},{7,5},{8,10},{9,11},{10,... | collective-permute-start | bytes 393224 | tf_op jit(solution)/shard_map/ppermute | solution.py:488

commit v24 on v21

--- a/solution.py
+++ b/solution.py
@@ -493,7 +493,6 @@
     tokens, heads, _ = key.shape
     count = lax.axis_size("seq")
     flat = lambda x: x.reshape(tokens * heads, C)
-    weight2 = swap(out_weight, "head", 1)
     q16, k32, v32, sums, betas, mix, wu, states, *sends = first_maps(
         flat(key), flat(value), beta, log_decay, flat(query)
     )
@@ -508,7 +507,8 @@
     both = jax.ShapeDtypeStruct((heads, C, 2 * C), BF16)
     added = jax.ShapeDtypeStruct((heads, C, C), F32)
     (state,) = small_call(group_state, [square], *parts)
-    state, q32 = lax.optimization_barrier((state, q32))
+    state, q32, sent_weight = lax.optimization_barrier((state, q32, out_weight))
+    weight2 = swap(sent_weight, "head", 1)
     (rows2,) = row_maps(heads, 1, 1, q32, *first)
     *maps, total = small_call(group_prefix, [both, added, jax.ShapeDtypeStruct((C, 2 * C), BF16)], *parts)
     if count == 2 * heads:

time: 43.6 us -> 43.7 us (level)
  transfers between devices with their start and end apart: 14 -> 14, of which waited for: 8 -> 6; matrix products, arithmetic and copies ran while one was open for 0% -> 0% of each run, Pallas kernels for 44% -> 30%
where the time goes in v24:
time: 43.7 us; the launch traced here: 43.5 us
  Pallas kernels  19.7 us (45%)
  starting transfers between devices  15.9 us (36%)
  waiting for transfers between devices  7.73 us (18%)
    ppermute x14, starting transfers between devices, swap(): return lax.ppermute(x, axis, [(i, i ^ bit) for i in range(count)])  15.9 us
    ppermute x14, waiting for transfers between devices, swap(): return lax.ppermute(x, axis, [(i, i ^ bit) for i in range(count)])  7.73 us
    pallas_call x1, Pallas kernels, first_maps(): pl.pallas_call(functools.partial(first_kernel, heads), in_specs=[pl.Block...  5.53 us
    pallas_call x4, Pallas kernels, row_maps(): pl.pallas_call(functools.partial(rows_kernel, heads, spot, slot), in_spec...  3.98 us
    pallas_call x4, Pallas kernels, add_part(): pl.pallas_call(add_kernel, grid=(1,), in_specs=[here, here] + [pl.BlockSp...  2.72 us
    pallas_call x8, Pallas kernels, project(): pl.pallas_call(functools.partial(project_kernel, start), out_shape=jax.Sh...  2.48 us
    pallas_call x1, Pallas kernels, own_maps(): pl.pallas_call(functools.partial(own_kernel, heads), in_specs=[here] * 4,...  2.39 us
    pallas_call x3, Pallas kernels, small_call(): pl.pallas_call(kernel, in_specs=[here] * len(args), out_specs=[here] * le...  1.96 us
  transfers between devices with their start and end apart: 14, of which 6 were waited for; matrix products, arithmetic and copies ran while one was open for 0% of the time, Pallas kernels for 30%

profile of v24, /device:TPU:0, one launch (start us, length us, event | category | flops | bytes accessed | tf_op | source)
XLA Modules:
  0.0 43.5 jit_solution(15364549071414655339)
XLA Ops:
  0.0 5.5 %first_maps.1 = (bf16[2048,128]{1,0:T(8,128)(2,1)S(1)}, f32[2048,128]{1,0:T(8,128)S(1)}, f32[2048,128]{1,0:T(8,128)S(1)}, f32[16,128]{1,0:T(8,128)S(1)}, f32[16,...) custom-call(bf16[2048,128]{1,0:T(8,128)(2,1)} %bitcast.3, ...), custom_call_target="tpu_custom_call" | custom-call | tf_op jit(solution)/shard_map/first_maps/pallas_call | solution.py:244
  5.5 4.0 %collective-permute-start = (bf16[128,256]{1,0:T(8,128)(2,1)S(1)}, bf16[128,256]{1,0:T(8,128)(2,1)S(1)}, u32[]{:S(2)}, u32[]{:S(2)}) collective-permute-start(bf16[128,256]{1,0:T(8,128)(2,1)S(1)} %get-tuple-element.53), channel_id=1, source_target_pairs={{0,12},{4,8},{8,4},{12,0},{16,28},{20,24},{24,20},{28,16},{1,13},{... | collective-permute-start | bytes 196616 | tf_op jit(solution)/shard_map/ppermute | solution.py:489
  9.6 0.5 %collective-permute-start.1 = (bf16[128,256]{1,0:T(8,128)(2,1)S(1)}, bf16[128,256]{1,0:T(8,128)(2,1)S(1)}, u32[]{:S(2)}, u32[]{:S(2)}) collective-permute-start(bf16[128,256]{1,0:T(8,128)(2,1)S(1)} %get-tuple-element.54), channel_id=1, source_target_pairs={{0,8},{4,12},{8,0},{12,4},{16,24},{20,28},{24,16},{28,20},{1,9},{5... | collective-permute-start | bytes 196616 | tf_op jit(solution)/shard_map/ppermute | solution.py:489
  10.2 2.4 %own_maps.1 = (f32[4,128,128]{2,1,0:T(8,128)S(1)}, f32[4,128,256]{2,1,0:T(8,128)S(1)}, f32[4,128,256]{2,1,0:T(8,128)S(1)}, bf16[128,256]{1,0:T(8,128)(2,1)S(1)}) custom-call(f32[2048,128]{1,0:T(8,128)S(1)} %get-tuple-element.47.k32, f32[2048,128]{1,0:T(8,128)S(1)} %get-tuple-element.56.v32, f32[16,128]{1,0:T(8,128)S(1)} %get-tuple-element.48.sums_ref, ...), custom_call_target="tpu_custom_call" | custom-call | flops 2000000000 | bytes 8000000 | tf_op jit(solution)/shard_map/own_maps/pallas_call | solution.py:270
  12.6 1.0 %row_maps.4 = (f32[512,256]{1,0:T(8,128)S(1)}, f32[2048,128]{1,0:T(8,128)S(1)}) custom-call(bf16[2048,128]{1,0:T(8,128)(2,1)S(1)} %get-tuple-element.46.q_ref, f32[2048,128]{1,0:T(8,128)S(1)} %get-tuple-element.47.k32, f32[16,128]{1,0:T(8,128)S(1)} %get-tuple-element.48.sums_ref, f32[12,128,128]{2,1,0:T(8,128)S(1)} %get-tuple-element.49.mix_ref, ...), custom_call_target="tpu_custom_call" | custom-call | flops 1000000000 | bytes 4000000 | tf_op jit(solution)/shard_map/row_maps/pallas_call | solution.py:311
  14.7 2.6 %collective-permute-start.3 = (bf16[128,128]{1,0:T(8,128)(2,1)S(1)}, bf16[128,128]{1,0:T(8,128)(2,1)S(1)}, u32[]{:S(2)}, u32[]{:S(2)}) collective-permute-start(bf16[128,128]{1,0:T(8,128)(2,1)S(1)} %group_state.1), channel_id=1, source_target_pairs={{0,16},{4,20},{8,24},{12,28},{16,0},{20,4},{24,8},{28,12},{1,17},{... | collective-permute-start | bytes 98312 | tf_op jit(solution)/shard_map/ppermute | solution.py:489
  17.4 1.0 %row_maps.5.refs_1_ = f32[512,256]{1,0:T(8,128)S(1)} custom-call(f32[2048,128]{1,0:T(8,128)S(1)} %get-tuple-element.74.q_ref, f32[2048,128]{1,0:T(8,128)S(1)} %get-tuple-element.47.k32, f32[16,128]{1,0:T(8,128)S(1)} %get-tuple-element.48.sums_ref, f32[12,128,128]{2,1,0:T(8,128)S(1)} %get-tuple-element.49.mix_ref, ...), custom_call_target="tpu_custom_call" | custom-call | flops 1000000000 | bytes 4000000 | tf_op jit(solution)/shard_map/row_maps/pallas_call | solution.py:311
  18.3 1.4 %group_prefix.1 = (bf16[4,128,256]{2,1,0:T(8,128)(2,1)S(1)}, f32[4,128,128]{2,1,0:T(8,128)S(1)}, bf16[128,256]{1,0:T(8,128)(2,1)}) custom-call(bf16[128,256]{1,0:T(8,128)(2,1)S(1)} %collective-permute-done.refs_0_, bf16[128,256]{1,0:T(8,128)(2,1)S(1)} %collective-permute-done.1.refs_1_, bf16[128,256]{1,0:T(8,128)(2,1)S(1)} %collective-permute-done.2.refs_2_, ...), custom_call_target="tpu_custom_call" | custom-call | tf_op jit(solution)/shard_map/group_prefix/pallas_call | solution.py:324
  20.0 2.3 %collective-permute-start.4 = (bf16[128,128]{1,0:T(8,128)(2,1)S(1)}, bf16[128,128]{1,0:T(8,128)(2,1)S(1)}, u32[]{:S(2)}, u32[]{:S(2)}) collective-permute-start(bf16[128,128]{1,0:T(8,128)(2,1)S(1)} %get-tuple-element.78), channel_id=1, source_target_pairs={{0,12},{4,8},{8,4},{12,0},{16,28},{20,24},{24,20},{28,16},{1,13},{... | collective-permute-start | bytes 98312 | tf_op jit(solution)/shard_map/ppermute | solution.py:489
  22.7 0.8 %collective-permute-start.6 = (bf16[128,128]{1,0:T(8,128)(2,1)S(1)}, bf16[128,128]{1,0:T(8,128)(2,1)S(1)}, u32[]{:S(2)}, u32[]{:S(2)}) collective-permute-start(bf16[128,128]{1,0:T(8,128)(2,1)S(1)} %get-tuple-element.80), channel_id=1, source_target_pairs={{0,4},{4,0},{8,12},{12,8},{16,20},{20,16},{24,28},{28,24},{1,5},{5... | collective-permute-start | bytes 98312 | tf_op jit(solution)/shard_map/ppermute | solution.py:489
  23.5 1.0 %row_maps.6.refs_2_ = f32[512,256]{1,0:T(8,128)S(1)} custom-call(f32[2048,128]{1,0:T(8,128)S(1)} %get-tuple-element.74.q_ref, f32[2048,128]{1,0:T(8,128)S(1)} %get-tuple-element.47.k32, f32[16,128]{1,0:T(8,128)S(1)} %get-tuple-element.48.sums_ref, f32[12,128,128]{2,1,0:T(8,128)S(1)} %get-tuple-element.49.mix_ref, ...), custom_call_target="tpu_custom_call" | custom-call | flops 1000000000 | bytes 4000000 | tf_op jit(solution)/shard_map/row_maps/pallas_call | solution.py:311
  24.5 1.0 %row_maps.7.refs_3_ = f32[512,256]{1,0:T(8,128)S(1)} custom-call(f32[2048,128]{1,0:T(8,128)S(1)} %get-tuple-element.74.q_ref, f32[2048,128]{1,0:T(8,128)S(1)} %get-tuple-element.47.k32, f32[16,128]{1,0:T(8,128)S(1)} %get-tuple-element.48.sums_ref, f32[4,128,128]{2,1,0:T(8,128)S(1)} %get-tuple-element.75.mix_ref, ...), custom_call_target="tpu_custom_call" | custom-call | flops 1000000000 | bytes 4000000 | tf_op jit(solution)/shard_map/row_maps/pallas_call | solution.py:311
  25.5 0.7 %collective-permute-done.5.refs_5_ = bf16[128,128]{1,0:T(8,128)(2,1)S(1)} collective-permute-done((bf16[128,128]{1,0:T(8,128)(2,1)S(1)}, bf16[128,128]{1,0:T(8,128)(2,1)S(1)}, u32[]{:S(2)}, u32[]{:S(2)}) %collective-permute-start.5) | collective-permute-done | bytes 32800 | tf_op jit(solution)/shard_map/ppermute | solution.py:489
  27.4 0.6 %collective-permute-start.7 = (bf16[128,512]{1,0:T(8,128)(2,1)S(1)}, bf16[128,512]{1,0:T(8,128)(2,1)S(1)}, u32[]{:S(2)}, u32[]{:S(2)}) collective-permute-start(bf16[128,512]{1,0:T(8,128)(2,1)S(1)} %get-tuple-element.83), channel_id=1, source_target_pairs={{0,1},{1,0},{2,3},{3,2},{4,5},{5,4},{6,7},{7,6},{8,9},{9,8},{10,11... | collective-permute-start | bytes 393224 | tf_op jit(solution)/shard_map/ppermute | solution.py:489
  27.9 0.5 %collective-permute-done.9.got_ref = bf16[128,512]{1,0:T(8,128)(2,1)S(1)} collective-permute-done((bf16[128,512]{1,0:T(8,128)(2,1)S(1)}, bf16[128,512]{1,0:T(8,128)(2,1)S(1)}, u32[]{:S(2)}, u32[]{:S(2)}) %collective-permute-start.9) | collective-permute-done | bytes 131104 | tf_op jit(solution)/shard_map/ppermute | solution.py:489
  28.7 1.6 %collective-permute-start.11 = (bf16[128,512]{1,0:T(8,128)(2,1)S(1)}, bf16[128,512]{1,0:T(8,128)(2,1)S(1)}, u32[]{:S(2)}, u32[]{:S(2)}) collective-permute-start(bf16[128,512]{1,0:T(8,128)(2,1)S(1)} %project.11), channel_id=1, source_target_pairs={{0,2},{1,3},{2,0},{3,1},{4,6},{5,7},{6,4},{7,5},{8,10},{9,11},{10,... | collective-permute-start | bytes 393224 | tf_op jit(solution)/shard_map/ppermute | solution.py:489
  30.6 0.6 %collective-permute-start.12 = (bf16[128,512]{1,0:T(8,128)(2,1)S(1)}, bf16[128,512]{1,0:T(8,128)(2,1)S(1)}, u32[]{:S(2)}, u32[]{:S(2)}) collective-permute-start(bf16[128,512]{1,0:T(8,128)(2,1)S(1)} %project.13), channel_id=1, source_target_pairs={{0,2},{1,3},{2,0},{3,1},{4,6},{5,7},{6,4},{7,5},{8,10},{9,11},{10,... | collective-permute-start | bytes 393224 | tf_op jit(solution)/shard_map/ppermute | solution.py:489
  31.5 1.6 %collective-permute-start.13 = (bf16[128,512]{1,0:T(8,128)(2,1)S(1)}, bf16[128,512]{1,0:T(8,128)(2,1)S(1)}, u32[]{:S(2)}, u32[]{:S(2)}) collective-permute-start(bf16[128,512]{1,0:T(8,128)(2,1)S(1)} %project.15), channel_id=1, source_target_pairs={{0,2},{1,3},{2,0},{3,1},{4,6},{5,7},{6,4},{7,5},{8,10},{9,11},{10,... | collective-permute-start | bytes 393224 | tf_op jit(solution)/shard_map/ppermute | solution.py:489
  33.4 0.6 %collective-permute-start.10 = (bf16[128,512]{1,0:T(8,128)(2,1)S(1)}, bf16[128,512]{1,0:T(8,128)(2,1)S(1)}, u32[]{:S(2)}, u32[]{:S(2)}) collective-permute-start(bf16[128,512]{1,0:T(8,128)(2,1)S(1)} %project.9), channel_id=1, source_target_pairs={{0,2},{1,3},{2,0},{3,1},{4,6},{5,7},{6,4},{7,5},{8,10},{9,11},{10,... | collective-permute-start | bytes 393224 | tf_op jit(solution)/shard_map/ppermute | solution.py:489
  35.2 5.5 %collective-permute-done.13.theirs_ref = bf16[128,512]{1,0:T(8,128)(2,1)S(1)} collective-permute-done((bf16[128,512]{1,0:T(8,128)(2,1)S(1)}, bf16[128,512]{1,0:T(8,128)(2,1)S(1)}, u32[]{:S(2)}, u32[]{:S(2)}) %collective-permute-start.13) | collective-permute-done | bytes 131104 | tf_op jit(solution)/shard_map/ppermute | solution.py:489
  40.7 0.7 %add_part.4.refs_0_ = bf16[128,2048]{1,0:T(8,128)(2,1)} custom-call(f32[128,512]{1,0:T(8,128)S(1)} %project.14.mine_ref, bf16[128,512]{1,0:T(8,128)(2,1)S(1)} %collective-permute-done.13.theirs_ref), custom_call_target="tpu_custom_call" | custom-call | tf_op jit(solution)/shard_map/add_part/pallas_call | solution.py:475
  41.4 0.7 %add_part.5.refs_0_ = bf16[128,2048]{1,0:T(8,128)(2,1)} custom-call(f32[128,512]{1,0:T(8,128)S(1)} %project.12.mine_ref, bf16[128,512]{1,0:T(8,128)(2,1)S(1)} %collective-permute-done.12.theirs_ref, bf16[128,2048]{1,0:T(8,128)(2,1)} %add_part.4.refs_0_), custom_call_target="tpu_custom_call", output_to_operand_aliasing={{}: (2, {})} | custom-call | tf_op jit(solution)/shard_map/add_part/pallas_call | solution.py:475
  42.1 0.7 %add_part.6.refs_0_ = bf16[128,2048]{1,0:T(8,128)(2,1)} custom-call(f32[128,512]{1,0:T(8,128)S(1)} %project.10.mine_ref, bf16[128,512]{1,0:T(8,128)(2,1)S(1)} %collective-permute-done.11.theirs_ref, bf16[128,2048]{1,0:T(8,128)(2,1)} %add_part.5.refs_0_), custom_call_target="tpu_custom_call", output_to_operand_aliasing={{}: (2, {})} | custom-call | tf_op jit(solution)/shard_map/add_part/pallas_call | solution.py:475
  42.8 0.7 %add_part.7 = bf16[128,2048]{1,0:T(8,128)(2,1)} custom-call(f32[128,512]{1,0:T(8,128)S(1)} %project.8.mine_ref, bf16[128,512]{1,0:T(8,128)(2,1)S(1)} %collective-permute-done.10.theirs_ref, bf16[128,2048]{1,0:T(8,128)(2,1)} %add_part.6.refs_0_), custom_call_target="tpu_custom_call", output_to_operand_aliasing={{}: (2, {})} | custom-call | tf_op jit(solution)/shard_map/add_part/pallas_call | solution.py:475
  (29 shorter events, 5.5 us)
Async XLA Ops:
  5.5 8.1 %collective-permute-start = (bf16[128,256]{1,0:T(8,128)(2,1)S(1)}, bf16[128,256]{1,0:T(8,128)(2,1)S(1)}, u32[]{:S(2)}, u32[]{:S(2)}) collective-permute-start(bf16[128,256]{1,0:T(8,128)(2,1)S(1)} %get-tuple-element.53), channel_id=1, source_target_pairs={{0,12},{4,8},{8,4},{12,0},{16,28},{20,24},{24,20},{28,16},{1,13},{... | collective-permute-start | bytes 196616 | tf_op jit(solution)/shard_map/ppermute | solution.py:489
  9.6 4.3 %collective-permute-start.1 = (bf16[128,256]{1,0:T(8,128)(2,1)S(1)}, bf16[128,256]{1,0:T(8,128)(2,1)S(1)}, u32[]{:S(2)}, u32[]{:S(2)}) collective-permute-start(bf16[128,256]{1,0:T(8,128)(2,1)S(1)} %get-tuple-element.54), channel_id=1, source_target_pairs={{0,8},{4,12},{8,0},{12,4},{16,24},{20,28},{24,16},{28,20},{1,9},{5... | collective-permute-start | bytes 196616 | tf_op jit(solution)/shard_map/ppermute | solution.py:489
  10.0 4.3 %collective-permute-start.2 = (bf16[128,256]{1,0:T(8,128)(2,1)S(1)}, bf16[128,256]{1,0:T(8,128)(2,1)S(1)}, u32[]{:S(2)}, u32[]{:S(2)}) collective-permute-start(bf16[128,256]{1,0:T(8,128)(2,1)S(1)} %get-tuple-element.55), channel_id=1, source_target_pairs={{0,4},{4,0},{8,12},{12,8},{16,20},{20,16},{24,28},{28,24},{1,5},{5... | collective-permute-start | bytes 196616 | tf_op jit(solution)/shard_map/ppermute | solution.py:489
  12.6 2.0 %copy-start = (bf16[512,2048]{1,0:T(8,128)(2,1)S(1)}, bf16[512,2048]{1,0:T(8,128)(2,1)}, u32[]{:S(2)}) copy-start(bf16[512,2048]{1,0:T(8,128)(2,1)} %w_ref.15) | copy-start | bytes 6291460
  14.6 13.8 %collective-permute-start.8 = (bf16[512,2048]{1,0:T(8,128)(2,1)S(1)}, bf16[512,2048]{1,0:T(8,128)(2,1)S(1)}, u32[]{:S(2)}, u32[]{:S(2)}) collective-permute-start(bf16[512,2048]{1,0:T(8,128)(2,1)S(1)} %copy-done), channel_id=1, source_target_pairs={{0,1},{1,0},{2,3},{3,2},{4,5},{5,4},{6,7},{7,6},{8,9},{9,8},{10,11... | collective-permute-start | bytes 6291464 | tf_op jit(solution)/shard_map/ppermute | solution.py:489
  14.7 5.0 %collective-permute-start.3 = (bf16[128,128]{1,0:T(8,128)(2,1)S(1)}, bf16[128,128]{1,0:T(8,128)(2,1)S(1)}, u32[]{:S(2)}, u32[]{:S(2)}) collective-permute-start(bf16[128,128]{1,0:T(8,128)(2,1)S(1)} %group_state.1), channel_id=1, source_target_pairs={{0,16},{4,20},{8,24},{12,28},{16,0},{20,4},{24,8},{28,12},{1,17},{... | collective-permute-start | bytes 98312 | tf_op jit(solution)/shard_map/ppermute | solution.py:489
  20.0 5.5 %collective-permute-start.4 = (bf16[128,128]{1,0:T(8,128)(2,1)S(1)}, bf16[128,128]{1,0:T(8,128)(2,1)S(1)}, u32[]{:S(2)}, u32[]{:S(2)}) collective-permute-start(bf16[128,128]{1,0:T(8,128)(2,1)S(1)} %get-tuple-element.78), channel_id=1, source_target_pairs={{0,12},{4,8},{8,4},{12,0},{16,28},{20,24},{24,20},{28,16},{1,13},{... | collective-permute-start | bytes 98312 | tf_op jit(solution)/shard_map/ppermute | solution.py:489
  22.3 3.9 %collective-permute-start.5 = (bf16[128,128]{1,0:T(8,128)(2,1)S(1)}, bf16[128,128]{1,0:T(8,128)(2,1)S(1)}, u32[]{:S(2)}, u32[]{:S(2)}) collective-permute-start(bf16[128,128]{1,0:T(8,128)(2,1)S(1)} %get-tuple-element.79), channel_id=1, source_target_pairs={{0,8},{4,12},{8,0},{12,4},{16,24},{20,28},{24,16},{28,20},{1,9},{5... | collective-permute-start | bytes 98312 | tf_op jit(solution)/shard_map/ppermute | solution.py:489
  22.7 3.9 %collective-permute-start.6 = (bf16[128,128]{1,0:T(8,128)(2,1)S(1)}, bf16[128,128]{1,0:T(8,128)(2,1)S(1)}, u32[]{:S(2)}, u32[]{:S(2)}) collective-permute-start(bf16[128,128]{1,0:T(8,128)(2,1)S(1)} %get-tuple-element.80), channel_id=1, source_target_pairs={{0,4},{4,0},{8,12},{12,8},{16,20},{20,16},{24,28},{28,24},{1,5},{5... | collective-permute-start | bytes 98312 | tf_op jit(solution)/shard_map/ppermute | solution.py:489
  27.0 1.4 %collective-permute-start.9 = (bf16[128,512]{1,0:T(8,128)(2,1)S(1)}, bf16[128,512]{1,0:T(8,128)(2,1)S(1)}, u32[]{:S(2)}, u32[]{:S(2)}) collective-permute-start(bf16[128,512]{1,0:T(8,128)(2,1)S(1)} %get-tuple-element.86), channel_id=1, source_target_pairs={{0,1},{1,0},{2,3},{3,2},{4,5},{5,4},{6,7},{7,6},{8,9},{9,8},{10,11... | collective-permute-start | bytes 393224 | tf_op jit(solution)/shard_map/ppermute | solution.py:489
  27.4 6.6 %collective-permute-start.7 = (bf16[128,512]{1,0:T(8,128)(2,1)S(1)}, bf16[128,512]{1,0:T(8,128)(2,1)S(1)}, u32[]{:S(2)}, u32[]{:S(2)}) collective-permute-start(bf16[128,512]{1,0:T(8,128)(2,1)S(1)} %get-tuple-element.83), channel_id=1, source_target_pairs={{0,1},{1,0},{2,3},{3,2},{4,5},{5,4},{6,7},{7,6},{8,9},{9,8},{10,11... | collective-permute-start | bytes 393224 | tf_op jit(solution)/shard_map/ppermute | solution.py:489
  28.7 13.4 %collective-permute-start.11 = (bf16[128,512]{1,0:T(8,128)(2,1)S(1)}, bf16[128,512]{1,0:T(8,128)(2,1)S(1)}, u32[]{:S(2)}, u32[]{:S(2)}) collective-permute-start(bf16[128,512]{1,0:T(8,128)(2,1)S(1)} %project.11), channel_id=1, source_target_pairs={{0,2},{1,3},{2,0},{3,1},{4,6},{5,7},{6,4},{7,5},{8,10},{9,11},{10,... | collective-permute-start | bytes 393224 | tf_op jit(solution)/shard_map/ppermute | solution.py:489
  30.6 10.8 %collective-permute-start.12 = (bf16[128,512]{1,0:T(8,128)(2,1)S(1)}, bf16[128,512]{1,0:T(8,128)(2,1)S(1)}, u32[]{:S(2)}, u32[]{:S(2)}) collective-permute-start(bf16[128,512]{1,0:T(8,128)(2,1)S(1)} %project.13), channel_id=1, source_target_pairs={{0,2},{1,3},{2,0},{3,1},{4,6},{5,7},{6,4},{7,5},{8,10},{9,11},{10,... | collective-permute-start | bytes 393224 | tf_op jit(solution)/shard_map/ppermute | solution.py:489
  31.5 9.2 %collective-permute-start.13 = (bf16[128,512]{1,0:T(8,128)(2,1)S(1)}, bf16[128,512]{1,0:T(8,128)(2,1)S(1)}, u32[]{:S(2)}, u32[]{:S(2)}) collective-permute-start(bf16[128,512]{1,0:T(8,128)(2,1)S(1)} %project.15), channel_id=1, source_target_pairs={{0,2},{1,3},{2,0},{3,1},{4,6},{5,7},{6,4},{7,5},{8,10},{9,11},{10,... | collective-permute-start | bytes 393224 | tf_op jit(solution)/shard_map/ppermute | solution.py:489
  33.4 9.4 %collective-permute-start.10 = (bf16[128,512]{1,0:T(8,128)(2,1)S(1)}, bf16[128,512]{1,0:T(8,128)(2,1)S(1)}, u32[]{:S(2)}, u32[]{:S(2)}) collective-permute-start(bf16[128,512]{1,0:T(8,128)(2,1)S(1)} %project.9), channel_id=1, source_target_pairs={{0,2},{1,3},{2,0},{3,1},{4,6},{5,7},{6,4},{7,5},{8,10},{9,11},{10,... | collective-permute-start | bytes 393224 | tf_op jit(solution)/shard_map/ppermute | solution.py:489
